TPU v7x, 32 devices: a whole 2x2x4 slice. The times are simulated.
32 devices in a mesh: dp: 8 (over y, x, core), mp: 4 (over z).
Axes of the slice: x: 2, y: 2, z: 4, core: 2. Of those that a mesh axis runs over, the one named last changes fastest.
Arguments:
- queries: bfloat16 [1024, 64, 128], P('dp', 'mp'), may hold values from -6 to 6
- key_cache: bfloat16 [1024, 8, 128, 128], P('dp', 'mp'), may hold values from -6 to 6
- value_cache: bfloat16 [1024, 8, 128, 128], P('dp', 'mp'), may hold values from -6 to 6
- key_new: bfloat16 [1024, 8, 128], P('dp', 'mp'), may hold values from -6 to 6
- value_new: bfloat16 [1024, 8, 128], P('dp', 'mp'), may hold values from -6 to 6
- lengths: int32 [1024], P('dp'), may hold values from 1 to 128, as said below
- occupied: int32 [1024], P('dp'), may hold values 0 or 1
- slot_request: int32 [1024], P('dp'), may hold values from 0 to 1023, as said below
- request_adapter: int32 [1024], replicated, may hold values from 0 to 15, as said below
- out_weight: bfloat16 [8192, 4096], P('mp'), may hold values from -0.375 to 0.375
- shrink_weight: bfloat16 [16, 8192, 64], P('dp', 'mp'), may hold values from -0.375 to 0.375
- expand_weight: bfloat16 [16, 64, 4096], P('dp', None, 'mp'), may hold values from -0.75 to 0.75
Outputs:
- mixed: bfloat16 [1024, 4096], P('dp', 'mp')
Inputs may be any that keep to these rules, and one draw needn't show every extreme that they name: `slot_request`: A permutation: each request stands in exactly one slot. `request_adapter`: adapter n is owned by dp index n // 2. Among the slots of one dp index, at most 32 hold requests whose adapters one dp index owns; in every draw some dp index owns the adapters of exactly 32 slots of every dp index. `lengths`: each dp index has a slot of length 128.
All inputs are finite; a program needn't handle non-finite values. No bound on the sum of `occupied` on one device may be relied on, other than what follows from the above.
Results may differ from a plain program's by a relative error of at most 0.011.
Values may be sent and summed in bfloat16 or wider, within the bound.
No kernel may reach another device: no remote copies, remote signals or barrier semaphores. Data moves between devices by JAX's collectives and lax.ppermute only.
A program may use at most 128 MiB of HBM per device.

v0:
```python
import math

import jax
import jax.numpy as jnp
from jax import lax
from jax.sharding import PartitionSpec as P


def attend(queries, key_cache, value_cache, key_new, value_new, lengths):
    rows, heads, width = queries.shape
    kv_local = key_cache.shape[1]
    group = heads // kv_local
    inverse = 1.0 / math.sqrt(width)
    grouped = queries.reshape(rows, kv_local, group, width)
    cached = (
        jnp.einsum("bgjd,bgtd->bgjt", grouped, key_cache, preferred_element_type=jnp.float32)
        * inverse
    )
    fresh = (
        jnp.einsum("bgjd,bgd->bgj", grouped, key_new, preferred_element_type=jnp.float32) * inverse
    )
    valid = jnp.arange(key_cache.shape[2])[None, :] < lengths[:, None]
    cached = jnp.where(valid[:, None, None, :], cached, -jnp.inf)
    top = jnp.maximum(jnp.max(cached, axis=-1), fresh)
    cached_exp = jnp.exp(cached - top[..., None])
    fresh_exp = jnp.exp(fresh - top)
    total = jnp.sum(cached_exp, axis=-1) + fresh_exp
    cached_w = (cached_exp / total[..., None]).astype(jnp.bfloat16)
    fresh_w = (fresh_exp / total).astype(jnp.bfloat16)
    summed = jnp.einsum(
        "bgjt,bgtd->bgjd", cached_w, value_cache, preferred_element_type=jnp.float32
    )
    summed = (
        summed
        + fresh_w.astype(jnp.float32)[..., None] * value_new.astype(jnp.float32)[:, :, None, :]
    )
    return summed.reshape(rows, heads * width).astype(jnp.bfloat16)


def body(
    queries,
    key_cache,
    value_cache,
    key_new,
    value_new,
    lengths,
    occupied,
    slot_request,
    request_adapter,
    out_weight,
    shrink_weight,
    expand_weight,
):
    rows = queries.shape[0]
    attended = attend(queries, key_cache, value_cache, key_new, value_new, lengths)
    owners_count = lax.axis_size("dp")
    adapters_here = shrink_weight.shape[0]
    rank_width = shrink_weight.shape[2]
    out_local = expand_weight.shape[2]
    capacity = 2 * rows // owners_count
    matches = (
        slot_request[:, None] == jnp.arange(request_adapter.shape[0], dtype=jnp.int32)[None, :]
    )
    slot_adapter = jnp.sum(jnp.where(matches, request_adapter[None, :], 0), axis=1)
    owner = slot_adapter // adapters_here
    local_ids = slot_adapter % adapters_here
    owner_onehot = (owner[:, None] == jnp.arange(owners_count, dtype=jnp.int32)[None, :]).astype(
        jnp.int32
    )
    earlier = jnp.cumsum(owner_onehot, axis=0) - owner_onehot
    position = jnp.sum(earlier * owner_onehot, axis=1)
    slot_code = owner * capacity + position
    dispatch = jnp.arange(owners_count * capacity, dtype=jnp.int32)[:, None] == slot_code[None, :]
    send_rows = jnp.dot(
        dispatch.astype(jnp.bfloat16), attended, preferred_element_type=jnp.float32
    ).astype(jnp.bfloat16)
    send_rows = send_rows.reshape(owners_count, capacity, attended.shape[1])
    send_ids = jnp.sum(jnp.where(dispatch, (local_ids + 1)[None, :], 0), axis=1).reshape(
        owners_count, capacity
    )
    combine = (
        slot_code[:, None] == jnp.arange(owners_count * capacity, dtype=jnp.int32)[None, :]
    ).astype(jnp.bfloat16)
    partial_value = jnp.dot(attended, out_weight, preferred_element_type=jnp.float32)
    full = lax.psum(partial_value, "mp")
    base = lax.dynamic_slice_in_dim(full, lax.axis_index("mp") * out_local, out_local, 1)
    got_rows = lax.all_to_all(send_rows, "dp", split_axis=0, concat_axis=0, tiled=True)
    got_ids = lax.all_to_all(send_ids, "dp", split_axis=0, concat_axis=0, tiled=True)
    flat = got_rows.reshape(owners_count * capacity, got_rows.shape[2])
    wanted = got_ids.reshape(owners_count * capacity) - 1
    partial_value = jnp.einsum(
        "md,adr->mar", flat, shrink_weight, preferred_element_type=jnp.float32
    )
    which = jnp.arange(adapters_here, dtype=jnp.int32)[None, :] == wanted[:, None]
    partial_value = jnp.where(which[:, :, None], partial_value, 0.0)
    summed = lax.psum(
        partial_value.reshape(owners_count * capacity, adapters_here * rank_width), "mp"
    )
    low = summed.astype(jnp.bfloat16).reshape(owners_count * capacity, adapters_here, rank_width)
    delta = 0.5 * jnp.einsum("mar,are->me", low, expand_weight, preferred_element_type=jnp.float32)
    delta = delta.astype(jnp.bfloat16).reshape(owners_count, capacity, out_local)
    back = lax.all_to_all(delta, "dp", split_axis=0, concat_axis=0, tiled=True)
    correction = jnp.dot(
        combine,
        back.reshape(owners_count * capacity, out_local),
        preferred_element_type=jnp.float32,
    )
    return (occupied.astype(jnp.float32)[:, None] * (base + correction)).astype(jnp.bfloat16)


def solution(mesh):
    placed = (
        P("dp", "mp", None),
        P("dp", "mp", None, None),
        P("dp", "mp", None, None),
        P("dp", "mp", None),
        P("dp", "mp", None),
        P("dp"),
        P("dp"),
        P("dp"),
        P(),
        P("mp", None),
        P("dp", "mp", None),
        P("dp", None, "mp"),
    )
    return jax.shard_map(body, mesh=mesh, in_specs=placed, out_specs=P("dp", "mp"), check_vma=False)
```

profile of v0, /device:TPU:0, one launch (start us, length us, event | category | flops | bytes accessed | tf_op | source)
XLA Modules:
  0.0 147.1 jit_solution(17990847659666558838)
XLA Ops:
  6.5 1.0 select_reduce_fusion
  7.5 0.1 fusion.20
  7.6 0.2 reduce_window_sum.11
  7.8 0.2 select_reduce_fusion.2
  8.0 0.1 select_reduce_fusion.1
  8.1 0.7 all_to_all.12
  8.8 5.2 %all-to-all-start = ((s32[8,1,32]{2,1,0:T(1,128)}), s32[8,1,32]{2,1,0:T(1,128)S(1)}, u32[]{:S(2)}, u32[]{:S(2)}) async-start(s32[8,1,32]{2,1,0:T(1,128)} %all_to_all.12), calls=%async_computation | async-start | bytes 8192 | tf_op jit(solution)/shard_map/all_to_all | solution.py:88
  14.0 0.7 iota_compare_fusion.6
  14.7 8.2 %fusion.25 = (f32[128,2,8]{2,1,0:T(2,128)S(1)}, f32[128,2,8,128]{3,2,1,0:T(8,128)S(1)}) fusion(bf16[128,2,128,128]{3,2,1,0:T(8,128)(2,1)} %param.13, bf16[128,16,128]{2,1,0:T(8,128)(2,1)} %param.12, pred[128,128]{1,0:T(8,128)(4,1)S(1)} %iota_compare_fusion.6), kind=kOutput, calls=%fused_computation.52 | convolution fusion | flops 67893248 | bytes 9986048 | tf_op jit(solution)/shard_map/bgjd,bgtd->bgjt/dot_general | solution.py:16
  22.9 0.1 copy.16
  23.0 0.4 fusion.10
  23.4 0.1 copy.22
  23.5 0.2 copy.17
  23.6 0.8 fusion.6
  24.4 0.1 copy.18
  24.5 0.1 copy.19
  24.7 0.1 copy.20
  24.9 5.7 %fusion.3 = bf16[128,2,8,128]{3,2,1,0:T(8,128)(2,1)S(1)} fusion(bf16[128,2,128,128]{3,2,1,0:T(8,128)(2,1)} %param.14, f32[128,2,8,128]{3,2,1,0:T(8,128)S(1)} %get-tuple-element.10, f32[128,2,128]{2,1,0:T(2,128)S(1)} %convert_element_type.42, f32[128,2,8]{2,1,0:T(2,128)S(1)} %copy.20, f32[128,2,8]{2,1,0:T(2,128)S(1)} %copy.19, f32[128,2,8]{2,1,0:T(2,128)S(1)} %copy.17), kind=kOutput, calls=%fused_computation.7 | convolution fusion | flops 68681728 | bytes 10117120 | tf_op jit(solution)/shard_map/bgjt,bgtd->bgjd/dot_general | solution.py:30
  30.6 1.4 convolution_convert_fusion
  32.1 4.2 %all-to-all-start.1 = ((bf16[8,32,2048]{2,1,0:T(8,128)(2,1)}), bf16[8,32,2048]{2,1,0:T(8,128)(2,1)S(1)}, u32[]{:S(2)}, u32[]{:S(2)}) async-start(bf16[8,32,2048]{2,1,0:T(8,128)(2,1)} %bitcast.3), calls=%async_computation.1 | async-start | bytes 2097152 | tf_op jit(solution)/shard_map/all_to_all | solution.py:87
  36.3 0.0 all-reduce.3.cloned.1.call-start
  36.3 9.4 %fusion.8 = f32[128,4096]{1,0:T(8,128)} fusion(bf16[2048,4096]{1,0:T(8,128)(2,1)} %param.21, bf16[16,8,16,128]{3,2,1,0:T(8,128)(2,1)S(1)} %bitcast.58), kind=kOutput, calls=%fused_computation.15 | convolution fusion | flops 2147483648 | bytes 19398656 | tf_op jit(solution)/shard_map/dot_general | solution.py:84
  45.8 0.0 all-reduce.3.cloned.1.call-update
  45.8 0.1 sub.32
  45.9 5.8 %all-to-all-done.1 = bf16[8,32,2048]{2,1,0:T(8,128)(2,1)S(1)} async-done(((bf16[8,32,2048]{2,1,0:T(8,128)(2,1)}), bf16[8,32,2048]{2,1,0:T(8,128)(2,1)S(1)}, u32[]{:S(2)}, u32[]{:S(2)}) %all-to-all-start.1) | async-done | bytes 1048608 | tf_op jit(solution)/shard_map/all_to_all | solution.py:87
  51.7 0.5 fusion.26
  52.2 25.4 %all-reduce.4 = bf16[256,128]{0,1:T(8,128)(2,1)S(1)} all-reduce(f32[256,128]{0,1:T(8,128)S(1)} %bitcast.60), channel_id=1, replica_groups=mesh['dp'=8,'mp'=4] {'mp'}, use_global_device_ids=true, to_apply=%region_7.8 | all-reduce | flops 32768 | bytes 196608 | tf_op jit(solution)/shard_map/psum | solution.py:96
  77.6 1.1 fusion.2
  78.7 3.5 %all-to-all-start.2 = ((bf16[8,32,1024]{2,1,0:T(8,128)(2,1)}), bf16[8,32,1024]{2,1,0:T(8,128)(2,1)S(1)}, u32[]{:S(2)}, u32[]{:S(2)}) async-start(bf16[8,32,1024]{2,1,0:T(8,128)(2,1)} %bitcast.11), calls=%async_computation.2 | async-start | bytes 1048576 | tf_op jit(solution)/shard_map/all_to_all | solution.py:102
  82.3 9.7 %all-to-all-done.2 = bf16[8,32,1024]{2,1,0:T(8,128)(2,1)S(1)} async-done(((bf16[8,32,1024]{2,1,0:T(8,128)(2,1)}), bf16[8,32,1024]{2,1,0:T(8,128)(2,1)S(1)}, u32[]{:S(2)}, u32[]{:S(2)}) %all-to-all-start.2) | async-done | bytes 524320 | tf_op jit(solution)/shard_map/all_to_all | solution.py:102
  91.9 46.4 %all-reduce.3.cloned.1.call-done = f32[128,4096]{1,0:T(8,128)} async-done(((f32[128,4096]{1,0:T(8,128)}), f32[128,4096]{1,0:T(8,128)}) %all-reduce.3.cloned.1.call-update) | async-done | bytes 2097168 | tf_op jit(solution)/shard_map/psum | solution.py:85
  138.3 2.0 %fusion.5 = bf16[128,1024]{1,0:T(8,128)(2,1)} fusion(bf16[256,1024]{1,0:T(8,128)(2,1)S(1)} %bitcast.59, f32[128,4096]{1,0:T(8,128)} %all-reduce.3.cloned.1.call-done, s32[]{:T(128)S(6)} %select_n.47, f32[128]{0:T(128)S(1)} %convert_element_type.38, s32[128]{0:T(128)S(1)} %multiply_add_fusion), kind=kOutput, calls=%fused_computation.10 | convolution fusion | flops 67534848 | bytes 1311748 | tf_op jit(solution)/shard_map/dot_general | solution.py:103
  (22 shorter events, 0.2 us)
Async XLA Ops:
  6.5 45.1 %copy-start = (bf16[2,2048,64]{1,2,0:T(8,128)(2,1)S(1)}, bf16[2,2048,64]{1,2,0:T(8,128)(2,1)}, u32[]{:S(2)}) copy-start(bf16[2,2048,64]{1,2,0:T(8,128)(2,1)} %param.22) | copy-start | bytes 1572868
  6.5 16.4 %copy-start.1 = (bf16[128,16,128]{2,1,0:T(8,128)(2,1)S(1)}, bf16[128,16,128]{2,1,0:T(8,128)(2,1)}, u32[]{:S(2)}) copy-start(bf16[128,16,128]{2,1,0:T(8,128)(2,1)} %param.12) | copy-start | bytes 1572868
  6.5 16.4 %copy-start.4 = (bf16[128,2,128]{2,1,0:T(2,128)(2,1)S(1)}, bf16[128,2,128]{2,1,0:T(2,128)(2,1)}, u32[]{:S(2)}) copy-start(bf16[128,2,128]{2,1,0:T(2,128)(2,1)} %param.15) | copy-start | bytes 196612
  6.5 18.3 %copy-start.3 = (bf16[128,2,128]{2,1,0:T(2,128)(2,1)S(1)}, bf16[128,2,128]{2,1,0:T(2,128)(2,1)}, u32[]{:S(2)}) copy-start(bf16[128,2,128]{2,1,0:T(2,128)(2,1)} %param.16) | copy-start | bytes 196612
  8.8 23.3 %all-to-all-start = ((s32[8,1,32]{2,1,0:T(1,128)}), s32[8,1,32]{2,1,0:T(1,128)S(1)}, u32[]{:S(2)}, u32[]{:S(2)}) async-start(s32[8,1,32]{2,1,0:T(1,128)} %all_to_all.12), calls=%async_computation | async-start | bytes 8192 | tf_op jit(solution)/shard_map/all_to_all | solution.py:88
  32.1 19.6 %all-to-all-start.1 = ((bf16[8,32,2048]{2,1,0:T(8,128)(2,1)}), bf16[8,32,2048]{2,1,0:T(8,128)(2,1)S(1)}, u32[]{:S(2)}, u32[]{:S(2)}) async-start(bf16[8,32,2048]{2,1,0:T(8,128)(2,1)} %bitcast.3), calls=%async_computation.1 | async-start | bytes 2097152 | tf_op jit(solution)/shard_map/all_to_all | solution.py:87
  36.3 41.3 %copy-start.2 = (bf16[2,64,1024]{2,1,0:T(8,128)(2,1)S(1)}, bf16[2,64,1024]{2,1,0:T(8,128)(2,1)}, u32[]{:S(2)}) copy-start(bf16[2,64,1024]{2,1,0:T(8,128)(2,1)} %param.23) | copy-start | bytes 786436
  36.3 46.0 %copy-start.5 = (s32[128]{0:T(128)S(1)}, s32[128]{0:T(128)}, u32[]{:S(2)}) copy-start(s32[128]{0:T(128)} %param.18) | copy-start | bytes 1540
  36.3 102.0 %all-reduce.3.cloned.1.call-start = ((), (), s32[]{:S(2)}) async-start(), calls=%async_computation.3 | async-start | bytes 4194304 | tf_op jit(solution)/shard_map/psum | solution.py:85
  78.7 13.2 %all-to-all-start.2 = ((bf16[8,32,1024]{2,1,0:T(8,128)(2,1)}), bf16[8,32,1024]{2,1,0:T(8,128)(2,1)S(1)}, u32[]{:S(2)}, u32[]{:S(2)}) async-start(bf16[8,32,1024]{2,1,0:T(8,128)(2,1)} %bitcast.11), calls=%async_computation.2 | async-start | bytes 1048576 | tf_op jit(solution)/shard_map/all_to_all | solution.py:102
Sparse Core Ops, SparseCore 0:
  45.9 92.3 all-reduce.2
where the time goes:
time: 148 us; the launch traced here: 147 us
  waiting for transfers between devices  61.8 us (42%)
  matrix products  28.8 us (19%)
  blocking collectives  25.4 us (17%)
  between operations  13.6 us (9%)
  starting transfers between devices  12.9 us (9%)
  other arithmetic  3.2 us (2%)
    psum x1, waiting for transfers between devices, body(): full = lax.psum(partial_value, 'mp')  46.4 us
    psum x1, blocking collectives, body(): lax.psum(partial_value.reshape(owners_count * capacity, adapters_here * r...  25.4 us
    all_to_all x1, waiting for transfers between devices, body(): back = lax.all_to_all(delta, 'dp', split_axis=0, concat_axis=0, tiled=True)  9.65 us
    dot_general x1, matrix products, body(): jnp.dot(attended, out_weight, preferred_element_type=jnp.float32)  9.44 us
    dot_general x1, matrix products, attend(): jnp.einsum('bgjd,bgtd->bgjt', grouped, key_cache, preferred_element_type=...  8.16 us
    all_to_all x1, waiting for transfers between devices, body(): lax.all_to_all(send_rows, 'dp', split_axis=0, concat_axis=0, tiled=True)  5.77 us
    dot_general x1, matrix products, attend(): jnp.einsum('bgjt,bgtd->bgjd', cached_w, value_cache, preferred_element_ty...  5.75 us
    all_to_all x1, starting transfers between devices, body(): lax.all_to_all(send_ids, 'dp', split_axis=0, concat_axis=0, tiled=True)  5.17 us
  transfers between devices with their start and end apart: 4, of which 3 were waited for; matrix products, arithmetic and copies ran while one was open for 20% of the time, Pallas kernels for 0%

commit v1 on v0

v1 whole, which is shorter than its diff:
```python
import functools
import math

import jax
import jax.numpy as jnp
from jax import lax
from jax.experimental import pallas as pl
from jax.experimental.pallas import tpu as pltpu
from jax.sharding import PartitionSpec as P

MIB = 1024 * 1024
TILE = 256
SMALL = pl.CostEstimate(flops=1, bytes_accessed=1, transcendentals=0)


def attend_block(lengths, q_ref, k_ref, v_ref, kn_ref, vn_ref, first, acc_ref):
    slots = len(lengths)
    heads, width = q_ref.shape[1:]
    kv_local, cache = k_ref.shape[1], k_ref.shape[2]
    group = heads // kv_local
    inverse = 1.0 / math.sqrt(width)
    lane = lax.broadcasted_iota(jnp.int32, (group, cache), 1)
    parts = []
    for s in range(slots):
        scores = lax.dot_general(
            q_ref[first + s],
            k_ref[first + s].reshape(kv_local * cache, width),
            (((1,), (1,)), ((), ())),
            preferred_element_type=jnp.float32,
        )
        valid = lane < lengths[s]
        for g in range(kv_local):
            part = scores[g * group : (g + 1) * group, g * cache : (g + 1) * cache]
            parts.append(jnp.where(valid, part * inverse, -jnp.inf))
    cached = jnp.concatenate(parts, axis=0)
    block = pl.ds(first, slots)
    q_all = q_ref[block].astype(jnp.float32).reshape(slots * kv_local, group, width)
    kn = kn_ref[block].astype(jnp.float32).reshape(slots * kv_local, 1, width)
    vn = vn_ref[block].astype(jnp.float32).reshape(slots * kv_local, 1, width)
    fresh = (jnp.sum(q_all * kn, axis=-1, keepdims=True) * inverse).reshape(slots * heads, 1)
    top = jnp.maximum(jnp.max(cached, axis=-1, keepdims=True), fresh)
    cached_exp = jnp.exp(cached - top)
    fresh_exp = jnp.exp(fresh - top)
    scale = 1.0 / (jnp.sum(cached_exp, axis=-1, keepdims=True) + fresh_exp)
    weights = (cached_exp * scale).astype(jnp.bfloat16)
    fresh_w = (fresh_exp * scale).astype(jnp.bfloat16).astype(jnp.float32)
    new_part = (fresh_w.reshape(slots * kv_local, group, 1) * vn).reshape(slots * heads, width)
    for s in range(slots):
        values = jnp.concatenate([v_ref[first + s, g] for g in range(kv_local)], axis=1)
        summed = jnp.dot(
            weights[s * heads : (s + 1) * heads], values, preferred_element_type=jnp.float32
        )
        for g in range(kv_local):
            row = s * heads + g * group
            acc_ref[row : row + group, :] = (
                summed[g * group : (g + 1) * group, g * width : (g + 1) * width]
                + new_part[row : row + group]
            )


def fetch(w_ref, buffer_ref, sem_ref, slot, column):
    return pltpu.make_async_copy(
        w_ref.at[:, pl.ds(pl.multiple_of(column, TILE), TILE)],
        buffer_ref.at[slot],
        sem_ref.at[slot],
    )


def project_tiles(a_ref, w_ref, buffer_ref, sem_ref, out_ref, first_slot, column):
    tiles = out_ref.shape[1] // TILE

    def tile(j, carry):
        slot = first_slot + j
        fetch(w_ref, buffer_ref, sem_ref, slot, column + j * TILE).wait()
        out_ref[:, pl.ds(pl.multiple_of(j * TILE, TILE), TILE)] = jnp.dot(
            a_ref[...], buffer_ref[slot], preferred_element_type=jnp.float32
        ).astype(out_ref.dtype)
        return carry

    lax.fori_loop(0, tiles, tile, 0)


def attend_kernel(
    block,
    lengths_ref,
    chunk_ref,
    q_hbm,
    k_hbm,
    v_hbm,
    kn_hbm,
    vn_hbm,
    w_ref,
    out_ref,
    piece_ref,
    q_ref,
    k_ref,
    v_ref,
    kn_ref,
    vn_ref,
    acc_ref,
    buffer_ref,
    new_sem,
    block_sem,
    sem_ref,
):
    rows, heads, width = q_ref.shape
    blocks = rows // block
    tiles = piece_ref.shape[1] // TILE
    column = chunk_ref[0] * piece_ref.shape[1]

    def block_copies(i):
        part = pl.ds(pl.multiple_of(i * block, block), block)
        return [
            pltpu.make_async_copy(source.at[part], target.at[part], block_sem.at[j, i])
            for j, (source, target) in enumerate(
                ((q_hbm, q_ref), (k_hbm, k_ref), (v_hbm, v_ref))
            )
        ]

    new_copies = [
        pltpu.make_async_copy(kn_hbm, kn_ref, new_sem.at[0]),
        pltpu.make_async_copy(vn_hbm, vn_ref, new_sem.at[1]),
    ]
    for copy in new_copies:
        copy.start()

    def begin(i, carry):
        for copy in block_copies(i):
            copy.start()
        return carry

    lax.fori_loop(0, blocks, begin, 0)
    for j in range(tiles):
        fetch(w_ref, buffer_ref, sem_ref, j, column + j * TILE).start()
    for copy in new_copies:
        copy.wait()

    def one_block(i, carry):
        for copy in block_copies(i):
            copy.wait()
        first = pl.multiple_of(i * block, block)
        attend_block(
            [lengths_ref[first + s] for s in range(block)],
            q_ref,
            k_ref,
            v_ref,
            kn_ref,
            vn_ref,
            first,
            acc_ref,
        )
        for h in range(heads):
            out_ref[pl.ds(first, block), h * width : (h + 1) * width] = acc_ref[
                pl.ds(h, block, stride=heads), :
            ].astype(out_ref.dtype)
        return carry

    lax.fori_loop(0, blocks, one_block, 0)
    project_tiles(out_ref, w_ref, buffer_ref, sem_ref, piece_ref, 0, column)


def attend(queries, key_cache, value_cache, key_new, value_new, lengths, out_weight, chunk, out_local):
    rows, heads, width = queries.shape
    cache = key_cache.shape[2]
    block = min(16, rows)
    depth = heads * width
    tiles = out_local // TILE
    smem = pl.BlockSpec(memory_space=pltpu.SMEM)
    hbm = pl.BlockSpec(memory_space=pltpu.HBM)
    vmem = pl.BlockSpec(memory_space=pltpu.VMEM)
    arrays = (queries, key_cache, value_cache, key_new, value_new)
    return pl.pallas_call(
        functools.partial(attend_kernel, block),
        in_specs=[smem, smem] + [hbm] * 6,
        out_specs=[vmem, vmem],
        scratch_shapes=[pltpu.VMEM(a.shape, a.dtype) for a in arrays]
        + [
            pltpu.VMEM((block * heads, width), jnp.float32),
            pltpu.VMEM((tiles, depth, TILE), jnp.bfloat16),
            pltpu.SemaphoreType.DMA((2,)),
            pltpu.SemaphoreType.DMA((3, rows // block)),
            pltpu.SemaphoreType.DMA((tiles,)),
        ],
        out_shape=[
            jax.ShapeDtypeStruct((rows, depth), jnp.bfloat16),
            jax.ShapeDtypeStruct((rows, out_local), jnp.bfloat16),
        ],
        compiler_params=pltpu.CompilerParams(vmem_limit_bytes=60 * MIB),
        cost_estimate=SMALL,
        name="attend",
    )(lengths, chunk.reshape(1), *arrays, out_weight)


def project_kernel(chunks_ref, a_hbm, w_ref, *refs):
    *out_refs, a_ref, buffer_ref, a_sem, sem_ref = refs
    out_local = out_refs[0].shape[1]
    tiles = out_local // TILE
    copy = pltpu.make_async_copy(a_hbm, a_ref, a_sem.at[0])
    copy.start()
    for i in range(len(out_refs)):
        for j in range(tiles):
            column = chunks_ref[i] * out_local + j * TILE
            fetch(w_ref, buffer_ref, sem_ref, i * tiles + j, column).start()
    copy.wait()
    for i, out_ref in enumerate(out_refs):
        project_tiles(
            a_ref, w_ref, buffer_ref, sem_ref, out_ref, i * tiles, chunks_ref[i] * out_local
        )


def project(attended, out_weight, chunks, out_local, dtypes):
    rows, depth = attended.shape
    slots = len(dtypes) * (out_local // TILE)
    vmem = pl.BlockSpec(memory_space=pltpu.VMEM)
    hbm = pl.BlockSpec(memory_space=pl.ANY)
    return pl.pallas_call(
        project_kernel,
        in_specs=[pl.BlockSpec(memory_space=pltpu.SMEM), hbm, hbm],
        out_specs=[vmem for _ in dtypes],
        scratch_shapes=[
            pltpu.VMEM(attended.shape, attended.dtype),
            pltpu.VMEM((slots, depth, TILE), jnp.bfloat16),
            pltpu.SemaphoreType.DMA((1,)),
            pltpu.SemaphoreType.DMA((slots,)),
        ],
        out_shape=[jax.ShapeDtypeStruct((rows, out_local), dtype) for dtype in dtypes],
        compiler_params=pltpu.CompilerParams(vmem_limit_bytes=52 * MIB),
        cost_estimate=SMALL,
        name="project",
    )(jnp.stack(chunks), attended, out_weight)


def fetch_all(sources, targets, sems):
    copies = [
        pltpu.make_async_copy(source, target, sems.at[i])
        for i, (source, target) in enumerate(zip(sources, targets))
    ]
    for copy in copies:
        copy.start()
    return copies


def masked(low, owner, adapters, ranks, adapters_here):
    terms = jnp.concatenate([low] * adapters_here, axis=0)
    row = lax.broadcasted_iota(jnp.int32, terms.shape, 0)
    return jnp.where(row // ranks + owner * adapters_here == adapters, terms, 0.0)


def low_kernel(ranks, sides, owners_ref, adapters_ref, *refs):
    count = (len(refs) - 2 - 2 * sides) // 2
    a_hbm, piece_hbm = refs[:sides], refs[sides : sides + count]
    out_ref = refs[sides + count]
    a_refs = refs[sides + count + 1 : 2 * sides + count + 1]
    piece_refs = refs[2 * sides + count + 1 : -1]
    copies = fetch_all(a_hbm + piece_hbm, a_refs + piece_refs, refs[-1])
    pair = piece_refs[0].shape[0]
    sides_t = []
    for a_ref, copy in zip(a_refs, copies):
        copy.wait()
        sides_t.append(a_ref[...].astype(jnp.float32).T.astype(jnp.bfloat16))
    a_t = jnp.concatenate(sides_t, axis=1)
    row = lax.broadcasted_iota(jnp.int32, (pair, a_t.shape[1]), 0)
    total = jnp.zeros(row.shape, jnp.float32)
    for i, piece_ref in enumerate(piece_refs):
        copies[sides + i].wait()
        part = jnp.dot(piece_ref[...], a_t, preferred_element_type=jnp.float32)
        first = owners_ref[i] * (pair // ranks)
        total += jnp.where(row // ranks + first == adapters_ref[...], part, 0.0)
    low = total[:ranks]
    for a in range(1, pair // ranks):
        low += total[a * ranks : (a + 1) * ranks]
    out_ref[...] = low.astype(out_ref.dtype)


def low_rank(attended, pieces, owners, adapters, rank):
    slots = adapters.shape[0]
    arrays = [*attended, *pieces]
    vmem = pl.BlockSpec(memory_space=pltpu.VMEM)
    return pl.pallas_call(
        functools.partial(low_kernel, rank, len(attended)),
        in_specs=[pl.BlockSpec(memory_space=pltpu.SMEM), vmem]
        + [pl.BlockSpec(memory_space=pl.ANY)] * len(arrays),
        out_specs=vmem,
        out_shape=jax.ShapeDtypeStruct((rank, slots), jnp.bfloat16),
        scratch_shapes=[pltpu.VMEM(a.shape, a.dtype) for a in arrays]
        + [pltpu.SemaphoreType.DMA((len(arrays),))],
        compiler_params=pltpu.CompilerParams(vmem_limit_bytes=32 * MIB),
        cost_estimate=SMALL,
        name="low_rank",
    )(jnp.stack(owners), adapters.reshape(1, slots), *arrays)


def delta_kernel(ranks, owners_ref, adapters_ref, low_ref, *refs):
    count = (len(refs) - 3) // 2
    out_refs, piece_refs = refs[count : count + 2], refs[count + 2 : -1]
    copies = fetch_all(refs[:count], piece_refs, refs[-1])
    pair = piece_refs[0].shape[0]
    low = low_ref[...].astype(jnp.float32)
    sides, weights = [], []
    for i, piece_ref in enumerate(piece_refs):
        mine = masked(low, owners_ref[i], adapters_ref[...], ranks, pair // ranks)
        sides.append(mine.T.astype(jnp.bfloat16))
    for copy, piece_ref in zip(copies, piece_refs):
        copy.wait()
        weights.append(piece_ref[...])
    delta = jnp.dot(
        jnp.concatenate(sides, axis=1),
        jnp.concatenate(weights, axis=0),
        preferred_element_type=jnp.float32,
    )
    delta = (0.5 * delta).astype(jnp.bfloat16)
    rows = out_refs[0].shape[0]
    out_refs[0][...] = delta[:rows]
    out_refs[1][...] = delta[rows:]


def correct(low, pieces, owners, adapters, rank):
    slots = adapters.shape[0]
    out_local = pieces[0].shape[1]
    vmem = pl.BlockSpec(memory_space=pltpu.VMEM)
    out = jax.ShapeDtypeStruct((slots // 2, out_local), jnp.bfloat16)
    return pl.pallas_call(
        functools.partial(delta_kernel, rank),
        in_specs=[pl.BlockSpec(memory_space=pltpu.SMEM), vmem, vmem]
        + [pl.BlockSpec(memory_space=pl.ANY)] * len(pieces),
        out_specs=[vmem, vmem],
        out_shape=[out, out],
        scratch_shapes=[pltpu.VMEM(a.shape, a.dtype) for a in pieces]
        + [pltpu.SemaphoreType.DMA((len(pieces),))],
        compiler_params=pltpu.CompilerParams(vmem_limit_bytes=32 * MIB),
        cost_estimate=SMALL,
        name="correct",
    )(jnp.stack(owners), adapters.reshape(1, slots), low, *pieces)


def finish_kernel(occupied_ref, own_ref, *refs):
    *part_refs, out_ref = refs
    rows = out_ref.shape[0]
    live = jnp.broadcast_to(occupied_ref[...].astype(jnp.float32), (128, rows)).T
    for j in range(0, out_ref.shape[1], 128):
        columns = slice(j, j + 128)
        total = own_ref[:, columns]
        for ref in part_refs:
            total += ref[:, columns].astype(jnp.float32)
        out_ref[:, columns] = (live * total).astype(out_ref.dtype)


def finish(own, parts, occupied):
    rows, out_local = own.shape
    vmem = pl.BlockSpec(memory_space=pltpu.VMEM)
    return pl.pallas_call(
        finish_kernel,
        in_specs=[vmem] * (2 + len(parts)),
        out_specs=vmem,
        out_shape=jax.ShapeDtypeStruct((rows, out_local), jnp.bfloat16),
        compiler_params=pltpu.CompilerParams(vmem_limit_bytes=32 * MIB),
        cost_estimate=SMALL,
        name="finish",
    )(occupied.reshape(1, rows), own, *parts)


def exchange(value, axis, step):
    count = lax.axis_size(axis)
    return lax.ppermute(value, axis, [(i, i ^ step) for i in range(count)])


def neighbours():
    return [1 << i for i in range(1, lax.axis_size("dp").bit_length() - 1)]


def near_blocks(own):
    return {0: own, **{bit: exchange(own, "dp", bit) for bit in neighbours()[:2]}}


def far_blocks(blocks):
    blocks = dict(blocks)
    a, b, *others = neighbours()
    half = blocks[0].shape[0] // 2
    blocks[a | b] = jnp.concatenate(
        [exchange(blocks[a][:half], "dp", b), exchange(blocks[b][half:], "dp", a)]
    )
    for bit in others:
        for key in list(blocks):
            blocks[key | bit] = exchange(blocks[key], "dp", bit)
    return blocks


def body(
    queries,
    key_cache,
    value_cache,
    key_new,
    value_new,
    lengths,
    occupied,
    slot_request,
    request_adapter,
    out_weight,
    shrink_weight,
    expand_weight,
):
    adapters_here, depth, rank = shrink_weight.shape
    out_local = expand_weight.shape[2]
    shares = lax.axis_size("mp")
    me = lax.axis_index("mp")
    here = lax.axis_index("dp")
    pair = adapters_here * rank
    steps = list(range(shares - 1, 0, -1))

    shrink = near_blocks(jnp.swapaxes(shrink_weight, 1, 2).reshape(pair, depth))
    requests = jnp.concatenate([slot_request, exchange(slot_request, "dp", 1)])

    attended, piece = attend(
        queries,
        key_cache,
        value_cache,
        key_new,
        value_new,
        lengths,
        out_weight,
        me ^ steps[0],
        out_local,
    )
    received = [exchange(piece, "mp", steps[0])]
    beside = exchange(attended, "dp", 1)
    (piece,) = project(attended, out_weight, [me ^ steps[1]], out_local, [jnp.bfloat16])
    received.append(exchange(piece, "mp", steps[1]))
    expand = expand_weight.reshape(pair, out_local)
    shrink, expand, requests, attended, _ = lax.optimization_barrier(
        (shrink, expand, requests, attended, piece)
    )
    shrink = far_blocks(shrink)
    expand = near_blocks(expand)
    *pieces, own = project(
        attended,
        out_weight,
        [me ^ step for step in steps[2:]] + [me],
        out_local,
        [jnp.bfloat16] * (shares - 3) + [jnp.float32],
    )
    received += [exchange(piece, "mp", step) for piece, step in zip(pieces, steps[2:])]
    requests, attended, _ = lax.optimization_barrier((requests, attended, own))

    matches = requests[:, None] == jnp.arange(request_adapter.shape[0], dtype=jnp.int32)[None, :]
    adapters = jnp.sum(jnp.where(matches, request_adapter[None, :], 0), axis=1)
    owners = [here ^ key for key in shrink]
    low = low_rank([attended, beside], list(shrink.values()), owners, adapters, rank)
    expand, low = lax.optimization_barrier((expand, low))
    expand = far_blocks(expand)
    low = low.astype(jnp.float32)
    step = 1
    while step < shares:
        low = low + exchange(low.astype(jnp.bfloat16), "mp", step).astype(jnp.float32)
        step *= 2
    low = low.astype(jnp.bfloat16)
    correction, other = correct(low, list(expand.values()), owners, adapters, rank)
    return finish(own, [*received, correction, exchange(other, "dp", 1)], occupied)


def solution(mesh):
    placed = (
        P("dp", "mp", None),
        P("dp", "mp", None, None),
        P("dp", "mp", None, None),
        P("dp", "mp", None),
        P("dp", "mp", None),
        P("dp"),
        P("dp"),
        P("dp"),
        P(),
        P("mp", None),
        P("dp", "mp", None),
        P("dp", None, "mp"),
    )
    return jax.shard_map(body, mesh=mesh, in_specs=placed, out_specs=P("dp", "mp"), check_vma=False)
```

time: 148 us -> 62.7 us (0.42)
  the two profiles are of different devices: /device:TPU:0 before, /device:TPU:8 now
where the time goes in v1:
time: 62.7 us; the launch traced here: 62.5 us
  Pallas kernels  22.5 us (36%)
  waiting for transfers between devices  19.7 us (31%)
  starting transfers between devices  17.5 us (28%)
  other arithmetic  1.46 us (2%)
  local copies, waits for them, and re-layouts  1.13 us (2%)
    ppermute x16, waiting for transfers between devices, exchange(): return lax.ppermute(value, axis, [(i, i ^ step) for i in range(count)])  19.7 us
    ppermute x16, starting transfers between devices, exchange(): return lax.ppermute(value, axis, [(i, i ^ step) for i in range(count)])  17.5 us
    pallas_call x1, Pallas kernels, attend(): pl.pallas_call(functools.partial(attend_kernel, block), in_specs=[smem, s...  10.1 us
    pallas_call x2, Pallas kernels, project(): pl.pallas_call(project_kernel, in_specs=[pl.BlockSpec(memory_space=pltpu....  7.17 us
    pallas_call x1, Pallas kernels, low_rank(): pl.pallas_call(functools.partial(low_kernel, rank, len(attended)), in_spe...  2.91 us
    pallas_call x1, Pallas kernels, correct(): pl.pallas_call(functools.partial(delta_kernel, rank), in_specs=[pl.BlockS...  1.29 us
  transfers between devices with their start and end apart: 16, of which 8 were waited for; matrix products, arithmetic and copies ran while one was open for 2% of the time, Pallas kernels for 34%

profile of v1, /device:TPU:8, one launch (start us, length us, event | category | flops | bytes accessed | tf_op | source)
XLA Modules:
  0.0 62.5 jit_solution(4315033991198426106)
XLA Ops:
  0.0 1.5 %collective-permute-start = (bf16[128,2048]{1,0:T(8,128)(2,1)}, bf16[128,2048]{1,0:T(8,128)(2,1)S(1)}, u32[]{:S(2)}, u32[]{:S(2)}) collective-permute-start(bf16[128,2048]{1,0:T(8,128)(2,1)} %bitcast.14), channel_id=1, source_target_pairs={{0,8},{4,12},{8,0},{12,4},{16,24},{20,28},{24,16},{28,20},{1,9},{5... | collective-permute-start | bytes 1572872 | tf_op jit(solution)/shard_map/ppermute | solution.py:364
  1.5 1.5 %collective-permute-start.1 = (bf16[128,2048]{1,0:T(8,128)(2,1)}, bf16[128,2048]{1,0:T(8,128)(2,1)S(1)}, u32[]{:S(2)}, u32[]{:S(2)}) collective-permute-start(bf16[128,2048]{1,0:T(8,128)(2,1)} %bitcast.15), channel_id=1, source_target_pairs={{0,16},{4,20},{8,24},{12,28},{16,0},{20,4},{24,8},{28,12},{1,17},{... | collective-permute-start | bytes 1572872 | tf_op jit(solution)/shard_map/ppermute | solution.py:364
  3.0 10.1 %attend.1 = (bf16[128,2048]{1,0:T(8,128)(2,1)}, bf16[128,1024]{1,0:T(8,128)(2,1)}) custom-call(s32[128]{0:T(128)} %lengths_ref.1, s32[1]{0:T(128)} %bitcast.7.chunk_ref, bf16[128,16,128]{2,1,0:T(8,128)(2,1)} %q_hbm.1, bf16[128,2,128,128]{3,2,1,0:T(8,128)(2,1)} %k_hbm.1, bf16[128,2,128,128]{3,2,1,0:T(8,128)(2,1)} %v_hbm.1, bf16[128,2,128]{2,1,0:T(2,128)(2,1)} %kn_hbm.1, ...), custom_call_target="tpu_custom_call" | custom-call | flops 1 | bytes 1 | tf_op jit(solution)/shard_map/attend/pallas_call | solution.py:172
  13.1 0.6 collective-permute-start.8
  13.7 1.0 %copy-done = bf16[128,2048]{1,0:T(8,128)(2,1)S(1)} copy-done((bf16[128,2048]{1,0:T(8,128)(2,1)S(1)}, bf16[128,2048]{1,0:T(8,128)(2,1)}, u32[]{:S(2)}) %copy-start) | copy-done | bytes 524312
  14.7 2.7 %project.2 = bf16[128,1024]{1,0:T(8,128)(2,1)S(1)} custom-call(s32[1]{0:T(128)} %bitcast.8.chunks_ref, bf16[128,2048]{1,0:T(8,128)(2,1)S(1)} %copy-done, bf16[2048,4096]{1,0:T(8,128)(2,1)} %w_ref.5), custom_call_target="tpu_custom_call" | custom-call | flops 1 | bytes 1 | tf_op jit(solution)/shard_map/project/pallas_call | solution.py:216
  17.5 0.6 collective-permute-start.10
  18.1 0.6 collective-permute-start.9
  18.8 0.1 pad_add_fusion.2.owners_ref
  18.9 1.6 %collective-permute-start.6 = (bf16[128,1024]{1,0:T(8,128)(2,1)S(1)}, bf16[128,1024]{1,0:T(8,128)(2,1)S(1)}, u32[]{:S(2)}, u32[]{:S(2)}) collective-permute-start(bf16[128,1024]{1,0:T(8,128)(2,1)S(1)} %bitcast.17), channel_id=1, source_target_pairs={{0,8},{4,12},{8,0},{12,4},{16,24},{20,28},{24,16},{28,20},{1,9},{5... | collective-permute-start | bytes 786440 | tf_op jit(solution)/shard_map/ppermute | solution.py:364
  20.4 1.5 %collective-permute-start.7 = (bf16[128,1024]{1,0:T(8,128)(2,1)S(1)}, bf16[128,1024]{1,0:T(8,128)(2,1)S(1)}, u32[]{:S(2)}, u32[]{:S(2)}) collective-permute-start(bf16[128,1024]{1,0:T(8,128)(2,1)S(1)} %bitcast.18), channel_id=1, source_target_pairs={{0,16},{4,20},{8,24},{12,28},{16,0},{20,4},{24,8},{28,12},{1,17},{... | collective-permute-start | bytes 786440 | tf_op jit(solution)/shard_map/ppermute | solution.py:364
  22.0 4.5 %project.3 = (bf16[128,1024]{1,0:T(8,128)(2,1)S(1)}, f32[128,1024]{1,0:T(8,128)S(1)}) custom-call(s32[2]{0:T(128)S(1)} %pad_add_fusion.1.chunks_ref, bf16[128,2048]{1,0:T(8,128)(2,1)S(1)} %copy-done.1, bf16[2048,4096]{1,0:T(8,128)(2,1)} %w_ref.5), custom_call_target="tpu_custom_call" | custom-call | flops 1 | bytes 1 | tf_op jit(solution)/shard_map/project/pallas_call | solution.py:216
  26.5 0.3 select_reduce_fusion
  26.8 0.7 %collective-permute-done.9 = bf16[64,2048]{1,0:T(8,128)(2,1)} collective-permute-done((bf16[64,2048]{1,0:T(8,128)(2,1)S(1)}, bf16[64,2048]{1,0:T(8,128)(2,1)}, u32[]{:S(2)}, u32[]{:S(2)}) %collective-permute-start.9) | collective-permute-done | bytes 262176 | tf_op jit(solution)/shard_map/ppermute | solution.py:364
  27.5 1.0 %pad_maximum_fusion.refs_5_ = bf16[128,2048]{1,0:T(8,128)(2,1)S(1)} fusion(bf16[64,2048]{1,0:T(8,128)(2,1)S(1)} %collective-permute-done.10, bf16[64,2048]{1,0:T(8,128)(2,1)} %collective-permute-done.9), kind=kLoop, calls=%fused_computation.2 | loop fusion | flops 1048576 | bytes 1048576 | tf_op jit(solution)/shard_map/concatenate | solution.py:379
  28.5 2.9 %low_rank.1 = bf16[64,256]{1,0:T(8,128)(2,1)S(1)} custom-call(s32[4]{0:T(128)S(1)} %pad_add_fusion.2.owners_ref, s32[1,256]{1,0:T(1,128)S(1)} %bitcast.20, bf16[128,2048]{1,0:T(8,128)(2,1)S(1)} %copy-done.1, bf16[128,2048]{1,0:T(8,128)(2,1)S(1)} %collective-permute-done.8.refs_1_, bf16[128,2048]{1,0:T(8,128)(2,1)S(1)} %bitcast.16, ...), custom_call_target="tpu_custom_call" | custom-call | flops 1 | bytes 1 | tf_op jit(solution)/shard_map/low_rank/pallas_call | solution.py:279
  31.4 0.3 collective-permute-done.7.refs_2_
  31.8 0.4 collective-permute-start.11
  32.2 3.5 %collective-permute-done.11 = bf16[64,256]{1,0:T(8,128)(2,1)S(1)} collective-permute-done((bf16[64,256]{1,0:T(8,128)(2,1)S(1)}, bf16[64,256]{1,0:T(8,128)(2,1)S(1)}, u32[]{:S(2)}, u32[]{:S(2)}) %collective-permute-start.11) | collective-permute-done | bytes 32800 | tf_op jit(solution)/shard_map/ppermute | solution.py:364
  35.7 2.6 %collective-permute-start.12 = (bf16[64,256]{1,0:T(8,128)(2,1)S(1)}, bf16[64,256]{1,0:T(8,128)(2,1)S(1)}, u32[]{:S(2)}, u32[]{:S(2)}) collective-permute-start(bf16[64,256]{1,0:T(8,128)(2,1)S(1)} %fusion), channel_id=1, source_target_pairs={{0,2},{1,3},{2,0},{3,1},{4,6},{5,7},{6,4},{7,5},{8,10},{9,11},{10,... | collective-permute-start | bytes 98312 | tf_op jit(solution)/shard_map/ppermute | solution.py:364
  38.3 0.3 collective-permute-start.4
  38.7 1.6 %collective-permute-start.3 = (bf16[128,1024]{1,0:T(8,128)(2,1)S(1)}, bf16[128,1024]{1,0:T(8,128)(2,1)S(1)}, u32[]{:S(2)}, u32[]{:S(2)}) collective-permute-start(bf16[128,1024]{1,0:T(8,128)(2,1)S(1)} %copy-done.7), channel_id=1, source_target_pairs={{0,3},{1,2},{2,1},{3,0},{4,7},{5,6},{6,5},{7,4},{8,11},{9,10},{10,... | collective-permute-start | bytes 786440 | tf_op jit(solution)/shard_map/ppermute | solution.py:364
  40.3 2.5 %collective-permute-start.5 = (bf16[128,1024]{1,0:T(8,128)(2,1)S(1)}, bf16[128,1024]{1,0:T(8,128)(2,1)S(1)}, u32[]{:S(2)}, u32[]{:S(2)}) collective-permute-start(bf16[128,1024]{1,0:T(8,128)(2,1)S(1)} %get-tuple-element.27), channel_id=1, source_target_pairs={{0,1},{1,0},{2,3},{3,2},{4,5},{5,4},{6,7},{7,6},{8,9},{9,8},{10,11... | collective-permute-start | bytes 786440 | tf_op jit(solution)/shard_map/ppermute | solution.py:364
  42.7 0.6 collective-permute-start.13
  43.3 2.7 %collective-permute-done.12 = bf16[64,256]{1,0:T(8,128)(2,1)S(1)} collective-permute-done((bf16[64,256]{1,0:T(8,128)(2,1)S(1)}, bf16[64,256]{1,0:T(8,128)(2,1)S(1)}, u32[]{:S(2)}, u32[]{:S(2)}) %collective-permute-start.12) | collective-permute-done | bytes 32800 | tf_op jit(solution)/shard_map/ppermute | solution.py:364
  46.1 1.5 %collective-permute-start.14 = (bf16[64,1024]{1,0:T(8,128)(2,1)S(1)}, bf16[64,1024]{1,0:T(8,128)(2,1)S(1)}, u32[]{:S(2)}, u32[]{:S(2)}) collective-permute-start(bf16[64,1024]{1,0:T(8,128)(2,1)S(1)} %slice.15), channel_id=1, source_target_pairs={{0,8},{4,12},{8,0},{12,4},{16,24},{20,28},{24,16},{28,20},{1,9},{5... | collective-permute-start | bytes 393224 | tf_op jit(solution)/shard_map/ppermute | solution.py:364
  47.6 0.2 collective-permute-done.13
  47.8 3.3 %collective-permute-done.14 = bf16[64,1024]{1,0:T(8,128)(2,1)S(1)} collective-permute-done((bf16[64,1024]{1,0:T(8,128)(2,1)S(1)}, bf16[64,1024]{1,0:T(8,128)(2,1)S(1)}, u32[]{:S(2)}, u32[]{:S(2)}) %collective-permute-start.14) | collective-permute-done | bytes 131104 | tf_op jit(solution)/shard_map/ppermute | solution.py:364
  51.1 1.3 %correct.1 = (bf16[128,1024]{1,0:T(8,128)(2,1)S(1)}, bf16[128,1024]{1,0:T(8,128)(2,1)S(1)}) custom-call(s32[4]{0:T(128)S(1)} %pad_add_fusion.2.owners_ref, s32[1,256]{1,0:T(1,128)S(1)} %bitcast.21, bf16[64,256]{1,0:T(8,128)(2,1)S(1)} %add_convert_fusion.low_ref, bf16[128,1024]{1,0:T(8,128)(2,1)S(1)} %bitcast.19, ...), custom_call_target="tpu_custom_call" | custom-call | flops 1 | bytes 1 | tf_op jit(solution)/shard_map/correct/pallas_call | solution.py:322
  52.4 2.0 %collective-permute-done.4.refs_1_ = bf16[128,1024]{1,0:T(8,128)(2,1)S(1)} collective-permute-done((bf16[128,1024]{1,0:T(8,128)(2,1)S(1)}, bf16[128,1024]{1,0:T(8,128)(2,1)S(1)}, u32[]{:S(2)}, u32[]{:S(2)}) %collective-permute-start.4) | collective-permute-done | bytes 262176 | tf_op jit(solution)/shard_map/ppermute | solution.py:364
  54.4 7.0 %collective-permute-done.3.refs_0_ = bf16[128,1024]{1,0:T(8,128)(2,1)S(1)} collective-permute-done((bf16[128,1024]{1,0:T(8,128)(2,1)S(1)}, bf16[128,1024]{1,0:T(8,128)(2,1)S(1)}, u32[]{:S(2)}, u32[]{:S(2)}) %collective-permute-start.3) | collective-permute-done | bytes 262176 | tf_op jit(solution)/shard_map/ppermute | solution.py:364
  61.4 1.0 %finish.1 = bf16[128,1024]{1,0:T(8,128)(2,1)} custom-call(s32[1,128]{1,0:T(1,128)S(1)} %bitcast.22, f32[128,1024]{1,0:T(8,128)S(1)} %get-tuple-element.25.own_ref, bf16[128,1024]{1,0:T(8,128)(2,1)S(1)} %collective-permute-done.3.refs_0_, bf16[128,1024]{1,0:T(8,128)(2,1)S(1)} %collective-permute-done.4.refs_1_, ...), custom_call_target="tpu_custom_call" | custom-call | flops 1 | bytes 1 | tf_op jit(solution)/shard_map/finish/pallas_call | solution.py:351
  (34 shorter events, 0.3 us)
Async XLA Ops:
  0.0 17.5 %collective-permute-start = (bf16[128,2048]{1,0:T(8,128)(2,1)}, bf16[128,2048]{1,0:T(8,128)(2,1)S(1)}, u32[]{:S(2)}, u32[]{:S(2)}) collective-permute-start(bf16[128,2048]{1,0:T(8,128)(2,1)} %bitcast.14), channel_id=1, source_target_pairs={{0,8},{4,12},{8,0},{12,4},{16,24},{20,28},{24,16},{28,20},{1,9},{5... | collective-permute-start | bytes 1572872 | tf_op jit(solution)/shard_map/ppermute | solution.py:364
  1.5 16.0 %collective-permute-start.1 = (bf16[128,2048]{1,0:T(8,128)(2,1)}, bf16[128,2048]{1,0:T(8,128)(2,1)S(1)}, u32[]{:S(2)}, u32[]{:S(2)}) collective-permute-start(bf16[128,2048]{1,0:T(8,128)(2,1)} %bitcast.15), channel_id=1, source_target_pairs={{0,16},{4,20},{8,24},{12,28},{16,0},{20,4},{24,8},{28,12},{1,17},{... | collective-permute-start | bytes 1572872 | tf_op jit(solution)/shard_map/ppermute | solution.py:364
  3.0 14.4 %collective-permute-start.2 = (s32[128]{0:T(128)}, s32[128]{0:T(128)S(1)}, u32[]{:S(2)}, u32[]{:S(2)}) collective-permute-start(s32[128]{0:T(128)} %param.19), channel_id=1, source_target_pairs={{0,4},{4,0},{8,12},{12,8},{16,20},{20,16},{24,28},{28,24},{1,5},{5... | collective-permute-start | bytes 1544 | tf_op jit(solution)/shard_map/ppermute | solution.py:364
  13.1 15.4 %collective-permute-start.8 = (bf16[128,2048]{1,0:T(8,128)(2,1)}, bf16[128,2048]{1,0:T(8,128)(2,1)S(1)}, u32[]{:S(2)}, u32[]{:S(2)}) collective-permute-start(bf16[128,2048]{1,0:T(8,128)(2,1)} %get-tuple-element.31.a_hbm.refs_0_), channel_id=1, source_target_pairs={{0,4},{4,0},{8,12},{12,8},{16,20},{20,16},{24,28},{28,24},{1,5},{5... | collective-permute-start | bytes 1572872 | tf_op jit(solution)/shard_map/ppermute | solution.py:364
  13.7 1.0 %copy-start = (bf16[128,2048]{1,0:T(8,128)(2,1)S(1)}, bf16[128,2048]{1,0:T(8,128)(2,1)}, u32[]{:S(2)}) copy-start(bf16[128,2048]{1,0:T(8,128)(2,1)} %get-tuple-element.31.a_hbm.refs_0_) | copy-start | bytes 1572868
  14.7 2.7 %copy-start.6 = (s32[128]{0:T(128)S(1)}, s32[128]{0:T(128)}, u32[]{:S(2)}) copy-start(s32[128]{0:T(128)} %param.19) | copy-start | bytes 1540
  14.7 4.1 %copy-start.3 = (bf16[2,64,1024]{2,1,0:T(8,128)(2,1)S(1)}, bf16[2,64,1024]{2,1,0:T(8,128)(2,1)}, u32[]{:S(2)}) copy-start(bf16[2,64,1024]{2,1,0:T(8,128)(2,1)} %param.23) | copy-start | bytes 786436
  14.7 7.2 %copy-start.1 = (bf16[128,2048]{1,0:T(8,128)(2,1)S(1)}, bf16[128,2048]{1,0:T(8,128)(2,1)}, u32[]{:S(2)}) copy-start(bf16[128,2048]{1,0:T(8,128)(2,1)} %get-tuple-element.31.a_hbm.refs_0_) | copy-start | bytes 1572868
  17.5 9.2 %collective-permute-start.10 = (bf16[64,2048]{1,0:T(8,128)(2,1)S(1)}, bf16[64,2048]{1,0:T(8,128)(2,1)S(1)}, u32[]{:S(2)}, u32[]{:S(2)}) collective-permute-start(bf16[64,2048]{1,0:T(8,128)(2,1)S(1)} %slice.13), channel_id=1, source_target_pairs={{0,8},{4,12},{8,0},{12,4},{16,24},{20,28},{24,16},{28,20},{1,9},{5... | collective-permute-start | bytes 786440 | tf_op jit(solution)/shard_map/ppermute | solution.py:364
  18.1 9.4 %collective-permute-start.9 = (bf16[64,2048]{1,0:T(8,128)(2,1)S(1)}, bf16[64,2048]{1,0:T(8,128)(2,1)}, u32[]{:S(2)}, u32[]{:S(2)}) collective-permute-start(bf16[64,2048]{1,0:T(8,128)(2,1)S(1)} %slice.12), channel_id=1, source_target_pairs={{0,16},{4,20},{8,24},{12,28},{16,0},{20,4},{24,8},{28,12},{1,17},{... | collective-permute-start | bytes 786440 | tf_op jit(solution)/shard_map/ppermute | solution.py:364
  18.9 7.6 %copy-start.5 = (s32[1024]{0:T(1024)S(1)}, s32[1024]{0:T(1024)}, u32[]{:S(2)}) copy-start(s32[1024]{0:T(1024)} %param.20) | copy-start | bytes 12292
  18.9 9.6 %copy-start.2 = (bf16[2,2048,64]{1,2,0:T(8,128)(2,1)S(1)}, bf16[2,2048,64]{1,2,0:T(8,128)(2,1)}, u32[]{:S(2)}) copy-start(bf16[2,2048,64]{1,2,0:T(8,128)(2,1)} %param.22) | copy-start | bytes 1572868
  18.9 19.8 %copy-start.7 = (bf16[128,1024]{1,0:T(8,128)(2,1)S(1)}, bf16[128,1024]{1,0:T(8,128)(2,1)}, u32[]{:S(2)}) copy-start(bf16[128,1024]{1,0:T(8,128)(2,1)} %get-tuple-element.26) | copy-start | bytes 786436
  18.9 42.6 %copy-start.4 = (s32[128]{0:T(128)S(1)}, s32[128]{0:T(128)}, u32[]{:S(2)}) copy-start(s32[128]{0:T(128)} %param.18) | copy-start | bytes 1540
  18.9 12.5 %collective-permute-start.6 = (bf16[128,1024]{1,0:T(8,128)(2,1)S(1)}, bf16[128,1024]{1,0:T(8,128)(2,1)S(1)}, u32[]{:S(2)}, u32[]{:S(2)}) collective-permute-start(bf16[128,1024]{1,0:T(8,128)(2,1)S(1)} %bitcast.17), channel_id=1, source_target_pairs={{0,8},{4,12},{8,0},{12,4},{16,24},{20,28},{24,16},{28,20},{1,9},{5... | collective-permute-start | bytes 786440 | tf_op jit(solution)/shard_map/ppermute | solution.py:364
  20.4 11.3 %collective-permute-start.7 = (bf16[128,1024]{1,0:T(8,128)(2,1)S(1)}, bf16[128,1024]{1,0:T(8,128)(2,1)S(1)}, u32[]{:S(2)}, u32[]{:S(2)}) collective-permute-start(bf16[128,1024]{1,0:T(8,128)(2,1)S(1)} %bitcast.18), channel_id=1, source_target_pairs={{0,16},{4,20},{8,24},{12,28},{16,0},{20,4},{24,8},{28,12},{1,17},{... | collective-permute-start | bytes 786440 | tf_op jit(solution)/shard_map/ppermute | solution.py:364
  31.8 3.9 %collective-permute-start.11 = (bf16[64,256]{1,0:T(8,128)(2,1)S(1)}, bf16[64,256]{1,0:T(8,128)(2,1)S(1)}, u32[]{:S(2)}, u32[]{:S(2)}) collective-permute-start(bf16[64,256]{1,0:T(8,128)(2,1)S(1)} %low_rank.1), channel_id=1, source_target_pairs={{0,1},{1,0},{2,3},{3,2},{4,5},{5,4},{6,7},{7,6},{8,9},{9,8},{10,11... | collective-permute-start | bytes 98312 | tf_op jit(solution)/shard_map/ppermute | solution.py:364
  35.7 10.4 %collective-permute-start.12 = (bf16[64,256]{1,0:T(8,128)(2,1)S(1)}, bf16[64,256]{1,0:T(8,128)(2,1)S(1)}, u32[]{:S(2)}, u32[]{:S(2)}) collective-permute-start(bf16[64,256]{1,0:T(8,128)(2,1)S(1)} %fusion), channel_id=1, source_target_pairs={{0,2},{1,3},{2,0},{3,1},{4,6},{5,7},{6,4},{7,5},{8,10},{9,11},{10,... | collective-permute-start | bytes 98312 | tf_op jit(solution)/shard_map/ppermute | solution.py:364
  38.3 16.1 %collective-permute-start.4 = (bf16[128,1024]{1,0:T(8,128)(2,1)S(1)}, bf16[128,1024]{1,0:T(8,128)(2,1)S(1)}, u32[]{:S(2)}, u32[]{:S(2)}) collective-permute-start(bf16[128,1024]{1,0:T(8,128)(2,1)S(1)} %project.2), channel_id=1, source_target_pairs={{0,2},{1,3},{2,0},{3,1},{4,6},{5,7},{6,4},{7,5},{8,10},{9,11},{10,... | collective-permute-start | bytes 786440 | tf_op jit(solution)/shard_map/ppermute | solution.py:364
  38.7 22.7 %collective-permute-start.3 = (bf16[128,1024]{1,0:T(8,128)(2,1)S(1)}, bf16[128,1024]{1,0:T(8,128)(2,1)S(1)}, u32[]{:S(2)}, u32[]{:S(2)}) collective-permute-start(bf16[128,1024]{1,0:T(8,128)(2,1)S(1)} %copy-done.7), channel_id=1, source_target_pairs={{0,3},{1,2},{2,1},{3,0},{4,7},{5,6},{6,5},{7,4},{8,11},{9,10},{10,... | collective-permute-start | bytes 786440 | tf_op jit(solution)/shard_map/ppermute | solution.py:364
  40.3 21.2 %collective-permute-start.5 = (bf16[128,1024]{1,0:T(8,128)(2,1)S(1)}, bf16[128,1024]{1,0:T(8,128)(2,1)S(1)}, u32[]{:S(2)}, u32[]{:S(2)}) collective-permute-start(bf16[128,1024]{1,0:T(8,128)(2,1)S(1)} %get-tuple-element.27), channel_id=1, source_target_pairs={{0,1},{1,0},{2,3},{3,2},{4,5},{5,4},{6,7},{7,6},{8,9},{9,8},{10,11... | collective-permute-start | bytes 786440 | tf_op jit(solution)/shard_map/ppermute | solution.py:364
  42.7 5.0 %collective-permute-start.13 = (bf16[64,1024]{1,0:T(8,128)(2,1)S(1)}, bf16[64,1024]{1,0:T(8,128)(2,1)S(1)}, u32[]{:S(2)}, u32[]{:S(2)}) collective-permute-start(bf16[64,1024]{1,0:T(8,128)(2,1)S(1)} %slice.14), channel_id=1, source_target_pairs={{0,16},{4,20},{8,24},{12,28},{16,0},{20,4},{24,8},{28,12},{1,17},{... | collective-permute-start | bytes 393224 | tf_op jit(solution)/shard_map/ppermute | solution.py:364
  46.1 5.0 %collective-permute-start.14 = (bf16[64,1024]{1,0:T(8,128)(2,1)S(1)}, bf16[64,1024]{1,0:T(8,128)(2,1)S(1)}, u32[]{:S(2)}, u32[]{:S(2)}) collective-permute-start(bf16[64,1024]{1,0:T(8,128)(2,1)S(1)} %slice.15), channel_id=1, source_target_pairs={{0,8},{4,12},{8,0},{12,4},{16,24},{20,28},{24,16},{28,20},{1,9},{5... | collective-permute-start | bytes 393224 | tf_op jit(solution)/shard_map/ppermute | solution.py:364
  52.3 9.1 %collective-permute-start.15 = (bf16[128,1024]{1,0:T(8,128)(2,1)S(1)}, bf16[128,1024]{1,0:T(8,128)(2,1)S(1)}, u32[]{:S(2)}, u32[]{:S(2)}) collective-permute-start(bf16[128,1024]{1,0:T(8,128)(2,1)S(1)} %get-tuple-element.40), channel_id=1, source_target_pairs={{0,4},{4,0},{8,12},{12,8},{16,20},{20,16},{24,28},{28,24},{1,5},{5... | collective-permute-start | bytes 786440 | tf_op jit(solution)/shard_map/ppermute | solution.py:364

commit v2 on v1

--- a/solution.py
+++ b/solution.py
@@ -11,6 +11,7 @@
 MIB = 1024 * 1024
 TILE = 256
 SMALL = pl.CostEstimate(flops=1, bytes_accessed=1, transcendentals=0)
+ID_ROWS = 16
 
 
 def attend_block(lengths, q_ref, k_ref, v_ref, kn_ref, vn_ref, first, acc_ref):
@@ -73,11 +74,32 @@
         slot = first_slot + j
         fetch(w_ref, buffer_ref, sem_ref, slot, column + j * TILE).wait()
         out_ref[:, pl.ds(pl.multiple_of(j * TILE, TILE), TILE)] = jnp.dot(
-            a_ref[...], buffer_ref[slot], preferred_element_type=jnp.float32
+            a_ref[: out_ref.shape[0]], buffer_ref[slot], preferred_element_type=jnp.float32
         ).astype(out_ref.dtype)
         return carry
 
     lax.fori_loop(0, tiles, tile, 0)
+
+
+def fetch_all(sources, targets, sems):
+    copies = [
+        pltpu.make_async_copy(source, target, sems.at[i])
+        for i, (source, target) in enumerate(zip(sources, targets))
+    ]
+    for copy in copies:
+        copy.start()
+    return copies
+
+
+def look_up(requests, adapters):
+    slots, known = requests.shape[1], adapters.shape[1]
+    matches = lax.broadcasted_iota(jnp.int32, (known, slots), 0) == requests
+    numbers = jnp.broadcast_to(adapters.astype(jnp.float32), (ID_ROWS, known))
+    return jnp.dot(
+        numbers.astype(jnp.bfloat16),
+        matches.astype(jnp.float32).astype(jnp.bfloat16),
+        preferred_element_type=jnp.float32,
+    )
 
 
 def attend_kernel(
@@ -89,6 +111,8 @@
     v_hbm,
     kn_hbm,
     vn_hbm,
+    request_hbm,
+    adapter_hbm,
     w_ref,
     out_ref,
     piece_ref,
@@ -97,6 +121,8 @@
     v_ref,
     kn_ref,
     vn_ref,
+    request_ref,
+    adapter_ref,
     acc_ref,
     buffer_ref,
     new_sem,
@@ -117,12 +143,11 @@
             )
         ]
 
-    new_copies = [
-        pltpu.make_async_copy(kn_hbm, kn_ref, new_sem.at[0]),
-        pltpu.make_async_copy(vn_hbm, vn_ref, new_sem.at[1]),
-    ]
-    for copy in new_copies:
-        copy.start()
+    new_copies = fetch_all(
+        (kn_hbm, vn_hbm, request_hbm, adapter_hbm),
+        (kn_ref, vn_ref, request_ref, adapter_ref),
+        new_sem,
+    )
 
     def begin(i, carry):
         for copy in block_copies(i):
@@ -134,6 +159,10 @@
         fetch(w_ref, buffer_ref, sem_ref, j, column + j * TILE).start()
     for copy in new_copies:
         copy.wait()
+    out_ref[pl.ds(rows, ID_ROWS), :] = jnp.zeros((ID_ROWS, out_ref.shape[1]), out_ref.dtype)
+    out_ref[pl.ds(rows, ID_ROWS), :rows] = look_up(request_ref[...], adapter_ref[...]).astype(
+        out_ref.dtype
+    )
 
     def one_block(i, carry):
         for copy in block_copies(i):
@@ -159,7 +188,8 @@
     project_tiles(out_ref, w_ref, buffer_ref, sem_ref, piece_ref, 0, column)
 
 
-def attend(queries, key_cache, value_cache, key_new, value_new, lengths, out_weight, chunk, out_local):
+def attend(arrays, lengths, out_weight, chunk, out_local):
+    queries, key_cache = arrays[:2]
     rows, heads, width = queries.shape
     cache = key_cache.shape[2]
     block = min(16, rows)
@@ -168,21 +198,20 @@
     smem = pl.BlockSpec(memory_space=pltpu.SMEM)
     hbm = pl.BlockSpec(memory_space=pltpu.HBM)
     vmem = pl.BlockSpec(memory_space=pltpu.VMEM)
-    arrays = (queries, key_cache, value_cache, key_new, value_new)
     return pl.pallas_call(
         functools.partial(attend_kernel, block),
-        in_specs=[smem, smem] + [hbm] * 6,
+        in_specs=[smem, smem] + [hbm] * (len(arrays) + 1),
         out_specs=[vmem, vmem],
         scratch_shapes=[pltpu.VMEM(a.shape, a.dtype) for a in arrays]
         + [
             pltpu.VMEM((block * heads, width), jnp.float32),
             pltpu.VMEM((tiles, depth, TILE), jnp.bfloat16),
-            pltpu.SemaphoreType.DMA((2,)),
+            pltpu.SemaphoreType.DMA((4,)),
             pltpu.SemaphoreType.DMA((3, rows // block)),
             pltpu.SemaphoreType.DMA((tiles,)),
         ],
         out_shape=[
-            jax.ShapeDtypeStruct((rows, depth), jnp.bfloat16),
+            jax.ShapeDtypeStruct((rows + ID_ROWS, depth), jnp.bfloat16),
             jax.ShapeDtypeStruct((rows, out_local), jnp.bfloat16),
         ],
         compiler_params=pltpu.CompilerParams(vmem_limit_bytes=60 * MIB),
@@ -209,7 +238,7 @@
 
 
 def project(attended, out_weight, chunks, out_local, dtypes):
-    rows, depth = attended.shape
+    rows, depth = attended.shape[0] - ID_ROWS, attended.shape[1]
     slots = len(dtypes) * (out_local // TILE)
     vmem = pl.BlockSpec(memory_space=pltpu.VMEM)
     hbm = pl.BlockSpec(memory_space=pl.ANY)
@@ -224,20 +253,10 @@
             pltpu.SemaphoreType.DMA((slots,)),
         ],
         out_shape=[jax.ShapeDtypeStruct((rows, out_local), dtype) for dtype in dtypes],
-        compiler_params=pltpu.CompilerParams(vmem_limit_bytes=52 * MIB),
+        compiler_params=pltpu.CompilerParams(vmem_limit_bytes=60 * MIB),
         cost_estimate=SMALL,
         name="project",
     )(jnp.stack(chunks), attended, out_weight)
-
-
-def fetch_all(sources, targets, sems):
-    copies = [
-        pltpu.make_async_copy(source, target, sems.at[i])
-        for i, (source, target) in enumerate(zip(sources, targets))
-    ]
-    for copy in copies:
-        copy.start()
-    return copies
 
 
 def masked(low, owner, adapters, ranks, adapters_here):
@@ -246,91 +265,130 @@
     return jnp.where(row // ranks + owner * adapters_here == adapters, terms, 0.0)
 
 
-def low_kernel(ranks, sides, owners_ref, adapters_ref, *refs):
-    count = (len(refs) - 2 - 2 * sides) // 2
-    a_hbm, piece_hbm = refs[:sides], refs[sides : sides + count]
-    out_ref = refs[sides + count]
-    a_refs = refs[sides + count + 1 : 2 * sides + count + 1]
-    piece_refs = refs[2 * sides + count + 1 : -1]
-    copies = fetch_all(a_hbm + piece_hbm, a_refs + piece_refs, refs[-1])
-    pair = piece_refs[0].shape[0]
-    sides_t = []
-    for a_ref, copy in zip(a_refs, copies):
+def block_parts(blocks):
+    arrays, places = [], []
+    for i, parts in enumerate(blocks):
+        first = 0
+        for part in parts:
+            arrays.append(part)
+            places.append((i, first, part.shape[0]))
+            first += part.shape[0]
+    return arrays, places
+
+
+def fetch_blocks(sources, places, column, target, sems, offset):
+    columns = pl.ds(column, target.shape[2])
+    return [
+        pltpu.make_async_copy(
+            source.at[:, columns], target.at[i, pl.ds(first, count)], sems.at[offset + j]
+        )
+        for j, (source, (i, first, count)) in enumerate(zip(sources, places))
+    ]
+
+
+def low_kernel(ranks, places, owners_ref, *refs):
+    sides, sources = refs[:2], refs[2 : 2 + len(places)]
+    out_ref, adapters_ref, side_ref, block_ref, sems = refs[2 + len(places) :]
+    copies = fetch_all(sides, [side_ref.at[i] for i in range(2)], sems)
+    parts = fetch_blocks(sources, places, 0, block_ref, sems, 2)
+    for copy in parts:
+        copy.start()
+    blocks, pair = block_ref.shape[:2]
+    rows = side_ref.shape[1] - ID_ROWS
+    sides_t, adapters = [], []
+    for i, copy in enumerate(copies):
         copy.wait()
-        sides_t.append(a_ref[...].astype(jnp.float32).T.astype(jnp.bfloat16))
+        sides_t.append(side_ref[i, :rows].astype(jnp.float32).T.astype(jnp.bfloat16))
+        ids = side_ref[i, rows:, :rows].astype(jnp.float32)
+        adapters.append(ids[:8].astype(jnp.int32))
     a_t = jnp.concatenate(sides_t, axis=1)
+    adapters_ref[...] = jnp.concatenate(adapters, axis=1)
+    adapters = adapters_ref[:1, :]
     row = lax.broadcasted_iota(jnp.int32, (pair, a_t.shape[1]), 0)
     total = jnp.zeros(row.shape, jnp.float32)
-    for i, piece_ref in enumerate(piece_refs):
-        copies[sides + i].wait()
-        part = jnp.dot(piece_ref[...], a_t, preferred_element_type=jnp.float32)
+    for i in range(blocks):
+        for copy, place in zip(parts, places):
+            if place[0] == i:
+                copy.wait()
+        part = jnp.dot(block_ref[i], a_t, preferred_element_type=jnp.float32)
         first = owners_ref[i] * (pair // ranks)
-        total += jnp.where(row // ranks + first == adapters_ref[...], part, 0.0)
+        total += jnp.where(row // ranks + first == adapters, part, 0.0)
     low = total[:ranks]
     for a in range(1, pair // ranks):
         low += total[a * ranks : (a + 1) * ranks]
     out_ref[...] = low.astype(out_ref.dtype)
 
 
-def low_rank(attended, pieces, owners, adapters, rank):
-    slots = adapters.shape[0]
-    arrays = [*attended, *pieces]
+def low_rank(sides, blocks, depth, owners, rank):
+    rows = sides[0].shape[0] - ID_ROWS
+    arrays, places = block_parts(blocks)
+    pair = sum(part.shape[0] for part in blocks[0])
     vmem = pl.BlockSpec(memory_space=pltpu.VMEM)
     return pl.pallas_call(
-        functools.partial(low_kernel, rank, len(attended)),
-        in_specs=[pl.BlockSpec(memory_space=pltpu.SMEM), vmem]
-        + [pl.BlockSpec(memory_space=pl.ANY)] * len(arrays),
-        out_specs=vmem,
-        out_shape=jax.ShapeDtypeStruct((rank, slots), jnp.bfloat16),
-        scratch_shapes=[pltpu.VMEM(a.shape, a.dtype) for a in arrays]
-        + [pltpu.SemaphoreType.DMA((len(arrays),))],
+        functools.partial(low_kernel, rank, places),
+        in_specs=[pl.BlockSpec(memory_space=pltpu.SMEM)]
+        + [pl.BlockSpec(memory_space=pl.ANY)] * (2 + len(arrays)),
+        out_specs=[vmem, vmem],
+        out_shape=[
+            jax.ShapeDtypeStruct((rank, 2 * rows), jnp.bfloat16),
+            jax.ShapeDtypeStruct((8, 2 * rows), jnp.int32),
+        ],
+        scratch_shapes=[
+            pltpu.VMEM((2, *sides[0].shape), jnp.bfloat16),
+            pltpu.VMEM((len(blocks), pair, depth), jnp.bfloat16),
+            pltpu.SemaphoreType.DMA((2 + len(arrays),)),
+        ],
         compiler_params=pltpu.CompilerParams(vmem_limit_bytes=32 * MIB),
         cost_estimate=SMALL,
         name="low_rank",
-    )(jnp.stack(owners), adapters.reshape(1, slots), *arrays)
-
-
-def delta_kernel(ranks, owners_ref, adapters_ref, low_ref, *refs):
-    count = (len(refs) - 3) // 2
-    out_refs, piece_refs = refs[count : count + 2], refs[count + 2 : -1]
-    copies = fetch_all(refs[:count], piece_refs, refs[-1])
-    pair = piece_refs[0].shape[0]
+    )(jnp.stack(owners), *sides, *arrays)
+
+
+def delta_kernel(ranks, places, column, owners_ref, adapters_ref, low_ref, *refs):
+    sources = refs[: len(places)]
+    here_ref, other_ref, block_ref, sems = refs[len(places) :]
+    parts = fetch_blocks(sources, places, column, block_ref, sems, 0)
+    for copy in parts:
+        copy.start()
+    blocks, pair, width = block_ref.shape
     low = low_ref[...].astype(jnp.float32)
-    sides, weights = [], []
-    for i, piece_ref in enumerate(piece_refs):
-        mine = masked(low, owners_ref[i], adapters_ref[...], ranks, pair // ranks)
+    sides = []
+    for i in range(blocks):
+        mine = masked(low, owners_ref[i], adapters_ref[:1, :], ranks, pair // ranks)
         sides.append(mine.T.astype(jnp.bfloat16))
-    for copy, piece_ref in zip(copies, piece_refs):
+    for copy in parts:
         copy.wait()
-        weights.append(piece_ref[...])
     delta = jnp.dot(
         jnp.concatenate(sides, axis=1),
-        jnp.concatenate(weights, axis=0),
+        block_ref[...].reshape(blocks * pair, width),
         preferred_element_type=jnp.float32,
     )
     delta = (0.5 * delta).astype(jnp.bfloat16)
-    rows = out_refs[0].shape[0]
-    out_refs[0][...] = delta[:rows]
-    out_refs[1][...] = delta[rows:]
-
-
-def correct(low, pieces, owners, adapters, rank):
-    slots = adapters.shape[0]
-    out_local = pieces[0].shape[1]
+    rows = here_ref.shape[0]
+    here_ref[...] = delta[:rows]
+    other_ref[...] = delta[rows:]
+
+
+def correct(low, adapters, blocks, column, out_local, owners, rank):
+    slots = adapters.shape[1]
+    arrays, places = block_parts(blocks)
+    pair = sum(part.shape[0] for part in blocks[0])
     vmem = pl.BlockSpec(memory_space=pltpu.VMEM)
     out = jax.ShapeDtypeStruct((slots // 2, out_local), jnp.bfloat16)
     return pl.pallas_call(
-        functools.partial(delta_kernel, rank),
+        functools.partial(delta_kernel, rank, places, column),
         in_specs=[pl.BlockSpec(memory_space=pltpu.SMEM), vmem, vmem]
-        + [pl.BlockSpec(memory_space=pl.ANY)] * len(pieces),
+        + [pl.BlockSpec(memory_space=pl.ANY)] * len(arrays),
         out_specs=[vmem, vmem],
         out_shape=[out, out],
-        scratch_shapes=[pltpu.VMEM(a.shape, a.dtype) for a in pieces]
-        + [pltpu.SemaphoreType.DMA((len(pieces),))],
+        scratch_shapes=[
+            pltpu.VMEM((len(blocks), pair, out_local), jnp.bfloat16),
+            pltpu.SemaphoreType.DMA((len(arrays),)),
+        ],
         compiler_params=pltpu.CompilerParams(vmem_limit_bytes=32 * MIB),
         cost_estimate=SMALL,
         name="correct",
-    )(jnp.stack(owners), adapters.reshape(1, slots), low, *pieces)
+    )(jnp.stack(owners), adapters, low, *arrays)
 
 
 def finish_kernel(occupied_ref, own_ref, *refs):
@@ -369,20 +427,25 @@
 
 
 def near_blocks(own):
-    return {0: own, **{bit: exchange(own, "dp", bit) for bit in neighbours()[:2]}}
+    return {0: [own], **{bit: [exchange(own, "dp", bit)] for bit in neighbours()[:2]}}
 
 
 def far_blocks(blocks):
     blocks = dict(blocks)
     a, b, *others = neighbours()
-    half = blocks[0].shape[0] // 2
-    blocks[a | b] = jnp.concatenate(
-        [exchange(blocks[a][:half], "dp", b), exchange(blocks[b][half:], "dp", a)]
-    )
+    half = blocks[0][0].shape[0] // 2
+    blocks[a | b] = [
+        exchange(blocks[a][0][:half], "dp", b),
+        exchange(blocks[b][0][half:], "dp", a),
+    ]
     for bit in others:
         for key in list(blocks):
-            blocks[key | bit] = exchange(blocks[key], "dp", bit)
+            blocks[key | bit] = [exchange(part, "dp", bit) for part in blocks[key]]
     return blocks
+
+
+def together(*values):
+    return lax.optimization_barrier(values)
 
 
 def body(
@@ -407,30 +470,43 @@
     pair = adapters_here * rank
     steps = list(range(shares - 1, 0, -1))
 
-    shrink = near_blocks(jnp.swapaxes(shrink_weight, 1, 2).reshape(pair, depth))
-    requests = jnp.concatenate([slot_request, exchange(slot_request, "dp", 1)])
-
+    own_block = jnp.concatenate(
+        [
+            jnp.swapaxes(shrink_weight, 1, 2).reshape(pair, depth),
+            expand_weight.reshape(pair, out_local),
+        ],
+        axis=1,
+    )
+    blocks = near_blocks(own_block)
     attended, piece = attend(
-        queries,
-        key_cache,
-        value_cache,
-        key_new,
-        value_new,
+        (
+            queries,
+            key_cache,
+            value_cache,
+            key_new,
+            value_new,
+            slot_request.reshape(1, -1),
+            request_adapter.reshape(1, -1),
+        ),
         lengths,
         out_weight,
         me ^ steps[0],
         out_local,
     )
-    received = [exchange(piece, "mp", steps[0])]
+    chained = shares == 4
+    if chained:
+        passed = lax.ppermute(piece, "mp", [(0, 1), (3, 2)])
+        received = [lax.ppermute(piece, "mp", [(1, 2), (2, 1)])]
+    else:
+        received = [exchange(piece, "mp", steps[0])]
+    (piece,) = project(attended, out_weight, [me ^ steps[1]], out_local, [jnp.bfloat16])
+    if chained:
+        piece, passed, received = together(piece, passed, received)
+        piece = (piece.astype(jnp.float32) + passed.astype(jnp.float32)).astype(jnp.bfloat16)
+    blocks, attended, piece = together(blocks, attended, piece)
+    received.append(exchange(piece, "mp", steps[1]))
+    blocks = far_blocks(blocks)
     beside = exchange(attended, "dp", 1)
-    (piece,) = project(attended, out_weight, [me ^ steps[1]], out_local, [jnp.bfloat16])
-    received.append(exchange(piece, "mp", steps[1]))
-    expand = expand_weight.reshape(pair, out_local)
-    shrink, expand, requests, attended, _ = lax.optimization_barrier(
-        (shrink, expand, requests, attended, piece)
-    )
-    shrink = far_blocks(shrink)
-    expand = near_blocks(expand)
     *pieces, own = project(
         attended,
         out_weight,
@@ -438,22 +514,19 @@
         out_local,
         [jnp.bfloat16] * (shares - 3) + [jnp.float32],
     )
+    attended, own = together(attended, own)
+
+    owners = [here ^ key for key in blocks]
+    blocks = list(blocks.values())
+    low, adapters = low_rank([attended, beside], blocks, depth, owners, rank)
     received += [exchange(piece, "mp", step) for piece, step in zip(pieces, steps[2:])]
-    requests, attended, _ = lax.optimization_barrier((requests, attended, own))
-
-    matches = requests[:, None] == jnp.arange(request_adapter.shape[0], dtype=jnp.int32)[None, :]
-    adapters = jnp.sum(jnp.where(matches, request_adapter[None, :], 0), axis=1)
-    owners = [here ^ key for key in shrink]
-    low = low_rank([attended, beside], list(shrink.values()), owners, adapters, rank)
-    expand, low = lax.optimization_barrier((expand, low))
-    expand = far_blocks(expand)
-    low = low.astype(jnp.float32)
+    low, received = together(low, received)
     step = 1
     while step < shares:
-        low = low + exchange(low.astype(jnp.bfloat16), "mp", step).astype(jnp.float32)
+        arrived = exchange(low, "mp", step)
+        low = (low.astype(jnp.float32) + arrived.astype(jnp.float32)).astype(jnp.bfloat16)
         step *= 2
-    low = low.astype(jnp.bfloat16)
-    correction, other = correct(low, list(expand.values()), owners, adapters, rank)
+    correction, other = correct(low, adapters, blocks, depth, out_local, owners, rank)
     return finish(own, [*received, correction, exchange(other, "dp", 1)], occupied)
 
 

time: 62.7 us -> 68.5 us (1.093)
  the two profiles are of different devices: /device:TPU:8 before, /device:TPU:0 now
where the time goes in v2:
time: 68.5 us; the launch traced here: 68.2 us
  Pallas kernels  28.7 us (42%)
  waiting for transfers between devices  17.3 us (25%)
  starting transfers between devices  15.9 us (23%)
  other arithmetic  3.57 us (5%)
  local copies, waits for them, and re-layouts  2.62 us (4%)
    ppermute x10, waiting for transfers between devices, exchange(): return lax.ppermute(value, axis, [(i, i ^ step) for i in range(count)])  16.4 us
    pallas_call x2, Pallas kernels, project(): pl.pallas_call(project_kernel, in_specs=[pl.BlockSpec(memory_space=pltpu....  11.5 us
    pallas_call x1, Pallas kernels, attend(): pl.pallas_call(functools.partial(attend_kernel, block), in_specs=[smem, s...  10.1 us
    ppermute x10, starting transfers between devices, exchange(): return lax.ppermute(value, axis, [(i, i ^ step) for i in range(count)])  8.92 us
    ppermute x1, starting transfers between devices, body(): passed = lax.ppermute(piece, 'mp', [(0, 1), (3, 2)])  6.31 us
    pallas_call x1, Pallas kernels, low_rank(): pl.pallas_call(functools.partial(low_kernel, rank, places), in_specs=[pl....  3.76 us
    pallas_call x1, Pallas kernels, finish(): pl.pallas_call(finish_kernel, in_specs=[vmem] * (2 + len(parts)), out_spe...  2.06 us
    convert_element_type x1, other arithmetic, body(): (piece.astype(jnp.float32) + passed.astype(jnp.float32)).astype(jnp.bfloa...  1.72 us
  transfers between devices with their start and end apart: 12, of which 8 were waited for; matrix products, arithmetic and copies ran while one was open for 6% of the time, Pallas kernels for 37%

profile of v2, /device:TPU:0, one launch (start us, length us, event | category | flops | bytes accessed | tf_op | source)
XLA Modules:
  0.0 68.2 jit_solution(9291164771020156748)
XLA Ops:
  0.0 1.2 %pad_maximum_fusion.refs_2_.refs_0_ = bf16[128,3072]{1,0:T(8,128)(2,1)S(1)} fusion(bf16[128,1024]{1,0:T(8,128)(2,1)} %bitcast.17, bf16[128,2048]{1,0:T(8,128)(2,1)} %bitcast.16), kind=kLoop, calls=%fused_computation | loop fusion | flops 1572864 | bytes 1572864 | tf_op jit(solution)/shard_map/concatenate | solution.py:473
  1.2 3.0 %collective-permute-start.1 = (bf16[128,3072]{1,0:T(8,128)(2,1)S(1)}, bf16[128,3072]{1,0:T(8,128)(2,1)S(1)}, u32[]{:S(2)}, u32[]{:S(2)}) collective-permute-start(bf16[128,3072]{1,0:T(8,128)(2,1)S(1)} %pad_maximum_fusion.refs_2_.refs_0_), channel_id=1, source_target_pairs={{0,16},{4,20},{8,24},{12,28},{16,0},{20,4},{24,8},{28,12},{1,17},{... | collective-permute-start | bytes 2359304 | tf_op jit(solution)/shard_map/ppermute | solution.py:422
  4.2 1.5 %collective-permute-start = (bf16[128,3072]{1,0:T(8,128)(2,1)S(1)}, bf16[128,3072]{1,0:T(8,128)(2,1)S(1)}, u32[]{:S(2)}, u32[]{:S(2)}) collective-permute-start(bf16[128,3072]{1,0:T(8,128)(2,1)S(1)} %pad_maximum_fusion.refs_2_.refs_0_), channel_id=1, source_target_pairs={{0,8},{4,12},{8,0},{12,4},{16,24},{20,28},{24,16},{28,20},{1,9},{5... | collective-permute-start | bytes 2359304 | tf_op jit(solution)/shard_map/ppermute | solution.py:422
  5.7 10.1 %attend.1 = (bf16[144,2048]{1,0:T(8,128)(2,1)}, bf16[128,1024]{1,0:T(8,128)(2,1)}) custom-call(s32[128]{0:T(128)} %lengths_ref.1, s32[1]{0:T(128)} %bitcast.4.chunk_ref, bf16[128,16,128]{2,1,0:T(8,128)(2,1)} %q_hbm.1, bf16[128,2,128,128]{3,2,1,0:T(8,128)(2,1)} %k_hbm.1, bf16[128,2,128,128]{3,2,1,0:T(8,128)(2,1)} %v_hbm.1, bf16[128,2,128]{2,1,0:T(2,128)(2,1)} %kn_hbm.1, ...), custom_call_target="tpu_custom_call" | custom-call | flops 1 | bytes 1 | tf_op jit(solution)/shard_map/attend/pallas_call | solution.py:201
  15.9 0.7 collective-permute-start.3
  16.5 6.3 %collective-permute-start.2 = (bf16[128,1024]{1,0:T(8,128)(2,1)}, bf16[128,1024]{1,0:T(8,128)(2,1)S(1)}, u32[]{:S(2)}, u32[]{:S(2)}) collective-permute-start(bf16[128,1024]{1,0:T(8,128)(2,1)} %get-tuple-element.28), channel_id=1, source_target_pairs={{0,1},{3,2},{4,5},{7,6},{8,9},{11,10},{12,13},{15,14},{16,17},{19,... | collective-permute-start | bytes 786440 | tf_op jit(solution)/shard_map/ppermute | solution.py:498
  22.9 4.1 %project.2 = bf16[128,1024]{1,0:T(8,128)(2,1)} custom-call(s32[1]{0:T(128)} %bitcast.7.chunks_ref, bf16[144,2048]{1,0:T(8,128)(2,1)} %get-tuple-element.34.a_hbm.refs_0_, bf16[2048,4096]{1,0:T(8,128)(2,1)} %w_ref.5), custom_call_target="tpu_custom_call" | custom-call | flops 1 | bytes 1 | tf_op jit(solution)/shard_map/project/pallas_call | solution.py:245
  26.9 0.9 %collective-permute-done.2 = bf16[128,1024]{1,0:T(8,128)(2,1)S(1)} collective-permute-done((bf16[128,1024]{1,0:T(8,128)(2,1)}, bf16[128,1024]{1,0:T(8,128)(2,1)S(1)}, u32[]{:S(2)}, u32[]{:S(2)}) %collective-permute-start.2) | collective-permute-done | bytes 262176 | tf_op jit(solution)/shard_map/ppermute | solution.py:498
  27.9 1.7 %add_convert_fusion = bf16[128,1024]{1,0:T(8,128)(2,1)} fusion(bf16[128,1024]{1,0:T(8,128)(2,1)S(1)} %collective-permute-done.2, bf16[128,1024]{1,0:T(8,128)(2,1)} %project.2), kind=kLoop, calls=%fused_computation.1 | loop fusion | flops 524288 | bytes 786432 | tf_op jit(solution)/shard_map/convert_element_type | solution.py:505
  29.6 0.0 collective-permute-done.1.refs_4_.refs_2_
  29.6 0.8 %slice.6 = bf16[64,3072]{1,0:T(8,128)(2,1)} slice(bf16[128,3072]{1,0:T(8,128)(2,1)S(1)} %collective-permute-done.refs_3_.refs_1_), slice={[0:64], [0:3072]} | slice | bytes 786432 | tf_op jit(solution)/shard_map/slice | solution.py:438
  30.4 0.8 %slice.7 = bf16[64,3072]{1,0:T(8,128)(2,1)} slice(bf16[128,3072]{1,0:T(8,128)(2,1)S(1)} %collective-permute-done.1.refs_4_.refs_2_), slice={[64:128], [0:3072]} | slice | bytes 786432 | tf_op jit(solution)/shard_map/slice | solution.py:439
  31.2 0.5 collective-permute-start.6
  31.7 0.5 collective-permute-start.5
  32.2 0.6 pad_add_fusion.chunks_ref
  32.8 2.3 %collective-permute-start.7 = (bf16[128,1024]{1,0:T(8,128)(2,1)}, bf16[128,1024]{1,0:T(8,128)(2,1)}, u32[]{:S(2)}, u32[]{:S(2)}) collective-permute-start(bf16[128,1024]{1,0:T(8,128)(2,1)} %add_convert_fusion), channel_id=1, source_target_pairs={{0,2},{1,3},{2,0},{3,1},{4,6},{5,7},{6,4},{7,5},{8,10},{9,11},{10,... | collective-permute-start | bytes 786440 | tf_op jit(solution)/shard_map/ppermute | solution.py:422
  35.1 7.4 %project.3 = (bf16[128,1024]{1,0:T(8,128)(2,1)}, f32[128,1024]{1,0:T(8,128)}) custom-call(s32[2]{0:T(128)} %pad_add_fusion.chunks_ref, bf16[144,2048]{1,0:T(8,128)(2,1)} %get-tuple-element.34.a_hbm.refs_0_, bf16[2048,4096]{1,0:T(8,128)(2,1)} %w_ref.5), custom_call_target="tpu_custom_call" | custom-call | flops 1 | bytes 1 | tf_op jit(solution)/shard_map/project/pallas_call | solution.py:245
  42.5 0.3 collective-permute-start.8
  42.8 0.1 pad_add_fusion.1.owners_ref
  42.9 0.1 collective-permute-done.6.refs_6_.refs_4_
  42.9 0.2 collective-permute-done.5.refs_5_.refs_3_
  43.2 3.8 %low_rank.1 = (bf16[64,256]{1,0:T(8,128)(2,1)S(1)}, s32[8,256]{1,0:T(8,128)S(1)}) custom-call(s32[4]{0:T(128)S(1)} %pad_add_fusion.1.owners_ref, bf16[144,2048]{1,0:T(8,128)(2,1)} %get-tuple-element.34.a_hbm.refs_0_, bf16[144,2048]{1,0:T(8,128)(2,1)} %collective-permute-done.4.refs_1_, bf16[128,3072]{1,0:T(8,128)(2,1)S(1)} %pad_maximum_fusion.refs_2_.refs_0_, ...), custom_call_target="tpu_custom_call" | custom-call | flops 1 | bytes 1 | tf_op jit(solution)/shard_map/low_rank/pallas_call | solution.py:327
  46.9 0.9 %collective-permute-done.7.refs_1_ = bf16[128,1024]{1,0:T(8,128)(2,1)} collective-permute-done((bf16[128,1024]{1,0:T(8,128)(2,1)}, bf16[128,1024]{1,0:T(8,128)(2,1)}, u32[]{:S(2)}, u32[]{:S(2)}) %collective-permute-start.7) | collective-permute-done | bytes 262176 | tf_op jit(solution)/shard_map/ppermute | solution.py:422
  47.9 5.5 %collective-permute-done.8.refs_2_ = bf16[128,1024]{1,0:T(8,128)(2,1)} collective-permute-done((bf16[128,1024]{1,0:T(8,128)(2,1)}, bf16[128,1024]{1,0:T(8,128)(2,1)}, u32[]{:S(2)}, u32[]{:S(2)}) %collective-permute-start.8) | collective-permute-done | bytes 262176 | tf_op jit(solution)/shard_map/ppermute | solution.py:422
  53.4 3.9 %collective-permute-done.9 = bf16[64,256]{1,0:T(8,128)(2,1)S(1)} collective-permute-done((bf16[64,256]{1,0:T(8,128)(2,1)S(1)}, bf16[64,256]{1,0:T(8,128)(2,1)S(1)}, u32[]{:S(2)}, u32[]{:S(2)}) %collective-permute-start.9) | collective-permute-done | bytes 32800 | tf_op jit(solution)/shard_map/ppermute | solution.py:422
  57.3 0.7 %collective-permute-start.10 = (bf16[64,256]{1,0:T(8,128)(2,1)S(1)}, bf16[64,256]{1,0:T(8,128)(2,1)S(1)}, u32[]{:S(2)}, u32[]{:S(2)}) collective-permute-start(bf16[64,256]{1,0:T(8,128)(2,1)S(1)} %add_convert_fusion.2), channel_id=1, source_target_pairs={{0,2},{1,3},{2,0},{3,1},{4,6},{5,7},{6,4},{7,5},{8,10},{9,11},{10,... | collective-permute-start | bytes 98312 | tf_op jit(solution)/shard_map/ppermute | solution.py:422
  58.0 4.2 %collective-permute-done.10 = bf16[64,256]{1,0:T(8,128)(2,1)S(1)} collective-permute-done((bf16[64,256]{1,0:T(8,128)(2,1)S(1)}, bf16[64,256]{1,0:T(8,128)(2,1)S(1)}, u32[]{:S(2)}, u32[]{:S(2)}) %collective-permute-start.10) | collective-permute-done | bytes 32800 | tf_op jit(solution)/shard_map/ppermute | solution.py:422
  62.2 1.3 %correct.1 = (bf16[128,1024]{1,0:T(8,128)(2,1)S(1)}, bf16[128,1024]{1,0:T(8,128)(2,1)S(1)}) custom-call(s32[4]{0:T(128)S(1)} %pad_add_fusion.1.owners_ref, s32[8,256]{1,0:T(8,128)S(1)} %get-tuple-element.45.adapters_ref, bf16[64,256]{1,0:T(8,128)(2,1)S(1)} %add_convert_fusion.1.low_ref, bf16[128,3072]{1,0:T(8,128)(2,1)S(1)} %pad_maximum_fusion.refs_2_.refs_0_, ...), custom_call_target="tpu_custom_call" | custom-call | flops 1 | bytes 1 | tf_op jit(solution)/shard_map/correct/pallas_call | solution.py:378
  63.5 0.1 collective-permute-start.11
  63.6 1.5 %collective-permute-done.11.refs_4_ = bf16[128,1024]{1,0:T(8,128)(2,1)S(1)} collective-permute-done((bf16[128,1024]{1,0:T(8,128)(2,1)S(1)}, bf16[128,1024]{1,0:T(8,128)(2,1)S(1)}, u32[]{:S(2)}, u32[]{:S(2)}) %collective-permute-start.11) | collective-permute-done | bytes 262176 | tf_op jit(solution)/shard_map/ppermute | solution.py:422
  65.1 1.0 %copy-done = f32[128,1024]{1,0:T(8,128)S(1)} copy-done((f32[128,1024]{1,0:T(8,128)S(1)}, f32[128,1024]{1,0:T(8,128)}, u32[]{:S(2)}) %copy-start) | copy-done | bytes 524312
  66.2 2.1 %finish.1 = bf16[128,1024]{1,0:T(8,128)(2,1)} custom-call(s32[1,128]{1,0:T(1,128)S(1)} %bitcast.15, f32[128,1024]{1,0:T(8,128)S(1)} %copy-done, bf16[128,1024]{1,0:T(8,128)(2,1)S(1)} %collective-permute-done.3.refs_0_, bf16[128,1024]{1,0:T(8,128)(2,1)} %collective-permute-done.7.refs_1_, bf16[128,1024]{1,0:T(8,128)(2,1)} %collective-permute-done.8.refs_2_, ...), custom_call_target="tpu_custom_call" | custom-call | flops 1 | bytes 1 | tf_op jit(solution)/shard_map/finish/pallas_call | solution.py:409
  (10 shorter events, 0.0 us)
Async XLA Ops:
  1.2 28.4 %collective-permute-start.1 = (bf16[128,3072]{1,0:T(8,128)(2,1)S(1)}, bf16[128,3072]{1,0:T(8,128)(2,1)S(1)}, u32[]{:S(2)}, u32[]{:S(2)}) collective-permute-start(bf16[128,3072]{1,0:T(8,128)(2,1)S(1)} %pad_maximum_fusion.refs_2_.refs_0_), channel_id=1, source_target_pairs={{0,16},{4,20},{8,24},{12,28},{16,0},{20,4},{24,8},{28,12},{1,17},{... | collective-permute-start | bytes 2359304 | tf_op jit(solution)/shard_map/ppermute | solution.py:422
  4.2 25.4 %collective-permute-start = (bf16[128,3072]{1,0:T(8,128)(2,1)S(1)}, bf16[128,3072]{1,0:T(8,128)(2,1)S(1)}, u32[]{:S(2)}, u32[]{:S(2)}) collective-permute-start(bf16[128,3072]{1,0:T(8,128)(2,1)S(1)} %pad_maximum_fusion.refs_2_.refs_0_), channel_id=1, source_target_pairs={{0,8},{4,12},{8,0},{12,4},{16,24},{20,28},{24,16},{28,20},{1,9},{5... | collective-permute-start | bytes 2359304 | tf_op jit(solution)/shard_map/ppermute | solution.py:422
  15.9 11.1 %collective-permute-start.3 = (bf16[128,1024]{1,0:T(8,128)(2,1)}, bf16[128,1024]{1,0:T(8,128)(2,1)S(1)}, u32[]{:S(2)}, u32[]{:S(2)}) collective-permute-start(bf16[128,1024]{1,0:T(8,128)(2,1)} %get-tuple-element.28), channel_id=1, source_target_pairs={{1,2},{2,1},{5,6},{6,5},{9,10},{10,9},{13,14},{14,13},{17,18},{18,... | collective-permute-start | bytes 786440 | tf_op jit(solution)/shard_map/ppermute | solution.py:499
  16.5 11.3 %collective-permute-start.2 = (bf16[128,1024]{1,0:T(8,128)(2,1)}, bf16[128,1024]{1,0:T(8,128)(2,1)S(1)}, u32[]{:S(2)}, u32[]{:S(2)}) collective-permute-start(bf16[128,1024]{1,0:T(8,128)(2,1)} %get-tuple-element.28), channel_id=1, source_target_pairs={{0,1},{3,2},{4,5},{7,6},{8,9},{11,10},{12,13},{15,14},{16,17},{19,... | collective-permute-start | bytes 786440 | tf_op jit(solution)/shard_map/ppermute | solution.py:498
  29.6 13.6 %collective-permute-start.4 = (bf16[144,2048]{1,0:T(8,128)(2,1)}, bf16[144,2048]{1,0:T(8,128)(2,1)}, u32[]{:S(2)}, u32[]{:S(2)}) collective-permute-start(bf16[144,2048]{1,0:T(8,128)(2,1)} %get-tuple-element.34.a_hbm.refs_0_), channel_id=1, source_target_pairs={{0,4},{4,0},{8,12},{12,8},{16,20},{20,16},{24,28},{28,24},{1,5},{5... | collective-permute-start | bytes 1769480 | tf_op jit(solution)/shard_map/ppermute | solution.py:422
  31.2 11.7 %collective-permute-start.6 = (bf16[64,3072]{1,0:T(8,128)(2,1)}, bf16[64,3072]{1,0:T(8,128)(2,1)S(1)}, u32[]{:S(2)}, u32[]{:S(2)}) collective-permute-start(bf16[64,3072]{1,0:T(8,128)(2,1)} %slice.7), channel_id=1, source_target_pairs={{0,8},{4,12},{8,0},{12,4},{16,24},{20,28},{24,16},{28,20},{1,9},{5... | collective-permute-start | bytes 1179656 | tf_op jit(solution)/shard_map/ppermute | solution.py:422
  31.7 11.5 %collective-permute-start.5 = (bf16[64,3072]{1,0:T(8,128)(2,1)}, bf16[64,3072]{1,0:T(8,128)(2,1)S(1)}, u32[]{:S(2)}, u32[]{:S(2)}) collective-permute-start(bf16[64,3072]{1,0:T(8,128)(2,1)} %slice.6), channel_id=1, source_target_pairs={{0,16},{4,20},{8,24},{12,28},{16,0},{20,4},{24,8},{28,12},{1,17},{... | collective-permute-start | bytes 1179656 | tf_op jit(solution)/shard_map/ppermute | solution.py:422
  32.8 32.3 %copy-start.1 = (s32[128]{0:T(128)S(1)}, s32[128]{0:T(128)}, u32[]{:S(2)}) copy-start(s32[128]{0:T(128)} %param.18) | copy-start | bytes 1540
  32.8 15.1 %collective-permute-start.7 = (bf16[128,1024]{1,0:T(8,128)(2,1)}, bf16[128,1024]{1,0:T(8,128)(2,1)}, u32[]{:S(2)}, u32[]{:S(2)}) collective-permute-start(bf16[128,1024]{1,0:T(8,128)(2,1)} %add_convert_fusion), channel_id=1, source_target_pairs={{0,2},{1,3},{2,0},{3,1},{4,6},{5,7},{6,4},{7,5},{8,10},{9,11},{10,... | collective-permute-start | bytes 786440 | tf_op jit(solution)/shard_map/ppermute | solution.py:422
  42.5 10.9 %collective-permute-start.8 = (bf16[128,1024]{1,0:T(8,128)(2,1)}, bf16[128,1024]{1,0:T(8,128)(2,1)}, u32[]{:S(2)}, u32[]{:S(2)}) collective-permute-start(bf16[128,1024]{1,0:T(8,128)(2,1)} %get-tuple-element.41), channel_id=1, source_target_pairs={{0,1},{1,0},{2,3},{3,2},{4,5},{5,4},{6,7},{7,6},{8,9},{9,8},{10,11... | collective-permute-start | bytes 786440 | tf_op jit(solution)/shard_map/ppermute | solution.py:422
  53.4 3.9 %collective-permute-start.9 = (bf16[64,256]{1,0:T(8,128)(2,1)S(1)}, bf16[64,256]{1,0:T(8,128)(2,1)S(1)}, u32[]{:S(2)}, u32[]{:S(2)}) collective-permute-start(bf16[64,256]{1,0:T(8,128)(2,1)S(1)} %get-tuple-element.46), channel_id=1, source_target_pairs={{0,1},{1,0},{2,3},{3,2},{4,5},{5,4},{6,7},{7,6},{8,9},{9,8},{10,11... | collective-permute-start | bytes 98312 | tf_op jit(solution)/shard_map/ppermute | solution.py:422
  57.3 4.9 %collective-permute-start.10 = (bf16[64,256]{1,0:T(8,128)(2,1)S(1)}, bf16[64,256]{1,0:T(8,128)(2,1)S(1)}, u32[]{:S(2)}, u32[]{:S(2)}) collective-permute-start(bf16[64,256]{1,0:T(8,128)(2,1)S(1)} %add_convert_fusion.2), channel_id=1, source_target_pairs={{0,2},{1,3},{2,0},{3,1},{4,6},{5,7},{6,4},{7,5},{8,10},{9,11},{10,... | collective-permute-start | bytes 98312 | tf_op jit(solution)/shard_map/ppermute | solution.py:422
  63.5 1.6 %collective-permute-start.11 = (bf16[128,1024]{1,0:T(8,128)(2,1)S(1)}, bf16[128,1024]{1,0:T(8,128)(2,1)S(1)}, u32[]{:S(2)}, u32[]{:S(2)}) collective-permute-start(bf16[128,1024]{1,0:T(8,128)(2,1)S(1)} %get-tuple-element.48), channel_id=1, source_target_pairs={{0,4},{4,0},{8,12},{12,8},{16,20},{20,16},{24,28},{28,24},{1,5},{5... | collective-permute-start | bytes 786440 | tf_op jit(solution)/shard_map/ppermute | solution.py:422
  65.1 1.0 %copy-start = (f32[128,1024]{1,0:T(8,128)S(1)}, f32[128,1024]{1,0:T(8,128)}, u32[]{:S(2)}) copy-start(f32[128,1024]{1,0:T(8,128)} %get-tuple-element.33.own_ref) | copy-start | bytes 1572868

commit v3 on v2

--- a/solution.py
+++ b/solution.py
@@ -105,7 +105,7 @@
 def attend_kernel(
     block,
     lengths_ref,
-    chunk_ref,
+    chunks_ref,
     q_hbm,
     k_hbm,
     v_hbm,
@@ -115,7 +115,8 @@
     adapter_hbm,
     w_ref,
     out_ref,
-    piece_ref,
+    first_ref,
+    second_ref,
     q_ref,
     k_ref,
     v_ref,
@@ -131,8 +132,9 @@
 ):
     rows, heads, width = q_ref.shape
     blocks = rows // block
-    tiles = piece_ref.shape[1] // TILE
-    column = chunk_ref[0] * piece_ref.shape[1]
+    piece_refs = (first_ref, second_ref)
+    out_local = first_ref.shape[1]
+    tiles = out_local // TILE
 
     def block_copies(i):
         part = pl.ds(pl.multiple_of(i * block, block), block)
@@ -155,8 +157,10 @@
         return carry
 
     lax.fori_loop(0, blocks, begin, 0)
-    for j in range(tiles):
-        fetch(w_ref, buffer_ref, sem_ref, j, column + j * TILE).start()
+    for i in range(len(piece_refs)):
+        for j in range(tiles):
+            column = chunks_ref[i] * out_local + j * TILE
+            fetch(w_ref, buffer_ref, sem_ref, i * tiles + j, column).start()
     for copy in new_copies:
         copy.wait()
     out_ref[pl.ds(rows, ID_ROWS), :] = jnp.zeros((ID_ROWS, out_ref.shape[1]), out_ref.dtype)
@@ -185,23 +189,25 @@
         return carry
 
     lax.fori_loop(0, blocks, one_block, 0)
-    project_tiles(out_ref, w_ref, buffer_ref, sem_ref, piece_ref, 0, column)
-
-
-def attend(arrays, lengths, out_weight, chunk, out_local):
+    for i, piece_ref in enumerate(piece_refs):
+        column = chunks_ref[i] * out_local
+        project_tiles(out_ref, w_ref, buffer_ref, sem_ref, piece_ref, i * tiles, column)
+
+
+def attend(arrays, lengths, out_weight, chunks, out_local):
     queries, key_cache = arrays[:2]
     rows, heads, width = queries.shape
     cache = key_cache.shape[2]
     block = min(16, rows)
     depth = heads * width
-    tiles = out_local // TILE
+    tiles = len(chunks) * (out_local // TILE)
     smem = pl.BlockSpec(memory_space=pltpu.SMEM)
     hbm = pl.BlockSpec(memory_space=pltpu.HBM)
     vmem = pl.BlockSpec(memory_space=pltpu.VMEM)
     return pl.pallas_call(
         functools.partial(attend_kernel, block),
         in_specs=[smem, smem] + [hbm] * (len(arrays) + 1),
-        out_specs=[vmem, vmem],
+        out_specs=[vmem, vmem, vmem],
         scratch_shapes=[pltpu.VMEM(a.shape, a.dtype) for a in arrays]
         + [
             pltpu.VMEM((block * heads, width), jnp.float32),
@@ -212,12 +218,12 @@
         ],
         out_shape=[
             jax.ShapeDtypeStruct((rows + ID_ROWS, depth), jnp.bfloat16),
-            jax.ShapeDtypeStruct((rows, out_local), jnp.bfloat16),
-        ],
-        compiler_params=pltpu.CompilerParams(vmem_limit_bytes=60 * MIB),
+        ]
+        + [jax.ShapeDtypeStruct((rows, out_local), jnp.bfloat16) for _ in chunks],
+        compiler_params=pltpu.CompilerParams(vmem_limit_bytes=57 * MIB),
         cost_estimate=SMALL,
         name="attend",
-    )(lengths, chunk.reshape(1), *arrays, out_weight)
+    )(lengths, jnp.stack(chunks), *arrays, out_weight)
 
 
 def project_kernel(chunks_ref, a_hbm, w_ref, *refs):
@@ -253,7 +259,7 @@
             pltpu.SemaphoreType.DMA((slots,)),
         ],
         out_shape=[jax.ShapeDtypeStruct((rows, out_local), dtype) for dtype in dtypes],
-        compiler_params=pltpu.CompilerParams(vmem_limit_bytes=60 * MIB),
+        compiler_params=pltpu.CompilerParams(vmem_limit_bytes=52 * MIB),
         cost_estimate=SMALL,
         name="project",
     )(jnp.stack(chunks), attended, out_weight)
@@ -478,7 +484,7 @@
         axis=1,
     )
     blocks = near_blocks(own_block)
-    attended, piece = attend(
+    attended, piece, second = attend(
         (
             queries,
             key_cache,
@@ -490,7 +496,7 @@
         ),
         lengths,
         out_weight,
-        me ^ steps[0],
+        [me ^ step for step in steps[:2]],
         out_local,
     )
     chained = shares == 4
@@ -499,14 +505,6 @@
         received = [lax.ppermute(piece, "mp", [(1, 2), (2, 1)])]
     else:
         received = [exchange(piece, "mp", steps[0])]
-    (piece,) = project(attended, out_weight, [me ^ steps[1]], out_local, [jnp.bfloat16])
-    if chained:
-        piece, passed, received = together(piece, passed, received)
-        piece = (piece.astype(jnp.float32) + passed.astype(jnp.float32)).astype(jnp.bfloat16)
-    blocks, attended, piece = together(blocks, attended, piece)
-    received.append(exchange(piece, "mp", steps[1]))
-    blocks = far_blocks(blocks)
-    beside = exchange(attended, "dp", 1)
     *pieces, own = project(
         attended,
         out_weight,
@@ -514,18 +512,21 @@
         out_local,
         [jnp.bfloat16] * (shares - 3) + [jnp.float32],
     )
-    attended, own = together(attended, own)
+    if chained:
+        passed, received, second, own = together(passed, received, second, own)
+        second = (second.astype(jnp.float32) + passed.astype(jnp.float32)).astype(jnp.bfloat16)
+    blocks, attended, own = together(blocks, attended, own)
+    received.append(exchange(second, "mp", steps[1]))
+    received += [exchange(piece, "mp", step) for piece, step in zip(pieces, steps[2:])]
+    blocks = far_blocks(blocks)
+    beside = exchange(attended, "dp", 1)
 
     owners = [here ^ key for key in blocks]
     blocks = list(blocks.values())
     low, adapters = low_rank([attended, beside], blocks, depth, owners, rank)
-    received += [exchange(piece, "mp", step) for piece, step in zip(pieces, steps[2:])]
     low, received = together(low, received)
-    step = 1
-    while step < shares:
-        arrived = exchange(low, "mp", step)
-        low = (low.astype(jnp.float32) + arrived.astype(jnp.float32)).astype(jnp.bfloat16)
-        step *= 2
+    lows = [low] + [exchange(low, "mp", step) for step in range(1, shares)]
+    low = sum(part.astype(jnp.float32) for part in lows).astype(jnp.bfloat16)
     correction, other = correct(low, adapters, blocks, depth, out_local, owners, rank)
     return finish(own, [*received, correction, exchange(other, "dp", 1)], occupied)
 

time: 68.5 us -> 64.3 us (0.939)
  waiting for transfers between devices: 17.3 us -> 13 us
  Pallas kernels: 28.7 us -> 25.5 us
  starting transfers between devices: 15.9 us -> 19 us
    pallas_call x2 -> x1, Pallas kernels: 11.5 us -> 6.93 us  [project(): pl.pallas_call(project_kernel, in_specs=[pl.BlockSpec(memory_space=pltpu....]
    ppermute x10 -> x11, waiting for transfers between devices: 16.4 us -> 13 us  [exchange(): return lax.ppermute(value, axis, [(i, i ^ step) for i in range(count)])]
    ppermute x10 -> x11, starting transfers between devices: 8.92 us -> 12.1 us  [exchange(): return lax.ppermute(value, axis, [(i, i ^ step) for i in range(count)])]
    pallas_call x1, Pallas kernels: 10.1 us -> 11.5 us  [attend(): pl.pallas_call(functools.partial(attend_kernel, block), in_specs=[smem, s...]
    ppermute x1, waiting for transfers between devices: 0.94 us -> 0.01 us  [body(): passed = lax.ppermute(piece, 'mp', [(0, 1), (3, 2)])]
    convert_element_type x3 -> x2, other arithmetic: 1.74 us -> 1.77 us  [the longest x1 1.74 us: body(): (second.astype(jnp.float32) + passed.astype(jnp.float32)).astype(jnp.bflo...]
  transfers between devices with their start and end apart: 12 -> 13, of which waited for: 8 -> 7; matrix products, arithmetic and copies ran while one was open for 6% -> 6% of each run, Pallas kernels for 37% -> 35%
where the time goes in v3:
time: 64.3 us; the launch traced here: 64 us
  Pallas kernels  25.5 us (40%)
  starting transfers between devices  19 us (30%)
  waiting for transfers between devices  13 us (20%)
  other arithmetic  3.71 us (6%)
  local copies, waits for them, and re-layouts  2.64 us (4%)
    ppermute x11, waiting for transfers between devices, exchange(): return lax.ppermute(value, axis, [(i, i ^ step) for i in range(count)])  13 us
    ppermute x11, starting transfers between devices, exchange(): return lax.ppermute(value, axis, [(i, i ^ step) for i in range(count)])  12.1 us
    pallas_call x1, Pallas kernels, attend(): pl.pallas_call(functools.partial(attend_kernel, block), in_specs=[smem, s...  11.5 us
    pallas_call x1, Pallas kernels, project(): pl.pallas_call(project_kernel, in_specs=[pl.BlockSpec(memory_space=pltpu....  6.93 us
    ppermute x1, starting transfers between devices, body(): passed = lax.ppermute(piece, 'mp', [(0, 1), (3, 2)])  6.3 us
    pallas_call x1, Pallas kernels, low_rank(): pl.pallas_call(functools.partial(low_kernel, rank, places), in_specs=[pl....  3.76 us
    pallas_call x1, Pallas kernels, finish(): pl.pallas_call(finish_kernel, in_specs=[vmem] * (2 + len(parts)), out_spe...  1.99 us
    convert_element_type x1, other arithmetic, body(): (second.astype(jnp.float32) + passed.astype(jnp.float32)).astype(jnp.bflo...  1.74 us
  transfers between devices with their start and end apart: 13, of which 7 were waited for; matrix products, arithmetic and copies ran while one was open for 6% of the time, Pallas kernels for 35%

profile of v3, /device:TPU:0, one launch (start us, length us, event | category | flops | bytes accessed | tf_op | source)
XLA Modules:
  0.0 64.0 jit_solution(7383463373469255507)
XLA Ops:
  0.0 1.2 %pad_maximum_fusion.refs_2_.refs_0_ = bf16[128,3072]{1,0:T(8,128)(2,1)S(1)} fusion(bf16[128,1024]{1,0:T(8,128)(2,1)} %bitcast.17, bf16[128,2048]{1,0:T(8,128)(2,1)} %bitcast.16), kind=kLoop, calls=%fused_computation | loop fusion | flops 1572864 | bytes 1572864 | tf_op jit(solution)/shard_map/concatenate | solution.py:479
  1.2 3.0 %collective-permute-start.1 = (bf16[128,3072]{1,0:T(8,128)(2,1)S(1)}, bf16[128,3072]{1,0:T(8,128)(2,1)S(1)}, u32[]{:S(2)}, u32[]{:S(2)}) collective-permute-start(bf16[128,3072]{1,0:T(8,128)(2,1)S(1)} %pad_maximum_fusion.refs_2_.refs_0_), channel_id=1, source_target_pairs={{0,16},{4,20},{8,24},{12,28},{16,0},{20,4},{24,8},{28,12},{1,17},{... | collective-permute-start | bytes 2359304 | tf_op jit(solution)/shard_map/ppermute | solution.py:428
  4.2 1.5 %collective-permute-start = (bf16[128,3072]{1,0:T(8,128)(2,1)S(1)}, bf16[128,3072]{1,0:T(8,128)(2,1)S(1)}, u32[]{:S(2)}, u32[]{:S(2)}) collective-permute-start(bf16[128,3072]{1,0:T(8,128)(2,1)S(1)} %pad_maximum_fusion.refs_2_.refs_0_), channel_id=1, source_target_pairs={{0,8},{4,12},{8,0},{12,4},{16,24},{20,28},{24,16},{28,20},{1,9},{5... | collective-permute-start | bytes 2359304 | tf_op jit(solution)/shard_map/ppermute | solution.py:428
  5.7 0.6 pad_add_fusion.chunks_ref
  6.3 11.5 %attend.1 = (bf16[144,2048]{1,0:T(8,128)(2,1)}, bf16[128,1024]{1,0:T(8,128)(2,1)}, bf16[128,1024]{1,0:T(8,128)(2,1)}) custom-call(s32[128]{0:T(128)} %lengths_ref.1, s32[2]{0:T(128)} %pad_add_fusion.chunks_ref, bf16[128,16,128]{2,1,0:T(8,128)(2,1)} %q_hbm.1, bf16[128,2,128,128]{3,2,1,0:T(8,128)(2,1)} %k_hbm.1, bf16[128,2,128,128]{3,2,1,0:T(8,128)(2,1)} %v_hbm.1, ...), custom_call_target="tpu_custom_call" | custom-call | flops 1 | bytes 1 | tf_op jit(solution)/shard_map/attend/pallas_call | solution.py:207
  17.9 0.7 %collective-permute-start.3 = (bf16[128,1024]{1,0:T(8,128)(2,1)}, bf16[128,1024]{1,0:T(8,128)(2,1)S(1)}, u32[]{:S(2)}, u32[]{:S(2)}) collective-permute-start(bf16[128,1024]{1,0:T(8,128)(2,1)} %get-tuple-element.28), channel_id=1, source_target_pairs={{1,2},{2,1},{5,6},{6,5},{9,10},{10,9},{13,14},{14,13},{17,18},{18,... | collective-permute-start | bytes 786440 | tf_op jit(solution)/shard_map/ppermute | solution.py:505
  18.6 6.3 %collective-permute-start.2 = (bf16[128,1024]{1,0:T(8,128)(2,1)}, bf16[128,1024]{1,0:T(8,128)(2,1)S(1)}, u32[]{:S(2)}, u32[]{:S(2)}) collective-permute-start(bf16[128,1024]{1,0:T(8,128)(2,1)} %get-tuple-element.28), channel_id=1, source_target_pairs={{0,1},{3,2},{4,5},{7,6},{8,9},{11,10},{12,13},{15,14},{16,17},{19,... | collective-permute-start | bytes 786440 | tf_op jit(solution)/shard_map/ppermute | solution.py:504
  24.9 0.1 pad_add_fusion.1.chunks_ref
  24.9 6.9 %project.1 = (bf16[128,1024]{1,0:T(8,128)(2,1)}, f32[128,1024]{1,0:T(8,128)S(1)}) custom-call(s32[2]{0:T(128)S(1)} %pad_add_fusion.1.chunks_ref, bf16[144,2048]{1,0:T(8,128)(2,1)} %get-tuple-element.33.a_hbm.refs_0_, bf16[2048,4096]{1,0:T(8,128)(2,1)} %w_ref.3), custom_call_target="tpu_custom_call" | custom-call | flops 1 | bytes 1 | tf_op jit(solution)/shard_map/project/pallas_call | solution.py:251
  32.0 0.1 collective-permute-start.4
  32.0 0.4 collective-permute-start.8
  32.4 0.8 %slice.6 = bf16[64,3072]{1,0:T(8,128)(2,1)} slice(bf16[128,3072]{1,0:T(8,128)(2,1)S(1)} %collective-permute-done.refs_3_.refs_1_), slice={[0:64], [0:3072]} | slice | bytes 786432 | tf_op jit(solution)/shard_map/slice | solution.py:444
  33.2 0.8 %slice.7 = bf16[64,3072]{1,0:T(8,128)(2,1)} slice(bf16[128,3072]{1,0:T(8,128)(2,1)S(1)} %collective-permute-done.1.refs_4_.refs_2_), slice={[64:128], [0:3072]} | slice | bytes 786432 | tf_op jit(solution)/shard_map/slice | solution.py:445
  34.0 0.5 collective-permute-start.6
  34.5 0.5 collective-permute-start.5
  35.0 1.7 %add_convert_fusion = bf16[128,1024]{1,0:T(8,128)(2,1)} fusion(bf16[128,1024]{1,0:T(8,128)(2,1)} %copy-done.4, bf16[128,1024]{1,0:T(8,128)(2,1)S(1)} %copy-done.3), kind=kLoop, calls=%fused_computation.1 | loop fusion | flops 524288 | bytes 786432 | tf_op jit(solution)/shard_map/convert_element_type | solution.py:517
  36.8 1.6 %collective-permute-start.7 = (bf16[128,1024]{1,0:T(8,128)(2,1)}, bf16[128,1024]{1,0:T(8,128)(2,1)}, u32[]{:S(2)}, u32[]{:S(2)}) collective-permute-start(bf16[128,1024]{1,0:T(8,128)(2,1)} %add_convert_fusion), channel_id=1, source_target_pairs={{0,2},{1,3},{2,0},{3,1},{4,6},{5,7},{6,4},{7,5},{8,10},{9,11},{10,... | collective-permute-start | bytes 786440 | tf_op jit(solution)/shard_map/ppermute | solution.py:428
  38.4 0.1 pad_add_fusion.2.owners_ref
  38.4 6.9 %collective-permute-done.6.refs_6_.refs_4_ = bf16[64,3072]{1,0:T(8,128)(2,1)S(1)} collective-permute-done((bf16[64,3072]{1,0:T(8,128)(2,1)}, bf16[64,3072]{1,0:T(8,128)(2,1)S(1)}, u32[]{:S(2)}, u32[]{:S(2)}) %collective-permute-start.6) | collective-permute-done | bytes 393248 | tf_op jit(solution)/shard_map/ppermute | solution.py:428
  45.4 0.3 collective-permute-done.5.refs_5_.refs_3_
  45.6 3.8 %low_rank.1 = (bf16[64,256]{1,0:T(8,128)(2,1)S(1)}, s32[8,256]{1,0:T(8,128)S(1)}) custom-call(s32[4]{0:T(128)S(1)} %pad_add_fusion.2.owners_ref, bf16[144,2048]{1,0:T(8,128)(2,1)} %get-tuple-element.33.a_hbm.refs_0_, bf16[144,2048]{1,0:T(8,128)(2,1)} %collective-permute-done.4.refs_1_, bf16[128,3072]{1,0:T(8,128)(2,1)S(1)} %pad_maximum_fusion.refs_2_.refs_0_, ...), custom_call_target="tpu_custom_call" | custom-call | flops 1 | bytes 1 | tf_op jit(solution)/shard_map/low_rank/pallas_call | solution.py:333
  49.4 2.0 %collective-permute-done.7.refs_1_ = bf16[128,1024]{1,0:T(8,128)(2,1)} collective-permute-done((bf16[128,1024]{1,0:T(8,128)(2,1)}, bf16[128,1024]{1,0:T(8,128)(2,1)}, u32[]{:S(2)}, u32[]{:S(2)}) %collective-permute-start.7) | collective-permute-done | bytes 262176 | tf_op jit(solution)/shard_map/ppermute | solution.py:428
  51.5 1.4 %collective-permute-start.11 = (bf16[64,256]{1,0:T(8,128)(2,1)S(1)}, bf16[64,256]{1,0:T(8,128)(2,1)S(1)}, u32[]{:S(2)}, u32[]{:S(2)}) collective-permute-start(bf16[64,256]{1,0:T(8,128)(2,1)S(1)} %get-tuple-element.46), channel_id=1, source_target_pairs={{0,3},{1,2},{2,1},{3,0},{4,7},{5,6},{6,5},{7,4},{8,11},{9,10},{10,... | collective-permute-start | bytes 98312 | tf_op jit(solution)/shard_map/ppermute | solution.py:428
  52.9 2.9 %collective-permute-start.9 = (bf16[64,256]{1,0:T(8,128)(2,1)S(1)}, bf16[64,256]{1,0:T(8,128)(2,1)S(1)}, u32[]{:S(2)}, u32[]{:S(2)}) collective-permute-start(bf16[64,256]{1,0:T(8,128)(2,1)S(1)} %get-tuple-element.46), channel_id=1, source_target_pairs={{0,1},{1,0},{2,3},{3,2},{4,5},{5,4},{6,7},{7,6},{8,9},{9,8},{10,11... | collective-permute-start | bytes 98312 | tf_op jit(solution)/shard_map/ppermute | solution.py:428
  55.9 1.3 %collective-permute-done.11 = bf16[64,256]{1,0:T(8,128)(2,1)S(1)} collective-permute-done((bf16[64,256]{1,0:T(8,128)(2,1)S(1)}, bf16[64,256]{1,0:T(8,128)(2,1)S(1)}, u32[]{:S(2)}, u32[]{:S(2)}) %collective-permute-start.11) | collective-permute-done | bytes 32800 | tf_op jit(solution)/shard_map/ppermute | solution.py:428
  57.2 0.8 %collective-permute-done.10 = bf16[64,256]{1,0:T(8,128)(2,1)S(1)} collective-permute-done((bf16[64,256]{1,0:T(8,128)(2,1)S(1)}, bf16[64,256]{1,0:T(8,128)(2,1)S(1)}, u32[]{:S(2)}, u32[]{:S(2)}) %collective-permute-start.10) | collective-permute-done | bytes 32800 | tf_op jit(solution)/shard_map/ppermute | solution.py:428
  58.0 0.1 collective-permute-done.9
  58.1 1.3 %correct.1 = (bf16[128,1024]{1,0:T(8,128)(2,1)S(1)}, bf16[128,1024]{1,0:T(8,128)(2,1)S(1)}) custom-call(s32[4]{0:T(128)S(1)} %pad_add_fusion.2.owners_ref, s32[8,256]{1,0:T(8,128)S(1)} %get-tuple-element.45.adapters_ref, bf16[64,256]{1,0:T(8,128)(2,1)S(1)} %add_convert_fusion.1.low_ref, bf16[128,3072]{1,0:T(8,128)(2,1)S(1)} %pad_maximum_fusion.refs_2_.refs_0_, ...), custom_call_target="tpu_custom_call" | custom-call | flops 1 | bytes 1 | tf_op jit(solution)/shard_map/correct/pallas_call | solution.py:384
  59.4 0.1 collective-permute-start.12
  59.5 1.5 %collective-permute-done.12.refs_4_ = bf16[128,1024]{1,0:T(8,128)(2,1)S(1)} collective-permute-done((bf16[128,1024]{1,0:T(8,128)(2,1)S(1)}, bf16[128,1024]{1,0:T(8,128)(2,1)S(1)}, u32[]{:S(2)}, u32[]{:S(2)}) %collective-permute-start.12) | collective-permute-done | bytes 262176 | tf_op jit(solution)/shard_map/ppermute | solution.py:428
  61.0 1.0 %copy-done.1 = f32[128,1024]{1,0:T(8,128)S(1)} copy-done((f32[128,1024]{1,0:T(8,128)S(1)}, f32[128,1024]{1,0:T(8,128)}, u32[]{:S(2)}) %copy-start.1) | copy-done | bytes 524312
  62.1 2.0 %finish.1 = bf16[128,1024]{1,0:T(8,128)(2,1)} custom-call(s32[1,128]{1,0:T(1,128)S(1)} %bitcast.15, f32[128,1024]{1,0:T(8,128)S(1)} %copy-done.1, bf16[128,1024]{1,0:T(8,128)(2,1)S(1)} %collective-permute-done.3.refs_0_, bf16[128,1024]{1,0:T(8,128)(2,1)} %collective-permute-done.7.refs_1_, bf16[128,1024]{1,0:T(8,128)(2,1)} %collective-permute-done.8.refs_2_, ...), custom_call_target="tpu_custom_call" | custom-call | flops 1 | bytes 1 | tf_op jit(solution)/shard_map/finish/pallas_call | solution.py:415
  (17 shorter events, 0.1 us)
Async XLA Ops:
  1.2 30.8 %collective-permute-start.1 = (bf16[128,3072]{1,0:T(8,128)(2,1)S(1)}, bf16[128,3072]{1,0:T(8,128)(2,1)S(1)}, u32[]{:S(2)}, u32[]{:S(2)}) collective-permute-start(bf16[128,3072]{1,0:T(8,128)(2,1)S(1)} %pad_maximum_fusion.refs_2_.refs_0_), channel_id=1, source_target_pairs={{0,16},{4,20},{8,24},{12,28},{16,0},{20,4},{24,8},{28,12},{1,17},{... | collective-permute-start | bytes 2359304 | tf_op jit(solution)/shard_map/ppermute | solution.py:428
  4.2 27.7 %collective-permute-start = (bf16[128,3072]{1,0:T(8,128)(2,1)S(1)}, bf16[128,3072]{1,0:T(8,128)(2,1)S(1)}, u32[]{:S(2)}, u32[]{:S(2)}) collective-permute-start(bf16[128,3072]{1,0:T(8,128)(2,1)S(1)} %pad_maximum_fusion.refs_2_.refs_0_), channel_id=1, source_target_pairs={{0,8},{4,12},{8,0},{12,4},{16,24},{20,28},{24,16},{28,20},{1,9},{5... | collective-permute-start | bytes 2359304 | tf_op jit(solution)/shard_map/ppermute | solution.py:428
  17.9 14.0 %collective-permute-start.3 = (bf16[128,1024]{1,0:T(8,128)(2,1)}, bf16[128,1024]{1,0:T(8,128)(2,1)S(1)}, u32[]{:S(2)}, u32[]{:S(2)}) collective-permute-start(bf16[128,1024]{1,0:T(8,128)(2,1)} %get-tuple-element.28), channel_id=1, source_target_pairs={{1,2},{2,1},{5,6},{6,5},{9,10},{10,9},{13,14},{14,13},{17,18},{18,... | collective-permute-start | bytes 786440 | tf_op jit(solution)/shard_map/ppermute | solution.py:505
  18.6 13.4 %collective-permute-start.2 = (bf16[128,1024]{1,0:T(8,128)(2,1)}, bf16[128,1024]{1,0:T(8,128)(2,1)S(1)}, u32[]{:S(2)}, u32[]{:S(2)}) collective-permute-start(bf16[128,1024]{1,0:T(8,128)(2,1)} %get-tuple-element.28), channel_id=1, source_target_pairs={{0,1},{3,2},{4,5},{7,6},{8,9},{11,10},{12,13},{15,14},{16,17},{19,... | collective-permute-start | bytes 786440 | tf_op jit(solution)/shard_map/ppermute | solution.py:504
  24.9 10.1 %copy-start.3 = (bf16[128,1024]{1,0:T(8,128)(2,1)S(1)}, bf16[128,1024]{1,0:T(8,128)(2,1)}, u32[]{:S(2)}) copy-start(bf16[128,1024]{1,0:T(8,128)(2,1)} %get-tuple-element.39) | copy-start | bytes 786436
  31.9 2.1 %copy-start = (f32[128,1024]{1,0:T(8,128)}, f32[128,1024]{1,0:T(8,128)S(1)}, u32[]{:S(2)}) copy-start(f32[128,1024]{1,0:T(8,128)S(1)} %get-tuple-element.32.own_ref) | copy-start | bytes 1572868
  31.9 29.1 %copy-start.2 = (s32[128]{0:T(128)S(1)}, s32[128]{0:T(128)}, u32[]{:S(2)}) copy-start(s32[128]{0:T(128)} %param.18) | copy-start | bytes 1540
  31.9 1.3 %copy-start.4 = (bf16[128,1024]{1,0:T(8,128)(2,1)}, bf16[128,1024]{1,0:T(8,128)(2,1)S(1)}, u32[]{:S(2)}) copy-start(bf16[128,1024]{1,0:T(8,128)(2,1)S(1)} %collective-permute-done.2) | copy-start | bytes 786436
  32.0 13.7 %collective-permute-start.4 = (bf16[144,2048]{1,0:T(8,128)(2,1)}, bf16[144,2048]{1,0:T(8,128)(2,1)}, u32[]{:S(2)}, u32[]{:S(2)}) collective-permute-start(bf16[144,2048]{1,0:T(8,128)(2,1)} %get-tuple-element.33.a_hbm.refs_0_), channel_id=1, source_target_pairs={{0,4},{4,0},{8,12},{12,8},{16,20},{20,16},{24,28},{28,24},{1,5},{5... | collective-permute-start | bytes 1769480 | tf_op jit(solution)/shard_map/ppermute | solution.py:428
  32.0 17.4 %collective-permute-start.8 = (bf16[128,1024]{1,0:T(8,128)(2,1)}, bf16[128,1024]{1,0:T(8,128)(2,1)}, u32[]{:S(2)}, u32[]{:S(2)}) collective-permute-start(bf16[128,1024]{1,0:T(8,128)(2,1)} %get-tuple-element.41), channel_id=1, source_target_pairs={{0,1},{1,0},{2,3},{3,2},{4,5},{5,4},{6,7},{7,6},{8,9},{9,8},{10,11... | collective-permute-start | bytes 786440 | tf_op jit(solution)/shard_map/ppermute | solution.py:428
  34.0 11.4 %collective-permute-start.6 = (bf16[64,3072]{1,0:T(8,128)(2,1)}, bf16[64,3072]{1,0:T(8,128)(2,1)S(1)}, u32[]{:S(2)}, u32[]{:S(2)}) collective-permute-start(bf16[64,3072]{1,0:T(8,128)(2,1)} %slice.7), channel_id=1, source_target_pairs={{0,8},{4,12},{8,0},{12,4},{16,24},{20,28},{24,16},{28,20},{1,9},{5... | collective-permute-start | bytes 1179656 | tf_op jit(solution)/shard_map/ppermute | solution.py:428
  34.5 11.1 %collective-permute-start.5 = (bf16[64,3072]{1,0:T(8,128)(2,1)}, bf16[64,3072]{1,0:T(8,128)(2,1)S(1)}, u32[]{:S(2)}, u32[]{:S(2)}) collective-permute-start(bf16[64,3072]{1,0:T(8,128)(2,1)} %slice.6), channel_id=1, source_target_pairs={{0,16},{4,20},{8,24},{12,28},{16,0},{20,4},{24,8},{28,12},{1,17},{... | collective-permute-start | bytes 1179656 | tf_op jit(solution)/shard_map/ppermute | solution.py:428
  36.8 14.7 %collective-permute-start.7 = (bf16[128,1024]{1,0:T(8,128)(2,1)}, bf16[128,1024]{1,0:T(8,128)(2,1)}, u32[]{:S(2)}, u32[]{:S(2)}) collective-permute-start(bf16[128,1024]{1,0:T(8,128)(2,1)} %add_convert_fusion), channel_id=1, source_target_pairs={{0,2},{1,3},{2,0},{3,1},{4,6},{5,7},{6,4},{7,5},{8,10},{9,11},{10,... | collective-permute-start | bytes 786440 | tf_op jit(solution)/shard_map/ppermute | solution.py:428
  51.5 5.7 %collective-permute-start.11 = (bf16[64,256]{1,0:T(8,128)(2,1)S(1)}, bf16[64,256]{1,0:T(8,128)(2,1)S(1)}, u32[]{:S(2)}, u32[]{:S(2)}) collective-permute-start(bf16[64,256]{1,0:T(8,128)(2,1)S(1)} %get-tuple-element.46), channel_id=1, source_target_pairs={{0,3},{1,2},{2,1},{3,0},{4,7},{5,6},{6,5},{7,4},{8,11},{9,10},{10,... | collective-permute-start | bytes 98312 | tf_op jit(solution)/shard_map/ppermute | solution.py:428
  52.9 5.1 %collective-permute-start.10 = (bf16[64,256]{1,0:T(8,128)(2,1)S(1)}, bf16[64,256]{1,0:T(8,128)(2,1)S(1)}, u32[]{:S(2)}, u32[]{:S(2)}) collective-permute-start(bf16[64,256]{1,0:T(8,128)(2,1)S(1)} %get-tuple-element.46), channel_id=1, source_target_pairs={{0,2},{1,3},{2,0},{3,1},{4,6},{5,7},{6,4},{7,5},{8,10},{9,11},{10,... | collective-permute-start | bytes 98312 | tf_op jit(solution)/shard_map/ppermute | solution.py:428
  52.9 5.2 %collective-permute-start.9 = (bf16[64,256]{1,0:T(8,128)(2,1)S(1)}, bf16[64,256]{1,0:T(8,128)(2,1)S(1)}, u32[]{:S(2)}, u32[]{:S(2)}) collective-permute-start(bf16[64,256]{1,0:T(8,128)(2,1)S(1)} %get-tuple-element.46), channel_id=1, source_target_pairs={{0,1},{1,0},{2,3},{3,2},{4,5},{5,4},{6,7},{7,6},{8,9},{9,8},{10,11... | collective-permute-start | bytes 98312 | tf_op jit(solution)/shard_map/ppermute | solution.py:428
  59.4 1.6 %collective-permute-start.12 = (bf16[128,1024]{1,0:T(8,128)(2,1)S(1)}, bf16[128,1024]{1,0:T(8,128)(2,1)S(1)}, u32[]{:S(2)}, u32[]{:S(2)}) collective-permute-start(bf16[128,1024]{1,0:T(8,128)(2,1)S(1)} %get-tuple-element.48), channel_id=1, source_target_pairs={{0,4},{4,0},{8,12},{12,8},{16,20},{20,16},{24,28},{28,24},{1,5},{5... | collective-permute-start | bytes 786440 | tf_op jit(solution)/shard_map/ppermute | solution.py:428
  61.0 1.0 %copy-start.1 = (f32[128,1024]{1,0:T(8,128)S(1)}, f32[128,1024]{1,0:T(8,128)}, u32[]{:S(2)}) copy-start(f32[128,1024]{1,0:T(8,128)} %copy-done) | copy-start | bytes 1572868

commit v4 on v3

--- a/solution.py
+++ b/solution.py
@@ -104,8 +104,9 @@
 
 def attend_kernel(
     block,
+    steps,
     lengths_ref,
-    chunks_ref,
+    me_ref,
     q_hbm,
     k_hbm,
     v_hbm,
@@ -157,9 +158,9 @@
         return carry
 
     lax.fori_loop(0, blocks, begin, 0)
-    for i in range(len(piece_refs)):
+    for i, step in enumerate(steps):
         for j in range(tiles):
-            column = chunks_ref[i] * out_local + j * TILE
+            column = (me_ref[0] ^ step) * out_local + j * TILE
             fetch(w_ref, buffer_ref, sem_ref, i * tiles + j, column).start()
     for copy in new_copies:
         copy.wait()
@@ -189,23 +190,23 @@
         return carry
 
     lax.fori_loop(0, blocks, one_block, 0)
-    for i, piece_ref in enumerate(piece_refs):
-        column = chunks_ref[i] * out_local
+    for i, (step, piece_ref) in enumerate(zip(steps, piece_refs)):
+        column = (me_ref[0] ^ step) * out_local
         project_tiles(out_ref, w_ref, buffer_ref, sem_ref, piece_ref, i * tiles, column)
 
 
-def attend(arrays, lengths, out_weight, chunks, out_local):
+def attend(arrays, lengths, out_weight, me, steps, out_local):
     queries, key_cache = arrays[:2]
     rows, heads, width = queries.shape
     cache = key_cache.shape[2]
     block = min(16, rows)
     depth = heads * width
-    tiles = len(chunks) * (out_local // TILE)
+    tiles = len(steps) * (out_local // TILE)
     smem = pl.BlockSpec(memory_space=pltpu.SMEM)
     hbm = pl.BlockSpec(memory_space=pltpu.HBM)
     vmem = pl.BlockSpec(memory_space=pltpu.VMEM)
     return pl.pallas_call(
-        functools.partial(attend_kernel, block),
+        functools.partial(attend_kernel, block, steps),
         in_specs=[smem, smem] + [hbm] * (len(arrays) + 1),
         out_specs=[vmem, vmem, vmem],
         scratch_shapes=[pltpu.VMEM(a.shape, a.dtype) for a in arrays]
@@ -219,50 +220,11 @@
         out_shape=[
             jax.ShapeDtypeStruct((rows + ID_ROWS, depth), jnp.bfloat16),
         ]
-        + [jax.ShapeDtypeStruct((rows, out_local), jnp.bfloat16) for _ in chunks],
+        + [jax.ShapeDtypeStruct((rows, out_local), jnp.bfloat16) for _ in steps],
         compiler_params=pltpu.CompilerParams(vmem_limit_bytes=57 * MIB),
         cost_estimate=SMALL,
         name="attend",
-    )(lengths, jnp.stack(chunks), *arrays, out_weight)
-
-
-def project_kernel(chunks_ref, a_hbm, w_ref, *refs):
-    *out_refs, a_ref, buffer_ref, a_sem, sem_ref = refs
-    out_local = out_refs[0].shape[1]
-    tiles = out_local // TILE
-    copy = pltpu.make_async_copy(a_hbm, a_ref, a_sem.at[0])
-    copy.start()
-    for i in range(len(out_refs)):
-        for j in range(tiles):
-            column = chunks_ref[i] * out_local + j * TILE
-            fetch(w_ref, buffer_ref, sem_ref, i * tiles + j, column).start()
-    copy.wait()
-    for i, out_ref in enumerate(out_refs):
-        project_tiles(
-            a_ref, w_ref, buffer_ref, sem_ref, out_ref, i * tiles, chunks_ref[i] * out_local
-        )
-
-
-def project(attended, out_weight, chunks, out_local, dtypes):
-    rows, depth = attended.shape[0] - ID_ROWS, attended.shape[1]
-    slots = len(dtypes) * (out_local // TILE)
-    vmem = pl.BlockSpec(memory_space=pltpu.VMEM)
-    hbm = pl.BlockSpec(memory_space=pl.ANY)
-    return pl.pallas_call(
-        project_kernel,
-        in_specs=[pl.BlockSpec(memory_space=pltpu.SMEM), hbm, hbm],
-        out_specs=[vmem for _ in dtypes],
-        scratch_shapes=[
-            pltpu.VMEM(attended.shape, attended.dtype),
-            pltpu.VMEM((slots, depth, TILE), jnp.bfloat16),
-            pltpu.SemaphoreType.DMA((1,)),
-            pltpu.SemaphoreType.DMA((slots,)),
-        ],
-        out_shape=[jax.ShapeDtypeStruct((rows, out_local), dtype) for dtype in dtypes],
-        compiler_params=pltpu.CompilerParams(vmem_limit_bytes=52 * MIB),
-        cost_estimate=SMALL,
-        name="project",
-    )(jnp.stack(chunks), attended, out_weight)
+    )(lengths, me.reshape(1), *arrays, out_weight)
 
 
 def masked(low, owner, adapters, ranks, adapters_here):
@@ -292,7 +254,7 @@
     ]
 
 
-def low_kernel(ranks, places, owners_ref, *refs):
+def low_kernel(ranks, places, keys, here_ref, *refs):
     sides, sources = refs[:2], refs[2 : 2 + len(places)]
     out_ref, adapters_ref, side_ref, block_ref, sems = refs[2 + len(places) :]
     copies = fetch_all(sides, [side_ref.at[i] for i in range(2)], sems)
@@ -317,7 +279,7 @@
             if place[0] == i:
                 copy.wait()
         part = jnp.dot(block_ref[i], a_t, preferred_element_type=jnp.float32)
-        first = owners_ref[i] * (pair // ranks)
+        first = (here_ref[0] ^ keys[i]) * (pair // ranks)
         total += jnp.where(row // ranks + first == adapters, part, 0.0)
     low = total[:ranks]
     for a in range(1, pair // ranks):
@@ -325,13 +287,13 @@
     out_ref[...] = low.astype(out_ref.dtype)
 
 
-def low_rank(sides, blocks, depth, owners, rank):
+def low_rank(sides, blocks, depth, here, keys, rank):
     rows = sides[0].shape[0] - ID_ROWS
     arrays, places = block_parts(blocks)
     pair = sum(part.shape[0] for part in blocks[0])
     vmem = pl.BlockSpec(memory_space=pltpu.VMEM)
     return pl.pallas_call(
-        functools.partial(low_kernel, rank, places),
+        functools.partial(low_kernel, rank, places, keys),
         in_specs=[pl.BlockSpec(memory_space=pltpu.SMEM)]
         + [pl.BlockSpec(memory_space=pl.ANY)] * (2 + len(arrays)),
         out_specs=[vmem, vmem],
@@ -344,15 +306,15 @@
             pltpu.VMEM((len(blocks), pair, depth), jnp.bfloat16),
             pltpu.SemaphoreType.DMA((2 + len(arrays),)),
         ],
-        compiler_params=pltpu.CompilerParams(vmem_limit_bytes=32 * MIB),
+        compiler_params=pltpu.CompilerParams(vmem_limit_bytes=16 * MIB),
         cost_estimate=SMALL,
         name="low_rank",
-    )(jnp.stack(owners), *sides, *arrays)
-
-
-def delta_kernel(ranks, places, column, owners_ref, adapters_ref, low_ref, *refs):
+    )(here.reshape(1), *sides, *arrays)
+
+
+def delta_kernel(ranks, places, column, keys, here_ref, adapters_ref, low_ref, *refs):
     sources = refs[: len(places)]
-    here_ref, other_ref, block_ref, sems = refs[len(places) :]
+    mine_ref, other_ref, block_ref, sems = refs[len(places) :]
     parts = fetch_blocks(sources, places, column, block_ref, sems, 0)
     for copy in parts:
         copy.start()
@@ -360,7 +322,7 @@
     low = low_ref[...].astype(jnp.float32)
     sides = []
     for i in range(blocks):
-        mine = masked(low, owners_ref[i], adapters_ref[:1, :], ranks, pair // ranks)
+        mine = masked(low, here_ref[0] ^ keys[i], adapters_ref[:1, :], ranks, pair // ranks)
         sides.append(mine.T.astype(jnp.bfloat16))
     for copy in parts:
         copy.wait()
@@ -370,19 +332,19 @@
         preferred_element_type=jnp.float32,
     )
     delta = (0.5 * delta).astype(jnp.bfloat16)
-    rows = here_ref.shape[0]
-    here_ref[...] = delta[:rows]
+    rows = mine_ref.shape[0]
+    mine_ref[...] = delta[:rows]
     other_ref[...] = delta[rows:]
 
 
-def correct(low, adapters, blocks, column, out_local, owners, rank):
+def correct(low, adapters, blocks, column, out_local, here, keys, rank):
     slots = adapters.shape[1]
     arrays, places = block_parts(blocks)
     pair = sum(part.shape[0] for part in blocks[0])
     vmem = pl.BlockSpec(memory_space=pltpu.VMEM)
     out = jax.ShapeDtypeStruct((slots // 2, out_local), jnp.bfloat16)
     return pl.pallas_call(
-        functools.partial(delta_kernel, rank, places, column),
+        functools.partial(delta_kernel, rank, places, column, keys),
         in_specs=[pl.BlockSpec(memory_space=pltpu.SMEM), vmem, vmem]
         + [pl.BlockSpec(memory_space=pl.ANY)] * len(arrays),
         out_specs=[vmem, vmem],
@@ -391,10 +353,10 @@
             pltpu.VMEM((len(blocks), pair, out_local), jnp.bfloat16),
             pltpu.SemaphoreType.DMA((len(arrays),)),
         ],
-        compiler_params=pltpu.CompilerParams(vmem_limit_bytes=32 * MIB),
+        compiler_params=pltpu.CompilerParams(vmem_limit_bytes=16 * MIB),
         cost_estimate=SMALL,
         name="correct",
-    )(jnp.stack(owners), adapters, low, *arrays)
+    )(here.reshape(1), adapters, low, *arrays)
 
 
 def finish_kernel(occupied_ref, own_ref, *refs):
@@ -417,7 +379,7 @@
         in_specs=[vmem] * (2 + len(parts)),
         out_specs=vmem,
         out_shape=jax.ShapeDtypeStruct((rows, out_local), jnp.bfloat16),
-        compiler_params=pltpu.CompilerParams(vmem_limit_bytes=32 * MIB),
+        compiler_params=pltpu.CompilerParams(vmem_limit_bytes=16 * MIB),
         cost_estimate=SMALL,
         name="finish",
     )(occupied.reshape(1, rows), own, *parts)
@@ -474,7 +436,6 @@
     me = lax.axis_index("mp")
     here = lax.axis_index("dp")
     pair = adapters_here * rank
-    steps = list(range(shares - 1, 0, -1))
 
     own_block = jnp.concatenate(
         [
@@ -484,7 +445,10 @@
         axis=1,
     )
     blocks = near_blocks(own_block)
-    attended, piece, second = attend(
+    halved = shares == 4
+    early = (3, 1) if halved else (shares - 1, shares - 2)
+    late = (2, 0) if halved else tuple(range(shares - 3, -1, -1))
+    attended, *pieces = attend(
         (
             queries,
             key_cache,
@@ -496,38 +460,40 @@
         ),
         lengths,
         out_weight,
-        [me ^ step for step in steps[:2]],
+        me,
+        early,
         out_local,
     )
-    chained = shares == 4
-    if chained:
-        passed = lax.ppermute(piece, "mp", [(0, 1), (3, 2)])
-        received = [lax.ppermute(piece, "mp", [(1, 2), (2, 1)])]
-    else:
-        received = [exchange(piece, "mp", steps[0])]
-    *pieces, own = project(
-        attended,
-        out_weight,
-        [me ^ step for step in steps[2:]] + [me],
-        out_local,
-        [jnp.bfloat16] * (shares - 3) + [jnp.float32],
-    )
-    if chained:
-        passed, received, second, own = together(passed, received, second, own)
-        second = (second.astype(jnp.float32) + passed.astype(jnp.float32)).astype(jnp.bfloat16)
-    blocks, attended, own = together(blocks, attended, own)
-    received.append(exchange(second, "mp", steps[1]))
-    received += [exchange(piece, "mp", step) for piece, step in zip(pieces, steps[2:])]
+    received = [
+        exchange(piece, "mp", 1 if halved else step) for piece, step in zip(pieces, early)
+    ]
+    blocks, attended = together(blocks, attended)
     blocks = far_blocks(blocks)
     beside = exchange(attended, "dp", 1)
-
-    owners = [here ^ key for key in blocks]
+    rows = queries.shape[0]
+    *pieces, own = [
+        jnp.dot(
+            attended[:rows],
+            lax.dynamic_slice_in_dim(out_weight, (me ^ step) * out_local, out_local, 1),
+            preferred_element_type=jnp.float32,
+        )
+        for step in late
+    ]
+    if not halved:
+        pieces = [piece.astype(jnp.bfloat16) for piece in pieces]
+    if halved:
+        passed = received.pop(0)
+        passed, attended, own, *pieces = together(passed, attended, own, *pieces)
+        pieces = [(pieces[0] + passed.astype(jnp.float32)).astype(jnp.bfloat16)]
+    received += [exchange(piece, "mp", step) for piece, step in zip(pieces, late)]
+
+    keys = tuple(blocks)
     blocks = list(blocks.values())
-    low, adapters = low_rank([attended, beside], blocks, depth, owners, rank)
-    low, received = together(low, received)
+    low, adapters = low_rank([attended, beside], blocks, depth, here, keys, rank)
     lows = [low] + [exchange(low, "mp", step) for step in range(1, shares)]
+    lows, received = together(lows, received)
     low = sum(part.astype(jnp.float32) for part in lows).astype(jnp.bfloat16)
-    correction, other = correct(low, adapters, blocks, depth, out_local, owners, rank)
+    correction, other = correct(low, adapters, blocks, depth, out_local, here, keys, rank)
     return finish(own, [*received, correction, exchange(other, "dp", 1)], occupied)
 
 

time: 64.3 us -> 62.4 us (0.970)
  Pallas kernels: 25.5 us -> 18 us
  matrix products: 0 us -> 6.13 us
  waiting for transfers between devices: 13 us -> 17.7 us
  starting transfers between devices: 19 us -> 15.8 us
  local copies, waits for them, and re-layouts: 2.64 us -> 1.57 us
  other arithmetic: 3.71 us -> 2.92 us
    pallas_call x4 -> x3, Pallas kernels: 23.5 us -> 16.1 us  [the longest x1 11.4 us: attend(): pl.pallas_call(functools.partial(attend_kernel, block, steps), in_specs=[...]
    ppermute x2 -> x0, starting transfers between devices: 6.98 us -> none  [the longest x1 6.3 us: body(): passed = lax.ppermute(piece, 'mp', [(0, 1), (3, 2)])]
    dot_general x0 -> x2, matrix products: none -> 6.13 us  [body(): jnp.dot(attended[:rows], lax.dynamic_slice_in_dim(out_weight, (me ^ step)...]
    ppermute x11 -> x12, waiting for transfers between devices: 13 us -> 17.7 us  [exchange(): return lax.ppermute(value, axis, [(i, i ^ step) for i in range(count)])]
    ppermute x11 -> x12, starting transfers between devices: 12.1 us -> 15.8 us  [exchange(): return lax.ppermute(value, axis, [(i, i ^ step) for i in range(count)])]
    unnamed x10 -> x4, local copies, waits for them, and re-layouts: 1.06 us -> 0.01 us
    another operation x3 -> x0, other arithmetic: 0.76 us -> none  [the longest x1 0.61 us: attend(): jnp.stack(chunks)]
  transfers between devices with their start and end apart: 13 -> 12, of which waited for: 7 -> 7; matrix products, arithmetic and copies ran while one was open for 6% -> 15% of each run, Pallas kernels for 35% -> 23%
where the time goes in v4:
time: 62.4 us; the launch traced here: 62.2 us
  Pallas kernels  18 us (29%)
  waiting for transfers between devices  17.7 us (28%)
  starting transfers between devices  15.8 us (25%)
  matrix products  6.13 us (10%)
  other arithmetic  2.92 us (5%)
  local copies, waits for them, and re-layouts  1.57 us (3%)
    ppermute x12, waiting for transfers between devices, exchange(): return lax.ppermute(value, axis, [(i, i ^ step) for i in range(count)])  17.7 us
    ppermute x12, starting transfers between devices, exchange(): return lax.ppermute(value, axis, [(i, i ^ step) for i in range(count)])  15.8 us
    pallas_call x1, Pallas kernels, attend(): pl.pallas_call(functools.partial(attend_kernel, block, steps), in_specs=[...  11.4 us
    dot_general x2, matrix products, body(): jnp.dot(attended[:rows], lax.dynamic_slice_in_dim(out_weight, (me ^ step)...  6.13 us
    pallas_call x1, Pallas kernels, low_rank(): pl.pallas_call(functools.partial(low_kernel, rank, places, keys), in_spec...  3.13 us
    pallas_call x1, Pallas kernels, finish(): pl.pallas_call(finish_kernel, in_specs=[vmem] * (2 + len(parts)), out_spe...  1.92 us
    convert_element_type x1, other arithmetic, body(): pieces = [(pieces[0] + passed.astype(jnp.float32)).astype(jnp.bfloat16)]  1.72 us
    pallas_call x1, Pallas kernels, correct(): pl.pallas_call(functools.partial(delta_kernel, rank, places, column, keys...  1.52 us
  transfers between devices with their start and end apart: 12, of which 7 were waited for; matrix products, arithmetic and copies ran while one was open for 15% of the time, Pallas kernels for 23%

profile of v4, /device:TPU:0, one launch (start us, length us, event | category | flops | bytes accessed | tf_op | source)
XLA Modules:
  0.0 62.2 jit_solution(7679244833899152012)
XLA Ops:
  0.0 1.2 %pad_maximum_fusion.refs_2_.refs_0_ = bf16[128,3072]{1,0:T(8,128)(2,1)S(1)} fusion(bf16[128,1024]{1,0:T(8,128)(2,1)} %bitcast.11, bf16[128,2048]{1,0:T(8,128)(2,1)} %bitcast.10), kind=kLoop, calls=%fused_computation.4 | loop fusion | flops 1572864 | bytes 1572864 | tf_op jit(solution)/shard_map/concatenate | solution.py:440
  1.2 3.0 %collective-permute-start.1 = (bf16[128,3072]{1,0:T(8,128)(2,1)S(1)}, bf16[128,3072]{1,0:T(8,128)(2,1)S(1)}, u32[]{:S(2)}, u32[]{:S(2)}) collective-permute-start(bf16[128,3072]{1,0:T(8,128)(2,1)S(1)} %pad_maximum_fusion.refs_2_.refs_0_), channel_id=1, source_target_pairs={{0,8},{4,12},{8,0},{12,4},{16,24},{20,28},{24,16},{28,20},{1,9},{5... | collective-permute-start | bytes 2359304 | tf_op jit(solution)/shard_map/ppermute | solution.py:390
  4.2 1.5 %collective-permute-start.2 = (bf16[128,3072]{1,0:T(8,128)(2,1)S(1)}, bf16[128,3072]{1,0:T(8,128)(2,1)S(1)}, u32[]{:S(2)}, u32[]{:S(2)}) collective-permute-start(bf16[128,3072]{1,0:T(8,128)(2,1)S(1)} %pad_maximum_fusion.refs_2_.refs_0_), channel_id=1, source_target_pairs={{0,16},{4,20},{8,24},{12,28},{16,0},{20,4},{24,8},{28,12},{1,17},{... | collective-permute-start | bytes 2359304 | tf_op jit(solution)/shard_map/ppermute | solution.py:390
  5.7 11.4 %attend.1 = (bf16[144,2048]{1,0:T(8,128)(2,1)}, bf16[128,1024]{1,0:T(8,128)(2,1)}, bf16[128,1024]{1,0:T(8,128)(2,1)}) custom-call(s32[128]{0:T(128)} %lengths_ref.1, s32[1]{0:T(128)} %bitcast.1.me_ref, bf16[128,16,128]{2,1,0:T(8,128)(2,1)} %q_hbm.1, bf16[128,2,128,128]{3,2,1,0:T(8,128)(2,1)} %k_hbm.1, bf16[128,2,128,128]{3,2,1,0:T(8,128)(2,1)} %v_hbm.1, ...), custom_call_target="tpu_custom_call" | custom-call | flops 1 | bytes 1 | tf_op jit(solution)/shard_map/attend/pallas_call | solution.py:208
  17.2 1.6 %collective-permute-start = (bf16[128,1024]{1,0:T(8,128)(2,1)}, bf16[128,1024]{1,0:T(8,128)(2,1)}, u32[]{:S(2)}, u32[]{:S(2)}) collective-permute-start(bf16[128,1024]{1,0:T(8,128)(2,1)} %get-tuple-element.26), channel_id=1, source_target_pairs={{0,1},{1,0},{2,3},{3,2},{4,5},{5,4},{6,7},{7,6},{8,9},{9,8},{10,11... | collective-permute-start | bytes 786440 | tf_op jit(solution)/shard_map/ppermute | solution.py:390
  18.8 0.5 collective-permute-start.9
  19.3 2.5 %collective-permute-done.1.refs_3_.refs_1_ = bf16[128,3072]{1,0:T(8,128)(2,1)S(1)} collective-permute-done((bf16[128,3072]{1,0:T(8,128)(2,1)S(1)}, bf16[128,3072]{1,0:T(8,128)(2,1)S(1)}, u32[]{:S(2)}, u32[]{:S(2)}) %collective-permute-start.1) | collective-permute-done | bytes 786464 | tf_op jit(solution)/shard_map/ppermute | solution.py:390
  21.7 1.5 %collective-permute-done.2.refs_4_.refs_2_ = bf16[128,3072]{1,0:T(8,128)(2,1)S(1)} collective-permute-done((bf16[128,3072]{1,0:T(8,128)(2,1)S(1)}, bf16[128,3072]{1,0:T(8,128)(2,1)S(1)}, u32[]{:S(2)}, u32[]{:S(2)}) %collective-permute-start.2) | collective-permute-done | bytes 786464 | tf_op jit(solution)/shard_map/ppermute | solution.py:390
  23.2 0.0 collective-permute-start.3
  23.2 3.1 %fusion = f32[128,1024]{1,0:T(8,128)S(1)} fusion(bf16[2048,4096]{1,0:T(8,128)(2,1)} %w_ref.1, s32[]{:T(128)S(6)} %select_n.7, bf16[144,2048]{1,0:T(8,128)(2,1)} %get-tuple-element.30.refs_0_), kind=kOutput, calls=%fused_computation | convolution fusion | flops 536870912 | bytes 5242884 | tf_op jit(solution)/shard_map/dot_general | solution.py:475
  26.3 0.0 copy-start.1
  26.3 3.1 %fusion.2.own_ref = f32[128,1024]{1,0:T(8,128)S(1)} fusion(bf16[2048,4096]{1,0:T(8,128)(2,1)} %w_ref.1, s32[]{:T(128)S(6)} %select_n.6, bf16[144,2048]{1,0:T(8,128)(2,1)} %get-tuple-element.30.refs_0_), kind=kOutput, calls=%fused_computation.2 | convolution fusion | flops 536870912 | bytes 5242884 | tf_op jit(solution)/shard_map/dot_general | solution.py:475
  29.4 0.0 collective-permute-done
  29.4 0.8 %slice.11 = bf16[64,3072]{1,0:T(8,128)(2,1)} slice(bf16[128,3072]{1,0:T(8,128)(2,1)S(1)} %collective-permute-done.1.refs_3_.refs_1_), slice={[0:64], [0:3072]} | slice | bytes 786432 | tf_op jit(solution)/shard_map/slice | solution.py:406
  30.2 1.5 %collective-permute-start.4 = (bf16[64,3072]{1,0:T(8,128)(2,1)}, bf16[64,3072]{1,0:T(8,128)(2,1)}, u32[]{:S(2)}, u32[]{:S(2)}) collective-permute-start(bf16[64,3072]{1,0:T(8,128)(2,1)} %slice.11), channel_id=1, source_target_pairs={{0,16},{4,20},{8,24},{12,28},{16,0},{20,4},{24,8},{28,12},{1,17},{... | collective-permute-start | bytes 1179656 | tf_op jit(solution)/shard_map/ppermute | solution.py:390
  31.7 0.8 %slice.12 = bf16[64,3072]{1,0:T(8,128)(2,1)} slice(bf16[128,3072]{1,0:T(8,128)(2,1)S(1)} %collective-permute-done.2.refs_4_.refs_2_), slice={[64:128], [0:3072]} | slice | bytes 786432 | tf_op jit(solution)/shard_map/slice | solution.py:407
  32.4 0.5 collective-permute-start.5
  33.0 1.7 %add_convert_fusion = bf16[128,1024]{1,0:T(8,128)(2,1)} fusion(f32[128,1024]{1,0:T(8,128)S(1)} %fusion, bf16[128,1024]{1,0:T(8,128)(2,1)} %collective-permute-done), kind=kLoop, calls=%fused_computation.5 | loop fusion | flops 393216 | bytes 1048576 | tf_op jit(solution)/shard_map/convert_element_type | solution.py:487
  34.7 2.6 %collective-permute-start.10 = (bf16[128,1024]{1,0:T(8,128)(2,1)}, bf16[128,1024]{1,0:T(8,128)(2,1)}, u32[]{:S(2)}, u32[]{:S(2)}) collective-permute-start(bf16[128,1024]{1,0:T(8,128)(2,1)} %add_convert_fusion), channel_id=1, source_target_pairs={{0,2},{1,3},{2,0},{3,1},{4,6},{5,7},{6,4},{7,5},{8,10},{9,11},{10,... | collective-permute-start | bytes 786440 | tf_op jit(solution)/shard_map/ppermute | solution.py:390
  37.3 4.7 %collective-permute-done.4.refs_5_.refs_3_ = bf16[64,3072]{1,0:T(8,128)(2,1)} collective-permute-done((bf16[64,3072]{1,0:T(8,128)(2,1)}, bf16[64,3072]{1,0:T(8,128)(2,1)}, u32[]{:S(2)}, u32[]{:S(2)}) %collective-permute-start.4) | collective-permute-done | bytes 393248 | tf_op jit(solution)/shard_map/ppermute | solution.py:390
  42.0 2.0 %collective-permute-done.5.refs_6_.refs_4_ = bf16[64,3072]{1,0:T(8,128)(2,1)} collective-permute-done((bf16[64,3072]{1,0:T(8,128)(2,1)}, bf16[64,3072]{1,0:T(8,128)(2,1)}, u32[]{:S(2)}, u32[]{:S(2)}) %collective-permute-start.5) | collective-permute-done | bytes 393248 | tf_op jit(solution)/shard_map/ppermute | solution.py:390
  44.0 0.0 collective-permute-done.3.refs_1_
  44.0 3.1 %low_rank.1 = (bf16[64,256]{1,0:T(8,128)(2,1)S(1)}, s32[8,256]{1,0:T(8,128)S(1)}) custom-call(s32[1]{0:T(128)} %bitcast.7.here_ref, bf16[144,2048]{1,0:T(8,128)(2,1)S(1)} %copy-done, bf16[144,2048]{1,0:T(8,128)(2,1)} %collective-permute-done.3.refs_1_, bf16[128,3072]{1,0:T(8,128)(2,1)S(1)} %pad_maximum_fusion.refs_2_.refs_0_, ...), custom_call_target="tpu_custom_call" | custom-call | flops 1 | bytes 1 | tf_op jit(solution)/shard_map/low_rank/pallas_call | solution.py:295
  47.1 1.6 %collective-permute-start.6 = (bf16[64,256]{1,0:T(8,128)(2,1)S(1)}, bf16[64,256]{1,0:T(8,128)(2,1)S(1)}, u32[]{:S(2)}, u32[]{:S(2)}) collective-permute-start(bf16[64,256]{1,0:T(8,128)(2,1)S(1)} %get-tuple-element.41), channel_id=1, source_target_pairs={{0,1},{1,0},{2,3},{3,2},{4,5},{5,4},{6,7},{7,6},{8,9},{9,8},{10,11... | collective-permute-start | bytes 98312 | tf_op jit(solution)/shard_map/ppermute | solution.py:390
  48.8 2.6 %collective-permute-start.7 = (bf16[64,256]{1,0:T(8,128)(2,1)S(1)}, bf16[64,256]{1,0:T(8,128)(2,1)S(1)}, u32[]{:S(2)}, u32[]{:S(2)}) collective-permute-start(bf16[64,256]{1,0:T(8,128)(2,1)S(1)} %get-tuple-element.41), channel_id=1, source_target_pairs={{0,2},{1,3},{2,0},{3,1},{4,6},{5,7},{6,4},{7,5},{8,10},{9,11},{10,... | collective-permute-start | bytes 98312 | tf_op jit(solution)/shard_map/ppermute | solution.py:390
  51.4 0.2 collective-permute-start.8
  51.6 2.2 %collective-permute-done.7 = bf16[64,256]{1,0:T(8,128)(2,1)S(1)} collective-permute-done((bf16[64,256]{1,0:T(8,128)(2,1)S(1)}, bf16[64,256]{1,0:T(8,128)(2,1)S(1)}, u32[]{:S(2)}, u32[]{:S(2)}) %collective-permute-start.7) | collective-permute-done | bytes 32800 | tf_op jit(solution)/shard_map/ppermute | solution.py:390
  53.9 3.2 %collective-permute-done.8 = bf16[64,256]{1,0:T(8,128)(2,1)S(1)} collective-permute-done((bf16[64,256]{1,0:T(8,128)(2,1)S(1)}, bf16[64,256]{1,0:T(8,128)(2,1)S(1)}, u32[]{:S(2)}, u32[]{:S(2)}) %collective-permute-start.8) | collective-permute-done | bytes 32800 | tf_op jit(solution)/shard_map/ppermute | solution.py:390
  57.1 1.5 %correct.1 = (bf16[128,1024]{1,0:T(8,128)(2,1)S(1)}, bf16[128,1024]{1,0:T(8,128)(2,1)S(1)}) custom-call(s32[1]{0:T(128)} %bitcast.7.here_ref, s32[8,256]{1,0:T(8,128)S(1)} %get-tuple-element.40.adapters_ref, bf16[64,256]{1,0:T(8,128)(2,1)S(1)} %add_convert_fusion.1.low_ref, bf16[128,3072]{1,0:T(8,128)(2,1)S(1)} %pad_maximum_fusion.refs_2_.refs_0_, ...), custom_call_target="tpu_custom_call" | custom-call | flops 1 | bytes 1 | tf_op jit(solution)/shard_map/correct/pallas_call | solution.py:346
  58.6 0.1 collective-permute-start.11
  58.7 1.5 %collective-permute-done.11.refs_3_ = bf16[128,1024]{1,0:T(8,128)(2,1)S(1)} collective-permute-done((bf16[128,1024]{1,0:T(8,128)(2,1)S(1)}, bf16[128,1024]{1,0:T(8,128)(2,1)S(1)}, u32[]{:S(2)}, u32[]{:S(2)}) %collective-permute-start.11) | collective-permute-done | bytes 262176 | tf_op jit(solution)/shard_map/ppermute | solution.py:390
  60.3 1.9 %finish.1 = bf16[128,1024]{1,0:T(8,128)(2,1)} custom-call(s32[1,128]{1,0:T(1,128)S(1)} %bitcast.9, f32[128,1024]{1,0:T(8,128)S(1)} %fusion.2.own_ref, bf16[128,1024]{1,0:T(8,128)(2,1)} %collective-permute-done.9.refs_0_, bf16[128,1024]{1,0:T(8,128)(2,1)} %collective-permute-done.10.refs_1_, bf16[128,1024]{1,0:T(8,128)(2,1)S(1)} %get-tuple-element.45.refs_2_, ...), custom_call_target="tpu_custom_call" | custom-call | flops 1 | bytes 1 | tf_op jit(solution)/shard_map/finish/pallas_call | solution.py:377
  (7 shorter events, 0.0 us)
Async XLA Ops:
  1.2 20.5 %collective-permute-start.1 = (bf16[128,3072]{1,0:T(8,128)(2,1)S(1)}, bf16[128,3072]{1,0:T(8,128)(2,1)S(1)}, u32[]{:S(2)}, u32[]{:S(2)}) collective-permute-start(bf16[128,3072]{1,0:T(8,128)(2,1)S(1)} %pad_maximum_fusion.refs_2_.refs_0_), channel_id=1, source_target_pairs={{0,8},{4,12},{8,0},{12,4},{16,24},{20,28},{24,16},{28,20},{1,9},{5... | collective-permute-start | bytes 2359304 | tf_op jit(solution)/shard_map/ppermute | solution.py:390
  4.2 19.0 %collective-permute-start.2 = (bf16[128,3072]{1,0:T(8,128)(2,1)S(1)}, bf16[128,3072]{1,0:T(8,128)(2,1)S(1)}, u32[]{:S(2)}, u32[]{:S(2)}) collective-permute-start(bf16[128,3072]{1,0:T(8,128)(2,1)S(1)} %pad_maximum_fusion.refs_2_.refs_0_), channel_id=1, source_target_pairs={{0,16},{4,20},{8,24},{12,28},{16,0},{20,4},{24,8},{28,12},{1,17},{... | collective-permute-start | bytes 2359304 | tf_op jit(solution)/shard_map/ppermute | solution.py:390
  17.2 26.9 %copy-start = (bf16[144,2048]{1,0:T(8,128)(2,1)S(1)}, bf16[144,2048]{1,0:T(8,128)(2,1)}, u32[]{:S(2)}) copy-start(bf16[144,2048]{1,0:T(8,128)(2,1)} %get-tuple-element.30.refs_0_) | copy-start | bytes 1769476
  17.2 12.2 %collective-permute-start = (bf16[128,1024]{1,0:T(8,128)(2,1)}, bf16[128,1024]{1,0:T(8,128)(2,1)}, u32[]{:S(2)}, u32[]{:S(2)}) collective-permute-start(bf16[128,1024]{1,0:T(8,128)(2,1)} %get-tuple-element.26), channel_id=1, source_target_pairs={{0,1},{1,0},{2,3},{3,2},{4,5},{5,4},{6,7},{7,6},{8,9},{9,8},{10,11... | collective-permute-start | bytes 786440 | tf_op jit(solution)/shard_map/ppermute | solution.py:390
  18.8 32.8 %collective-permute-start.9 = (bf16[128,1024]{1,0:T(8,128)(2,1)}, bf16[128,1024]{1,0:T(8,128)(2,1)}, u32[]{:S(2)}, u32[]{:S(2)}) collective-permute-start(bf16[128,1024]{1,0:T(8,128)(2,1)} %get-tuple-element.35), channel_id=1, source_target_pairs={{0,1},{1,0},{2,3},{3,2},{4,5},{5,4},{6,7},{7,6},{8,9},{9,8},{10,11... | collective-permute-start | bytes 786440 | tf_op jit(solution)/shard_map/ppermute | solution.py:390
  23.2 20.8 %collective-permute-start.3 = (bf16[144,2048]{1,0:T(8,128)(2,1)}, bf16[144,2048]{1,0:T(8,128)(2,1)}, u32[]{:S(2)}, u32[]{:S(2)}) collective-permute-start(bf16[144,2048]{1,0:T(8,128)(2,1)} %get-tuple-element.30.refs_0_), channel_id=1, source_target_pairs={{0,4},{4,0},{8,12},{12,8},{16,20},{20,16},{24,28},{28,24},{1,5},{5... | collective-permute-start | bytes 1769480 | tf_op jit(solution)/shard_map/ppermute | solution.py:390
  26.3 34.0 %copy-start.1 = (s32[128]{0:T(128)S(1)}, s32[128]{0:T(128)}, u32[]{:S(2)}) copy-start(s32[128]{0:T(128)} %param.18) | copy-start | bytes 1540
  30.2 11.8 %collective-permute-start.4 = (bf16[64,3072]{1,0:T(8,128)(2,1)}, bf16[64,3072]{1,0:T(8,128)(2,1)}, u32[]{:S(2)}, u32[]{:S(2)}) collective-permute-start(bf16[64,3072]{1,0:T(8,128)(2,1)} %slice.11), channel_id=1, source_target_pairs={{0,16},{4,20},{8,24},{12,28},{16,0},{20,4},{24,8},{28,12},{1,17},{... | collective-permute-start | bytes 1179656 | tf_op jit(solution)/shard_map/ppermute | solution.py:390
  32.4 11.6 %collective-permute-start.5 = (bf16[64,3072]{1,0:T(8,128)(2,1)}, bf16[64,3072]{1,0:T(8,128)(2,1)}, u32[]{:S(2)}, u32[]{:S(2)}) collective-permute-start(bf16[64,3072]{1,0:T(8,128)(2,1)} %slice.12), channel_id=1, source_target_pairs={{0,8},{4,12},{8,0},{12,4},{16,24},{20,28},{24,16},{28,20},{1,9},{5... | collective-permute-start | bytes 1179656 | tf_op jit(solution)/shard_map/ppermute | solution.py:390
  34.7 16.9 %collective-permute-start.10 = (bf16[128,1024]{1,0:T(8,128)(2,1)}, bf16[128,1024]{1,0:T(8,128)(2,1)}, u32[]{:S(2)}, u32[]{:S(2)}) collective-permute-start(bf16[128,1024]{1,0:T(8,128)(2,1)} %add_convert_fusion), channel_id=1, source_target_pairs={{0,2},{1,3},{2,0},{3,1},{4,6},{5,7},{6,4},{7,5},{8,10},{9,11},{10,... | collective-permute-start | bytes 786440 | tf_op jit(solution)/shard_map/ppermute | solution.py:390
  47.1 4.5 %collective-permute-start.6 = (bf16[64,256]{1,0:T(8,128)(2,1)S(1)}, bf16[64,256]{1,0:T(8,128)(2,1)S(1)}, u32[]{:S(2)}, u32[]{:S(2)}) collective-permute-start(bf16[64,256]{1,0:T(8,128)(2,1)S(1)} %get-tuple-element.41), channel_id=1, source_target_pairs={{0,1},{1,0},{2,3},{3,2},{4,5},{5,4},{6,7},{7,6},{8,9},{9,8},{10,11... | collective-permute-start | bytes 98312 | tf_op jit(solution)/shard_map/ppermute | solution.py:390
  48.8 5.1 %collective-permute-start.7 = (bf16[64,256]{1,0:T(8,128)(2,1)S(1)}, bf16[64,256]{1,0:T(8,128)(2,1)S(1)}, u32[]{:S(2)}, u32[]{:S(2)}) collective-permute-start(bf16[64,256]{1,0:T(8,128)(2,1)S(1)} %get-tuple-element.41), channel_id=1, source_target_pairs={{0,2},{1,3},{2,0},{3,1},{4,6},{5,7},{6,4},{7,5},{8,10},{9,11},{10,... | collective-permute-start | bytes 98312 | tf_op jit(solution)/shard_map/ppermute | solution.py:390
  51.4 5.7 %collective-permute-start.8 = (bf16[64,256]{1,0:T(8,128)(2,1)S(1)}, bf16[64,256]{1,0:T(8,128)(2,1)S(1)}, u32[]{:S(2)}, u32[]{:S(2)}) collective-permute-start(bf16[64,256]{1,0:T(8,128)(2,1)S(1)} %get-tuple-element.41), channel_id=1, source_target_pairs={{0,3},{1,2},{2,1},{3,0},{4,7},{5,6},{6,5},{7,4},{8,11},{9,10},{10,... | collective-permute-start | bytes 98312 | tf_op jit(solution)/shard_map/ppermute | solution.py:390
  58.6 1.6 %collective-permute-start.11 = (bf16[128,1024]{1,0:T(8,128)(2,1)S(1)}, bf16[128,1024]{1,0:T(8,128)(2,1)S(1)}, u32[]{:S(2)}, u32[]{:S(2)}) collective-permute-start(bf16[128,1024]{1,0:T(8,128)(2,1)S(1)} %get-tuple-element.46), channel_id=1, source_target_pairs={{0,4},{4,0},{8,12},{12,8},{16,20},{20,16},{24,28},{28,24},{1,5},{5... | collective-permute-start | bytes 786440 | tf_op jit(solution)/shard_map/ppermute | solution.py:390

commit v5 on v4

--- a/solution.py
+++ b/solution.py
@@ -67,14 +67,13 @@
     )
 
 
-def project_tiles(a_ref, w_ref, buffer_ref, sem_ref, out_ref, first_slot, column):
+def project_tiles(a_ref, w_ref, buffer_ref, sem_ref, out_ref, column):
     tiles = out_ref.shape[1] // TILE
 
     def tile(j, carry):
-        slot = first_slot + j
-        fetch(w_ref, buffer_ref, sem_ref, slot, column + j * TILE).wait()
+        fetch(w_ref, buffer_ref, sem_ref, j, column + j * TILE).wait()
         out_ref[:, pl.ds(pl.multiple_of(j * TILE, TILE), TILE)] = jnp.dot(
-            a_ref[: out_ref.shape[0]], buffer_ref[slot], preferred_element_type=jnp.float32
+            a_ref[: out_ref.shape[0]], buffer_ref[j], preferred_element_type=jnp.float32
         ).astype(out_ref.dtype)
         return carry
 
@@ -104,7 +103,7 @@
 
 def attend_kernel(
     block,
-    steps,
+    step,
     lengths_ref,
     me_ref,
     q_hbm,
@@ -116,8 +115,7 @@
     adapter_hbm,
     w_ref,
     out_ref,
-    first_ref,
-    second_ref,
+    piece_ref,
     q_ref,
     k_ref,
     v_ref,
@@ -133,8 +131,7 @@
 ):
     rows, heads, width = q_ref.shape
     blocks = rows // block
-    piece_refs = (first_ref, second_ref)
-    out_local = first_ref.shape[1]
+    out_local = piece_ref.shape[1]
     tiles = out_local // TILE
 
     def block_copies(i):
@@ -158,10 +155,9 @@
         return carry
 
     lax.fori_loop(0, blocks, begin, 0)
-    for i, step in enumerate(steps):
-        for j in range(tiles):
-            column = (me_ref[0] ^ step) * out_local + j * TILE
-            fetch(w_ref, buffer_ref, sem_ref, i * tiles + j, column).start()
+    column = (me_ref[0] ^ step) * out_local
+    for j in range(tiles):
+        fetch(w_ref, buffer_ref, sem_ref, j, column + j * TILE).start()
     for copy in new_copies:
         copy.wait()
     out_ref[pl.ds(rows, ID_ROWS), :] = jnp.zeros((ID_ROWS, out_ref.shape[1]), out_ref.dtype)
@@ -190,25 +186,23 @@
         return carry
 
     lax.fori_loop(0, blocks, one_block, 0)
-    for i, (step, piece_ref) in enumerate(zip(steps, piece_refs)):
-        column = (me_ref[0] ^ step) * out_local
-        project_tiles(out_ref, w_ref, buffer_ref, sem_ref, piece_ref, i * tiles, column)
-
-
-def attend(arrays, lengths, out_weight, me, steps, out_local):
+    project_tiles(out_ref, w_ref, buffer_ref, sem_ref, piece_ref, column)
+
+
+def attend(arrays, lengths, out_weight, me, step, out_local):
     queries, key_cache = arrays[:2]
     rows, heads, width = queries.shape
     cache = key_cache.shape[2]
     block = min(16, rows)
     depth = heads * width
-    tiles = len(steps) * (out_local // TILE)
+    tiles = out_local // TILE
     smem = pl.BlockSpec(memory_space=pltpu.SMEM)
     hbm = pl.BlockSpec(memory_space=pltpu.HBM)
     vmem = pl.BlockSpec(memory_space=pltpu.VMEM)
     return pl.pallas_call(
-        functools.partial(attend_kernel, block, steps),
+        functools.partial(attend_kernel, block, step),
         in_specs=[smem, smem] + [hbm] * (len(arrays) + 1),
-        out_specs=[vmem, vmem, vmem],
+        out_specs=[vmem, vmem],
         scratch_shapes=[pltpu.VMEM(a.shape, a.dtype) for a in arrays]
         + [
             pltpu.VMEM((block * heads, width), jnp.float32),
@@ -219,8 +213,8 @@
         ],
         out_shape=[
             jax.ShapeDtypeStruct((rows + ID_ROWS, depth), jnp.bfloat16),
-        ]
-        + [jax.ShapeDtypeStruct((rows, out_local), jnp.bfloat16) for _ in steps],
+            jax.ShapeDtypeStruct((rows, out_local), jnp.bfloat16),
+        ],
         compiler_params=pltpu.CompilerParams(vmem_limit_bytes=57 * MIB),
         cost_estimate=SMALL,
         name="attend",
@@ -398,18 +392,21 @@
     return {0: [own], **{bit: [exchange(own, "dp", bit)] for bit in neighbours()[:2]}}
 
 
-def far_blocks(blocks):
-    blocks = dict(blocks)
-    a, b, *others = neighbours()
+def farther_blocks(blocks):
+    for bit in neighbours()[2:]:
+        for key in list(blocks):
+            blocks[key | bit] = [exchange(part, "dp", bit) for part in blocks[key]]
+    return blocks
+
+
+def forwarded_blocks(blocks):
+    a, b = neighbours()[:2]
     half = blocks[0][0].shape[0] // 2
-    blocks[a | b] = [
+    diagonal = [
         exchange(blocks[a][0][:half], "dp", b),
         exchange(blocks[b][0][half:], "dp", a),
     ]
-    for bit in others:
-        for key in list(blocks):
-            blocks[key | bit] = [exchange(part, "dp", bit) for part in blocks[key]]
-    return blocks
+    return farther_blocks({**blocks, a | b: diagonal})
 
 
 def together(*values):
@@ -437,18 +434,11 @@
     here = lax.axis_index("dp")
     pair = adapters_here * rank
 
-    own_block = jnp.concatenate(
-        [
-            jnp.swapaxes(shrink_weight, 1, 2).reshape(pair, depth),
-            expand_weight.reshape(pair, out_local),
-        ],
-        axis=1,
-    )
-    blocks = near_blocks(own_block)
+    shrink = near_blocks(jnp.swapaxes(shrink_weight, 1, 2).reshape(pair, depth))
+    expand = expand_weight.reshape(pair, out_local)
+
     halved = shares == 4
-    early = (3, 1) if halved else (shares - 1, shares - 2)
-    late = (2, 0) if halved else tuple(range(shares - 3, -1, -1))
-    attended, *pieces = attend(
+    attended, piece = attend(
         (
             queries,
             key_cache,
@@ -461,39 +451,49 @@
         lengths,
         out_weight,
         me,
-        early,
+        shares - 1,
         out_local,
     )
-    received = [
-        exchange(piece, "mp", 1 if halved else step) for piece, step in zip(pieces, early)
-    ]
-    blocks, attended = together(blocks, attended)
-    blocks = far_blocks(blocks)
+    passed = exchange(piece, "mp", 1 if halved else shares - 1)
+    shrink, attended = together(shrink, attended)
+    shrink = forwarded_blocks(shrink)
     beside = exchange(attended, "dp", 1)
-    rows = queries.shape[0]
-    *pieces, own = [
-        jnp.dot(
-            attended[:rows],
-            lax.dynamic_slice_in_dim(out_weight, (me ^ step) * out_local, out_local, 1),
-            preferred_element_type=jnp.float32,
+
+    def chunk(rows, step, dtype):
+        columns = lax.dynamic_slice_in_dim(out_weight, (me ^ step) * out_local, out_local, 1)
+        return jnp.dot(
+            rows[: queries.shape[0]], columns, preferred_element_type=jnp.float32
+        ).astype(dtype)
+
+    pieces = {step: chunk(attended, step, jnp.bfloat16) for step in range(shares - 2, 0, -1)}
+    pieces, passed, attended, shrink, expand = together(
+        pieces, passed, attended, shrink, expand
+    )
+    expand = near_blocks(expand)
+    if halved:
+        received = []
+        pieces[2] = (pieces[2].astype(jnp.float32) + passed.astype(jnp.float32)).astype(
+            jnp.bfloat16
         )
-        for step in late
-    ]
-    if not halved:
-        pieces = [piece.astype(jnp.bfloat16) for piece in pieces]
-    if halved:
-        passed = received.pop(0)
-        passed, attended, own, *pieces = together(passed, attended, own, *pieces)
-        pieces = [(pieces[0] + passed.astype(jnp.float32)).astype(jnp.bfloat16)]
-    received += [exchange(piece, "mp", step) for piece, step in zip(pieces, late)]
-
-    keys = tuple(blocks)
-    blocks = list(blocks.values())
-    low, adapters = low_rank([attended, beside], blocks, depth, here, keys, rank)
-    lows = [low] + [exchange(low, "mp", step) for step in range(1, shares)]
-    lows, received = together(lows, received)
-    low = sum(part.astype(jnp.float32) for part in lows).astype(jnp.bfloat16)
-    correction, other = correct(low, adapters, blocks, depth, out_local, here, keys, rank)
+    else:
+        received = [passed]
+    received += [exchange(piece, "mp", step) for step, piece in pieces.items()]
+
+    keys = tuple(shrink)
+    low, adapters = low_rank(
+        [attended, beside], list(shrink.values()), depth, here, keys, rank
+    )
+    expand, low = together(expand, low)
+    expand = forwarded_blocks(expand)
+    attended, low = together(attended, low)
+    own = chunk(attended, 0, jnp.float32)
+    step = 1
+    while step < shares:
+        arrived = exchange(low, "mp", step)
+        low = (low.astype(jnp.float32) + arrived.astype(jnp.float32)).astype(jnp.bfloat16)
+        step *= 2
+    blocks = [expand[key] for key in keys]
+    correction, other = correct(low, adapters, blocks, 0, out_local, here, keys, rank)
     return finish(own, [*received, correction, exchange(other, "dp", 1)], occupied)
 
 

time: 62.4 us -> 59.7 us (0.957)
  waiting for transfers between devices: 17.7 us -> 12 us
  matrix products: 6.13 us -> 10.5 us
  Pallas kernels: 18 us -> 14.6 us
  starting transfers between devices: 15.8 us -> 17.7 us
  local copies, waits for them, and re-layouts: 1.57 us -> 3.37 us
  other arithmetic: 2.92 us -> 1.12 us
    ppermute x12 -> x15, waiting for transfers between devices: 17.7 us -> 12 us  [exchange(): return lax.ppermute(value, axis, [(i, i ^ step) for i in range(count)])]
    dot_general x2 -> x3, matrix products: 6.13 us -> 10.5 us  [chunk(): jnp.dot(rows[:queries.shape[0]], columns, preferred_element_type=jnp.floa...]
    unnamed x4 -> x16, local copies, waits for them, and re-layouts: 0.01 us -> 3.32 us
    ppermute x12 -> x15, starting transfers between devices: 15.8 us -> 17.7 us  [exchange(): return lax.ppermute(value, axis, [(i, i ^ step) for i in range(count)])]
    slice x2 -> x4, local copies, waits for them, and re-layouts: 1.56 us -> 0.05 us  [the longest x2 0.03 us: forwarded_blocks(): blocks[a][0][:half]]
    pallas_call x1, Pallas kernels: 11.4 us -> 10.1 us  [attend(): pl.pallas_call(functools.partial(attend_kernel, block, step), in_specs=[s...]
    concatenate x1 -> x0, other arithmetic: 1.18 us -> none  [body(): jnp.concatenate([jnp.swapaxes(shrink_weight, 1, 2).reshape(pair, depth),...]
    pallas_call x1, Pallas kernels: 1.92 us -> 0.91 us  [finish(): pl.pallas_call(finish_kernel, in_specs=[vmem] * (2 + len(parts)), out_spe...]
  transfers between devices with their start and end apart: 12 -> 15, of which waited for: 7 -> 7; matrix products, arithmetic and copies ran while one was open for 15% -> 20% of each run, Pallas kernels for 23% -> 23%
where the time goes in v5:
time: 59.7 us; the launch traced here: 59.4 us
  starting transfers between devices  17.7 us (30%)
  Pallas kernels  14.6 us (24%)
  waiting for transfers between devices  12 us (20%)
  matrix products  10.5 us (18%)
  local copies, waits for them, and re-layouts  3.37 us (6%)
  other arithmetic  1.12 us (2%)
    ppermute x15, starting transfers between devices, exchange(): return lax.ppermute(value, axis, [(i, i ^ step) for i in range(count)])  17.7 us
    ppermute x15, waiting for transfers between devices, exchange(): return lax.ppermute(value, axis, [(i, i ^ step) for i in range(count)])  12 us
    dot_general x3, matrix products, chunk(): jnp.dot(rows[:queries.shape[0]], columns, preferred_element_type=jnp.floa...  10.5 us
    pallas_call x1, Pallas kernels, attend(): pl.pallas_call(functools.partial(attend_kernel, block, step), in_specs=[s...  10.1 us
    unnamed x16, local copies, waits for them, and re-layouts  3.32 us
    pallas_call x1, Pallas kernels, low_rank(): pl.pallas_call(functools.partial(low_kernel, rank, places, keys), in_spec...  2.54 us
  transfers between devices with their start and end apart: 15, of which 7 were waited for; matrix products, arithmetic and copies ran while one was open for 20% of the time, Pallas kernels for 23%

profile of v5, /device:TPU:0, one launch (start us, length us, event | category | flops | bytes accessed | tf_op | source)
XLA Modules:
  0.0 59.4 jit_solution(7048060063656023656)
XLA Ops:
  0.0 2.9 %collective-permute-start = (bf16[128,2048]{1,0:T(8,128)(2,1)}, bf16[128,2048]{1,0:T(8,128)(2,1)S(1)}, u32[]{:S(2)}, u32[]{:S(2)}) collective-permute-start(bf16[128,2048]{1,0:T(8,128)(2,1)} %bitcast.9), channel_id=1, source_target_pairs={{0,8},{4,12},{8,0},{12,4},{16,24},{20,28},{24,16},{28,20},{1,9},{5... | collective-permute-start | bytes 1572872 | tf_op jit(solution)/shard_map/ppermute | solution.py:384
  2.9 1.5 %collective-permute-start.1 = (bf16[128,2048]{1,0:T(8,128)(2,1)}, bf16[128,2048]{1,0:T(8,128)(2,1)S(1)}, u32[]{:S(2)}, u32[]{:S(2)}) collective-permute-start(bf16[128,2048]{1,0:T(8,128)(2,1)} %bitcast.10), channel_id=1, source_target_pairs={{0,16},{4,20},{8,24},{12,28},{16,0},{20,4},{24,8},{28,12},{1,17},{... | collective-permute-start | bytes 1572872 | tf_op jit(solution)/shard_map/ppermute | solution.py:384
  4.5 10.1 %attend.1 = (bf16[144,2048]{1,0:T(8,128)(2,1)}, bf16[128,1024]{1,0:T(8,128)(2,1)}) custom-call(s32[128]{0:T(128)} %lengths_ref.1, s32[1]{0:T(128)} %bitcast.4.me_ref, bf16[128,16,128]{2,1,0:T(8,128)(2,1)} %q_hbm.1, bf16[128,2,128,128]{3,2,1,0:T(8,128)(2,1)} %k_hbm.1, bf16[128,2,128,128]{3,2,1,0:T(8,128)(2,1)} %v_hbm.1, bf16[128,2,128]{2,1,0:T(2,128)(2,1)} %kn_hbm.1, ...), custom_call_target="tpu_custom_call" | custom-call | flops 1 | bytes 1 | tf_op jit(solution)/shard_map/attend/pallas_call | solution.py:202
  14.6 1.6 %collective-permute-start.2 = (bf16[128,1024]{1,0:T(8,128)(2,1)}, bf16[128,1024]{1,0:T(8,128)(2,1)}, u32[]{:S(2)}, u32[]{:S(2)}) collective-permute-start(bf16[128,1024]{1,0:T(8,128)(2,1)} %get-tuple-element.33), channel_id=1, source_target_pairs={{0,1},{1,0},{2,3},{3,2},{4,5},{5,4},{6,7},{7,6},{8,9},{9,8},{10,11... | collective-permute-start | bytes 786440 | tf_op jit(solution)/shard_map/ppermute | solution.py:384
  16.3 0.2 collective-permute-done.1.refs_4_
  16.6 1.6 %collective-permute-start.3 = (bf16[64,2048]{1,0:T(8,128)(2,1)S(1)}, bf16[64,2048]{1,0:T(8,128)(2,1)S(1)}, u32[]{:S(2)}, u32[]{:S(2)}) collective-permute-start(bf16[64,2048]{1,0:T(8,128)(2,1)S(1)} %slice.20), channel_id=1, source_target_pairs={{0,16},{4,20},{8,24},{12,28},{16,0},{20,4},{24,8},{28,12},{1,17},{... | collective-permute-start | bytes 786440 | tf_op jit(solution)/shard_map/ppermute | solution.py:384
  18.2 0.6 %collective-permute-start.4 = (bf16[64,2048]{1,0:T(8,128)(2,1)S(1)}, bf16[64,2048]{1,0:T(8,128)(2,1)S(1)}, u32[]{:S(2)}, u32[]{:S(2)}) collective-permute-start(bf16[64,2048]{1,0:T(8,128)(2,1)S(1)} %slice.21), channel_id=1, source_target_pairs={{0,8},{4,12},{8,0},{12,4},{16,24},{20,28},{24,16},{28,20},{1,9},{5... | collective-permute-start | bytes 786440 | tf_op jit(solution)/shard_map/ppermute | solution.py:384
  18.8 3.8 %fusion.9 = bf16[128,1024]{1,0:T(8,128)(2,1)} fusion(bf16[2048,4096]{1,0:T(8,128)(2,1)} %w_ref.1, s32[]{:T(128)S(6)} %select_n.10, bf16[144,2048]{1,0:T(8,128)(2,1)} %get-tuple-element.46.refs_0_), kind=kOutput, calls=%fused_computation.7 | convolution fusion | flops 537001984 | bytes 4980740 | tf_op jit(solution)/shard_map/dot_general | solution.py:464
  22.5 3.8 %fusion.6 = bf16[128,1024]{1,0:T(8,128)(2,1)} fusion(bf16[2048,4096]{1,0:T(8,128)(2,1)} %w_ref.1, s32[]{:T(128)S(6)} %select_n.9, bf16[144,2048]{1,0:T(8,128)(2,1)} %get-tuple-element.46.refs_0_), kind=kOutput, calls=%fused_computation.6 | convolution fusion | flops 537001984 | bytes 4980740 | tf_op jit(solution)/shard_map/dot_general | solution.py:464
  26.3 0.7 %copy-done.3 = bf16[64,2048]{1,0:T(8,128)(2,1)} copy-done((bf16[64,2048]{1,0:T(8,128)(2,1)}, bf16[64,2048]{1,0:T(8,128)(2,1)S(1)}, u32[]{:S(2)}) %copy-start.3) | copy-done | bytes 262168
  27.0 0.7 %copy-done.5 = bf16[64,2048]{1,0:T(8,128)(2,1)} copy-done((bf16[64,2048]{1,0:T(8,128)(2,1)}, bf16[64,2048]{1,0:T(8,128)(2,1)S(1)}, u32[]{:S(2)}) %copy-start.5) | copy-done | bytes 262168
  27.7 1.5 %collective-permute-start.5 = (bf16[128,1024]{1,0:T(8,128)(2,1)S(1)}, bf16[128,1024]{1,0:T(8,128)(2,1)S(1)}, u32[]{:S(2)}, u32[]{:S(2)}) collective-permute-start(bf16[128,1024]{1,0:T(8,128)(2,1)S(1)} %bitcast.12), channel_id=1, source_target_pairs={{0,8},{4,12},{8,0},{12,4},{16,24},{20,28},{24,16},{28,20},{1,9},{5... | collective-permute-start | bytes 786440 | tf_op jit(solution)/shard_map/ppermute | solution.py:384
  29.2 0.5 collective-permute-start.6
  29.8 0.9 %copy-done.4 = bf16[64,2048]{1,0:T(8,128)(2,1)S(1)} copy-done((bf16[64,2048]{1,0:T(8,128)(2,1)S(1)}, bf16[64,2048]{1,0:T(8,128)(2,1)}, u32[]{:S(2)}) %copy-start.4) | copy-done | bytes 262168
  30.7 0.9 %copy-done.6 = bf16[64,2048]{1,0:T(8,128)(2,1)S(1)} copy-done((bf16[64,2048]{1,0:T(8,128)(2,1)S(1)}, bf16[64,2048]{1,0:T(8,128)(2,1)}, u32[]{:S(2)}) %copy-start.6) | copy-done | bytes 262168
  31.7 2.5 %low_rank.1 = (bf16[64,256]{1,0:T(8,128)(2,1)S(1)}, s32[8,256]{1,0:T(8,128)S(1)}) custom-call(s32[1]{0:T(128)} %bitcast.8.here_ref, bf16[144,2048]{1,0:T(8,128)(2,1)S(1)} %copy-done, bf16[144,2048]{1,0:T(8,128)(2,1)S(1)} %collective-permute-done.7.refs_1_, bf16[128,2048]{1,0:T(8,128)(2,1)S(1)} %bitcast.11, ...), custom_call_target="tpu_custom_call" | custom-call | flops 1 | bytes 1 | tf_op jit(solution)/shard_map/low_rank/pallas_call | solution.py:289
  34.2 2.3 %collective-permute-done.5.refs_1_ = bf16[128,1024]{1,0:T(8,128)(2,1)S(1)} collective-permute-done((bf16[128,1024]{1,0:T(8,128)(2,1)S(1)}, bf16[128,1024]{1,0:T(8,128)(2,1)S(1)}, u32[]{:S(2)}, u32[]{:S(2)}) %collective-permute-start.5) | collective-permute-done | bytes 262176 | tf_op jit(solution)/shard_map/ppermute | solution.py:384
  36.5 1.2 %collective-permute-done.6.refs_2_ = bf16[128,1024]{1,0:T(8,128)(2,1)S(1)} collective-permute-done((bf16[128,1024]{1,0:T(8,128)(2,1)S(1)}, bf16[128,1024]{1,0:T(8,128)(2,1)S(1)}, u32[]{:S(2)}, u32[]{:S(2)}) %collective-permute-start.6) | collective-permute-done | bytes 262176 | tf_op jit(solution)/shard_map/ppermute | solution.py:384
  37.7 1.6 %collective-permute-start.10 = (bf16[64,256]{1,0:T(8,128)(2,1)S(1)}, bf16[64,256]{1,0:T(8,128)(2,1)S(1)}, u32[]{:S(2)}, u32[]{:S(2)}) collective-permute-start(bf16[64,256]{1,0:T(8,128)(2,1)S(1)} %get-tuple-element.51), channel_id=1, source_target_pairs={{0,1},{1,0},{2,3},{3,2},{4,5},{5,4},{6,7},{7,6},{8,9},{9,8},{10,11... | collective-permute-start | bytes 98312 | tf_op jit(solution)/shard_map/ppermute | solution.py:384
  39.3 2.3 %collective-permute-done.10 = bf16[64,256]{1,0:T(8,128)(2,1)S(1)} collective-permute-done((bf16[64,256]{1,0:T(8,128)(2,1)S(1)}, bf16[64,256]{1,0:T(8,128)(2,1)S(1)}, u32[]{:S(2)}, u32[]{:S(2)}) %collective-permute-start.10) | collective-permute-done | bytes 32800 | tf_op jit(solution)/shard_map/ppermute | solution.py:384
  41.6 2.7 %collective-permute-start.11 = (bf16[64,256]{1,0:T(8,128)(2,1)S(1)}, bf16[64,256]{1,0:T(8,128)(2,1)S(1)}, u32[]{:S(2)}, u32[]{:S(2)}) collective-permute-start(bf16[64,256]{1,0:T(8,128)(2,1)S(1)} %add_convert_fusion.2), channel_id=1, source_target_pairs={{0,2},{1,3},{2,0},{3,1},{4,6},{5,7},{6,4},{7,5},{8,10},{9,11},{10,... | collective-permute-start | bytes 98312 | tf_op jit(solution)/shard_map/ppermute | solution.py:384
  44.3 1.1 %add_convert_fusion = bf16[128,1024]{1,0:T(8,128)(2,1)S(1)} fusion(bf16[128,1024]{1,0:T(8,128)(2,1)} %collective-permute-done.2, bf16[128,1024]{1,0:T(8,128)(2,1)} %fusion.9), kind=kLoop, calls=%fused_computation.8 | loop fusion | flops 524288 | bytes 786432 | tf_op jit(solution)/shard_map/convert_element_type | solution.py:475
  45.4 0.4 collective-permute-start.9
  45.8 1.6 %collective-permute-start.8 = (bf16[128,1024]{1,0:T(8,128)(2,1)}, bf16[128,1024]{1,0:T(8,128)(2,1)S(1)}, u32[]{:S(2)}, u32[]{:S(2)}) collective-permute-start(bf16[128,1024]{1,0:T(8,128)(2,1)} %fusion.6), channel_id=1, source_target_pairs={{0,1},{1,0},{2,3},{3,2},{4,5},{5,4},{6,7},{7,6},{8,9},{9,8},{10,11... | collective-permute-start | bytes 786440 | tf_op jit(solution)/shard_map/ppermute | solution.py:384
  47.4 0.6 collective-permute-start.12
  47.9 0.6 %collective-permute-start.13 = (bf16[64,1024]{1,0:T(8,128)(2,1)S(1)}, bf16[64,1024]{1,0:T(8,128)(2,1)S(1)}, u32[]{:S(2)}, u32[]{:S(2)}) collective-permute-start(bf16[64,1024]{1,0:T(8,128)(2,1)S(1)} %slice.24), channel_id=1, source_target_pairs={{0,8},{4,12},{8,0},{12,4},{16,24},{20,28},{24,16},{28,20},{1,9},{5... | collective-permute-start | bytes 393224 | tf_op jit(solution)/shard_map/ppermute | solution.py:384
  48.6 3.8 %collective-permute-done.12.refs_3_ = bf16[64,1024]{1,0:T(8,128)(2,1)S(1)} collective-permute-done((bf16[64,1024]{1,0:T(8,128)(2,1)S(1)}, bf16[64,1024]{1,0:T(8,128)(2,1)S(1)}, u32[]{:S(2)}, u32[]{:S(2)}) %collective-permute-start.12) | collective-permute-done | bytes 131104 | tf_op jit(solution)/shard_map/ppermute | solution.py:384
  52.4 0.6 collective-permute-done.13.refs_4_
  53.0 1.0 %correct.1 = (bf16[128,1024]{1,0:T(8,128)(2,1)S(1)}, bf16[128,1024]{1,0:T(8,128)(2,1)S(1)}) custom-call(s32[1]{0:T(128)} %bitcast.8.here_ref, s32[8,256]{1,0:T(8,128)S(1)} %get-tuple-element.50.adapters_ref, bf16[64,256]{1,0:T(8,128)(2,1)S(1)} %add_convert_fusion.1.low_ref, bf16[128,1024]{1,0:T(8,128)(2,1)S(1)} %bitcast.14, ...), custom_call_target="tpu_custom_call" | custom-call | flops 1 | bytes 1 | tf_op jit(solution)/shard_map/correct/pallas_call | solution.py:340
  54.1 2.9 %fusion.own_ref = f32[128,1024]{1,0:T(8,128)S(1)} fusion(bf16[2048,4096]{1,0:T(8,128)(2,1)} %w_ref.1, s32[]{:T(128)S(6)} %select_n.11, bf16[144,2048]{1,0:T(8,128)(2,1)S(1)} %copy-done), kind=kOutput, calls=%fused_computation | convolution fusion | flops 536870912 | bytes 5242884 | tf_op jit(solution)/shard_map/dot_general | solution.py:464
  57.0 1.5 %collective-permute-done.9.refs_1_ = bf16[128,1024]{1,0:T(8,128)(2,1)S(1)} collective-permute-done((bf16[128,1024]{1,0:T(8,128)(2,1)S(1)}, bf16[128,1024]{1,0:T(8,128)(2,1)S(1)}, u32[]{:S(2)}, u32[]{:S(2)}) %collective-permute-start.9) | collective-permute-done | bytes 262176 | tf_op jit(solution)/shard_map/ppermute | solution.py:384
  58.5 0.9 %finish.1 = bf16[128,1024]{1,0:T(8,128)(2,1)} custom-call(s32[1,128]{1,0:T(1,128)S(1)} %bitcast.15, f32[128,1024]{1,0:T(8,128)S(1)} %fusion.own_ref, bf16[128,1024]{1,0:T(8,128)(2,1)S(1)} %collective-permute-done.8.refs_0_, bf16[128,1024]{1,0:T(8,128)(2,1)S(1)} %collective-permute-done.9.refs_1_, bf16[128,1024]{1,0:T(8,128)(2,1)S(1)} %get-tuple-element.55.refs_2_, ...), custom_call_target="tpu_custom_call" | custom-call | flops 1 | bytes 1 | tf_op jit(solution)/shard_map/finish/pallas_call | solution.py:371
  (28 shorter events, 0.2 us)
Async XLA Ops:
  0.0 16.3 %collective-permute-start = (bf16[128,2048]{1,0:T(8,128)(2,1)}, bf16[128,2048]{1,0:T(8,128)(2,1)S(1)}, u32[]{:S(2)}, u32[]{:S(2)}) collective-permute-start(bf16[128,2048]{1,0:T(8,128)(2,1)} %bitcast.9), channel_id=1, source_target_pairs={{0,8},{4,12},{8,0},{12,4},{16,24},{20,28},{24,16},{28,20},{1,9},{5... | collective-permute-start | bytes 1572872 | tf_op jit(solution)/shard_map/ppermute | solution.py:384
  2.9 13.6 %collective-permute-start.1 = (bf16[128,2048]{1,0:T(8,128)(2,1)}, bf16[128,2048]{1,0:T(8,128)(2,1)S(1)}, u32[]{:S(2)}, u32[]{:S(2)}) collective-permute-start(bf16[128,2048]{1,0:T(8,128)(2,1)} %bitcast.10), channel_id=1, source_target_pairs={{0,16},{4,20},{8,24},{12,28},{16,0},{20,4},{24,8},{28,12},{1,17},{... | collective-permute-start | bytes 1572872 | tf_op jit(solution)/shard_map/ppermute | solution.py:384
  14.6 13.1 %copy-start.2 = (bf16[2,64,1024]{2,1,0:T(8,128)(2,1)S(1)}, bf16[2,64,1024]{2,1,0:T(8,128)(2,1)}, u32[]{:S(2)}) copy-start(bf16[2,64,1024]{2,1,0:T(8,128)(2,1)} %param.23) | copy-start | bytes 786436
  14.6 15.1 %copy-start = (bf16[144,2048]{1,0:T(8,128)(2,1)S(1)}, bf16[144,2048]{1,0:T(8,128)(2,1)}, u32[]{:S(2)}) copy-start(bf16[144,2048]{1,0:T(8,128)(2,1)} %get-tuple-element.46.refs_0_) | copy-start | bytes 1769476
  14.6 15.1 %copy-start.1 = (bf16[2,2048,64]{1,2,0:T(8,128)(2,1)S(1)}, bf16[2,2048,64]{1,2,0:T(8,128)(2,1)}, u32[]{:S(2)}) copy-start(bf16[2,2048,64]{1,2,0:T(8,128)(2,1)} %param.22) | copy-start | bytes 1572868
  14.6 11.7 %collective-permute-start.2 = (bf16[128,1024]{1,0:T(8,128)(2,1)}, bf16[128,1024]{1,0:T(8,128)(2,1)}, u32[]{:S(2)}, u32[]{:S(2)}) collective-permute-start(bf16[128,1024]{1,0:T(8,128)(2,1)} %get-tuple-element.33), channel_id=1, source_target_pairs={{0,1},{1,0},{2,3},{3,2},{4,5},{5,4},{6,7},{7,6},{8,9},{9,8},{10,11... | collective-permute-start | bytes 786440 | tf_op jit(solution)/shard_map/ppermute | solution.py:384
  16.6 9.8 %collective-permute-start.3 = (bf16[64,2048]{1,0:T(8,128)(2,1)S(1)}, bf16[64,2048]{1,0:T(8,128)(2,1)S(1)}, u32[]{:S(2)}, u32[]{:S(2)}) collective-permute-start(bf16[64,2048]{1,0:T(8,128)(2,1)S(1)} %slice.20), channel_id=1, source_target_pairs={{0,16},{4,20},{8,24},{12,28},{16,0},{20,4},{24,8},{28,12},{1,17},{... | collective-permute-start | bytes 786440 | tf_op jit(solution)/shard_map/ppermute | solution.py:384
  18.2 8.9 %collective-permute-start.4 = (bf16[64,2048]{1,0:T(8,128)(2,1)S(1)}, bf16[64,2048]{1,0:T(8,128)(2,1)S(1)}, u32[]{:S(2)}, u32[]{:S(2)}) collective-permute-start(bf16[64,2048]{1,0:T(8,128)(2,1)S(1)} %slice.21), channel_id=1, source_target_pairs={{0,8},{4,12},{8,0},{12,4},{16,24},{20,28},{24,16},{28,20},{1,9},{5... | collective-permute-start | bytes 786440 | tf_op jit(solution)/shard_map/ppermute | solution.py:384
  18.8 11.0 %collective-permute-start.7 = (bf16[144,2048]{1,0:T(8,128)(2,1)}, bf16[144,2048]{1,0:T(8,128)(2,1)S(1)}, u32[]{:S(2)}, u32[]{:S(2)}) collective-permute-start(bf16[144,2048]{1,0:T(8,128)(2,1)} %get-tuple-element.46.refs_0_), channel_id=1, source_target_pairs={{0,4},{4,0},{8,12},{12,8},{16,20},{20,16},{24,28},{28,24},{1,5},{5... | collective-permute-start | bytes 1769480 | tf_op jit(solution)/shard_map/ppermute | solution.py:384
  22.5 36.0 %copy-start.7 = (s32[128]{0:T(128)S(1)}, s32[128]{0:T(128)}, u32[]{:S(2)}) copy-start(s32[128]{0:T(128)} %param.18) | copy-start | bytes 1540
  26.3 0.7 %copy-start.3 = (bf16[64,2048]{1,0:T(8,128)(2,1)}, bf16[64,2048]{1,0:T(8,128)(2,1)S(1)}, u32[]{:S(2)}) copy-start(bf16[64,2048]{1,0:T(8,128)(2,1)S(1)} %collective-permute-done.3.refs_5_) | copy-start | bytes 786436
  27.0 0.7 %copy-start.5 = (bf16[64,2048]{1,0:T(8,128)(2,1)}, bf16[64,2048]{1,0:T(8,128)(2,1)S(1)}, u32[]{:S(2)}) copy-start(bf16[64,2048]{1,0:T(8,128)(2,1)S(1)} %collective-permute-done.4.refs_6_) | copy-start | bytes 786436
  27.7 8.7 %collective-permute-start.5 = (bf16[128,1024]{1,0:T(8,128)(2,1)S(1)}, bf16[128,1024]{1,0:T(8,128)(2,1)S(1)}, u32[]{:S(2)}, u32[]{:S(2)}) collective-permute-start(bf16[128,1024]{1,0:T(8,128)(2,1)S(1)} %bitcast.12), channel_id=1, source_target_pairs={{0,8},{4,12},{8,0},{12,4},{16,24},{20,28},{24,16},{28,20},{1,9},{5... | collective-permute-start | bytes 786440 | tf_op jit(solution)/shard_map/ppermute | solution.py:384
  29.2 8.4 %collective-permute-start.6 = (bf16[128,1024]{1,0:T(8,128)(2,1)S(1)}, bf16[128,1024]{1,0:T(8,128)(2,1)S(1)}, u32[]{:S(2)}, u32[]{:S(2)}) collective-permute-start(bf16[128,1024]{1,0:T(8,128)(2,1)S(1)} %bitcast.13), channel_id=1, source_target_pairs={{0,16},{4,20},{8,24},{12,28},{16,0},{20,4},{24,8},{28,12},{1,17},{... | collective-permute-start | bytes 786440 | tf_op jit(solution)/shard_map/ppermute | solution.py:384
  29.8 1.0 %copy-start.4 = (bf16[64,2048]{1,0:T(8,128)(2,1)S(1)}, bf16[64,2048]{1,0:T(8,128)(2,1)}, u32[]{:S(2)}) copy-start(bf16[64,2048]{1,0:T(8,128)(2,1)} %copy-done.3) | copy-start | bytes 786436
  30.7 0.9 %copy-start.6 = (bf16[64,2048]{1,0:T(8,128)(2,1)S(1)}, bf16[64,2048]{1,0:T(8,128)(2,1)}, u32[]{:S(2)}) copy-start(bf16[64,2048]{1,0:T(8,128)(2,1)} %copy-done.5) | copy-start | bytes 786436
  37.7 3.9 %collective-permute-start.10 = (bf16[64,256]{1,0:T(8,128)(2,1)S(1)}, bf16[64,256]{1,0:T(8,128)(2,1)S(1)}, u32[]{:S(2)}, u32[]{:S(2)}) collective-permute-start(bf16[64,256]{1,0:T(8,128)(2,1)S(1)} %get-tuple-element.51), channel_id=1, source_target_pairs={{0,1},{1,0},{2,3},{3,2},{4,5},{5,4},{6,7},{7,6},{8,9},{9,8},{10,11... | collective-permute-start | bytes 98312 | tf_op jit(solution)/shard_map/ppermute | solution.py:384
  41.6 6.9 %collective-permute-start.11 = (bf16[64,256]{1,0:T(8,128)(2,1)S(1)}, bf16[64,256]{1,0:T(8,128)(2,1)S(1)}, u32[]{:S(2)}, u32[]{:S(2)}) collective-permute-start(bf16[64,256]{1,0:T(8,128)(2,1)S(1)} %add_convert_fusion.2), channel_id=1, source_target_pairs={{0,2},{1,3},{2,0},{3,1},{4,6},{5,7},{6,4},{7,5},{8,10},{9,11},{10,... | collective-permute-start | bytes 98312 | tf_op jit(solution)/shard_map/ppermute | solution.py:384
  45.4 13.1 %collective-permute-start.9 = (bf16[128,1024]{1,0:T(8,128)(2,1)S(1)}, bf16[128,1024]{1,0:T(8,128)(2,1)S(1)}, u32[]{:S(2)}, u32[]{:S(2)}) collective-permute-start(bf16[128,1024]{1,0:T(8,128)(2,1)S(1)} %add_convert_fusion), channel_id=1, source_target_pairs={{0,2},{1,3},{2,0},{3,1},{4,6},{5,7},{6,4},{7,5},{8,10},{9,11},{10,... | collective-permute-start | bytes 786440 | tf_op jit(solution)/shard_map/ppermute | solution.py:384
  45.8 12.7 %collective-permute-start.8 = (bf16[128,1024]{1,0:T(8,128)(2,1)}, bf16[128,1024]{1,0:T(8,128)(2,1)S(1)}, u32[]{:S(2)}, u32[]{:S(2)}) collective-permute-start(bf16[128,1024]{1,0:T(8,128)(2,1)} %fusion.6), channel_id=1, source_target_pairs={{0,1},{1,0},{2,3},{3,2},{4,5},{5,4},{6,7},{7,6},{8,9},{9,8},{10,11... | collective-permute-start | bytes 786440 | tf_op jit(solution)/shard_map/ppermute | solution.py:384
  47.4 5.0 %collective-permute-start.12 = (bf16[64,1024]{1,0:T(8,128)(2,1)S(1)}, bf16[64,1024]{1,0:T(8,128)(2,1)S(1)}, u32[]{:S(2)}, u32[]{:S(2)}) collective-permute-start(bf16[64,1024]{1,0:T(8,128)(2,1)S(1)} %slice.23), channel_id=1, source_target_pairs={{0,16},{4,20},{8,24},{12,28},{16,0},{20,4},{24,8},{28,12},{1,17},{... | collective-permute-start | bytes 393224 | tf_op jit(solution)/shard_map/ppermute | solution.py:384
  47.9 5.0 %collective-permute-start.13 = (bf16[64,1024]{1,0:T(8,128)(2,1)S(1)}, bf16[64,1024]{1,0:T(8,128)(2,1)S(1)}, u32[]{:S(2)}, u32[]{:S(2)}) collective-permute-start(bf16[64,1024]{1,0:T(8,128)(2,1)S(1)} %slice.24), channel_id=1, source_target_pairs={{0,8},{4,12},{8,0},{12,4},{16,24},{20,28},{24,16},{28,20},{1,9},{5... | collective-permute-start | bytes 393224 | tf_op jit(solution)/shard_map/ppermute | solution.py:384
  54.0 4.5 %collective-permute-start.14 = (bf16[128,1024]{1,0:T(8,128)(2,1)S(1)}, bf16[128,1024]{1,0:T(8,128)(2,1)S(1)}, u32[]{:S(2)}, u32[]{:S(2)}) collective-permute-start(bf16[128,1024]{1,0:T(8,128)(2,1)S(1)} %get-tuple-element.56), channel_id=1, source_target_pairs={{0,4},{4,0},{8,12},{12,8},{16,20},{20,16},{24,28},{28,24},{1,5},{5... | collective-permute-start | bytes 786440 | tf_op jit(solution)/shard_map/ppermute | solution.py:384

commit v6 on v5

--- a/solution.py
+++ b/solution.py
@@ -67,13 +67,14 @@
     )
 
 
-def project_tiles(a_ref, w_ref, buffer_ref, sem_ref, out_ref, column):
-    tiles = out_ref.shape[1] // TILE
-
+def project_tiles(
+    a_ref, w_ref, buffer_ref, sem_ref, out_ref, tiles, first_slot, column, out_column
+):
     def tile(j, carry):
-        fetch(w_ref, buffer_ref, sem_ref, j, column + j * TILE).wait()
-        out_ref[:, pl.ds(pl.multiple_of(j * TILE, TILE), TILE)] = jnp.dot(
-            a_ref[: out_ref.shape[0]], buffer_ref[j], preferred_element_type=jnp.float32
+        slot = first_slot + j
+        fetch(w_ref, buffer_ref, sem_ref, slot, column + j * TILE).wait()
+        out_ref[:, pl.ds(pl.multiple_of(out_column + j * TILE, TILE), TILE)] = jnp.dot(
+            a_ref[: out_ref.shape[0]], buffer_ref[slot], preferred_element_type=jnp.float32
         ).astype(out_ref.dtype)
         return carry
 
@@ -103,7 +104,7 @@
 
 def attend_kernel(
     block,
-    step,
+    steps,
     lengths_ref,
     me_ref,
     q_hbm,
@@ -131,7 +132,7 @@
 ):
     rows, heads, width = q_ref.shape
     blocks = rows // block
-    out_local = piece_ref.shape[1]
+    out_local = piece_ref.shape[1] // len(steps)
     tiles = out_local // TILE
 
     def block_copies(i):
@@ -155,9 +156,10 @@
         return carry
 
     lax.fori_loop(0, blocks, begin, 0)
-    column = (me_ref[0] ^ step) * out_local
-    for j in range(tiles):
-        fetch(w_ref, buffer_ref, sem_ref, j, column + j * TILE).start()
+    columns = [(me_ref[0] ^ step) * out_local for step in steps]
+    for i, column in enumerate(columns):
+        for j in range(tiles):
+            fetch(w_ref, buffer_ref, sem_ref, i * tiles + j, column + j * TILE).start()
     for copy in new_copies:
         copy.wait()
     out_ref[pl.ds(rows, ID_ROWS), :] = jnp.zeros((ID_ROWS, out_ref.shape[1]), out_ref.dtype)
@@ -186,21 +188,24 @@
         return carry
 
     lax.fori_loop(0, blocks, one_block, 0)
-    project_tiles(out_ref, w_ref, buffer_ref, sem_ref, piece_ref, column)
-
-
-def attend(arrays, lengths, out_weight, me, step, out_local):
+    for i, column in enumerate(columns):
+        project_tiles(
+            out_ref, w_ref, buffer_ref, sem_ref, piece_ref, tiles, i * tiles, column, i * out_local
+        )
+
+
+def attend(arrays, lengths, out_weight, me, steps, out_local):
     queries, key_cache = arrays[:2]
     rows, heads, width = queries.shape
     cache = key_cache.shape[2]
     block = min(16, rows)
     depth = heads * width
-    tiles = out_local // TILE
+    tiles = len(steps) * (out_local // TILE)
     smem = pl.BlockSpec(memory_space=pltpu.SMEM)
     hbm = pl.BlockSpec(memory_space=pltpu.HBM)
     vmem = pl.BlockSpec(memory_space=pltpu.VMEM)
     return pl.pallas_call(
-        functools.partial(attend_kernel, block, step),
+        functools.partial(attend_kernel, block, steps),
         in_specs=[smem, smem] + [hbm] * (len(arrays) + 1),
         out_specs=[vmem, vmem],
         scratch_shapes=[pltpu.VMEM(a.shape, a.dtype) for a in arrays]
@@ -213,12 +218,50 @@
         ],
         out_shape=[
             jax.ShapeDtypeStruct((rows + ID_ROWS, depth), jnp.bfloat16),
-            jax.ShapeDtypeStruct((rows, out_local), jnp.bfloat16),
+            jax.ShapeDtypeStruct((rows, len(steps) * out_local), jnp.bfloat16),
         ],
         compiler_params=pltpu.CompilerParams(vmem_limit_bytes=57 * MIB),
         cost_estimate=SMALL,
         name="attend",
     )(lengths, me.reshape(1), *arrays, out_weight)
+
+
+def project_kernel(steps, me_ref, a_hbm, w_ref, *refs):
+    *out_refs, a_ref, buffer_ref, a_sem, sem_ref = refs
+    out_local = out_refs[0].shape[1]
+    tiles = out_local // TILE
+    copy = pltpu.make_async_copy(a_hbm, a_ref, a_sem.at[0])
+    copy.start()
+    for i, step in enumerate(steps):
+        for j in range(tiles):
+            column = (me_ref[0] ^ step) * out_local + j * TILE
+            fetch(w_ref, buffer_ref, sem_ref, i * tiles + j, column).start()
+    copy.wait()
+    for i, (step, out_ref) in enumerate(zip(steps, out_refs)):
+        column = (me_ref[0] ^ step) * out_local
+        project_tiles(a_ref, w_ref, buffer_ref, sem_ref, out_ref, tiles, i * tiles, column, 0)
+
+
+def project(attended, out_weight, me, steps, out_local, dtypes):
+    rows, depth = attended.shape[0] - ID_ROWS, attended.shape[1]
+    slots = len(dtypes) * (out_local // TILE)
+    vmem = pl.BlockSpec(memory_space=pltpu.VMEM)
+    hbm = pl.BlockSpec(memory_space=pl.ANY)
+    return pl.pallas_call(
+        functools.partial(project_kernel, steps),
+        in_specs=[pl.BlockSpec(memory_space=pltpu.SMEM), hbm, hbm],
+        out_specs=[vmem for _ in dtypes],
+        scratch_shapes=[
+            pltpu.VMEM(attended.shape, attended.dtype),
+            pltpu.VMEM((slots, depth, TILE), jnp.bfloat16),
+            pltpu.SemaphoreType.DMA((1,)),
+            pltpu.SemaphoreType.DMA((slots,)),
+        ],
+        out_shape=[jax.ShapeDtypeStruct((rows, out_local), dtype) for dtype in dtypes],
+        compiler_params=pltpu.CompilerParams(vmem_limit_bytes=40 * MIB),
+        cost_estimate=SMALL,
+        name="project",
+    )(me.reshape(1), attended, out_weight)
 
 
 def masked(low, owner, adapters, ranks, adapters_here):
@@ -361,7 +404,8 @@
         columns = slice(j, j + 128)
         total = own_ref[:, columns]
         for ref in part_refs:
-            total += ref[:, columns].astype(jnp.float32)
+            first = ref.shape[1] - out_ref.shape[1] + j
+            total += ref[:, first : first + 128].astype(jnp.float32)
         out_ref[:, columns] = (live * total).astype(out_ref.dtype)
 
 
@@ -407,6 +451,11 @@
         exchange(blocks[b][0][half:], "dp", a),
     ]
     return farther_blocks({**blocks, a | b: diagonal})
+
+
+def direct_blocks(own):
+    a, b = neighbours()[:2]
+    return farther_blocks({**near_blocks(own), a | b: [exchange(own, "dp", a | b)]})
 
 
 def together(*values):
@@ -438,6 +487,8 @@
     expand = expand_weight.reshape(pair, out_local)
 
     halved = shares == 4
+    early = (3, 1) if halved else (shares - 1, shares - 2)
+    late = (2, 0) if halved else tuple(range(shares - 3, -1, -1))
     attended, piece = attend(
         (
             queries,
@@ -451,50 +502,49 @@
         lengths,
         out_weight,
         me,
-        shares - 1,
+        early,
         out_local,
     )
-    passed = exchange(piece, "mp", 1 if halved else shares - 1)
+    if halved:
+        received = [exchange(piece, "mp", 1)]
+    else:
+        received = [
+            exchange(part, "mp", step) for part, step in zip(jnp.split(piece, 2, 1), early)
+        ]
     shrink, attended = together(shrink, attended)
     shrink = forwarded_blocks(shrink)
     beside = exchange(attended, "dp", 1)
-
-    def chunk(rows, step, dtype):
-        columns = lax.dynamic_slice_in_dim(out_weight, (me ^ step) * out_local, out_local, 1)
-        return jnp.dot(
-            rows[: queries.shape[0]], columns, preferred_element_type=jnp.float32
-        ).astype(dtype)
-
-    pieces = {step: chunk(attended, step, jnp.bfloat16) for step in range(shares - 2, 0, -1)}
-    pieces, passed, attended, shrink, expand = together(
-        pieces, passed, attended, shrink, expand
-    )
-    expand = near_blocks(expand)
+    *pieces, own = project(
+        attended,
+        out_weight,
+        me,
+        late,
+        out_local,
+        [jnp.float32 if halved else jnp.bfloat16] * (len(late) - 1) + [jnp.float32],
+    )
+    pieces, own, received, attended, shrink, expand = together(
+        pieces, own, received, attended, shrink, expand
+    )
+    expand = direct_blocks(expand)
     if halved:
-        received = []
-        pieces[2] = (pieces[2].astype(jnp.float32) + passed.astype(jnp.float32)).astype(
-            jnp.bfloat16
-        )
-    else:
-        received = [passed]
-    received += [exchange(piece, "mp", step) for step, piece in pieces.items()]
+        passed = received[0][:, :out_local].astype(jnp.float32)
+        pieces = [(pieces[0] + passed).astype(jnp.bfloat16)]
+    last = [exchange(part, "mp", step) for part, step in zip(pieces, late)]
 
     keys = tuple(shrink)
     low, adapters = low_rank(
         [attended, beside], list(shrink.values()), depth, here, keys, rank
     )
-    expand, low = together(expand, low)
-    expand = forwarded_blocks(expand)
-    attended, low = together(attended, low)
-    own = chunk(attended, 0, jnp.float32)
     step = 1
     while step < shares:
         arrived = exchange(low, "mp", step)
         low = (low.astype(jnp.float32) + arrived.astype(jnp.float32)).astype(jnp.bfloat16)
         step *= 2
+    low, last = together(low, last)
     blocks = [expand[key] for key in keys]
     correction, other = correct(low, adapters, blocks, 0, out_local, here, keys, rank)
-    return finish(own, [*received, correction, exchange(other, "dp", 1)], occupied)
+    parts = [*received, *last, correction, exchange(other, "dp", 1)]
+    return finish(own, parts, occupied)
 
 
 def solution(mesh):

time: 59.7 us -> 57.2 us (0.958)
  matrix products: 10.5 us -> 0 us
  Pallas kernels: 14.6 us -> 19.8 us
  waiting for transfers between devices: 12 us -> 17.1 us
  local copies, waits for them, and re-layouts: 3.37 us -> 1.11 us
  starting transfers between devices: 17.7 us -> 18.8 us
  other arithmetic: 1.12 us -> 0.08 us
    dot_general x3 -> x0, matrix products: 10.5 us -> none  [chunk(): jnp.dot(rows[:queries.shape[0]], columns, preferred_element_type=jnp.floa...]
    pallas_call x1 -> x2, Pallas kernels: 10.1 us -> 15.6 us  [the longest x1 11.5 us: attend(): pl.pallas_call(functools.partial(attend_kernel, block, steps), in_specs=[...]
    ppermute x15 -> x13, waiting for transfers between devices: 12 us -> 17.1 us  [exchange(): return lax.ppermute(value, axis, [(i, i ^ step) for i in range(count)])]
    unnamed x16 -> x8, local copies, waits for them, and re-layouts: 3.32 us -> 1.07 us
    ppermute x15 -> x13, starting transfers between devices: 17.7 us -> 18.8 us  [exchange(): return lax.ppermute(value, axis, [(i, i ^ step) for i in range(count)])]
    convert_element_type x1, other arithmetic: 1.09 us -> 0.06 us  [body(): pieces = [(pieces[0] + passed).astype(jnp.bfloat16)]]
  transfers between devices with their start and end apart: 15 -> 13, of which waited for: 7 -> 4; matrix products, arithmetic and copies ran while one was open for 20% -> 0% of each run, Pallas kernels for 23% -> 32%
where the time goes in v6:
time: 57.2 us; the launch traced here: 57 us
  Pallas kernels  19.8 us (35%)
  starting transfers between devices  18.8 us (33%)
  waiting for transfers between devices  17.1 us (30%)
  local copies, waits for them, and re-layouts  1.11 us (2%)
    ppermute x13, starting transfers between devices, exchange(): return lax.ppermute(value, axis, [(i, i ^ step) for i in range(count)])  18.8 us
    ppermute x13, waiting for transfers between devices, exchange(): return lax.ppermute(value, axis, [(i, i ^ step) for i in range(count)])  17.1 us
    pallas_call x1, Pallas kernels, attend(): pl.pallas_call(functools.partial(attend_kernel, block, steps), in_specs=[...  11.5 us
    pallas_call x1, Pallas kernels, project(): pl.pallas_call(functools.partial(project_kernel, steps), in_specs=[pl.Blo...  4.08 us
    pallas_call x1, Pallas kernels, low_rank(): pl.pallas_call(functools.partial(low_kernel, rank, places, keys), in_spec...  2.54 us
  transfers between devices with their start and end apart: 13, of which 4 were waited for; matrix products, arithmetic and copies ran while one was open for 0% of the time, Pallas kernels for 32%

profile of v6, /device:TPU:0, one launch (start us, length us, event | category | flops | bytes accessed | tf_op | source)
XLA Modules:
  0.0 57.0 jit_solution(16933717143619383631)
XLA Ops:
  0.0 2.9 %collective-permute-start = (bf16[128,2048]{1,0:T(8,128)(2,1)}, bf16[128,2048]{1,0:T(8,128)(2,1)S(1)}, u32[]{:S(2)}, u32[]{:S(2)}) collective-permute-start(bf16[128,2048]{1,0:T(8,128)(2,1)} %bitcast.9), channel_id=1, source_target_pairs={{0,8},{4,12},{8,0},{12,4},{16,24},{20,28},{24,16},{28,20},{1,9},{5... | collective-permute-start | bytes 1572872 | tf_op jit(solution)/shard_map/ppermute | solution.py:428
  2.9 1.5 %collective-permute-start.1 = (bf16[128,2048]{1,0:T(8,128)(2,1)}, bf16[128,2048]{1,0:T(8,128)(2,1)S(1)}, u32[]{:S(2)}, u32[]{:S(2)}) collective-permute-start(bf16[128,2048]{1,0:T(8,128)(2,1)} %bitcast.10), channel_id=1, source_target_pairs={{0,16},{4,20},{8,24},{12,28},{16,0},{20,4},{24,8},{28,12},{1,17},{... | collective-permute-start | bytes 1572872 | tf_op jit(solution)/shard_map/ppermute | solution.py:428
  4.5 11.5 %attend.1 = (bf16[144,2048]{1,0:T(8,128)(2,1)}, bf16[128,2048]{1,0:T(8,128)(2,1)}) custom-call(s32[128]{0:T(128)} %lengths_ref.1, s32[1]{0:T(128)} %bitcast.1.me_ref, bf16[128,16,128]{2,1,0:T(8,128)(2,1)} %q_hbm.1, bf16[128,2,128,128]{3,2,1,0:T(8,128)(2,1)} %k_hbm.1, bf16[128,2,128,128]{3,2,1,0:T(8,128)(2,1)} %v_hbm.1, bf16[128,2,128]{2,1,0:T(2,128)(2,1)} %kn_hbm.1, ...), custom_call_target="tpu_custom_call" | custom-call | flops 1 | bytes 1 | tf_op jit(solution)/shard_map/attend/pallas_call | solution.py:207
  16.0 0.0 collective-permute-done.refs_3_
  16.0 0.5 collective-permute-done.1.refs_4_
  16.5 0.0 collective-permute-start.5
  16.5 1.6 %collective-permute-start.2 = (bf16[128,2048]{1,0:T(8,128)(2,1)}, bf16[128,2048]{1,0:T(8,128)(2,1)S(1)}, u32[]{:S(2)}, u32[]{:S(2)}) collective-permute-start(bf16[128,2048]{1,0:T(8,128)(2,1)} %get-tuple-element.33), channel_id=1, source_target_pairs={{0,1},{1,0},{2,3},{3,2},{4,5},{5,4},{6,7},{7,6},{8,9},{9,8},{10,11... | collective-permute-start | bytes 1572872 | tf_op jit(solution)/shard_map/ppermute | solution.py:428
  18.1 1.6 %collective-permute-start.3 = (bf16[64,2048]{1,0:T(8,128)(2,1)S(1)}, bf16[64,2048]{1,0:T(8,128)(2,1)S(1)}, u32[]{:S(2)}, u32[]{:S(2)}) collective-permute-start(bf16[64,2048]{1,0:T(8,128)(2,1)S(1)} %slice.9), channel_id=1, source_target_pairs={{0,16},{4,20},{8,24},{12,28},{16,0},{20,4},{24,8},{28,12},{1,17},{... | collective-permute-start | bytes 786440 | tf_op jit(solution)/shard_map/ppermute | solution.py:428
  19.7 0.6 %collective-permute-start.4 = (bf16[64,2048]{1,0:T(8,128)(2,1)S(1)}, bf16[64,2048]{1,0:T(8,128)(2,1)S(1)}, u32[]{:S(2)}, u32[]{:S(2)}) collective-permute-start(bf16[64,2048]{1,0:T(8,128)(2,1)S(1)} %slice.10), channel_id=1, source_target_pairs={{0,8},{4,12},{8,0},{12,4},{16,24},{20,28},{24,16},{28,20},{1,9},{5... | collective-permute-start | bytes 786440 | tf_op jit(solution)/shard_map/ppermute | solution.py:428
  20.3 1.1 %copy-done = bf16[144,2048]{1,0:T(8,128)(2,1)S(1)} copy-done((bf16[144,2048]{1,0:T(8,128)(2,1)S(1)}, bf16[144,2048]{1,0:T(8,128)(2,1)}, u32[]{:S(2)}) %copy-start) | copy-done | bytes 589848
  21.4 4.1 %project.1 = (f32[128,1024]{1,0:T(8,128)S(1)}, f32[128,1024]{1,0:T(8,128)S(1)}) custom-call(s32[1]{0:T(128)} %bitcast.1.me_ref, bf16[144,2048]{1,0:T(8,128)(2,1)S(1)} %copy-done, bf16[2048,4096]{1,0:T(8,128)(2,1)} %w_ref.3), custom_call_target="tpu_custom_call" | custom-call | flops 1 | bytes 1 | tf_op jit(solution)/shard_map/project/pallas_call | solution.py:250
  25.5 5.6 %collective-permute-done.2.refs_0_ = bf16[128,2048]{1,0:T(8,128)(2,1)S(1)} collective-permute-done((bf16[128,2048]{1,0:T(8,128)(2,1)}, bf16[128,2048]{1,0:T(8,128)(2,1)S(1)}, u32[]{:S(2)}, u32[]{:S(2)}) %collective-permute-start.2) | collective-permute-done | bytes 524320 | tf_op jit(solution)/shard_map/ppermute | solution.py:428
  31.1 0.0 collective-permute-done.3.refs_5_
  31.1 0.0 collective-permute-done.4.refs_6_
  31.1 1.6 %collective-permute-start.10 = (bf16[128,1024]{1,0:T(8,128)(2,1)S(1)}, bf16[128,1024]{1,0:T(8,128)(2,1)S(1)}, u32[]{:S(2)}, u32[]{:S(2)}) collective-permute-start(bf16[128,1024]{1,0:T(8,128)(2,1)S(1)} %bitcast.12), channel_id=1, source_target_pairs={{0,16},{4,20},{8,24},{12,28},{16,0},{20,4},{24,8},{28,12},{1,17},{... | collective-permute-start | bytes 786440 | tf_op jit(solution)/shard_map/ppermute | solution.py:428
  32.7 0.3 collective-permute-start.11
  33.0 1.7 %collective-permute-start.9 = (bf16[128,1024]{1,0:T(8,128)(2,1)S(1)}, bf16[128,1024]{1,0:T(8,128)(2,1)S(1)}, u32[]{:S(2)}, u32[]{:S(2)}) collective-permute-start(bf16[128,1024]{1,0:T(8,128)(2,1)S(1)} %bitcast.14), channel_id=1, source_target_pairs={{0,8},{4,12},{8,0},{12,4},{16,24},{20,28},{24,16},{28,20},{1,9},{5... | collective-permute-start | bytes 786440 | tf_op jit(solution)/shard_map/ppermute | solution.py:428
  34.7 0.0 collective-permute-done.5.refs_1_
  34.7 2.5 %low_rank.1 = (bf16[64,256]{1,0:T(8,128)(2,1)S(1)}, s32[8,256]{1,0:T(8,128)S(1)}) custom-call(s32[1]{0:T(128)} %bitcast.8.here_ref, bf16[144,2048]{1,0:T(8,128)(2,1)S(1)} %copy-done, bf16[144,2048]{1,0:T(8,128)(2,1)S(1)} %collective-permute-done.5.refs_1_, bf16[128,2048]{1,0:T(8,128)(2,1)S(1)} %bitcast.11, ...), custom_call_target="tpu_custom_call" | custom-call | flops 1 | bytes 1 | tf_op jit(solution)/shard_map/low_rank/pallas_call | solution.py:332
  37.2 1.6 %collective-permute-start.6 = (bf16[64,256]{1,0:T(8,128)(2,1)S(1)}, bf16[64,256]{1,0:T(8,128)(2,1)S(1)}, u32[]{:S(2)}, u32[]{:S(2)}) collective-permute-start(bf16[64,256]{1,0:T(8,128)(2,1)S(1)} %get-tuple-element.45), channel_id=1, source_target_pairs={{0,1},{1,0},{2,3},{3,2},{4,5},{5,4},{6,7},{7,6},{8,9},{9,8},{10,11... | collective-permute-start | bytes 98312 | tf_op jit(solution)/shard_map/ppermute | solution.py:428
  38.8 0.1 add_convert_fusion
  38.9 2.7 %collective-permute-start.8 = (bf16[128,1024]{1,0:T(8,128)(2,1)S(1)}, bf16[128,1024]{1,0:T(8,128)(2,1)S(1)}, u32[]{:S(2)}, u32[]{:S(2)}) collective-permute-start(bf16[128,1024]{1,0:T(8,128)(2,1)S(1)} %add_convert_fusion), channel_id=1, source_target_pairs={{0,2},{1,3},{2,0},{3,1},{4,6},{5,7},{6,4},{7,5},{8,10},{9,11},{10,... | collective-permute-start | bytes 786440 | tf_op jit(solution)/shard_map/ppermute | solution.py:428
  41.6 0.0 collective-permute-done.6
  41.6 2.7 %collective-permute-start.7 = (bf16[64,256]{1,0:T(8,128)(2,1)S(1)}, bf16[64,256]{1,0:T(8,128)(2,1)S(1)}, u32[]{:S(2)}, u32[]{:S(2)}) collective-permute-start(bf16[64,256]{1,0:T(8,128)(2,1)S(1)} %add_convert_fusion.2), channel_id=1, source_target_pairs={{0,2},{1,3},{2,0},{3,1},{4,6},{5,7},{6,4},{7,5},{8,10},{9,11},{10,... | collective-permute-start | bytes 98312 | tf_op jit(solution)/shard_map/ppermute | solution.py:428
  44.3 9.5 %collective-permute-done.7 = bf16[64,256]{1,0:T(8,128)(2,1)S(1)} collective-permute-done((bf16[64,256]{1,0:T(8,128)(2,1)S(1)}, bf16[64,256]{1,0:T(8,128)(2,1)S(1)}, u32[]{:S(2)}, u32[]{:S(2)}) %collective-permute-start.7) | collective-permute-done | bytes 32800 | tf_op jit(solution)/shard_map/ppermute | solution.py:428
  53.7 0.0 collective-permute-done.8.refs_1_
  53.8 0.0 collective-permute-done.11.refs_3_
  53.8 0.0 collective-permute-done.9.refs_1_
  53.8 0.7 %correct.1 = (bf16[128,1024]{1,0:T(8,128)(2,1)S(1)}, bf16[128,1024]{1,0:T(8,128)(2,1)S(1)}) custom-call(s32[1]{0:T(128)} %bitcast.8.here_ref, s32[8,256]{1,0:T(8,128)S(1)} %get-tuple-element.48.adapters_ref, bf16[64,256]{1,0:T(8,128)(2,1)S(1)} %add_convert_fusion.1.low_ref, bf16[128,1024]{1,0:T(8,128)(2,1)S(1)} %bitcast.15, ...), custom_call_target="tpu_custom_call" | custom-call | flops 1 | bytes 1 | tf_op jit(solution)/shard_map/correct/pallas_call | solution.py:383
  54.5 0.1 collective-permute-start.12
  54.6 1.5 %collective-permute-done.12.refs_3_ = bf16[128,1024]{1,0:T(8,128)(2,1)S(1)} collective-permute-done((bf16[128,1024]{1,0:T(8,128)(2,1)S(1)}, bf16[128,1024]{1,0:T(8,128)(2,1)S(1)}, u32[]{:S(2)}, u32[]{:S(2)}) %collective-permute-start.12) | collective-permute-done | bytes 262176 | tf_op jit(solution)/shard_map/ppermute | solution.py:428
  56.1 0.9 %finish.1 = bf16[128,1024]{1,0:T(8,128)(2,1)} custom-call(s32[1,128]{1,0:T(1,128)S(1)} %bitcast.16, f32[128,1024]{1,0:T(8,128)S(1)} %get-tuple-element.37.own_ref, bf16[128,2048]{1,0:T(8,128)(2,1)S(1)} %collective-permute-done.2.refs_0_, bf16[128,1024]{1,0:T(8,128)(2,1)S(1)} %collective-permute-done.8.refs_1_, ...), custom_call_target="tpu_custom_call" | custom-call | flops 1 | bytes 1 | tf_op jit(solution)/shard_map/finish/pallas_call | solution.py:415
  (12 shorter events, 0.1 us)
Async XLA Ops:
  0.0 16.0 %collective-permute-start = (bf16[128,2048]{1,0:T(8,128)(2,1)}, bf16[128,2048]{1,0:T(8,128)(2,1)S(1)}, u32[]{:S(2)}, u32[]{:S(2)}) collective-permute-start(bf16[128,2048]{1,0:T(8,128)(2,1)} %bitcast.9), channel_id=1, source_target_pairs={{0,8},{4,12},{8,0},{12,4},{16,24},{20,28},{24,16},{28,20},{1,9},{5... | collective-permute-start | bytes 1572872 | tf_op jit(solution)/shard_map/ppermute | solution.py:428
  2.9 13.6 %collective-permute-start.1 = (bf16[128,2048]{1,0:T(8,128)(2,1)}, bf16[128,2048]{1,0:T(8,128)(2,1)S(1)}, u32[]{:S(2)}, u32[]{:S(2)}) collective-permute-start(bf16[128,2048]{1,0:T(8,128)(2,1)} %bitcast.10), channel_id=1, source_target_pairs={{0,16},{4,20},{8,24},{12,28},{16,0},{20,4},{24,8},{28,12},{1,17},{... | collective-permute-start | bytes 1572872 | tf_op jit(solution)/shard_map/ppermute | solution.py:428
  16.5 18.1 %collective-permute-start.5 = (bf16[144,2048]{1,0:T(8,128)(2,1)}, bf16[144,2048]{1,0:T(8,128)(2,1)S(1)}, u32[]{:S(2)}, u32[]{:S(2)}) collective-permute-start(bf16[144,2048]{1,0:T(8,128)(2,1)} %get-tuple-element.39.a_hbm.refs_0_), channel_id=1, source_target_pairs={{0,4},{4,0},{8,12},{12,8},{16,20},{20,16},{24,28},{28,24},{1,5},{5... | collective-permute-start | bytes 1769480 | tf_op jit(solution)/shard_map/ppermute | solution.py:428
  16.5 14.5 %collective-permute-start.2 = (bf16[128,2048]{1,0:T(8,128)(2,1)}, bf16[128,2048]{1,0:T(8,128)(2,1)S(1)}, u32[]{:S(2)}, u32[]{:S(2)}) collective-permute-start(bf16[128,2048]{1,0:T(8,128)(2,1)} %get-tuple-element.33), channel_id=1, source_target_pairs={{0,1},{1,0},{2,3},{3,2},{4,5},{5,4},{6,7},{7,6},{8,9},{9,8},{10,11... | collective-permute-start | bytes 1572872 | tf_op jit(solution)/shard_map/ppermute | solution.py:428
  18.1 13.0 %collective-permute-start.3 = (bf16[64,2048]{1,0:T(8,128)(2,1)S(1)}, bf16[64,2048]{1,0:T(8,128)(2,1)S(1)}, u32[]{:S(2)}, u32[]{:S(2)}) collective-permute-start(bf16[64,2048]{1,0:T(8,128)(2,1)S(1)} %slice.9), channel_id=1, source_target_pairs={{0,16},{4,20},{8,24},{12,28},{16,0},{20,4},{24,8},{28,12},{1,17},{... | collective-permute-start | bytes 786440 | tf_op jit(solution)/shard_map/ppermute | solution.py:428
  19.7 11.3 %collective-permute-start.4 = (bf16[64,2048]{1,0:T(8,128)(2,1)S(1)}, bf16[64,2048]{1,0:T(8,128)(2,1)S(1)}, u32[]{:S(2)}, u32[]{:S(2)}) collective-permute-start(bf16[64,2048]{1,0:T(8,128)(2,1)S(1)} %slice.10), channel_id=1, source_target_pairs={{0,8},{4,12},{8,0},{12,4},{16,24},{20,28},{24,16},{28,20},{1,9},{5... | collective-permute-start | bytes 786440 | tf_op jit(solution)/shard_map/ppermute | solution.py:428
  20.3 1.1 %copy-start = (bf16[144,2048]{1,0:T(8,128)(2,1)S(1)}, bf16[144,2048]{1,0:T(8,128)(2,1)}, u32[]{:S(2)}) copy-start(bf16[144,2048]{1,0:T(8,128)(2,1)} %get-tuple-element.39.a_hbm.refs_0_) | copy-start | bytes 1769476
  21.4 9.7 %copy-start.2 = (bf16[2,64,1024]{2,1,0:T(8,128)(2,1)S(1)}, bf16[2,64,1024]{2,1,0:T(8,128)(2,1)}, u32[]{:S(2)}) copy-start(bf16[2,64,1024]{2,1,0:T(8,128)(2,1)} %param.23) | copy-start | bytes 786436
  21.4 13.2 %copy-start.1 = (bf16[2,2048,64]{1,2,0:T(8,128)(2,1)S(1)}, bf16[2,2048,64]{1,2,0:T(8,128)(2,1)}, u32[]{:S(2)}) copy-start(bf16[2,2048,64]{1,2,0:T(8,128)(2,1)} %param.22) | copy-start | bytes 1572868
  21.4 34.7 %copy-start.3 = (s32[128]{0:T(128)S(1)}, s32[128]{0:T(128)}, u32[]{:S(2)}) copy-start(s32[128]{0:T(128)} %param.18) | copy-start | bytes 1540
  31.1 22.7 %collective-permute-start.10 = (bf16[128,1024]{1,0:T(8,128)(2,1)S(1)}, bf16[128,1024]{1,0:T(8,128)(2,1)S(1)}, u32[]{:S(2)}, u32[]{:S(2)}) collective-permute-start(bf16[128,1024]{1,0:T(8,128)(2,1)S(1)} %bitcast.12), channel_id=1, source_target_pairs={{0,16},{4,20},{8,24},{12,28},{16,0},{20,4},{24,8},{28,12},{1,17},{... | collective-permute-start | bytes 786440 | tf_op jit(solution)/shard_map/ppermute | solution.py:428
  32.7 21.1 %collective-permute-start.11 = (bf16[128,1024]{1,0:T(8,128)(2,1)S(1)}, bf16[128,1024]{1,0:T(8,128)(2,1)S(1)}, u32[]{:S(2)}, u32[]{:S(2)}) collective-permute-start(bf16[128,1024]{1,0:T(8,128)(2,1)S(1)} %bitcast.13), channel_id=1, source_target_pairs={{0,24},{4,28},{8,16},{12,20},{16,8},{20,12},{24,0},{28,4},{1,25},{... | collective-permute-start | bytes 786440 | tf_op jit(solution)/shard_map/ppermute | solution.py:428
  33.0 20.8 %collective-permute-start.9 = (bf16[128,1024]{1,0:T(8,128)(2,1)S(1)}, bf16[128,1024]{1,0:T(8,128)(2,1)S(1)}, u32[]{:S(2)}, u32[]{:S(2)}) collective-permute-start(bf16[128,1024]{1,0:T(8,128)(2,1)S(1)} %bitcast.14), channel_id=1, source_target_pairs={{0,8},{4,12},{8,0},{12,4},{16,24},{20,28},{24,16},{28,20},{1,9},{5... | collective-permute-start | bytes 786440 | tf_op jit(solution)/shard_map/ppermute | solution.py:428
  37.2 4.4 %collective-permute-start.6 = (bf16[64,256]{1,0:T(8,128)(2,1)S(1)}, bf16[64,256]{1,0:T(8,128)(2,1)S(1)}, u32[]{:S(2)}, u32[]{:S(2)}) collective-permute-start(bf16[64,256]{1,0:T(8,128)(2,1)S(1)} %get-tuple-element.45), channel_id=1, source_target_pairs={{0,1},{1,0},{2,3},{3,2},{4,5},{5,4},{6,7},{7,6},{8,9},{9,8},{10,11... | collective-permute-start | bytes 98312 | tf_op jit(solution)/shard_map/ppermute | solution.py:428
  38.9 14.8 %collective-permute-start.8 = (bf16[128,1024]{1,0:T(8,128)(2,1)S(1)}, bf16[128,1024]{1,0:T(8,128)(2,1)S(1)}, u32[]{:S(2)}, u32[]{:S(2)}) collective-permute-start(bf16[128,1024]{1,0:T(8,128)(2,1)S(1)} %add_convert_fusion), channel_id=1, source_target_pairs={{0,2},{1,3},{2,0},{3,1},{4,6},{5,7},{6,4},{7,5},{8,10},{9,11},{10,... | collective-permute-start | bytes 786440 | tf_op jit(solution)/shard_map/ppermute | solution.py:428
  41.6 12.1 %collective-permute-start.7 = (bf16[64,256]{1,0:T(8,128)(2,1)S(1)}, bf16[64,256]{1,0:T(8,128)(2,1)S(1)}, u32[]{:S(2)}, u32[]{:S(2)}) collective-permute-start(bf16[64,256]{1,0:T(8,128)(2,1)S(1)} %add_convert_fusion.2), channel_id=1, source_target_pairs={{0,2},{1,3},{2,0},{3,1},{4,6},{5,7},{6,4},{7,5},{8,10},{9,11},{10,... | collective-permute-start | bytes 98312 | tf_op jit(solution)/shard_map/ppermute | solution.py:428
  54.5 1.6 %collective-permute-start.12 = (bf16[128,1024]{1,0:T(8,128)(2,1)S(1)}, bf16[128,1024]{1,0:T(8,128)(2,1)S(1)}, u32[]{:S(2)}, u32[]{:S(2)}) collective-permute-start(bf16[128,1024]{1,0:T(8,128)(2,1)S(1)} %get-tuple-element.52), channel_id=1, source_target_pairs={{0,4},{4,0},{8,12},{12,8},{16,20},{20,16},{24,28},{28,24},{1,5},{5... | collective-permute-start | bytes 786440 | tf_op jit(solution)/shard_map/ppermute | solution.py:428

commit v7 on v6

--- a/solution.py
+++ b/solution.py
@@ -67,13 +67,11 @@
     )
 
 
-def project_tiles(
-    a_ref, w_ref, buffer_ref, sem_ref, out_ref, tiles, first_slot, column, out_column
-):
+def project_tiles(a_ref, w_ref, buffer_ref, sem_ref, out_ref, tiles, first_slot, column):
     def tile(j, carry):
         slot = first_slot + j
         fetch(w_ref, buffer_ref, sem_ref, slot, column + j * TILE).wait()
-        out_ref[:, pl.ds(pl.multiple_of(out_column + j * TILE, TILE), TILE)] = jnp.dot(
+        out_ref[:, pl.ds(pl.multiple_of(j * TILE, TILE), TILE)] = jnp.dot(
             a_ref[: out_ref.shape[0]], buffer_ref[slot], preferred_element_type=jnp.float32
         ).astype(out_ref.dtype)
         return carry
@@ -116,7 +114,8 @@
     adapter_hbm,
     w_ref,
     out_ref,
-    piece_ref,
+    first_ref,
+    second_ref,
     q_ref,
     k_ref,
     v_ref,
@@ -132,7 +131,7 @@
 ):
     rows, heads, width = q_ref.shape
     blocks = rows // block
-    out_local = piece_ref.shape[1] // len(steps)
+    out_local = first_ref.shape[1]
     tiles = out_local // TILE
 
     def block_copies(i):
@@ -188,10 +187,8 @@
         return carry
 
     lax.fori_loop(0, blocks, one_block, 0)
-    for i, column in enumerate(columns):
-        project_tiles(
-            out_ref, w_ref, buffer_ref, sem_ref, piece_ref, tiles, i * tiles, column, i * out_local
-        )
+    for i, (column, piece_ref) in enumerate(zip(columns, (first_ref, second_ref))):
+        project_tiles(out_ref, w_ref, buffer_ref, sem_ref, piece_ref, tiles, i * tiles, column)
 
 
 def attend(arrays, lengths, out_weight, me, steps, out_local):
@@ -207,7 +204,7 @@
     return pl.pallas_call(
         functools.partial(attend_kernel, block, steps),
         in_specs=[smem, smem] + [hbm] * (len(arrays) + 1),
-        out_specs=[vmem, vmem],
+        out_specs=[vmem, vmem, vmem],
         scratch_shapes=[pltpu.VMEM(a.shape, a.dtype) for a in arrays]
         + [
             pltpu.VMEM((block * heads, width), jnp.float32),
@@ -218,8 +215,8 @@
         ],
         out_shape=[
             jax.ShapeDtypeStruct((rows + ID_ROWS, depth), jnp.bfloat16),
-            jax.ShapeDtypeStruct((rows, len(steps) * out_local), jnp.bfloat16),
-        ],
+        ]
+        + [jax.ShapeDtypeStruct((rows, out_local), jnp.bfloat16) for _ in steps],
         compiler_params=pltpu.CompilerParams(vmem_limit_bytes=57 * MIB),
         cost_estimate=SMALL,
         name="attend",
@@ -239,7 +236,7 @@
     copy.wait()
     for i, (step, out_ref) in enumerate(zip(steps, out_refs)):
         column = (me_ref[0] ^ step) * out_local
-        project_tiles(a_ref, w_ref, buffer_ref, sem_ref, out_ref, tiles, i * tiles, column, 0)
+        project_tiles(a_ref, w_ref, buffer_ref, sem_ref, out_ref, tiles, i * tiles, column)
 
 
 def project(attended, out_weight, me, steps, out_local, dtypes):
@@ -404,8 +401,7 @@
         columns = slice(j, j + 128)
         total = own_ref[:, columns]
         for ref in part_refs:
-            first = ref.shape[1] - out_ref.shape[1] + j
-            total += ref[:, first : first + 128].astype(jnp.float32)
+            total += ref[:, columns].astype(jnp.float32)
         out_ref[:, columns] = (live * total).astype(out_ref.dtype)
 
 
@@ -489,7 +485,7 @@
     halved = shares == 4
     early = (3, 1) if halved else (shares - 1, shares - 2)
     late = (2, 0) if halved else tuple(range(shares - 3, -1, -1))
-    attended, piece = attend(
+    attended, *pieces = attend(
         (
             queries,
             key_cache,
@@ -505,12 +501,9 @@
         early,
         out_local,
     )
-    if halved:
-        received = [exchange(piece, "mp", 1)]
-    else:
-        received = [
-            exchange(part, "mp", step) for part, step in zip(jnp.split(piece, 2, 1), early)
-        ]
+    received = [
+        exchange(piece, "mp", 1 if halved else step) for piece, step in zip(pieces, early)
+    ]
     shrink, attended = together(shrink, attended)
     shrink = forwarded_blocks(shrink)
     beside = exchange(attended, "dp", 1)
@@ -522,12 +515,12 @@
         out_local,
         [jnp.float32 if halved else jnp.bfloat16] * (len(late) - 1) + [jnp.float32],
     )
-    pieces, own, received, attended, shrink, expand = together(
-        pieces, own, received, attended, shrink, expand
+    pieces, received[0], attended, shrink, expand = together(
+        pieces, received[0], attended, shrink, expand
     )
     expand = direct_blocks(expand)
     if halved:
-        passed = received[0][:, :out_local].astype(jnp.float32)
+        passed = received.pop(0).astype(jnp.float32)
         pieces = [(pieces[0] + passed).astype(jnp.bfloat16)]
     last = [exchange(part, "mp", step) for part, step in zip(pieces, late)]
 
@@ -535,11 +528,12 @@
     low, adapters = low_rank(
         [attended, beside], list(shrink.values()), depth, here, keys, rank
     )
-    step = 1
-    while step < shares:
+    low, received = together(low, received)
+    step = shares // 2
+    while step:
         arrived = exchange(low, "mp", step)
         low = (low.astype(jnp.float32) + arrived.astype(jnp.float32)).astype(jnp.bfloat16)
-        step *= 2
+        step //= 2
     low, last = together(low, last)
     blocks = [expand[key] for key in keys]
     correction, other = correct(low, adapters, blocks, 0, out_local, here, keys, rank)

time: 57.2 us -> 53.9 us (0.942)
  starting transfers between devices: 18.8 us -> 15.4 us
    ppermute x13 -> x14, starting transfers between devices: 18.8 us -> 15.4 us  [exchange(): return lax.ppermute(value, axis, [(i, i ^ step) for i in range(count)])]
    ppermute x13 -> x14, waiting for transfers between devices: 17.1 us -> 17.4 us  [exchange(): return lax.ppermute(value, axis, [(i, i ^ step) for i in range(count)])]
  transfers between devices with their start and end apart: 13 -> 14, of which waited for: 4 -> 6; matrix products, arithmetic and copies ran while one was open for 0% -> 0% of each run, Pallas kernels for 32% -> 34%
where the time goes in v7:
time: 53.9 us; the launch traced here: 53.7 us
  Pallas kernels  19.6 us (36%)
  waiting for transfers between devices  17.4 us (32%)
  starting transfers between devices  15.4 us (29%)
  local copies, waits for them, and re-layouts  1.11 us (2%)
    ppermute x14, waiting for transfers between devices, exchange(): return lax.ppermute(value, axis, [(i, i ^ step) for i in range(count)])  17.4 us
    ppermute x14, starting transfers between devices, exchange(): return lax.ppermute(value, axis, [(i, i ^ step) for i in range(count)])  15.4 us
    pallas_call x1, Pallas kernels, attend(): pl.pallas_call(functools.partial(attend_kernel, block, steps), in_specs=[...  11.4 us
    pallas_call x1, Pallas kernels, project(): pl.pallas_call(functools.partial(project_kernel, steps), in_specs=[pl.Blo...  4.08 us
    pallas_call x1, Pallas kernels, low_rank(): pl.pallas_call(functools.partial(low_kernel, rank, places, keys), in_spec...  2.54 us
  transfers between devices with their start and end apart: 14, of which 6 were waited for; matrix products, arithmetic and copies ran while one was open for 0% of the time, Pallas kernels for 34%

profile of v7, /device:TPU:0, one launch (start us, length us, event | category | flops | bytes accessed | tf_op | source)
XLA Modules:
  0.0 53.7 jit_solution(5156169085170067097)
XLA Ops:
  0.0 2.9 %collective-permute-start = (bf16[128,2048]{1,0:T(8,128)(2,1)}, bf16[128,2048]{1,0:T(8,128)(2,1)S(1)}, u32[]{:S(2)}, u32[]{:S(2)}) collective-permute-start(bf16[128,2048]{1,0:T(8,128)(2,1)} %bitcast.9), channel_id=1, source_target_pairs={{0,8},{4,12},{8,0},{12,4},{16,24},{20,28},{24,16},{28,20},{1,9},{5... | collective-permute-start | bytes 1572872 | tf_op jit(solution)/shard_map/ppermute | solution.py:424
  2.9 1.5 %collective-permute-start.1 = (bf16[128,2048]{1,0:T(8,128)(2,1)}, bf16[128,2048]{1,0:T(8,128)(2,1)S(1)}, u32[]{:S(2)}, u32[]{:S(2)}) collective-permute-start(bf16[128,2048]{1,0:T(8,128)(2,1)} %bitcast.10), channel_id=1, source_target_pairs={{0,16},{4,20},{8,24},{12,28},{16,0},{20,4},{24,8},{28,12},{1,17},{... | collective-permute-start | bytes 1572872 | tf_op jit(solution)/shard_map/ppermute | solution.py:424
  4.5 11.4 %attend.1 = (bf16[144,2048]{1,0:T(8,128)(2,1)}, bf16[128,1024]{1,0:T(8,128)(2,1)}, bf16[128,1024]{1,0:T(8,128)(2,1)}) custom-call(s32[128]{0:T(128)} %lengths_ref.1, s32[1]{0:T(128)} %bitcast.1.me_ref, bf16[128,16,128]{2,1,0:T(8,128)(2,1)} %q_hbm.1, bf16[128,2,128,128]{3,2,1,0:T(8,128)(2,1)} %k_hbm.1, bf16[128,2,128,128]{3,2,1,0:T(8,128)(2,1)} %v_hbm.1, ...), custom_call_target="tpu_custom_call" | custom-call | flops 1 | bytes 1 | tf_op jit(solution)/shard_map/attend/pallas_call | solution.py:204
  15.9 0.0 collective-permute-done.refs_3_
  15.9 0.6 %collective-permute-done.1.refs_4_ = bf16[128,2048]{1,0:T(8,128)(2,1)S(1)} collective-permute-done((bf16[128,2048]{1,0:T(8,128)(2,1)}, bf16[128,2048]{1,0:T(8,128)(2,1)S(1)}, u32[]{:S(2)}, u32[]{:S(2)}) %collective-permute-start.1) | collective-permute-done | bytes 524320 | tf_op jit(solution)/shard_map/ppermute | solution.py:424
  16.5 1.6 %collective-permute-start.2 = (bf16[128,1024]{1,0:T(8,128)(2,1)}, bf16[128,1024]{1,0:T(8,128)(2,1)S(1)}, u32[]{:S(2)}, u32[]{:S(2)}) collective-permute-start(bf16[128,1024]{1,0:T(8,128)(2,1)} %get-tuple-element.35), channel_id=1, source_target_pairs={{0,1},{1,0},{2,3},{3,2},{4,5},{5,4},{6,7},{7,6},{8,9},{9,8},{10,11... | collective-permute-start | bytes 786440 | tf_op jit(solution)/shard_map/ppermute | solution.py:424
  18.1 1.6 %collective-permute-start.3 = (bf16[64,2048]{1,0:T(8,128)(2,1)S(1)}, bf16[64,2048]{1,0:T(8,128)(2,1)S(1)}, u32[]{:S(2)}, u32[]{:S(2)}) collective-permute-start(bf16[64,2048]{1,0:T(8,128)(2,1)S(1)} %slice.6), channel_id=1, source_target_pairs={{0,16},{4,20},{8,24},{12,28},{16,0},{20,4},{24,8},{28,12},{1,17},{... | collective-permute-start | bytes 786440 | tf_op jit(solution)/shard_map/ppermute | solution.py:424
  19.7 0.6 %collective-permute-start.4 = (bf16[64,2048]{1,0:T(8,128)(2,1)S(1)}, bf16[64,2048]{1,0:T(8,128)(2,1)S(1)}, u32[]{:S(2)}, u32[]{:S(2)}) collective-permute-start(bf16[64,2048]{1,0:T(8,128)(2,1)S(1)} %slice.7), channel_id=1, source_target_pairs={{0,8},{4,12},{8,0},{12,4},{16,24},{20,28},{24,16},{28,20},{1,9},{5... | collective-permute-start | bytes 786440 | tf_op jit(solution)/shard_map/ppermute | solution.py:424
  20.3 0.4 collective-permute-start.6
  20.8 1.1 %copy-done = bf16[144,2048]{1,0:T(8,128)(2,1)S(1)} copy-done((bf16[144,2048]{1,0:T(8,128)(2,1)S(1)}, bf16[144,2048]{1,0:T(8,128)(2,1)}, u32[]{:S(2)}) %copy-start) | copy-done | bytes 589848
  21.9 4.1 %project.1 = (f32[128,1024]{1,0:T(8,128)S(1)}, f32[128,1024]{1,0:T(8,128)S(1)}) custom-call(s32[1]{0:T(128)} %bitcast.1.me_ref, bf16[144,2048]{1,0:T(8,128)(2,1)S(1)} %copy-done, bf16[2048,4096]{1,0:T(8,128)(2,1)} %w_ref.3), custom_call_target="tpu_custom_call" | custom-call | flops 1 | bytes 1 | tf_op jit(solution)/shard_map/project/pallas_call | solution.py:247
  26.0 0.0 collective-permute-done.2
  26.0 0.7 %collective-permute-done.3.refs_5_ = bf16[64,2048]{1,0:T(8,128)(2,1)S(1)} collective-permute-done((bf16[64,2048]{1,0:T(8,128)(2,1)S(1)}, bf16[64,2048]{1,0:T(8,128)(2,1)S(1)}, u32[]{:S(2)}, u32[]{:S(2)}) %collective-permute-start.3) | collective-permute-done | bytes 262176 | tf_op jit(solution)/shard_map/ppermute | solution.py:424
  26.6 1.3 %collective-permute-done.4.refs_6_ = bf16[64,2048]{1,0:T(8,128)(2,1)S(1)} collective-permute-done((bf16[64,2048]{1,0:T(8,128)(2,1)S(1)}, bf16[64,2048]{1,0:T(8,128)(2,1)S(1)}, u32[]{:S(2)}, u32[]{:S(2)}) %collective-permute-start.4) | collective-permute-done | bytes 262176 | tf_op jit(solution)/shard_map/ppermute | solution.py:424
  28.0 0.5 collective-permute-start.10
  28.5 0.5 collective-permute-start.11
  29.0 2.4 %collective-permute-start.12 = (bf16[128,1024]{1,0:T(8,128)(2,1)S(1)}, bf16[128,1024]{1,0:T(8,128)(2,1)S(1)}, u32[]{:S(2)}, u32[]{:S(2)}) collective-permute-start(bf16[128,1024]{1,0:T(8,128)(2,1)S(1)} %bitcast.14), channel_id=1, source_target_pairs={{0,24},{4,28},{8,16},{12,20},{16,8},{20,12},{24,0},{28,4},{1,25},{... | collective-permute-start | bytes 786440 | tf_op jit(solution)/shard_map/ppermute | solution.py:424
  31.5 0.0 collective-permute-done.5.refs_1_
  31.5 2.5 %low_rank.1 = (bf16[64,256]{1,0:T(8,128)(2,1)S(1)}, s32[8,256]{1,0:T(8,128)S(1)}) custom-call(s32[1]{0:T(128)} %bitcast.7.here_ref, bf16[144,2048]{1,0:T(8,128)(2,1)S(1)} %copy-done, bf16[144,2048]{1,0:T(8,128)(2,1)S(1)} %collective-permute-done.5.refs_1_, bf16[128,2048]{1,0:T(8,128)(2,1)S(1)} %bitcast.11, ...), custom_call_target="tpu_custom_call" | custom-call | flops 1 | bytes 1 | tf_op jit(solution)/shard_map/low_rank/pallas_call | solution.py:329
  34.0 0.0 collective-permute-done.6.refs_0_
  34.0 2.7 %collective-permute-start.7 = (bf16[64,256]{1,0:T(8,128)(2,1)S(1)}, bf16[64,256]{1,0:T(8,128)(2,1)S(1)}, u32[]{:S(2)}, u32[]{:S(2)}) collective-permute-start(bf16[64,256]{1,0:T(8,128)(2,1)S(1)} %get-tuple-element.48), channel_id=1, source_target_pairs={{0,2},{1,3},{2,0},{3,1},{4,6},{5,7},{6,4},{7,5},{8,10},{9,11},{10,... | collective-permute-start | bytes 98312 | tf_op jit(solution)/shard_map/ppermute | solution.py:424
  36.7 0.1 add_convert_fusion
  36.7 0.4 collective-permute-start.9
  37.1 7.7 %collective-permute-done.7 = bf16[64,256]{1,0:T(8,128)(2,1)S(1)} collective-permute-done((bf16[64,256]{1,0:T(8,128)(2,1)S(1)}, bf16[64,256]{1,0:T(8,128)(2,1)S(1)}, u32[]{:S(2)}, u32[]{:S(2)}) %collective-permute-start.7) | collective-permute-done | bytes 32800 | tf_op jit(solution)/shard_map/ppermute | solution.py:424
  44.9 0.1 collective-permute-start.8
  44.9 5.5 %collective-permute-done.8 = bf16[64,256]{1,0:T(8,128)(2,1)S(1)} collective-permute-done((bf16[64,256]{1,0:T(8,128)(2,1)S(1)}, bf16[64,256]{1,0:T(8,128)(2,1)S(1)}, u32[]{:S(2)}, u32[]{:S(2)}) %collective-permute-start.8) | collective-permute-done | bytes 32800 | tf_op jit(solution)/shard_map/ppermute | solution.py:424
  50.5 0.0 collective-permute-done.10.refs_1_
  50.5 0.0 collective-permute-done.11.refs_2_
  50.5 0.7 %correct.1 = (bf16[128,1024]{1,0:T(8,128)(2,1)S(1)}, bf16[128,1024]{1,0:T(8,128)(2,1)S(1)}) custom-call(s32[1]{0:T(128)} %bitcast.7.here_ref, s32[8,256]{1,0:T(8,128)S(1)} %get-tuple-element.52.adapters_ref, bf16[64,256]{1,0:T(8,128)(2,1)S(1)} %add_convert_fusion.1.low_ref, bf16[128,1024]{1,0:T(8,128)(2,1)S(1)} %bitcast.15, ...), custom_call_target="tpu_custom_call" | custom-call | flops 1 | bytes 1 | tf_op jit(solution)/shard_map/correct/pallas_call | solution.py:380
  51.2 0.1 collective-permute-start.13
  51.3 1.5 %collective-permute-done.13.refs_3_ = bf16[128,1024]{1,0:T(8,128)(2,1)S(1)} collective-permute-done((bf16[128,1024]{1,0:T(8,128)(2,1)S(1)}, bf16[128,1024]{1,0:T(8,128)(2,1)S(1)}, u32[]{:S(2)}, u32[]{:S(2)}) %collective-permute-start.13) | collective-permute-done | bytes 262176 | tf_op jit(solution)/shard_map/ppermute | solution.py:424
  52.8 0.9 %finish.1 = bf16[128,1024]{1,0:T(8,128)(2,1)} custom-call(s32[1,128]{1,0:T(1,128)S(1)} %bitcast.16, f32[128,1024]{1,0:T(8,128)S(1)} %get-tuple-element.33.own_ref, bf16[128,1024]{1,0:T(8,128)(2,1)S(1)} %collective-permute-done.6.refs_0_, bf16[128,1024]{1,0:T(8,128)(2,1)S(1)} %collective-permute-done.9.refs_1_, ...), custom_call_target="tpu_custom_call" | custom-call | flops 1 | bytes 1 | tf_op jit(solution)/shard_map/finish/pallas_call | solution.py:411
  (14 shorter events, 0.1 us)
Async XLA Ops:
  0.0 15.9 %collective-permute-start = (bf16[128,2048]{1,0:T(8,128)(2,1)}, bf16[128,2048]{1,0:T(8,128)(2,1)S(1)}, u32[]{:S(2)}, u32[]{:S(2)}) collective-permute-start(bf16[128,2048]{1,0:T(8,128)(2,1)} %bitcast.9), channel_id=1, source_target_pairs={{0,8},{4,12},{8,0},{12,4},{16,24},{20,28},{24,16},{28,20},{1,9},{5... | collective-permute-start | bytes 1572872 | tf_op jit(solution)/shard_map/ppermute | solution.py:424
  2.9 13.6 %collective-permute-start.1 = (bf16[128,2048]{1,0:T(8,128)(2,1)}, bf16[128,2048]{1,0:T(8,128)(2,1)S(1)}, u32[]{:S(2)}, u32[]{:S(2)}) collective-permute-start(bf16[128,2048]{1,0:T(8,128)(2,1)} %bitcast.10), channel_id=1, source_target_pairs={{0,16},{4,20},{8,24},{12,28},{16,0},{20,4},{24,8},{28,12},{1,17},{... | collective-permute-start | bytes 1572872 | tf_op jit(solution)/shard_map/ppermute | solution.py:424
  16.5 14.9 %collective-permute-start.5 = (bf16[144,2048]{1,0:T(8,128)(2,1)}, bf16[144,2048]{1,0:T(8,128)(2,1)S(1)}, u32[]{:S(2)}, u32[]{:S(2)}) collective-permute-start(bf16[144,2048]{1,0:T(8,128)(2,1)} %get-tuple-element.39.a_hbm.refs_0_), channel_id=1, source_target_pairs={{0,4},{4,0},{8,12},{12,8},{16,20},{20,16},{24,28},{28,24},{1,5},{5... | collective-permute-start | bytes 1769480 | tf_op jit(solution)/shard_map/ppermute | solution.py:424
  16.5 9.4 %collective-permute-start.2 = (bf16[128,1024]{1,0:T(8,128)(2,1)}, bf16[128,1024]{1,0:T(8,128)(2,1)S(1)}, u32[]{:S(2)}, u32[]{:S(2)}) collective-permute-start(bf16[128,1024]{1,0:T(8,128)(2,1)} %get-tuple-element.35), channel_id=1, source_target_pairs={{0,1},{1,0},{2,3},{3,2},{4,5},{5,4},{6,7},{7,6},{8,9},{9,8},{10,11... | collective-permute-start | bytes 786440 | tf_op jit(solution)/shard_map/ppermute | solution.py:424
  18.1 8.5 %collective-permute-start.3 = (bf16[64,2048]{1,0:T(8,128)(2,1)S(1)}, bf16[64,2048]{1,0:T(8,128)(2,1)S(1)}, u32[]{:S(2)}, u32[]{:S(2)}) collective-permute-start(bf16[64,2048]{1,0:T(8,128)(2,1)S(1)} %slice.6), channel_id=1, source_target_pairs={{0,16},{4,20},{8,24},{12,28},{16,0},{20,4},{24,8},{28,12},{1,17},{... | collective-permute-start | bytes 786440 | tf_op jit(solution)/shard_map/ppermute | solution.py:424
  19.7 8.2 %collective-permute-start.4 = (bf16[64,2048]{1,0:T(8,128)(2,1)S(1)}, bf16[64,2048]{1,0:T(8,128)(2,1)S(1)}, u32[]{:S(2)}, u32[]{:S(2)}) collective-permute-start(bf16[64,2048]{1,0:T(8,128)(2,1)S(1)} %slice.7), channel_id=1, source_target_pairs={{0,8},{4,12},{8,0},{12,4},{16,24},{20,28},{24,16},{28,20},{1,9},{5... | collective-permute-start | bytes 786440 | tf_op jit(solution)/shard_map/ppermute | solution.py:424
  20.3 13.7 %collective-permute-start.6 = (bf16[128,1024]{1,0:T(8,128)(2,1)}, bf16[128,1024]{1,0:T(8,128)(2,1)S(1)}, u32[]{:S(2)}, u32[]{:S(2)}) collective-permute-start(bf16[128,1024]{1,0:T(8,128)(2,1)} %get-tuple-element.46), channel_id=1, source_target_pairs={{0,1},{1,0},{2,3},{3,2},{4,5},{5,4},{6,7},{7,6},{8,9},{9,8},{10,11... | collective-permute-start | bytes 786440 | tf_op jit(solution)/shard_map/ppermute | solution.py:424
  20.8 1.1 %copy-start = (bf16[144,2048]{1,0:T(8,128)(2,1)S(1)}, bf16[144,2048]{1,0:T(8,128)(2,1)}, u32[]{:S(2)}) copy-start(bf16[144,2048]{1,0:T(8,128)(2,1)} %get-tuple-element.39.a_hbm.refs_0_) | copy-start | bytes 1769476
  21.9 6.1 %copy-start.2 = (bf16[2,64,1024]{2,1,0:T(8,128)(2,1)S(1)}, bf16[2,64,1024]{2,1,0:T(8,128)(2,1)}, u32[]{:S(2)}) copy-start(bf16[2,64,1024]{2,1,0:T(8,128)(2,1)} %param.23) | copy-start | bytes 786436
  21.9 9.6 %copy-start.1 = (bf16[2,2048,64]{1,2,0:T(8,128)(2,1)S(1)}, bf16[2,2048,64]{1,2,0:T(8,128)(2,1)}, u32[]{:S(2)}) copy-start(bf16[2,2048,64]{1,2,0:T(8,128)(2,1)} %param.22) | copy-start | bytes 1572868
  21.9 31.0 %copy-start.3 = (s32[128]{0:T(128)S(1)}, s32[128]{0:T(128)}, u32[]{:S(2)}) copy-start(s32[128]{0:T(128)} %param.18) | copy-start | bytes 1540
  28.0 22.5 %collective-permute-start.10 = (bf16[128,1024]{1,0:T(8,128)(2,1)S(1)}, bf16[128,1024]{1,0:T(8,128)(2,1)S(1)}, u32[]{:S(2)}, u32[]{:S(2)}) collective-permute-start(bf16[128,1024]{1,0:T(8,128)(2,1)S(1)} %bitcast.12), channel_id=1, source_target_pairs={{0,8},{4,12},{8,0},{12,4},{16,24},{20,28},{24,16},{28,20},{1,9},{5... | collective-permute-start | bytes 786440 | tf_op jit(solution)/shard_map/ppermute | solution.py:424
  28.5 22.0 %collective-permute-start.11 = (bf16[128,1024]{1,0:T(8,128)(2,1)S(1)}, bf16[128,1024]{1,0:T(8,128)(2,1)S(1)}, u32[]{:S(2)}, u32[]{:S(2)}) collective-permute-start(bf16[128,1024]{1,0:T(8,128)(2,1)S(1)} %bitcast.13), channel_id=1, source_target_pairs={{0,16},{4,20},{8,24},{12,28},{16,0},{20,4},{24,8},{28,12},{1,17},{... | collective-permute-start | bytes 786440 | tf_op jit(solution)/shard_map/ppermute | solution.py:424
  29.0 21.5 %collective-permute-start.12 = (bf16[128,1024]{1,0:T(8,128)(2,1)S(1)}, bf16[128,1024]{1,0:T(8,128)(2,1)S(1)}, u32[]{:S(2)}, u32[]{:S(2)}) collective-permute-start(bf16[128,1024]{1,0:T(8,128)(2,1)S(1)} %bitcast.14), channel_id=1, source_target_pairs={{0,24},{4,28},{8,16},{12,20},{16,8},{20,12},{24,0},{28,4},{1,25},{... | collective-permute-start | bytes 786440 | tf_op jit(solution)/shard_map/ppermute | solution.py:424
  34.0 10.8 %collective-permute-start.7 = (bf16[64,256]{1,0:T(8,128)(2,1)S(1)}, bf16[64,256]{1,0:T(8,128)(2,1)S(1)}, u32[]{:S(2)}, u32[]{:S(2)}) collective-permute-start(bf16[64,256]{1,0:T(8,128)(2,1)S(1)} %get-tuple-element.48), channel_id=1, source_target_pairs={{0,2},{1,3},{2,0},{3,1},{4,6},{5,7},{6,4},{7,5},{8,10},{9,11},{10,... | collective-permute-start | bytes 98312 | tf_op jit(solution)/shard_map/ppermute | solution.py:424
  36.7 13.7 %collective-permute-start.9 = (bf16[128,1024]{1,0:T(8,128)(2,1)S(1)}, bf16[128,1024]{1,0:T(8,128)(2,1)S(1)}, u32[]{:S(2)}, u32[]{:S(2)}) collective-permute-start(bf16[128,1024]{1,0:T(8,128)(2,1)S(1)} %add_convert_fusion), channel_id=1, source_target_pairs={{0,2},{1,3},{2,0},{3,1},{4,6},{5,7},{6,4},{7,5},{8,10},{9,11},{10,... | collective-permute-start | bytes 786440 | tf_op jit(solution)/shard_map/ppermute | solution.py:424
  44.9 5.6 %collective-permute-start.8 = (bf16[64,256]{1,0:T(8,128)(2,1)S(1)}, bf16[64,256]{1,0:T(8,128)(2,1)S(1)}, u32[]{:S(2)}, u32[]{:S(2)}) collective-permute-start(bf16[64,256]{1,0:T(8,128)(2,1)S(1)} %add_convert_fusion.2), channel_id=1, source_target_pairs={{0,1},{1,0},{2,3},{3,2},{4,5},{5,4},{6,7},{7,6},{8,9},{9,8},{10,11... | collective-permute-start | bytes 98312 | tf_op jit(solution)/shard_map/ppermute | solution.py:424
  51.2 1.6 %collective-permute-start.13 = (bf16[128,1024]{1,0:T(8,128)(2,1)S(1)}, bf16[128,1024]{1,0:T(8,128)(2,1)S(1)}, u32[]{:S(2)}, u32[]{:S(2)}) collective-permute-start(bf16[128,1024]{1,0:T(8,128)(2,1)S(1)} %get-tuple-element.56), channel_id=1, source_target_pairs={{0,4},{4,0},{8,12},{12,8},{16,20},{20,16},{24,28},{28,24},{1,5},{5... | collective-permute-start | bytes 786440 | tf_op jit(solution)/shard_map/ppermute | solution.py:424

commit v8 on v7

--- a/solution.py
+++ b/solution.py
@@ -529,12 +529,13 @@
         [attended, beside], list(shrink.values()), depth, here, keys, rank
     )
     low, received = together(low, received)
-    step = shares // 2
-    while step:
+    step = 1
+    while step < shares:
         arrived = exchange(low, "mp", step)
         low = (low.astype(jnp.float32) + arrived.astype(jnp.float32)).astype(jnp.bfloat16)
-        step //= 2
-    low, last = together(low, last)
+        if step == 1:
+            low, last, expand = together(low, last, expand)
+        step *= 2
     blocks = [expand[key] for key in keys]
     correction, other = correct(low, adapters, blocks, 0, out_local, here, keys, rank)
     parts = [*received, *last, correction, exchange(other, "dp", 1)]

time: 53.9 us -> 55.8 us (1.035)
  waiting for transfers between devices: 17.4 us -> 14.2 us
  Pallas kernels: 19.6 us -> 21.6 us
  local copies, waits for them, and re-layouts: 1.11 us -> 3.02 us
  other arithmetic: 0.08 us -> 0.81 us
    ppermute x14, waiting for transfers between devices: 17.4 us -> 14.2 us  [exchange(): return lax.ppermute(value, axis, [(i, i ^ step) for i in range(count)])]
    unnamed x8 -> x18, local copies, waits for them, and re-layouts: 1.07 us -> 2.99 us
    pallas_call x1, Pallas kernels: 0.9 us -> 1.92 us  [finish(): pl.pallas_call(finish_kernel, in_specs=[vmem] * (2 + len(parts)), out_spe...]
    pallas_call x1, Pallas kernels: 0.71 us -> 1.61 us  [correct(): pl.pallas_call(functools.partial(delta_kernel, rank, places, column, keys...]
    convert_element_type x1, other arithmetic: 0.06 us -> 0.79 us  [body(): pieces = [(pieces[0] + passed).astype(jnp.bfloat16)]]
  transfers between devices with their start and end apart: 14 -> 14, of which waited for: 6 -> 8; matrix products, arithmetic and copies ran while one was open for 0% -> 2% of each run, Pallas kernels for 34% -> 33%
where the time goes in v8:
time: 55.8 us; the launch traced here: 55.5 us
  Pallas kernels  21.6 us (39%)
  starting transfers between devices  15.7 us (28%)
  waiting for transfers between devices  14.2 us (25%)
  local copies, waits for them, and re-layouts  3.02 us (5%)
  other arithmetic  0.81 us (1%)
    ppermute x14, starting transfers between devices, exchange(): return lax.ppermute(value, axis, [(i, i ^ step) for i in range(count)])  15.7 us
    ppermute x14, waiting for transfers between devices, exchange(): return lax.ppermute(value, axis, [(i, i ^ step) for i in range(count)])  14.2 us
    pallas_call x1, Pallas kernels, attend(): pl.pallas_call(functools.partial(attend_kernel, block, steps), in_specs=[...  11.4 us
    pallas_call x1, Pallas kernels, project(): pl.pallas_call(functools.partial(project_kernel, steps), in_specs=[pl.Blo...  4.12 us
    unnamed x18, local copies, waits for them, and re-layouts  2.99 us
    pallas_call x1, Pallas kernels, low_rank(): pl.pallas_call(functools.partial(low_kernel, rank, places, keys), in_spec...  2.54 us
    pallas_call x1, Pallas kernels, finish(): pl.pallas_call(finish_kernel, in_specs=[vmem] * (2 + len(parts)), out_spe...  1.92 us
    pallas_call x1, Pallas kernels, correct(): pl.pallas_call(functools.partial(delta_kernel, rank, places, column, keys...  1.61 us
  transfers between devices with their start and end apart: 14, of which 8 were waited for; matrix products, arithmetic and copies ran while one was open for 2% of the time, Pallas kernels for 33%

profile of v8, /device:TPU:0, one launch (start us, length us, event | category | flops | bytes accessed | tf_op | source)
XLA Modules:
  0.0 55.5 jit_solution(16760375195179831118)
XLA Ops:
  0.0 2.9 %collective-permute-start = (bf16[128,2048]{1,0:T(8,128)(2,1)}, bf16[128,2048]{1,0:T(8,128)(2,1)S(1)}, u32[]{:S(2)}, u32[]{:S(2)}) collective-permute-start(bf16[128,2048]{1,0:T(8,128)(2,1)} %bitcast.9), channel_id=1, source_target_pairs={{0,8},{4,12},{8,0},{12,4},{16,24},{20,28},{24,16},{28,20},{1,9},{5... | collective-permute-start | bytes 1572872 | tf_op jit(solution)/shard_map/ppermute | solution.py:424
  2.9 1.5 %collective-permute-start.1 = (bf16[128,2048]{1,0:T(8,128)(2,1)}, bf16[128,2048]{1,0:T(8,128)(2,1)S(1)}, u32[]{:S(2)}, u32[]{:S(2)}) collective-permute-start(bf16[128,2048]{1,0:T(8,128)(2,1)} %bitcast.10), channel_id=1, source_target_pairs={{0,16},{4,20},{8,24},{12,28},{16,0},{20,4},{24,8},{28,12},{1,17},{... | collective-permute-start | bytes 1572872 | tf_op jit(solution)/shard_map/ppermute | solution.py:424
  4.5 11.4 %attend.1 = (bf16[144,2048]{1,0:T(8,128)(2,1)}, bf16[128,1024]{1,0:T(8,128)(2,1)}, bf16[128,1024]{1,0:T(8,128)(2,1)}) custom-call(s32[128]{0:T(128)} %lengths_ref.1, s32[1]{0:T(128)} %bitcast.1.me_ref, bf16[128,16,128]{2,1,0:T(8,128)(2,1)} %q_hbm.1, bf16[128,2,128,128]{3,2,1,0:T(8,128)(2,1)} %k_hbm.1, bf16[128,2,128,128]{3,2,1,0:T(8,128)(2,1)} %v_hbm.1, ...), custom_call_target="tpu_custom_call" | custom-call | flops 1 | bytes 1 | tf_op jit(solution)/shard_map/attend/pallas_call | solution.py:204
  15.9 0.6 %collective-permute-done.1.refs_4_ = bf16[128,2048]{1,0:T(8,128)(2,1)S(1)} collective-permute-done((bf16[128,2048]{1,0:T(8,128)(2,1)}, bf16[128,2048]{1,0:T(8,128)(2,1)S(1)}, u32[]{:S(2)}, u32[]{:S(2)}) %collective-permute-start.1) | collective-permute-done | bytes 524320 | tf_op jit(solution)/shard_map/ppermute | solution.py:424
  16.5 1.6 %collective-permute-start.2 = (bf16[128,1024]{1,0:T(8,128)(2,1)}, bf16[128,1024]{1,0:T(8,128)(2,1)S(1)}, u32[]{:S(2)}, u32[]{:S(2)}) collective-permute-start(bf16[128,1024]{1,0:T(8,128)(2,1)} %get-tuple-element.39), channel_id=1, source_target_pairs={{0,1},{1,0},{2,3},{3,2},{4,5},{5,4},{6,7},{7,6},{8,9},{9,8},{10,11... | collective-permute-start | bytes 786440 | tf_op jit(solution)/shard_map/ppermute | solution.py:424
  18.1 1.6 %collective-permute-start.3 = (bf16[64,2048]{1,0:T(8,128)(2,1)S(1)}, bf16[64,2048]{1,0:T(8,128)(2,1)S(1)}, u32[]{:S(2)}, u32[]{:S(2)}) collective-permute-start(bf16[64,2048]{1,0:T(8,128)(2,1)S(1)} %slice.6), channel_id=1, source_target_pairs={{0,16},{4,20},{8,24},{12,28},{16,0},{20,4},{24,8},{28,12},{1,17},{... | collective-permute-start | bytes 786440 | tf_op jit(solution)/shard_map/ppermute | solution.py:424
  19.7 0.6 %collective-permute-start.4 = (bf16[64,2048]{1,0:T(8,128)(2,1)S(1)}, bf16[64,2048]{1,0:T(8,128)(2,1)S(1)}, u32[]{:S(2)}, u32[]{:S(2)}) collective-permute-start(bf16[64,2048]{1,0:T(8,128)(2,1)S(1)} %slice.7), channel_id=1, source_target_pairs={{0,8},{4,12},{8,0},{12,4},{16,24},{20,28},{24,16},{28,20},{1,9},{5... | collective-permute-start | bytes 786440 | tf_op jit(solution)/shard_map/ppermute | solution.py:424
  20.3 0.4 collective-permute-start.6
  20.8 1.1 %copy-done = bf16[144,2048]{1,0:T(8,128)(2,1)S(1)} copy-done((bf16[144,2048]{1,0:T(8,128)(2,1)S(1)}, bf16[144,2048]{1,0:T(8,128)(2,1)}, u32[]{:S(2)}) %copy-start) | copy-done | bytes 589848
  21.9 4.1 %project.1 = (f32[128,1024]{1,0:T(8,128)S(1)}, f32[128,1024]{1,0:T(8,128)S(1)}) custom-call(s32[1]{0:T(128)} %bitcast.1.me_ref, bf16[144,2048]{1,0:T(8,128)(2,1)S(1)} %copy-done, bf16[2048,4096]{1,0:T(8,128)(2,1)} %w_ref.3), custom_call_target="tpu_custom_call" | custom-call | flops 1 | bytes 1 | tf_op jit(solution)/shard_map/project/pallas_call | solution.py:247
  26.0 0.6 %collective-permute-done.3.refs_5_ = bf16[64,2048]{1,0:T(8,128)(2,1)S(1)} collective-permute-done((bf16[64,2048]{1,0:T(8,128)(2,1)S(1)}, bf16[64,2048]{1,0:T(8,128)(2,1)S(1)}, u32[]{:S(2)}, u32[]{:S(2)}) %collective-permute-start.3) | collective-permute-done | bytes 262176 | tf_op jit(solution)/shard_map/ppermute | solution.py:424
  26.6 1.3 %collective-permute-done.4.refs_6_ = bf16[64,2048]{1,0:T(8,128)(2,1)S(1)} collective-permute-done((bf16[64,2048]{1,0:T(8,128)(2,1)S(1)}, bf16[64,2048]{1,0:T(8,128)(2,1)S(1)}, u32[]{:S(2)}, u32[]{:S(2)}) %collective-permute-start.4) | collective-permute-done | bytes 262176 | tf_op jit(solution)/shard_map/ppermute | solution.py:424
  28.0 0.8 %add_convert_fusion = bf16[128,1024]{1,0:T(8,128)(2,1)} fusion(f32[128,1024]{1,0:T(8,128)S(1)} %get-tuple-element.53, bf16[128,1024]{1,0:T(8,128)(2,1)S(1)} %collective-permute-done.2), kind=kLoop, calls=%fused_computation | loop fusion | flops 393216 | bytes 1048576 | tf_op jit(solution)/shard_map/convert_element_type | solution.py:524
  28.8 2.6 %collective-permute-start.8 = (bf16[128,1024]{1,0:T(8,128)(2,1)}, bf16[128,1024]{1,0:T(8,128)(2,1)}, u32[]{:S(2)}, u32[]{:S(2)}) collective-permute-start(bf16[128,1024]{1,0:T(8,128)(2,1)} %add_convert_fusion), channel_id=1, source_target_pairs={{0,2},{1,3},{2,0},{3,1},{4,6},{5,7},{6,4},{7,5},{8,10},{9,11},{10,... | collective-permute-start | bytes 786440 | tf_op jit(solution)/shard_map/ppermute | solution.py:424
  31.3 0.5 collective-permute-start.10
  31.9 1.5 %collective-permute-start.11 = (bf16[128,1024]{1,0:T(8,128)(2,1)S(1)}, bf16[128,1024]{1,0:T(8,128)(2,1)}, u32[]{:S(2)}, u32[]{:S(2)}) collective-permute-start(bf16[128,1024]{1,0:T(8,128)(2,1)S(1)} %bitcast.13), channel_id=1, source_target_pairs={{0,24},{4,28},{8,16},{12,20},{16,8},{20,12},{24,0},{28,4},{1,25},{... | collective-permute-start | bytes 786440 | tf_op jit(solution)/shard_map/ppermute | solution.py:424
  33.3 0.0 collective-permute-done.5.refs_1_
  33.4 1.6 %collective-permute-start.9 = (bf16[128,1024]{1,0:T(8,128)(2,1)S(1)}, bf16[128,1024]{1,0:T(8,128)(2,1)}, u32[]{:S(2)}, u32[]{:S(2)}) collective-permute-start(bf16[128,1024]{1,0:T(8,128)(2,1)S(1)} %bitcast.14), channel_id=1, source_target_pairs={{0,8},{4,12},{8,0},{12,4},{16,24},{20,28},{24,16},{28,20},{1,9},{5... | collective-permute-start | bytes 786440 | tf_op jit(solution)/shard_map/ppermute | solution.py:424
  34.9 0.9 %copy-done.5 = bf16[64,2048]{1,0:T(8,128)(2,1)S(1)} copy-done((bf16[64,2048]{1,0:T(8,128)(2,1)S(1)}, bf16[64,2048]{1,0:T(8,128)(2,1)}, u32[]{:S(2)}) %copy-start.5) | copy-done | bytes 262168
  35.9 0.9 %copy-done.7 = bf16[64,2048]{1,0:T(8,128)(2,1)S(1)} copy-done((bf16[64,2048]{1,0:T(8,128)(2,1)S(1)}, bf16[64,2048]{1,0:T(8,128)(2,1)}, u32[]{:S(2)}) %copy-start.7) | copy-done | bytes 262168
  36.8 2.5 %low_rank.1 = (bf16[64,256]{1,0:T(8,128)(2,1)S(1)}, s32[8,256]{1,0:T(8,128)S(1)}) custom-call(s32[1]{0:T(128)} %bitcast.7.here_ref, bf16[144,2048]{1,0:T(8,128)(2,1)S(1)} %copy-done.1, bf16[144,2048]{1,0:T(8,128)(2,1)S(1)} %collective-permute-done.5.refs_1_, bf16[128,2048]{1,0:T(8,128)(2,1)S(1)} %bitcast.11, ...), custom_call_target="tpu_custom_call" | custom-call | flops 1 | bytes 1 | tf_op jit(solution)/shard_map/low_rank/pallas_call | solution.py:329
  39.4 0.0 collective-permute-done.6.refs_0_
  39.4 0.5 collective-permute-start.7
  39.9 3.7 %collective-permute-done.7 = bf16[64,256]{1,0:T(8,128)(2,1)S(1)} collective-permute-done((bf16[64,256]{1,0:T(8,128)(2,1)S(1)}, bf16[64,256]{1,0:T(8,128)(2,1)S(1)}, u32[]{:S(2)}, u32[]{:S(2)}) %collective-permute-start.7) | collective-permute-done | bytes 32800 | tf_op jit(solution)/shard_map/ppermute | solution.py:424
  43.6 0.6 %collective-permute-done.10.refs_2_ = bf16[128,1024]{1,0:T(8,128)(2,1)} collective-permute-done((bf16[128,1024]{1,0:T(8,128)(2,1)S(1)}, bf16[128,1024]{1,0:T(8,128)(2,1)}, u32[]{:S(2)}, u32[]{:S(2)}) %collective-permute-start.10) | collective-permute-done | bytes 262176 | tf_op jit(solution)/shard_map/ppermute | solution.py:424
  44.2 1.2 %collective-permute-done.9.refs_1_ = bf16[128,1024]{1,0:T(8,128)(2,1)} collective-permute-done((bf16[128,1024]{1,0:T(8,128)(2,1)S(1)}, bf16[128,1024]{1,0:T(8,128)(2,1)}, u32[]{:S(2)}, u32[]{:S(2)}) %collective-permute-start.9) | collective-permute-done | bytes 262176 | tf_op jit(solution)/shard_map/ppermute | solution.py:424
  45.4 0.3 collective-permute-start.12
  45.8 4.6 %collective-permute-done.12 = bf16[64,256]{1,0:T(8,128)(2,1)S(1)} collective-permute-done((bf16[64,256]{1,0:T(8,128)(2,1)S(1)}, bf16[64,256]{1,0:T(8,128)(2,1)S(1)}, u32[]{:S(2)}, u32[]{:S(2)}) %collective-permute-start.12) | collective-permute-done | bytes 32800 | tf_op jit(solution)/shard_map/ppermute | solution.py:424
  50.4 1.6 %correct.1 = (bf16[128,1024]{1,0:T(8,128)(2,1)S(1)}, bf16[128,1024]{1,0:T(8,128)(2,1)S(1)}) custom-call(s32[1]{0:T(128)} %bitcast.7.here_ref, s32[8,256]{1,0:T(8,128)S(1)} %get-tuple-element.57.adapters_ref, bf16[64,256]{1,0:T(8,128)(2,1)S(1)} %add_convert_fusion.1.low_ref, bf16[128,1024]{1,0:T(8,128)(2,1)S(1)} %bitcast.15, ...), custom_call_target="tpu_custom_call" | custom-call | flops 1 | bytes 1 | tf_op jit(solution)/shard_map/correct/pallas_call | solution.py:380
  52.0 0.1 collective-permute-start.13
  52.1 1.5 %collective-permute-done.13.refs_3_ = bf16[128,1024]{1,0:T(8,128)(2,1)S(1)} collective-permute-done((bf16[128,1024]{1,0:T(8,128)(2,1)S(1)}, bf16[128,1024]{1,0:T(8,128)(2,1)S(1)}, u32[]{:S(2)}, u32[]{:S(2)}) %collective-permute-start.13) | collective-permute-done | bytes 262176 | tf_op jit(solution)/shard_map/ppermute | solution.py:424
  53.6 1.9 %finish.1 = bf16[128,1024]{1,0:T(8,128)(2,1)} custom-call(s32[1,128]{1,0:T(1,128)S(1)} %bitcast.16, f32[128,1024]{1,0:T(8,128)S(1)} %get-tuple-element.37.own_ref, bf16[128,1024]{1,0:T(8,128)(2,1)} %collective-permute-done.6.refs_0_, bf16[128,1024]{1,0:T(8,128)(2,1)} %collective-permute-done.8.refs_1_, bf16[128,1024]{1,0:T(8,128)(2,1)S(1)} %get-tuple-element.63.refs_2_, ...), custom_call_target="tpu_custom_call" | custom-call | flops 1 | bytes 1 | tf_op jit(solution)/shard_map/finish/pallas_call | solution.py:411
  (24 shorter events, 0.1 us)
Async XLA Ops:
  0.0 15.9 %collective-permute-start = (bf16[128,2048]{1,0:T(8,128)(2,1)}, bf16[128,2048]{1,0:T(8,128)(2,1)S(1)}, u32[]{:S(2)}, u32[]{:S(2)}) collective-permute-start(bf16[128,2048]{1,0:T(8,128)(2,1)} %bitcast.9), channel_id=1, source_target_pairs={{0,8},{4,12},{8,0},{12,4},{16,24},{20,28},{24,16},{28,20},{1,9},{5... | collective-permute-start | bytes 1572872 | tf_op jit(solution)/shard_map/ppermute | solution.py:424
  2.9 13.6 %collective-permute-start.1 = (bf16[128,2048]{1,0:T(8,128)(2,1)}, bf16[128,2048]{1,0:T(8,128)(2,1)S(1)}, u32[]{:S(2)}, u32[]{:S(2)}) collective-permute-start(bf16[128,2048]{1,0:T(8,128)(2,1)} %bitcast.10), channel_id=1, source_target_pairs={{0,16},{4,20},{8,24},{12,28},{16,0},{20,4},{24,8},{28,12},{1,17},{... | collective-permute-start | bytes 1572872 | tf_op jit(solution)/shard_map/ppermute | solution.py:424
  16.5 16.8 %collective-permute-start.5 = (bf16[144,2048]{1,0:T(8,128)(2,1)}, bf16[144,2048]{1,0:T(8,128)(2,1)S(1)}, u32[]{:S(2)}, u32[]{:S(2)}) collective-permute-start(bf16[144,2048]{1,0:T(8,128)(2,1)} %get-tuple-element.43.a_hbm.refs_0_), channel_id=1, source_target_pairs={{0,4},{4,0},{8,12},{12,8},{16,20},{20,16},{24,28},{28,24},{1,5},{5... | collective-permute-start | bytes 1769480 | tf_op jit(solution)/shard_map/ppermute | solution.py:424
  16.5 9.5 %collective-permute-start.2 = (bf16[128,1024]{1,0:T(8,128)(2,1)}, bf16[128,1024]{1,0:T(8,128)(2,1)S(1)}, u32[]{:S(2)}, u32[]{:S(2)}) collective-permute-start(bf16[128,1024]{1,0:T(8,128)(2,1)} %get-tuple-element.39), channel_id=1, source_target_pairs={{0,1},{1,0},{2,3},{3,2},{4,5},{5,4},{6,7},{7,6},{8,9},{9,8},{10,11... | collective-permute-start | bytes 786440 | tf_op jit(solution)/shard_map/ppermute | solution.py:424
  18.1 8.5 %collective-permute-start.3 = (bf16[64,2048]{1,0:T(8,128)(2,1)S(1)}, bf16[64,2048]{1,0:T(8,128)(2,1)S(1)}, u32[]{:S(2)}, u32[]{:S(2)}) collective-permute-start(bf16[64,2048]{1,0:T(8,128)(2,1)S(1)} %slice.6), channel_id=1, source_target_pairs={{0,16},{4,20},{8,24},{12,28},{16,0},{20,4},{24,8},{28,12},{1,17},{... | collective-permute-start | bytes 786440 | tf_op jit(solution)/shard_map/ppermute | solution.py:424
  19.7 8.2 %collective-permute-start.4 = (bf16[64,2048]{1,0:T(8,128)(2,1)S(1)}, bf16[64,2048]{1,0:T(8,128)(2,1)S(1)}, u32[]{:S(2)}, u32[]{:S(2)}) collective-permute-start(bf16[64,2048]{1,0:T(8,128)(2,1)S(1)} %slice.7), channel_id=1, source_target_pairs={{0,8},{4,12},{8,0},{12,4},{16,24},{20,28},{24,16},{28,20},{1,9},{5... | collective-permute-start | bytes 786440 | tf_op jit(solution)/shard_map/ppermute | solution.py:424
  20.3 19.0 %collective-permute-start.6 = (bf16[128,1024]{1,0:T(8,128)(2,1)}, bf16[128,1024]{1,0:T(8,128)(2,1)}, u32[]{:S(2)}, u32[]{:S(2)}) collective-permute-start(bf16[128,1024]{1,0:T(8,128)(2,1)} %get-tuple-element.50), channel_id=1, source_target_pairs={{0,1},{1,0},{2,3},{3,2},{4,5},{5,4},{6,7},{7,6},{8,9},{9,8},{10,11... | collective-permute-start | bytes 786440 | tf_op jit(solution)/shard_map/ppermute | solution.py:424
  20.8 1.1 %copy-start = (bf16[144,2048]{1,0:T(8,128)(2,1)S(1)}, bf16[144,2048]{1,0:T(8,128)(2,1)}, u32[]{:S(2)}) copy-start(bf16[144,2048]{1,0:T(8,128)(2,1)} %get-tuple-element.43.a_hbm.refs_0_) | copy-start | bytes 1769476
  21.9 9.5 %copy-start.3 = (bf16[2,64,1024]{2,1,0:T(8,128)(2,1)S(1)}, bf16[2,64,1024]{2,1,0:T(8,128)(2,1)}, u32[]{:S(2)}) copy-start(bf16[2,64,1024]{2,1,0:T(8,128)(2,1)} %param.23) | copy-start | bytes 786436
  21.9 13.1 %copy-start.1 = (bf16[144,2048]{1,0:T(8,128)(2,1)S(1)}, bf16[144,2048]{1,0:T(8,128)(2,1)}, u32[]{:S(2)}) copy-start(bf16[144,2048]{1,0:T(8,128)(2,1)} %get-tuple-element.43.a_hbm.refs_0_) | copy-start | bytes 1769476
  21.9 13.1 %copy-start.2 = (bf16[2,2048,64]{1,2,0:T(8,128)(2,1)S(1)}, bf16[2,2048,64]{1,2,0:T(8,128)(2,1)}, u32[]{:S(2)}) copy-start(bf16[2,2048,64]{1,2,0:T(8,128)(2,1)} %param.22) | copy-start | bytes 1572868
  21.9 31.7 %copy-start.8 = (s32[128]{0:T(128)S(1)}, s32[128]{0:T(128)}, u32[]{:S(2)}) copy-start(s32[128]{0:T(128)} %param.18) | copy-start | bytes 1540
  26.6 6.7 %copy-start.4 = (bf16[64,2048]{1,0:T(8,128)(2,1)}, bf16[64,2048]{1,0:T(8,128)(2,1)S(1)}, u32[]{:S(2)}) copy-start(bf16[64,2048]{1,0:T(8,128)(2,1)S(1)} %collective-permute-done.3.refs_5_) | copy-start | bytes 786436
  28.0 5.4 %copy-start.6 = (bf16[64,2048]{1,0:T(8,128)(2,1)}, bf16[64,2048]{1,0:T(8,128)(2,1)S(1)}, u32[]{:S(2)}) copy-start(bf16[64,2048]{1,0:T(8,128)(2,1)S(1)} %collective-permute-done.4.refs_6_) | copy-start | bytes 786436
  28.8 14.9 %collective-permute-start.8 = (bf16[128,1024]{1,0:T(8,128)(2,1)}, bf16[128,1024]{1,0:T(8,128)(2,1)}, u32[]{:S(2)}, u32[]{:S(2)}) collective-permute-start(bf16[128,1024]{1,0:T(8,128)(2,1)} %add_convert_fusion), channel_id=1, source_target_pairs={{0,2},{1,3},{2,0},{3,1},{4,6},{5,7},{6,4},{7,5},{8,10},{9,11},{10,... | collective-permute-start | bytes 786440 | tf_op jit(solution)/shard_map/ppermute | solution.py:424
  31.3 12.8 %collective-permute-start.10 = (bf16[128,1024]{1,0:T(8,128)(2,1)S(1)}, bf16[128,1024]{1,0:T(8,128)(2,1)}, u32[]{:S(2)}, u32[]{:S(2)}) collective-permute-start(bf16[128,1024]{1,0:T(8,128)(2,1)S(1)} %bitcast.12), channel_id=1, source_target_pairs={{0,16},{4,20},{8,24},{12,28},{16,0},{20,4},{24,8},{28,12},{1,17},{... | collective-permute-start | bytes 786440 | tf_op jit(solution)/shard_map/ppermute | solution.py:424
  31.9 12.3 %collective-permute-start.11 = (bf16[128,1024]{1,0:T(8,128)(2,1)S(1)}, bf16[128,1024]{1,0:T(8,128)(2,1)}, u32[]{:S(2)}, u32[]{:S(2)}) collective-permute-start(bf16[128,1024]{1,0:T(8,128)(2,1)S(1)} %bitcast.13), channel_id=1, source_target_pairs={{0,24},{4,28},{8,16},{12,20},{16,8},{20,12},{24,0},{28,4},{1,25},{... | collective-permute-start | bytes 786440 | tf_op jit(solution)/shard_map/ppermute | solution.py:424
  33.4 12.1 %collective-permute-start.9 = (bf16[128,1024]{1,0:T(8,128)(2,1)S(1)}, bf16[128,1024]{1,0:T(8,128)(2,1)}, u32[]{:S(2)}, u32[]{:S(2)}) collective-permute-start(bf16[128,1024]{1,0:T(8,128)(2,1)S(1)} %bitcast.14), channel_id=1, source_target_pairs={{0,8},{4,12},{8,0},{12,4},{16,24},{20,28},{24,16},{28,20},{1,9},{5... | collective-permute-start | bytes 786440 | tf_op jit(solution)/shard_map/ppermute | solution.py:424
  34.9 1.0 %copy-start.5 = (bf16[64,2048]{1,0:T(8,128)(2,1)S(1)}, bf16[64,2048]{1,0:T(8,128)(2,1)}, u32[]{:S(2)}) copy-start(bf16[64,2048]{1,0:T(8,128)(2,1)} %copy-done.4) | copy-start | bytes 786436
  35.9 0.9 %copy-start.7 = (bf16[64,2048]{1,0:T(8,128)(2,1)S(1)}, bf16[64,2048]{1,0:T(8,128)(2,1)}, u32[]{:S(2)}) copy-start(bf16[64,2048]{1,0:T(8,128)(2,1)} %copy-done.6) | copy-start | bytes 786436
  39.4 4.2 %collective-permute-start.7 = (bf16[64,256]{1,0:T(8,128)(2,1)S(1)}, bf16[64,256]{1,0:T(8,128)(2,1)S(1)}, u32[]{:S(2)}, u32[]{:S(2)}) collective-permute-start(bf16[64,256]{1,0:T(8,128)(2,1)S(1)} %get-tuple-element.52), channel_id=1, source_target_pairs={{0,1},{1,0},{2,3},{3,2},{4,5},{5,4},{6,7},{7,6},{8,9},{9,8},{10,11... | collective-permute-start | bytes 98312 | tf_op jit(solution)/shard_map/ppermute | solution.py:424
  45.4 4.9 %collective-permute-start.12 = (bf16[64,256]{1,0:T(8,128)(2,1)S(1)}, bf16[64,256]{1,0:T(8,128)(2,1)S(1)}, u32[]{:S(2)}, u32[]{:S(2)}) collective-permute-start(bf16[64,256]{1,0:T(8,128)(2,1)S(1)} %add_convert_fusion.2), channel_id=1, source_target_pairs={{0,2},{1,3},{2,0},{3,1},{4,6},{5,7},{6,4},{7,5},{8,10},{9,11},{10,... | collective-permute-start | bytes 98312 | tf_op jit(solution)/shard_map/ppermute | solution.py:424
  52.0 1.6 %collective-permute-start.13 = (bf16[128,1024]{1,0:T(8,128)(2,1)S(1)}, bf16[128,1024]{1,0:T(8,128)(2,1)S(1)}, u32[]{:S(2)}, u32[]{:S(2)}) collective-permute-start(bf16[128,1024]{1,0:T(8,128)(2,1)S(1)} %get-tuple-element.64), channel_id=1, source_target_pairs={{0,4},{4,0},{8,12},{12,8},{16,20},{20,16},{24,28},{28,24},{1,5},{5... | collective-permute-start | bytes 786440 | tf_op jit(solution)/shard_map/ppermute | solution.py:424

commit v9 on v8

--- a/solution.py
+++ b/solution.py
@@ -399,7 +399,7 @@
     live = jnp.broadcast_to(occupied_ref[...].astype(jnp.float32), (128, rows)).T
     for j in range(0, out_ref.shape[1], 128):
         columns = slice(j, j + 128)
-        total = own_ref[:, columns]
+        total = own_ref[:, columns].astype(jnp.float32)
         for ref in part_refs:
             total += ref[:, columns].astype(jnp.float32)
         out_ref[:, columns] = (live * total).astype(out_ref.dtype)
@@ -513,7 +513,7 @@
         me,
         late,
         out_local,
-        [jnp.float32 if halved else jnp.bfloat16] * (len(late) - 1) + [jnp.float32],
+        [jnp.bfloat16] * len(late),
     )
     pieces, received[0], attended, shrink, expand = together(
         pieces, received[0], attended, shrink, expand
@@ -521,7 +521,7 @@
     expand = direct_blocks(expand)
     if halved:
         passed = received.pop(0).astype(jnp.float32)
-        pieces = [(pieces[0] + passed).astype(jnp.bfloat16)]
+        pieces = [(pieces[0].astype(jnp.float32) + passed).astype(jnp.bfloat16)]
     last = [exchange(part, "mp", step) for part, step in zip(pieces, late)]
 
     keys = tuple(shrink)

time: 55.8 us -> 55.8 us (level)
  transfers between devices with their start and end apart: 14 -> 14, of which waited for: 8 -> 8; matrix products, arithmetic and copies ran while one was open for 2% -> 1% of each run, Pallas kernels for 33% -> 33%
where the time goes in v9:
time: 55.8 us; the launch traced here: 55.6 us
  Pallas kernels  21.7 us (39%)
  starting transfers between devices  15.7 us (28%)
  waiting for transfers between devices  14.2 us (25%)
  local copies, waits for them, and re-layouts  3.02 us (5%)
  other arithmetic  0.81 us (1%)
    ppermute x14, starting transfers between devices, exchange(): return lax.ppermute(value, axis, [(i, i ^ step) for i in range(count)])  15.7 us
    ppermute x14, waiting for transfers between devices, exchange(): return lax.ppermute(value, axis, [(i, i ^ step) for i in range(count)])  14.2 us
    pallas_call x1, Pallas kernels, attend(): pl.pallas_call(functools.partial(attend_kernel, block, steps), in_specs=[...  11.5 us
    pallas_call x1, Pallas kernels, project(): pl.pallas_call(functools.partial(project_kernel, steps), in_specs=[pl.Blo...  4.12 us
    unnamed x18, local copies, waits for them, and re-layouts  2.99 us
    pallas_call x1, Pallas kernels, low_rank(): pl.pallas_call(functools.partial(low_kernel, rank, places, keys), in_spec...  2.54 us
    pallas_call x1, Pallas kernels, finish(): pl.pallas_call(finish_kernel, in_specs=[vmem] * (2 + len(parts)), out_spe...  1.94 us
    pallas_call x1, Pallas kernels, correct(): pl.pallas_call(functools.partial(delta_kernel, rank, places, column, keys...  1.61 us
  transfers between devices with their start and end apart: 14, of which 8 were waited for; matrix products, arithmetic and copies ran while one was open for 1% of the time, Pallas kernels for 33%

profile of v9, /device:TPU:0, one launch (start us, length us, event | category | flops | bytes accessed | tf_op | source)
XLA Modules:
  0.0 55.6 jit_solution(1772181624411122242)
XLA Ops:
  0.0 2.9 %collective-permute-start = (bf16[128,2048]{1,0:T(8,128)(2,1)}, bf16[128,2048]{1,0:T(8,128)(2,1)S(1)}, u32[]{:S(2)}, u32[]{:S(2)}) collective-permute-start(bf16[128,2048]{1,0:T(8,128)(2,1)} %bitcast.9), channel_id=1, source_target_pairs={{0,8},{4,12},{8,0},{12,4},{16,24},{20,28},{24,16},{28,20},{1,9},{5... | collective-permute-start | bytes 1572872 | tf_op jit(solution)/shard_map/ppermute | solution.py:424
  2.9 1.5 %collective-permute-start.1 = (bf16[128,2048]{1,0:T(8,128)(2,1)}, bf16[128,2048]{1,0:T(8,128)(2,1)S(1)}, u32[]{:S(2)}, u32[]{:S(2)}) collective-permute-start(bf16[128,2048]{1,0:T(8,128)(2,1)} %bitcast.10), channel_id=1, source_target_pairs={{0,16},{4,20},{8,24},{12,28},{16,0},{20,4},{24,8},{28,12},{1,17},{... | collective-permute-start | bytes 1572872 | tf_op jit(solution)/shard_map/ppermute | solution.py:424
  4.5 11.5 %attend.1 = (bf16[144,2048]{1,0:T(8,128)(2,1)}, bf16[128,1024]{1,0:T(8,128)(2,1)}, bf16[128,1024]{1,0:T(8,128)(2,1)}) custom-call(s32[128]{0:T(128)} %lengths_ref.1, s32[1]{0:T(128)} %bitcast.1.me_ref, bf16[128,16,128]{2,1,0:T(8,128)(2,1)} %q_hbm.1, bf16[128,2,128,128]{3,2,1,0:T(8,128)(2,1)} %k_hbm.1, bf16[128,2,128,128]{3,2,1,0:T(8,128)(2,1)} %v_hbm.1, ...), custom_call_target="tpu_custom_call" | custom-call | flops 1 | bytes 1 | tf_op jit(solution)/shard_map/attend/pallas_call | solution.py:204
  15.9 0.0 collective-permute-done.refs_3_
  15.9 0.6 %collective-permute-done.1.refs_4_ = bf16[128,2048]{1,0:T(8,128)(2,1)S(1)} collective-permute-done((bf16[128,2048]{1,0:T(8,128)(2,1)}, bf16[128,2048]{1,0:T(8,128)(2,1)S(1)}, u32[]{:S(2)}, u32[]{:S(2)}) %collective-permute-start.1) | collective-permute-done | bytes 524320 | tf_op jit(solution)/shard_map/ppermute | solution.py:424
  16.5 1.6 %collective-permute-start.2 = (bf16[128,1024]{1,0:T(8,128)(2,1)}, bf16[128,1024]{1,0:T(8,128)(2,1)S(1)}, u32[]{:S(2)}, u32[]{:S(2)}) collective-permute-start(bf16[128,1024]{1,0:T(8,128)(2,1)} %get-tuple-element.39), channel_id=1, source_target_pairs={{0,1},{1,0},{2,3},{3,2},{4,5},{5,4},{6,7},{7,6},{8,9},{9,8},{10,11... | collective-permute-start | bytes 786440 | tf_op jit(solution)/shard_map/ppermute | solution.py:424
  18.1 1.6 %collective-permute-start.3 = (bf16[64,2048]{1,0:T(8,128)(2,1)S(1)}, bf16[64,2048]{1,0:T(8,128)(2,1)S(1)}, u32[]{:S(2)}, u32[]{:S(2)}) collective-permute-start(bf16[64,2048]{1,0:T(8,128)(2,1)S(1)} %slice.6), channel_id=1, source_target_pairs={{0,16},{4,20},{8,24},{12,28},{16,0},{20,4},{24,8},{28,12},{1,17},{... | collective-permute-start | bytes 786440 | tf_op jit(solution)/shard_map/ppermute | solution.py:424
  19.7 0.6 %collective-permute-start.4 = (bf16[64,2048]{1,0:T(8,128)(2,1)S(1)}, bf16[64,2048]{1,0:T(8,128)(2,1)S(1)}, u32[]{:S(2)}, u32[]{:S(2)}) collective-permute-start(bf16[64,2048]{1,0:T(8,128)(2,1)S(1)} %slice.7), channel_id=1, source_target_pairs={{0,8},{4,12},{8,0},{12,4},{16,24},{20,28},{24,16},{28,20},{1,9},{5... | collective-permute-start | bytes 786440 | tf_op jit(solution)/shard_map/ppermute | solution.py:424
  20.3 0.4 collective-permute-start.6
  20.8 1.1 %copy-done = bf16[144,2048]{1,0:T(8,128)(2,1)S(1)} copy-done((bf16[144,2048]{1,0:T(8,128)(2,1)S(1)}, bf16[144,2048]{1,0:T(8,128)(2,1)}, u32[]{:S(2)}) %copy-start) | copy-done | bytes 589848
  21.9 4.1 %project.1 = (bf16[128,1024]{1,0:T(8,128)(2,1)S(1)}, bf16[128,1024]{1,0:T(8,128)(2,1)S(1)}) custom-call(s32[1]{0:T(128)} %bitcast.1.me_ref, bf16[144,2048]{1,0:T(8,128)(2,1)S(1)} %copy-done, bf16[2048,4096]{1,0:T(8,128)(2,1)} %w_ref.3), custom_call_target="tpu_custom_call" | custom-call | flops 1 | bytes 1 | tf_op jit(solution)/shard_map/project/pallas_call | solution.py:247
  26.0 0.0 collective-permute-done.2
  26.0 0.6 %collective-permute-done.3.refs_5_ = bf16[64,2048]{1,0:T(8,128)(2,1)S(1)} collective-permute-done((bf16[64,2048]{1,0:T(8,128)(2,1)S(1)}, bf16[64,2048]{1,0:T(8,128)(2,1)S(1)}, u32[]{:S(2)}, u32[]{:S(2)}) %collective-permute-start.3) | collective-permute-done | bytes 262176 | tf_op jit(solution)/shard_map/ppermute | solution.py:424
  26.6 1.3 %collective-permute-done.4.refs_6_ = bf16[64,2048]{1,0:T(8,128)(2,1)S(1)} collective-permute-done((bf16[64,2048]{1,0:T(8,128)(2,1)S(1)}, bf16[64,2048]{1,0:T(8,128)(2,1)S(1)}, u32[]{:S(2)}, u32[]{:S(2)}) %collective-permute-start.4) | collective-permute-done | bytes 262176 | tf_op jit(solution)/shard_map/ppermute | solution.py:424
  28.0 0.8 %add_convert_fusion = bf16[128,1024]{1,0:T(8,128)(2,1)} fusion(bf16[128,1024]{1,0:T(8,128)(2,1)S(1)} %collective-permute-done.2, bf16[128,1024]{1,0:T(8,128)(2,1)S(1)} %get-tuple-element.53), kind=kLoop, calls=%fused_computation | loop fusion | flops 524288 | bytes 786432 | tf_op jit(solution)/shard_map/convert_element_type | solution.py:524
  28.8 2.6 %collective-permute-start.8 = (bf16[128,1024]{1,0:T(8,128)(2,1)}, bf16[128,1024]{1,0:T(8,128)(2,1)}, u32[]{:S(2)}, u32[]{:S(2)}) collective-permute-start(bf16[128,1024]{1,0:T(8,128)(2,1)} %add_convert_fusion), channel_id=1, source_target_pairs={{0,2},{1,3},{2,0},{3,1},{4,6},{5,7},{6,4},{7,5},{8,10},{9,11},{10,... | collective-permute-start | bytes 786440 | tf_op jit(solution)/shard_map/ppermute | solution.py:424
  31.3 0.5 collective-permute-start.10
  31.9 1.5 %collective-permute-start.11 = (bf16[128,1024]{1,0:T(8,128)(2,1)S(1)}, bf16[128,1024]{1,0:T(8,128)(2,1)}, u32[]{:S(2)}, u32[]{:S(2)}) collective-permute-start(bf16[128,1024]{1,0:T(8,128)(2,1)S(1)} %bitcast.13), channel_id=1, source_target_pairs={{0,24},{4,28},{8,16},{12,20},{16,8},{20,12},{24,0},{28,4},{1,25},{... | collective-permute-start | bytes 786440 | tf_op jit(solution)/shard_map/ppermute | solution.py:424
  33.4 1.6 %collective-permute-start.9 = (bf16[128,1024]{1,0:T(8,128)(2,1)S(1)}, bf16[128,1024]{1,0:T(8,128)(2,1)}, u32[]{:S(2)}, u32[]{:S(2)}) collective-permute-start(bf16[128,1024]{1,0:T(8,128)(2,1)S(1)} %bitcast.14), channel_id=1, source_target_pairs={{0,8},{4,12},{8,0},{12,4},{16,24},{20,28},{24,16},{28,20},{1,9},{5... | collective-permute-start | bytes 786440 | tf_op jit(solution)/shard_map/ppermute | solution.py:424
  34.9 0.9 %copy-done.5 = bf16[64,2048]{1,0:T(8,128)(2,1)S(1)} copy-done((bf16[64,2048]{1,0:T(8,128)(2,1)S(1)}, bf16[64,2048]{1,0:T(8,128)(2,1)}, u32[]{:S(2)}) %copy-start.5) | copy-done | bytes 262168
  35.9 0.9 %copy-done.7 = bf16[64,2048]{1,0:T(8,128)(2,1)S(1)} copy-done((bf16[64,2048]{1,0:T(8,128)(2,1)S(1)}, bf16[64,2048]{1,0:T(8,128)(2,1)}, u32[]{:S(2)}) %copy-start.7) | copy-done | bytes 262168
  36.8 2.5 %low_rank.1 = (bf16[64,256]{1,0:T(8,128)(2,1)S(1)}, s32[8,256]{1,0:T(8,128)S(1)}) custom-call(s32[1]{0:T(128)} %bitcast.7.here_ref, bf16[144,2048]{1,0:T(8,128)(2,1)S(1)} %copy-done.1, bf16[144,2048]{1,0:T(8,128)(2,1)S(1)} %collective-permute-done.5.refs_1_, bf16[128,2048]{1,0:T(8,128)(2,1)S(1)} %bitcast.11, ...), custom_call_target="tpu_custom_call" | custom-call | flops 1 | bytes 1 | tf_op jit(solution)/shard_map/low_rank/pallas_call | solution.py:329
  39.4 0.5 collective-permute-start.7
  39.9 3.6 %collective-permute-done.7 = bf16[64,256]{1,0:T(8,128)(2,1)S(1)} collective-permute-done((bf16[64,256]{1,0:T(8,128)(2,1)S(1)}, bf16[64,256]{1,0:T(8,128)(2,1)S(1)}, u32[]{:S(2)}, u32[]{:S(2)}) %collective-permute-start.7) | collective-permute-done | bytes 32800 | tf_op jit(solution)/shard_map/ppermute | solution.py:424
  43.5 0.6 %collective-permute-done.10.refs_2_ = bf16[128,1024]{1,0:T(8,128)(2,1)} collective-permute-done((bf16[128,1024]{1,0:T(8,128)(2,1)S(1)}, bf16[128,1024]{1,0:T(8,128)(2,1)}, u32[]{:S(2)}, u32[]{:S(2)}) %collective-permute-start.10) | collective-permute-done | bytes 262176 | tf_op jit(solution)/shard_map/ppermute | solution.py:424
  44.1 1.2 %collective-permute-done.9.refs_1_ = bf16[128,1024]{1,0:T(8,128)(2,1)} collective-permute-done((bf16[128,1024]{1,0:T(8,128)(2,1)S(1)}, bf16[128,1024]{1,0:T(8,128)(2,1)}, u32[]{:S(2)}, u32[]{:S(2)}) %collective-permute-start.9) | collective-permute-done | bytes 262176 | tf_op jit(solution)/shard_map/ppermute | solution.py:424
  45.3 0.3 collective-permute-start.12
  45.7 4.7 %collective-permute-done.12 = bf16[64,256]{1,0:T(8,128)(2,1)S(1)} collective-permute-done((bf16[64,256]{1,0:T(8,128)(2,1)S(1)}, bf16[64,256]{1,0:T(8,128)(2,1)S(1)}, u32[]{:S(2)}, u32[]{:S(2)}) %collective-permute-start.12) | collective-permute-done | bytes 32800 | tf_op jit(solution)/shard_map/ppermute | solution.py:424
  50.4 1.6 %correct.1 = (bf16[128,1024]{1,0:T(8,128)(2,1)S(1)}, bf16[128,1024]{1,0:T(8,128)(2,1)S(1)}) custom-call(s32[1]{0:T(128)} %bitcast.7.here_ref, s32[8,256]{1,0:T(8,128)S(1)} %get-tuple-element.57.adapters_ref, bf16[64,256]{1,0:T(8,128)(2,1)S(1)} %add_convert_fusion.1.low_ref, bf16[128,1024]{1,0:T(8,128)(2,1)S(1)} %bitcast.15, ...), custom_call_target="tpu_custom_call" | custom-call | flops 1 | bytes 1 | tf_op jit(solution)/shard_map/correct/pallas_call | solution.py:380
  52.0 0.1 collective-permute-start.13
  52.1 1.5 %collective-permute-done.13.refs_3_ = bf16[128,1024]{1,0:T(8,128)(2,1)S(1)} collective-permute-done((bf16[128,1024]{1,0:T(8,128)(2,1)S(1)}, bf16[128,1024]{1,0:T(8,128)(2,1)S(1)}, u32[]{:S(2)}, u32[]{:S(2)}) %collective-permute-start.13) | collective-permute-done | bytes 262176 | tf_op jit(solution)/shard_map/ppermute | solution.py:424
  53.6 1.9 %finish.1 = bf16[128,1024]{1,0:T(8,128)(2,1)} custom-call(s32[1,128]{1,0:T(1,128)S(1)} %bitcast.16, bf16[128,1024]{1,0:T(8,128)(2,1)S(1)} %get-tuple-element.37.own_ref, bf16[128,1024]{1,0:T(8,128)(2,1)S(1)} %collective-permute-done.6.refs_0_, bf16[128,1024]{1,0:T(8,128)(2,1)} %collective-permute-done.8.refs_1_, ...), custom_call_target="tpu_custom_call" | custom-call | flops 1 | bytes 1 | tf_op jit(solution)/shard_map/finish/pallas_call | solution.py:411
  (24 shorter events, 0.1 us)
Async XLA Ops:
  0.0 15.9 %collective-permute-start = (bf16[128,2048]{1,0:T(8,128)(2,1)}, bf16[128,2048]{1,0:T(8,128)(2,1)S(1)}, u32[]{:S(2)}, u32[]{:S(2)}) collective-permute-start(bf16[128,2048]{1,0:T(8,128)(2,1)} %bitcast.9), channel_id=1, source_target_pairs={{0,8},{4,12},{8,0},{12,4},{16,24},{20,28},{24,16},{28,20},{1,9},{5... | collective-permute-start | bytes 1572872 | tf_op jit(solution)/shard_map/ppermute | solution.py:424
  2.9 13.6 %collective-permute-start.1 = (bf16[128,2048]{1,0:T(8,128)(2,1)}, bf16[128,2048]{1,0:T(8,128)(2,1)S(1)}, u32[]{:S(2)}, u32[]{:S(2)}) collective-permute-start(bf16[128,2048]{1,0:T(8,128)(2,1)} %bitcast.10), channel_id=1, source_target_pairs={{0,16},{4,20},{8,24},{12,28},{16,0},{20,4},{24,8},{28,12},{1,17},{... | collective-permute-start | bytes 1572872 | tf_op jit(solution)/shard_map/ppermute | solution.py:424
  16.5 16.8 %collective-permute-start.5 = (bf16[144,2048]{1,0:T(8,128)(2,1)}, bf16[144,2048]{1,0:T(8,128)(2,1)S(1)}, u32[]{:S(2)}, u32[]{:S(2)}) collective-permute-start(bf16[144,2048]{1,0:T(8,128)(2,1)} %get-tuple-element.43.a_hbm.refs_0_), channel_id=1, source_target_pairs={{0,4},{4,0},{8,12},{12,8},{16,20},{20,16},{24,28},{28,24},{1,5},{5... | collective-permute-start | bytes 1769480 | tf_op jit(solution)/shard_map/ppermute | solution.py:424
  16.5 9.5 %collective-permute-start.2 = (bf16[128,1024]{1,0:T(8,128)(2,1)}, bf16[128,1024]{1,0:T(8,128)(2,1)S(1)}, u32[]{:S(2)}, u32[]{:S(2)}) collective-permute-start(bf16[128,1024]{1,0:T(8,128)(2,1)} %get-tuple-element.39), channel_id=1, source_target_pairs={{0,1},{1,0},{2,3},{3,2},{4,5},{5,4},{6,7},{7,6},{8,9},{9,8},{10,11... | collective-permute-start | bytes 786440 | tf_op jit(solution)/shard_map/ppermute | solution.py:424
  18.1 8.5 %collective-permute-start.3 = (bf16[64,2048]{1,0:T(8,128)(2,1)S(1)}, bf16[64,2048]{1,0:T(8,128)(2,1)S(1)}, u32[]{:S(2)}, u32[]{:S(2)}) collective-permute-start(bf16[64,2048]{1,0:T(8,128)(2,1)S(1)} %slice.6), channel_id=1, source_target_pairs={{0,16},{4,20},{8,24},{12,28},{16,0},{20,4},{24,8},{28,12},{1,17},{... | collective-permute-start | bytes 786440 | tf_op jit(solution)/shard_map/ppermute | solution.py:424
  19.7 8.2 %collective-permute-start.4 = (bf16[64,2048]{1,0:T(8,128)(2,1)S(1)}, bf16[64,2048]{1,0:T(8,128)(2,1)S(1)}, u32[]{:S(2)}, u32[]{:S(2)}) collective-permute-start(bf16[64,2048]{1,0:T(8,128)(2,1)S(1)} %slice.7), channel_id=1, source_target_pairs={{0,8},{4,12},{8,0},{12,4},{16,24},{20,28},{24,16},{28,20},{1,9},{5... | collective-permute-start | bytes 786440 | tf_op jit(solution)/shard_map/ppermute | solution.py:424
  20.3 19.0 %collective-permute-start.6 = (bf16[128,1024]{1,0:T(8,128)(2,1)}, bf16[128,1024]{1,0:T(8,128)(2,1)S(1)}, u32[]{:S(2)}, u32[]{:S(2)}) collective-permute-start(bf16[128,1024]{1,0:T(8,128)(2,1)} %get-tuple-element.50), channel_id=1, source_target_pairs={{0,1},{1,0},{2,3},{3,2},{4,5},{5,4},{6,7},{7,6},{8,9},{9,8},{10,11... | collective-permute-start | bytes 786440 | tf_op jit(solution)/shard_map/ppermute | solution.py:424
  20.8 1.1 %copy-start = (bf16[144,2048]{1,0:T(8,128)(2,1)S(1)}, bf16[144,2048]{1,0:T(8,128)(2,1)}, u32[]{:S(2)}) copy-start(bf16[144,2048]{1,0:T(8,128)(2,1)} %get-tuple-element.43.a_hbm.refs_0_) | copy-start | bytes 1769476
  21.9 9.5 %copy-start.3 = (bf16[2,64,1024]{2,1,0:T(8,128)(2,1)S(1)}, bf16[2,64,1024]{2,1,0:T(8,128)(2,1)}, u32[]{:S(2)}) copy-start(bf16[2,64,1024]{2,1,0:T(8,128)(2,1)} %param.23) | copy-start | bytes 786436
  21.9 13.1 %copy-start.1 = (bf16[144,2048]{1,0:T(8,128)(2,1)S(1)}, bf16[144,2048]{1,0:T(8,128)(2,1)}, u32[]{:S(2)}) copy-start(bf16[144,2048]{1,0:T(8,128)(2,1)} %get-tuple-element.43.a_hbm.refs_0_) | copy-start | bytes 1769476
  21.9 13.1 %copy-start.2 = (bf16[2,2048,64]{1,2,0:T(8,128)(2,1)S(1)}, bf16[2,2048,64]{1,2,0:T(8,128)(2,1)}, u32[]{:S(2)}) copy-start(bf16[2,2048,64]{1,2,0:T(8,128)(2,1)} %param.22) | copy-start | bytes 1572868
  21.9 31.7 %copy-start.8 = (s32[128]{0:T(128)S(1)}, s32[128]{0:T(128)}, u32[]{:S(2)}) copy-start(s32[128]{0:T(128)} %param.18) | copy-start | bytes 1540
  26.6 6.7 %copy-start.4 = (bf16[64,2048]{1,0:T(8,128)(2,1)}, bf16[64,2048]{1,0:T(8,128)(2,1)S(1)}, u32[]{:S(2)}) copy-start(bf16[64,2048]{1,0:T(8,128)(2,1)S(1)} %collective-permute-done.3.refs_5_) | copy-start | bytes 786436
  28.0 5.4 %copy-start.6 = (bf16[64,2048]{1,0:T(8,128)(2,1)}, bf16[64,2048]{1,0:T(8,128)(2,1)S(1)}, u32[]{:S(2)}) copy-start(bf16[64,2048]{1,0:T(8,128)(2,1)S(1)} %collective-permute-done.4.refs_6_) | copy-start | bytes 786436
  28.8 14.7 %collective-permute-start.8 = (bf16[128,1024]{1,0:T(8,128)(2,1)}, bf16[128,1024]{1,0:T(8,128)(2,1)}, u32[]{:S(2)}, u32[]{:S(2)}) collective-permute-start(bf16[128,1024]{1,0:T(8,128)(2,1)} %add_convert_fusion), channel_id=1, source_target_pairs={{0,2},{1,3},{2,0},{3,1},{4,6},{5,7},{6,4},{7,5},{8,10},{9,11},{10,... | collective-permute-start | bytes 786440 | tf_op jit(solution)/shard_map/ppermute | solution.py:424
  31.3 12.7 %collective-permute-start.10 = (bf16[128,1024]{1,0:T(8,128)(2,1)S(1)}, bf16[128,1024]{1,0:T(8,128)(2,1)}, u32[]{:S(2)}, u32[]{:S(2)}) collective-permute-start(bf16[128,1024]{1,0:T(8,128)(2,1)S(1)} %bitcast.12), channel_id=1, source_target_pairs={{0,16},{4,20},{8,24},{12,28},{16,0},{20,4},{24,8},{28,12},{1,17},{... | collective-permute-start | bytes 786440 | tf_op jit(solution)/shard_map/ppermute | solution.py:424
  31.9 12.2 %collective-permute-start.11 = (bf16[128,1024]{1,0:T(8,128)(2,1)S(1)}, bf16[128,1024]{1,0:T(8,128)(2,1)}, u32[]{:S(2)}, u32[]{:S(2)}) collective-permute-start(bf16[128,1024]{1,0:T(8,128)(2,1)S(1)} %bitcast.13), channel_id=1, source_target_pairs={{0,24},{4,28},{8,16},{12,20},{16,8},{20,12},{24,0},{28,4},{1,25},{... | collective-permute-start | bytes 786440 | tf_op jit(solution)/shard_map/ppermute | solution.py:424
  33.4 12.0 %collective-permute-start.9 = (bf16[128,1024]{1,0:T(8,128)(2,1)S(1)}, bf16[128,1024]{1,0:T(8,128)(2,1)}, u32[]{:S(2)}, u32[]{:S(2)}) collective-permute-start(bf16[128,1024]{1,0:T(8,128)(2,1)S(1)} %bitcast.14), channel_id=1, source_target_pairs={{0,8},{4,12},{8,0},{12,4},{16,24},{20,28},{24,16},{28,20},{1,9},{5... | collective-permute-start | bytes 786440 | tf_op jit(solution)/shard_map/ppermute | solution.py:424
  34.9 1.0 %copy-start.5 = (bf16[64,2048]{1,0:T(8,128)(2,1)S(1)}, bf16[64,2048]{1,0:T(8,128)(2,1)}, u32[]{:S(2)}) copy-start(bf16[64,2048]{1,0:T(8,128)(2,1)} %copy-done.4) | copy-start | bytes 786436
  35.9 0.9 %copy-start.7 = (bf16[64,2048]{1,0:T(8,128)(2,1)S(1)}, bf16[64,2048]{1,0:T(8,128)(2,1)}, u32[]{:S(2)}) copy-start(bf16[64,2048]{1,0:T(8,128)(2,1)} %copy-done.6) | copy-start | bytes 786436
  39.4 4.1 %collective-permute-start.7 = (bf16[64,256]{1,0:T(8,128)(2,1)S(1)}, bf16[64,256]{1,0:T(8,128)(2,1)S(1)}, u32[]{:S(2)}, u32[]{:S(2)}) collective-permute-start(bf16[64,256]{1,0:T(8,128)(2,1)S(1)} %get-tuple-element.52), channel_id=1, source_target_pairs={{0,1},{1,0},{2,3},{3,2},{4,5},{5,4},{6,7},{7,6},{8,9},{9,8},{10,11... | collective-permute-start | bytes 98312 | tf_op jit(solution)/shard_map/ppermute | solution.py:424
  45.3 5.0 %collective-permute-start.12 = (bf16[64,256]{1,0:T(8,128)(2,1)S(1)}, bf16[64,256]{1,0:T(8,128)(2,1)S(1)}, u32[]{:S(2)}, u32[]{:S(2)}) collective-permute-start(bf16[64,256]{1,0:T(8,128)(2,1)S(1)} %add_convert_fusion.2), channel_id=1, source_target_pairs={{0,2},{1,3},{2,0},{3,1},{4,6},{5,7},{6,4},{7,5},{8,10},{9,11},{10,... | collective-permute-start | bytes 98312 | tf_op jit(solution)/shard_map/ppermute | solution.py:424
  52.0 1.6 %collective-permute-start.13 = (bf16[128,1024]{1,0:T(8,128)(2,1)S(1)}, bf16[128,1024]{1,0:T(8,128)(2,1)S(1)}, u32[]{:S(2)}, u32[]{:S(2)}) collective-permute-start(bf16[128,1024]{1,0:T(8,128)(2,1)S(1)} %get-tuple-element.64), channel_id=1, source_target_pairs={{0,4},{4,0},{8,12},{12,8},{16,20},{20,16},{24,28},{28,24},{1,5},{5... | collective-permute-start | bytes 786440 | tf_op jit(solution)/shard_map/ppermute | solution.py:424

commit v10 on v9

--- a/solution.py
+++ b/solution.py
@@ -534,7 +534,7 @@
         arrived = exchange(low, "mp", step)
         low = (low.astype(jnp.float32) + arrived.astype(jnp.float32)).astype(jnp.bfloat16)
         if step == 1:
-            low, last, expand = together(low, last, expand)
+            low, last = together(low, last)
         step *= 2
     blocks = [expand[key] for key in keys]
     correction, other = correct(low, adapters, blocks, 0, out_local, here, keys, rank)

time: 55.8 us -> 54 us (0.968)
  Pallas kernels: 21.7 us -> 20.7 us
  waiting for transfers between devices: 14.2 us -> 13.6 us
    pallas_call x1, Pallas kernels: 1.61 us -> 0.7 us  [correct(): pl.pallas_call(functools.partial(delta_kernel, rank, places, column, keys...]
    ppermute x14, waiting for transfers between devices: 14.2 us -> 13.6 us  [exchange(): return lax.ppermute(value, axis, [(i, i ^ step) for i in range(count)])]
  transfers between devices with their start and end apart: 14 -> 14, of which waited for: 8 -> 7; matrix products, arithmetic and copies ran while one was open for 1% -> 2% of each run, Pallas kernels for 33% -> 34%
where the time goes in v10:
time: 54 us; the launch traced here: 53.7 us
  Pallas kernels  20.7 us (38%)
  starting transfers between devices  15.4 us (29%)
  waiting for transfers between devices  13.6 us (25%)
  local copies, waits for them, and re-layouts  3.01 us (6%)
  other arithmetic  0.81 us (2%)
    ppermute x14, starting transfers between devices, exchange(): return lax.ppermute(value, axis, [(i, i ^ step) for i in range(count)])  15.4 us
    ppermute x14, waiting for transfers between devices, exchange(): return lax.ppermute(value, axis, [(i, i ^ step) for i in range(count)])  13.6 us
    pallas_call x1, Pallas kernels, attend(): pl.pallas_call(functools.partial(attend_kernel, block, steps), in_specs=[...  11.4 us
    pallas_call x1, Pallas kernels, project(): pl.pallas_call(functools.partial(project_kernel, steps), in_specs=[pl.Blo...  4.12 us
    unnamed x18, local copies, waits for them, and re-layouts  2.98 us
    pallas_call x1, Pallas kernels, low_rank(): pl.pallas_call(functools.partial(low_kernel, rank, places, keys), in_spec...  2.54 us
    pallas_call x1, Pallas kernels, finish(): pl.pallas_call(finish_kernel, in_specs=[vmem] * (2 + len(parts)), out_spe...  1.94 us
  transfers between devices with their start and end apart: 14, of which 7 were waited for; matrix products, arithmetic and copies ran while one was open for 2% of the time, Pallas kernels for 34%

profile of v10, /device:TPU:0, one launch (start us, length us, event | category | flops | bytes accessed | tf_op | source)
XLA Modules:
  0.0 53.7 jit_solution(15658311522990752940)
XLA Ops:
  0.0 2.9 %collective-permute-start = (bf16[128,2048]{1,0:T(8,128)(2,1)}, bf16[128,2048]{1,0:T(8,128)(2,1)S(1)}, u32[]{:S(2)}, u32[]{:S(2)}) collective-permute-start(bf16[128,2048]{1,0:T(8,128)(2,1)} %bitcast.9), channel_id=1, source_target_pairs={{0,8},{4,12},{8,0},{12,4},{16,24},{20,28},{24,16},{28,20},{1,9},{5... | collective-permute-start | bytes 1572872 | tf_op jit(solution)/shard_map/ppermute | solution.py:424
  2.9 1.5 %collective-permute-start.1 = (bf16[128,2048]{1,0:T(8,128)(2,1)}, bf16[128,2048]{1,0:T(8,128)(2,1)S(1)}, u32[]{:S(2)}, u32[]{:S(2)}) collective-permute-start(bf16[128,2048]{1,0:T(8,128)(2,1)} %bitcast.10), channel_id=1, source_target_pairs={{0,16},{4,20},{8,24},{12,28},{16,0},{20,4},{24,8},{28,12},{1,17},{... | collective-permute-start | bytes 1572872 | tf_op jit(solution)/shard_map/ppermute | solution.py:424
  4.5 11.4 %attend.1 = (bf16[144,2048]{1,0:T(8,128)(2,1)}, bf16[128,1024]{1,0:T(8,128)(2,1)}, bf16[128,1024]{1,0:T(8,128)(2,1)}) custom-call(s32[128]{0:T(128)} %lengths_ref.1, s32[1]{0:T(128)} %bitcast.1.me_ref, bf16[128,16,128]{2,1,0:T(8,128)(2,1)} %q_hbm.1, bf16[128,2,128,128]{3,2,1,0:T(8,128)(2,1)} %k_hbm.1, bf16[128,2,128,128]{3,2,1,0:T(8,128)(2,1)} %v_hbm.1, ...), custom_call_target="tpu_custom_call" | custom-call | flops 1 | bytes 1 | tf_op jit(solution)/shard_map/attend/pallas_call | solution.py:204
  15.9 0.0 collective-permute-done.refs_3_
  15.9 0.6 %collective-permute-done.1.refs_4_ = bf16[128,2048]{1,0:T(8,128)(2,1)S(1)} collective-permute-done((bf16[128,2048]{1,0:T(8,128)(2,1)}, bf16[128,2048]{1,0:T(8,128)(2,1)S(1)}, u32[]{:S(2)}, u32[]{:S(2)}) %collective-permute-start.1) | collective-permute-done | bytes 524320 | tf_op jit(solution)/shard_map/ppermute | solution.py:424
  16.5 0.0 collective-permute-start.5
  16.5 1.6 %collective-permute-start.2 = (bf16[128,1024]{1,0:T(8,128)(2,1)}, bf16[128,1024]{1,0:T(8,128)(2,1)S(1)}, u32[]{:S(2)}, u32[]{:S(2)}) collective-permute-start(bf16[128,1024]{1,0:T(8,128)(2,1)} %get-tuple-element.35), channel_id=1, source_target_pairs={{0,1},{1,0},{2,3},{3,2},{4,5},{5,4},{6,7},{7,6},{8,9},{9,8},{10,11... | collective-permute-start | bytes 786440 | tf_op jit(solution)/shard_map/ppermute | solution.py:424
  18.1 1.6 %collective-permute-start.3 = (bf16[64,2048]{1,0:T(8,128)(2,1)S(1)}, bf16[64,2048]{1,0:T(8,128)(2,1)S(1)}, u32[]{:S(2)}, u32[]{:S(2)}) collective-permute-start(bf16[64,2048]{1,0:T(8,128)(2,1)S(1)} %slice.6), channel_id=1, source_target_pairs={{0,16},{4,20},{8,24},{12,28},{16,0},{20,4},{24,8},{28,12},{1,17},{... | collective-permute-start | bytes 786440 | tf_op jit(solution)/shard_map/ppermute | solution.py:424
  19.7 0.6 %collective-permute-start.4 = (bf16[64,2048]{1,0:T(8,128)(2,1)S(1)}, bf16[64,2048]{1,0:T(8,128)(2,1)S(1)}, u32[]{:S(2)}, u32[]{:S(2)}) collective-permute-start(bf16[64,2048]{1,0:T(8,128)(2,1)S(1)} %slice.7), channel_id=1, source_target_pairs={{0,8},{4,12},{8,0},{12,4},{16,24},{20,28},{24,16},{28,20},{1,9},{5... | collective-permute-start | bytes 786440 | tf_op jit(solution)/shard_map/ppermute | solution.py:424
  20.3 0.4 collective-permute-start.6
  20.8 1.1 %copy-done = bf16[144,2048]{1,0:T(8,128)(2,1)S(1)} copy-done((bf16[144,2048]{1,0:T(8,128)(2,1)S(1)}, bf16[144,2048]{1,0:T(8,128)(2,1)}, u32[]{:S(2)}) %copy-start) | copy-done | bytes 589848
  21.9 4.1 %project.1 = (bf16[128,1024]{1,0:T(8,128)(2,1)S(1)}, bf16[128,1024]{1,0:T(8,128)(2,1)S(1)}) custom-call(s32[1]{0:T(128)} %bitcast.1.me_ref, bf16[144,2048]{1,0:T(8,128)(2,1)S(1)} %copy-done, bf16[2048,4096]{1,0:T(8,128)(2,1)} %w_ref.3), custom_call_target="tpu_custom_call" | custom-call | flops 1 | bytes 1 | tf_op jit(solution)/shard_map/project/pallas_call | solution.py:247
  26.0 0.6 %collective-permute-done.3.refs_5_ = bf16[64,2048]{1,0:T(8,128)(2,1)S(1)} collective-permute-done((bf16[64,2048]{1,0:T(8,128)(2,1)S(1)}, bf16[64,2048]{1,0:T(8,128)(2,1)S(1)}, u32[]{:S(2)}, u32[]{:S(2)}) %collective-permute-start.3) | collective-permute-done | bytes 262176 | tf_op jit(solution)/shard_map/ppermute | solution.py:424
  26.6 1.3 %collective-permute-done.4.refs_6_ = bf16[64,2048]{1,0:T(8,128)(2,1)S(1)} collective-permute-done((bf16[64,2048]{1,0:T(8,128)(2,1)S(1)}, bf16[64,2048]{1,0:T(8,128)(2,1)S(1)}, u32[]{:S(2)}, u32[]{:S(2)}) %collective-permute-start.4) | collective-permute-done | bytes 262176 | tf_op jit(solution)/shard_map/ppermute | solution.py:424
  28.0 0.8 %add_convert_fusion = bf16[128,1024]{1,0:T(8,128)(2,1)} fusion(bf16[128,1024]{1,0:T(8,128)(2,1)S(1)} %collective-permute-done.2, bf16[128,1024]{1,0:T(8,128)(2,1)S(1)} %get-tuple-element.49), kind=kLoop, calls=%fused_computation | loop fusion | flops 524288 | bytes 786432 | tf_op jit(solution)/shard_map/convert_element_type | solution.py:524
  28.8 2.6 %collective-permute-start.8 = (bf16[128,1024]{1,0:T(8,128)(2,1)}, bf16[128,1024]{1,0:T(8,128)(2,1)}, u32[]{:S(2)}, u32[]{:S(2)}) collective-permute-start(bf16[128,1024]{1,0:T(8,128)(2,1)} %add_convert_fusion), channel_id=1, source_target_pairs={{0,2},{1,3},{2,0},{3,1},{4,6},{5,7},{6,4},{7,5},{8,10},{9,11},{10,... | collective-permute-start | bytes 786440 | tf_op jit(solution)/shard_map/ppermute | solution.py:424
  31.4 0.9 %copy-done.5 = bf16[64,2048]{1,0:T(8,128)(2,1)S(1)} copy-done((bf16[64,2048]{1,0:T(8,128)(2,1)S(1)}, bf16[64,2048]{1,0:T(8,128)(2,1)}, u32[]{:S(2)}) %copy-start.5) | copy-done | bytes 262168
  32.3 0.9 %copy-done.7 = bf16[64,2048]{1,0:T(8,128)(2,1)S(1)} copy-done((bf16[64,2048]{1,0:T(8,128)(2,1)S(1)}, bf16[64,2048]{1,0:T(8,128)(2,1)}, u32[]{:S(2)}) %copy-start.7) | copy-done | bytes 262168
  33.3 2.5 %low_rank.1 = (bf16[64,256]{1,0:T(8,128)(2,1)S(1)}, s32[8,256]{1,0:T(8,128)S(1)}) custom-call(s32[1]{0:T(128)} %bitcast.7.here_ref, bf16[144,2048]{1,0:T(8,128)(2,1)S(1)} %copy-done.1, bf16[144,2048]{1,0:T(8,128)(2,1)S(1)} %collective-permute-done.5.refs_1_, bf16[128,2048]{1,0:T(8,128)(2,1)S(1)} %bitcast.11, ...), custom_call_target="tpu_custom_call" | custom-call | flops 1 | bytes 1 | tf_op jit(solution)/shard_map/low_rank/pallas_call | solution.py:329
  35.8 0.5 collective-permute-start.7
  36.3 0.8 %collective-permute-start.10 = (bf16[128,1024]{1,0:T(8,128)(2,1)S(1)}, bf16[128,1024]{1,0:T(8,128)(2,1)S(1)}, u32[]{:S(2)}, u32[]{:S(2)}) collective-permute-start(bf16[128,1024]{1,0:T(8,128)(2,1)S(1)} %bitcast.12), channel_id=1, source_target_pairs={{0,8},{4,12},{8,0},{12,4},{16,24},{20,28},{24,16},{28,20},{1,9},{5... | collective-permute-start | bytes 786440 | tf_op jit(solution)/shard_map/ppermute | solution.py:424
  37.1 0.5 collective-permute-start.11
  37.6 2.2 %collective-permute-start.12 = (bf16[128,1024]{1,0:T(8,128)(2,1)S(1)}, bf16[128,1024]{1,0:T(8,128)(2,1)S(1)}, u32[]{:S(2)}, u32[]{:S(2)}) collective-permute-start(bf16[128,1024]{1,0:T(8,128)(2,1)S(1)} %bitcast.14), channel_id=1, source_target_pairs={{0,24},{4,28},{8,16},{12,20},{16,8},{20,12},{24,0},{28,4},{1,25},{... | collective-permute-start | bytes 786440 | tf_op jit(solution)/shard_map/ppermute | solution.py:424
  39.8 3.3 %collective-permute-done.7 = bf16[64,256]{1,0:T(8,128)(2,1)S(1)} collective-permute-done((bf16[64,256]{1,0:T(8,128)(2,1)S(1)}, bf16[64,256]{1,0:T(8,128)(2,1)S(1)}, u32[]{:S(2)}, u32[]{:S(2)}) %collective-permute-start.7) | collective-permute-done | bytes 32800 | tf_op jit(solution)/shard_map/ppermute | solution.py:424
  43.2 0.0 collective-permute-done.8.refs_1_
  43.2 0.1 collective-permute-start.9
  43.2 4.8 %collective-permute-done.9 = bf16[64,256]{1,0:T(8,128)(2,1)S(1)} collective-permute-done((bf16[64,256]{1,0:T(8,128)(2,1)S(1)}, bf16[64,256]{1,0:T(8,128)(2,1)S(1)}, u32[]{:S(2)}, u32[]{:S(2)}) %collective-permute-start.9) | collective-permute-done | bytes 32800 | tf_op jit(solution)/shard_map/ppermute | solution.py:424
  48.1 1.4 %collective-permute-done.11.refs_2_ = bf16[128,1024]{1,0:T(8,128)(2,1)S(1)} collective-permute-done((bf16[128,1024]{1,0:T(8,128)(2,1)S(1)}, bf16[128,1024]{1,0:T(8,128)(2,1)S(1)}, u32[]{:S(2)}, u32[]{:S(2)}) %collective-permute-start.11) | collective-permute-done | bytes 262176 | tf_op jit(solution)/shard_map/ppermute | solution.py:424
  49.5 0.7 %correct.1 = (bf16[128,1024]{1,0:T(8,128)(2,1)S(1)}, bf16[128,1024]{1,0:T(8,128)(2,1)S(1)}) custom-call(s32[1]{0:T(128)} %bitcast.7.here_ref, s32[8,256]{1,0:T(8,128)S(1)} %get-tuple-element.52.adapters_ref, bf16[64,256]{1,0:T(8,128)(2,1)S(1)} %add_convert_fusion.1.low_ref, bf16[128,1024]{1,0:T(8,128)(2,1)S(1)} %bitcast.15, ...), custom_call_target="tpu_custom_call" | custom-call | flops 1 | bytes 1 | tf_op jit(solution)/shard_map/correct/pallas_call | solution.py:380
  50.2 0.1 collective-permute-start.13
  50.3 1.5 %collective-permute-done.13.refs_3_ = bf16[128,1024]{1,0:T(8,128)(2,1)S(1)} collective-permute-done((bf16[128,1024]{1,0:T(8,128)(2,1)S(1)}, bf16[128,1024]{1,0:T(8,128)(2,1)S(1)}, u32[]{:S(2)}, u32[]{:S(2)}) %collective-permute-start.13) | collective-permute-done | bytes 262176 | tf_op jit(solution)/shard_map/ppermute | solution.py:424
  51.8 1.9 %finish.1 = bf16[128,1024]{1,0:T(8,128)(2,1)} custom-call(s32[1,128]{1,0:T(1,128)S(1)} %bitcast.16, bf16[128,1024]{1,0:T(8,128)(2,1)S(1)} %get-tuple-element.33.own_ref, bf16[128,1024]{1,0:T(8,128)(2,1)S(1)} %collective-permute-done.6.refs_0_, bf16[128,1024]{1,0:T(8,128)(2,1)} %collective-permute-done.8.refs_1_, ...), custom_call_target="tpu_custom_call" | custom-call | flops 1 | bytes 1 | tf_op jit(solution)/shard_map/finish/pallas_call | solution.py:411
  (24 shorter events, 0.1 us)
Async XLA Ops:
  0.0 15.9 %collective-permute-start = (bf16[128,2048]{1,0:T(8,128)(2,1)}, bf16[128,2048]{1,0:T(8,128)(2,1)S(1)}, u32[]{:S(2)}, u32[]{:S(2)}) collective-permute-start(bf16[128,2048]{1,0:T(8,128)(2,1)} %bitcast.9), channel_id=1, source_target_pairs={{0,8},{4,12},{8,0},{12,4},{16,24},{20,28},{24,16},{28,20},{1,9},{5... | collective-permute-start | bytes 1572872 | tf_op jit(solution)/shard_map/ppermute | solution.py:424
  2.9 13.6 %collective-permute-start.1 = (bf16[128,2048]{1,0:T(8,128)(2,1)}, bf16[128,2048]{1,0:T(8,128)(2,1)S(1)}, u32[]{:S(2)}, u32[]{:S(2)}) collective-permute-start(bf16[128,2048]{1,0:T(8,128)(2,1)} %bitcast.10), channel_id=1, source_target_pairs={{0,16},{4,20},{8,24},{12,28},{16,0},{20,4},{24,8},{28,12},{1,17},{... | collective-permute-start | bytes 1572872 | tf_op jit(solution)/shard_map/ppermute | solution.py:424
  16.5 14.8 %collective-permute-start.5 = (bf16[144,2048]{1,0:T(8,128)(2,1)}, bf16[144,2048]{1,0:T(8,128)(2,1)S(1)}, u32[]{:S(2)}, u32[]{:S(2)}) collective-permute-start(bf16[144,2048]{1,0:T(8,128)(2,1)} %get-tuple-element.39.a_hbm.refs_0_), channel_id=1, source_target_pairs={{0,4},{4,0},{8,12},{12,8},{16,20},{20,16},{24,28},{28,24},{1,5},{5... | collective-permute-start | bytes 1769480 | tf_op jit(solution)/shard_map/ppermute | solution.py:424
  16.5 9.5 %collective-permute-start.2 = (bf16[128,1024]{1,0:T(8,128)(2,1)}, bf16[128,1024]{1,0:T(8,128)(2,1)S(1)}, u32[]{:S(2)}, u32[]{:S(2)}) collective-permute-start(bf16[128,1024]{1,0:T(8,128)(2,1)} %get-tuple-element.35), channel_id=1, source_target_pairs={{0,1},{1,0},{2,3},{3,2},{4,5},{5,4},{6,7},{7,6},{8,9},{9,8},{10,11... | collective-permute-start | bytes 786440 | tf_op jit(solution)/shard_map/ppermute | solution.py:424
  18.1 8.5 %collective-permute-start.3 = (bf16[64,2048]{1,0:T(8,128)(2,1)S(1)}, bf16[64,2048]{1,0:T(8,128)(2,1)S(1)}, u32[]{:S(2)}, u32[]{:S(2)}) collective-permute-start(bf16[64,2048]{1,0:T(8,128)(2,1)S(1)} %slice.6), channel_id=1, source_target_pairs={{0,16},{4,20},{8,24},{12,28},{16,0},{20,4},{24,8},{28,12},{1,17},{... | collective-permute-start | bytes 786440 | tf_op jit(solution)/shard_map/ppermute | solution.py:424
  19.7 8.2 %collective-permute-start.4 = (bf16[64,2048]{1,0:T(8,128)(2,1)S(1)}, bf16[64,2048]{1,0:T(8,128)(2,1)S(1)}, u32[]{:S(2)}, u32[]{:S(2)}) collective-permute-start(bf16[64,2048]{1,0:T(8,128)(2,1)S(1)} %slice.7), channel_id=1, source_target_pairs={{0,8},{4,12},{8,0},{12,4},{16,24},{20,28},{24,16},{28,20},{1,9},{5... | collective-permute-start | bytes 786440 | tf_op jit(solution)/shard_map/ppermute | solution.py:424
  20.3 15.5 %collective-permute-start.6 = (bf16[128,1024]{1,0:T(8,128)(2,1)}, bf16[128,1024]{1,0:T(8,128)(2,1)S(1)}, u32[]{:S(2)}, u32[]{:S(2)}) collective-permute-start(bf16[128,1024]{1,0:T(8,128)(2,1)} %get-tuple-element.46), channel_id=1, source_target_pairs={{0,1},{1,0},{2,3},{3,2},{4,5},{5,4},{6,7},{7,6},{8,9},{9,8},{10,11... | collective-permute-start | bytes 786440 | tf_op jit(solution)/shard_map/ppermute | solution.py:424
  20.8 1.1 %copy-start = (bf16[144,2048]{1,0:T(8,128)(2,1)S(1)}, bf16[144,2048]{1,0:T(8,128)(2,1)}, u32[]{:S(2)}) copy-start(bf16[144,2048]{1,0:T(8,128)(2,1)} %get-tuple-element.39.a_hbm.refs_0_) | copy-start | bytes 1769476
  21.9 9.5 %copy-start.1 = (bf16[144,2048]{1,0:T(8,128)(2,1)S(1)}, bf16[144,2048]{1,0:T(8,128)(2,1)}, u32[]{:S(2)}) copy-start(bf16[144,2048]{1,0:T(8,128)(2,1)} %get-tuple-element.39.a_hbm.refs_0_) | copy-start | bytes 1769476
  21.9 9.5 %copy-start.2 = (bf16[2,2048,64]{1,2,0:T(8,128)(2,1)S(1)}, bf16[2,2048,64]{1,2,0:T(8,128)(2,1)}, u32[]{:S(2)}) copy-start(bf16[2,2048,64]{1,2,0:T(8,128)(2,1)} %param.22) | copy-start | bytes 1572868
  21.9 14.5 %copy-start.3 = (bf16[2,64,1024]{2,1,0:T(8,128)(2,1)S(1)}, bf16[2,64,1024]{2,1,0:T(8,128)(2,1)}, u32[]{:S(2)}) copy-start(bf16[2,64,1024]{2,1,0:T(8,128)(2,1)} %param.23) | copy-start | bytes 786436
  21.9 29.9 %copy-start.8 = (s32[128]{0:T(128)S(1)}, s32[128]{0:T(128)}, u32[]{:S(2)}) copy-start(s32[128]{0:T(128)} %param.18) | copy-start | bytes 1540
  26.6 2.1 %copy-start.4 = (bf16[64,2048]{1,0:T(8,128)(2,1)}, bf16[64,2048]{1,0:T(8,128)(2,1)S(1)}, u32[]{:S(2)}) copy-start(bf16[64,2048]{1,0:T(8,128)(2,1)S(1)} %collective-permute-done.3.refs_5_) | copy-start | bytes 786436
  28.0 0.8 %copy-start.6 = (bf16[64,2048]{1,0:T(8,128)(2,1)}, bf16[64,2048]{1,0:T(8,128)(2,1)S(1)}, u32[]{:S(2)}) copy-start(bf16[64,2048]{1,0:T(8,128)(2,1)S(1)} %collective-permute-done.4.refs_6_) | copy-start | bytes 786436
  28.8 14.4 %collective-permute-start.8 = (bf16[128,1024]{1,0:T(8,128)(2,1)}, bf16[128,1024]{1,0:T(8,128)(2,1)}, u32[]{:S(2)}, u32[]{:S(2)}) collective-permute-start(bf16[128,1024]{1,0:T(8,128)(2,1)} %add_convert_fusion), channel_id=1, source_target_pairs={{0,2},{1,3},{2,0},{3,1},{4,6},{5,7},{6,4},{7,5},{8,10},{9,11},{10,... | collective-permute-start | bytes 786440 | tf_op jit(solution)/shard_map/ppermute | solution.py:424
  31.4 1.0 %copy-start.5 = (bf16[64,2048]{1,0:T(8,128)(2,1)S(1)}, bf16[64,2048]{1,0:T(8,128)(2,1)}, u32[]{:S(2)}) copy-start(bf16[64,2048]{1,0:T(8,128)(2,1)} %copy-done.4) | copy-start | bytes 786436
  32.3 0.9 %copy-start.7 = (bf16[64,2048]{1,0:T(8,128)(2,1)S(1)}, bf16[64,2048]{1,0:T(8,128)(2,1)}, u32[]{:S(2)}) copy-start(bf16[64,2048]{1,0:T(8,128)(2,1)} %copy-done.6) | copy-start | bytes 786436
  35.8 7.3 %collective-permute-start.7 = (bf16[64,256]{1,0:T(8,128)(2,1)S(1)}, bf16[64,256]{1,0:T(8,128)(2,1)S(1)}, u32[]{:S(2)}, u32[]{:S(2)}) collective-permute-start(bf16[64,256]{1,0:T(8,128)(2,1)S(1)} %get-tuple-element.48), channel_id=1, source_target_pairs={{0,1},{1,0},{2,3},{3,2},{4,5},{5,4},{6,7},{7,6},{8,9},{9,8},{10,11... | collective-permute-start | bytes 98312 | tf_op jit(solution)/shard_map/ppermute | solution.py:424
  36.3 11.7 %collective-permute-start.10 = (bf16[128,1024]{1,0:T(8,128)(2,1)S(1)}, bf16[128,1024]{1,0:T(8,128)(2,1)S(1)}, u32[]{:S(2)}, u32[]{:S(2)}) collective-permute-start(bf16[128,1024]{1,0:T(8,128)(2,1)S(1)} %bitcast.12), channel_id=1, source_target_pairs={{0,8},{4,12},{8,0},{12,4},{16,24},{20,28},{24,16},{28,20},{1,9},{5... | collective-permute-start | bytes 786440 | tf_op jit(solution)/shard_map/ppermute | solution.py:424
  37.1 12.4 %collective-permute-start.11 = (bf16[128,1024]{1,0:T(8,128)(2,1)S(1)}, bf16[128,1024]{1,0:T(8,128)(2,1)S(1)}, u32[]{:S(2)}, u32[]{:S(2)}) collective-permute-start(bf16[128,1024]{1,0:T(8,128)(2,1)S(1)} %bitcast.13), channel_id=1, source_target_pairs={{0,16},{4,20},{8,24},{12,28},{16,0},{20,4},{24,8},{28,12},{1,17},{... | collective-permute-start | bytes 786440 | tf_op jit(solution)/shard_map/ppermute | solution.py:424
  37.6 11.9 %collective-permute-start.12 = (bf16[128,1024]{1,0:T(8,128)(2,1)S(1)}, bf16[128,1024]{1,0:T(8,128)(2,1)S(1)}, u32[]{:S(2)}, u32[]{:S(2)}) collective-permute-start(bf16[128,1024]{1,0:T(8,128)(2,1)S(1)} %bitcast.14), channel_id=1, source_target_pairs={{0,24},{4,28},{8,16},{12,20},{16,8},{20,12},{24,0},{28,4},{1,25},{... | collective-permute-start | bytes 786440 | tf_op jit(solution)/shard_map/ppermute | solution.py:424
  43.2 4.9 %collective-permute-start.9 = (bf16[64,256]{1,0:T(8,128)(2,1)S(1)}, bf16[64,256]{1,0:T(8,128)(2,1)S(1)}, u32[]{:S(2)}, u32[]{:S(2)}) collective-permute-start(bf16[64,256]{1,0:T(8,128)(2,1)S(1)} %add_convert_fusion.2), channel_id=1, source_target_pairs={{0,2},{1,3},{2,0},{3,1},{4,6},{5,7},{6,4},{7,5},{8,10},{9,11},{10,... | collective-permute-start | bytes 98312 | tf_op jit(solution)/shard_map/ppermute | solution.py:424
  50.2 1.6 %collective-permute-start.13 = (bf16[128,1024]{1,0:T(8,128)(2,1)S(1)}, bf16[128,1024]{1,0:T(8,128)(2,1)S(1)}, u32[]{:S(2)}, u32[]{:S(2)}) collective-permute-start(bf16[128,1024]{1,0:T(8,128)(2,1)S(1)} %get-tuple-element.56), channel_id=1, source_target_pairs={{0,4},{4,0},{8,12},{12,8},{16,20},{20,16},{24,28},{28,24},{1,5},{5... | collective-permute-start | bytes 786440 | tf_op jit(solution)/shard_map/ppermute | solution.py:424

commit v11 on v10

--- a/solution.py
+++ b/solution.py
@@ -419,6 +419,24 @@
     )(occupied.reshape(1, rows), own, *parts)
 
 
+def add_kernel(a_ref, b_ref, out_ref):
+    total = a_ref[...].astype(jnp.float32) + b_ref[...].astype(jnp.float32)
+    out_ref[...] = total.astype(out_ref.dtype)
+
+
+def add(a, b):
+    vmem = pl.BlockSpec(memory_space=pltpu.VMEM)
+    return pl.pallas_call(
+        add_kernel,
+        in_specs=[vmem, vmem],
+        out_specs=vmem,
+        out_shape=jax.ShapeDtypeStruct(a.shape, a.dtype),
+        compiler_params=pltpu.CompilerParams(vmem_limit_bytes=16 * MIB),
+        cost_estimate=SMALL,
+        name="add",
+    )(a, b)
+
+
 def exchange(value, axis, step):
     count = lax.axis_size(axis)
     return lax.ppermute(value, axis, [(i, i ^ step) for i in range(count)])
@@ -520,8 +538,7 @@
     )
     expand = direct_blocks(expand)
     if halved:
-        passed = received.pop(0).astype(jnp.float32)
-        pieces = [(pieces[0].astype(jnp.float32) + passed).astype(jnp.bfloat16)]
+        pieces = [add(pieces[0], received.pop(0))]
     last = [exchange(part, "mp", step) for part, step in zip(pieces, late)]
 
     keys = tuple(shrink)

time: 54 us -> 55.6 us (1.030)
  local copies, waits for them, and re-layouts: 3.01 us -> 5.3 us
  other arithmetic: 0.81 us -> 0.02 us
    unnamed x18 -> x22, local copies, waits for them, and re-layouts: 2.98 us -> 5.26 us
    convert_element_type x1 -> x0, other arithmetic: 0.79 us -> none  [body(): pieces = [(pieces[0].astype(jnp.float32) + passed).astype(jnp.bfloat16)]]
  transfers between devices with their start and end apart: 14 -> 14, of which waited for: 7 -> 7; matrix products, arithmetic and copies ran while one was open for 2% -> 0% of each run, Pallas kernels for 34% -> 33%
where the time goes in v11:
time: 55.6 us; the launch traced here: 55.3 us
  Pallas kernels  20.8 us (37%)
  starting transfers between devices  15.4 us (28%)
  waiting for transfers between devices  13.6 us (24%)
  local copies, waits for them, and re-layouts  5.3 us (10%)
    ppermute x14, starting transfers between devices, exchange(): return lax.ppermute(value, axis, [(i, i ^ step) for i in range(count)])  15.4 us
    ppermute x14, waiting for transfers between devices, exchange(): return lax.ppermute(value, axis, [(i, i ^ step) for i in range(count)])  13.6 us
    pallas_call x1, Pallas kernels, attend(): pl.pallas_call(functools.partial(attend_kernel, block, steps), in_specs=[...  11.4 us
    unnamed x22, local copies, waits for them, and re-layouts  5.26 us
    pallas_call x1, Pallas kernels, project(): pl.pallas_call(functools.partial(project_kernel, steps), in_specs=[pl.Blo...  4.12 us
    pallas_call x1, Pallas kernels, low_rank(): pl.pallas_call(functools.partial(low_kernel, rank, places, keys), in_spec...  2.54 us
    pallas_call x1, Pallas kernels, finish(): pl.pallas_call(finish_kernel, in_specs=[vmem] * (2 + len(parts)), out_spe...  1.94 us
  transfers between devices with their start and end apart: 14, of which 7 were waited for; matrix products, arithmetic and copies ran while one was open for 0% of the time, Pallas kernels for 33%

profile of v11, /device:TPU:0, one launch (start us, length us, event | category | flops | bytes accessed | tf_op | source)
XLA Modules:
  0.0 55.3 jit_solution(5644092478481152747)
XLA Ops:
  0.0 2.9 %collective-permute-start = (bf16[128,2048]{1,0:T(8,128)(2,1)}, bf16[128,2048]{1,0:T(8,128)(2,1)S(1)}, u32[]{:S(2)}, u32[]{:S(2)}) collective-permute-start(bf16[128,2048]{1,0:T(8,128)(2,1)} %bitcast.9), channel_id=1, source_target_pairs={{0,8},{4,12},{8,0},{12,4},{16,24},{20,28},{24,16},{28,20},{1,9},{5... | collective-permute-start | bytes 1572872 | tf_op jit(solution)/shard_map/ppermute | solution.py:442
  2.9 1.5 %collective-permute-start.1 = (bf16[128,2048]{1,0:T(8,128)(2,1)}, bf16[128,2048]{1,0:T(8,128)(2,1)S(1)}, u32[]{:S(2)}, u32[]{:S(2)}) collective-permute-start(bf16[128,2048]{1,0:T(8,128)(2,1)} %bitcast.10), channel_id=1, source_target_pairs={{0,16},{4,20},{8,24},{12,28},{16,0},{20,4},{24,8},{28,12},{1,17},{... | collective-permute-start | bytes 1572872 | tf_op jit(solution)/shard_map/ppermute | solution.py:442
  4.5 11.4 %attend.1 = (bf16[144,2048]{1,0:T(8,128)(2,1)}, bf16[128,1024]{1,0:T(8,128)(2,1)}, bf16[128,1024]{1,0:T(8,128)(2,1)}) custom-call(s32[128]{0:T(128)} %lengths_ref.1, s32[1]{0:T(128)} %bitcast.1.me_ref, bf16[128,16,128]{2,1,0:T(8,128)(2,1)} %q_hbm.1, bf16[128,2,128,128]{3,2,1,0:T(8,128)(2,1)} %k_hbm.1, bf16[128,2,128,128]{3,2,1,0:T(8,128)(2,1)} %v_hbm.1, ...), custom_call_target="tpu_custom_call" | custom-call | flops 1 | bytes 1 | tf_op jit(solution)/shard_map/attend/pallas_call | solution.py:204
  15.9 0.6 %collective-permute-done.1.refs_4_ = bf16[128,2048]{1,0:T(8,128)(2,1)S(1)} collective-permute-done((bf16[128,2048]{1,0:T(8,128)(2,1)}, bf16[128,2048]{1,0:T(8,128)(2,1)S(1)}, u32[]{:S(2)}, u32[]{:S(2)}) %collective-permute-start.1) | collective-permute-done | bytes 524320 | tf_op jit(solution)/shard_map/ppermute | solution.py:442
  16.5 1.6 %collective-permute-start.2 = (bf16[128,1024]{1,0:T(8,128)(2,1)}, bf16[128,1024]{1,0:T(8,128)(2,1)S(1)}, u32[]{:S(2)}, u32[]{:S(2)}) collective-permute-start(bf16[128,1024]{1,0:T(8,128)(2,1)} %get-tuple-element.35), channel_id=1, source_target_pairs={{0,1},{1,0},{2,3},{3,2},{4,5},{5,4},{6,7},{7,6},{8,9},{9,8},{10,11... | collective-permute-start | bytes 786440 | tf_op jit(solution)/shard_map/ppermute | solution.py:442
  18.1 1.6 %collective-permute-start.3 = (bf16[64,2048]{1,0:T(8,128)(2,1)S(1)}, bf16[64,2048]{1,0:T(8,128)(2,1)S(1)}, u32[]{:S(2)}, u32[]{:S(2)}) collective-permute-start(bf16[64,2048]{1,0:T(8,128)(2,1)S(1)} %slice.6), channel_id=1, source_target_pairs={{0,16},{4,20},{8,24},{12,28},{16,0},{20,4},{24,8},{28,12},{1,17},{... | collective-permute-start | bytes 786440 | tf_op jit(solution)/shard_map/ppermute | solution.py:442
  19.7 0.6 %collective-permute-start.4 = (bf16[64,2048]{1,0:T(8,128)(2,1)S(1)}, bf16[64,2048]{1,0:T(8,128)(2,1)S(1)}, u32[]{:S(2)}, u32[]{:S(2)}) collective-permute-start(bf16[64,2048]{1,0:T(8,128)(2,1)S(1)} %slice.7), channel_id=1, source_target_pairs={{0,8},{4,12},{8,0},{12,4},{16,24},{20,28},{24,16},{28,20},{1,9},{5... | collective-permute-start | bytes 786440 | tf_op jit(solution)/shard_map/ppermute | solution.py:442
  20.3 0.4 collective-permute-start.6
  20.8 1.1 %copy-done = bf16[144,2048]{1,0:T(8,128)(2,1)S(1)} copy-done((bf16[144,2048]{1,0:T(8,128)(2,1)S(1)}, bf16[144,2048]{1,0:T(8,128)(2,1)}, u32[]{:S(2)}) %copy-start) | copy-done | bytes 589848
  21.9 4.1 %project.1 = (bf16[128,1024]{1,0:T(8,128)(2,1)S(1)}, bf16[128,1024]{1,0:T(8,128)(2,1)S(1)}) custom-call(s32[1]{0:T(128)} %bitcast.1.me_ref, bf16[144,2048]{1,0:T(8,128)(2,1)S(1)} %copy-done, bf16[2048,4096]{1,0:T(8,128)(2,1)} %w_ref.3), custom_call_target="tpu_custom_call" | custom-call | flops 1 | bytes 1 | tf_op jit(solution)/shard_map/project/pallas_call | solution.py:247
  26.0 0.6 %collective-permute-done.3.refs_5_ = bf16[64,2048]{1,0:T(8,128)(2,1)S(1)} collective-permute-done((bf16[64,2048]{1,0:T(8,128)(2,1)S(1)}, bf16[64,2048]{1,0:T(8,128)(2,1)S(1)}, u32[]{:S(2)}, u32[]{:S(2)}) %collective-permute-start.3) | collective-permute-done | bytes 262176 | tf_op jit(solution)/shard_map/ppermute | solution.py:442
  26.6 0.7 %copy-done.6 = bf16[64,2048]{1,0:T(8,128)(2,1)} copy-done((bf16[64,2048]{1,0:T(8,128)(2,1)}, bf16[64,2048]{1,0:T(8,128)(2,1)S(1)}, u32[]{:S(2)}) %copy-start.6) | copy-done | bytes 262168
  27.3 0.6 %collective-permute-done.4.refs_6_ = bf16[64,2048]{1,0:T(8,128)(2,1)S(1)} collective-permute-done((bf16[64,2048]{1,0:T(8,128)(2,1)S(1)}, bf16[64,2048]{1,0:T(8,128)(2,1)S(1)}, u32[]{:S(2)}, u32[]{:S(2)}) %collective-permute-start.4) | collective-permute-done | bytes 262176 | tf_op jit(solution)/shard_map/ppermute | solution.py:442
  28.0 0.1 add.11
  28.0 0.6 %copy-done.8 = bf16[64,2048]{1,0:T(8,128)(2,1)} copy-done((bf16[64,2048]{1,0:T(8,128)(2,1)}, bf16[64,2048]{1,0:T(8,128)(2,1)S(1)}, u32[]{:S(2)}) %copy-start.8) | copy-done | bytes 262168
  28.7 2.6 %collective-permute-start.8 = (bf16[128,1024]{1,0:T(8,128)(2,1)S(1)}, bf16[128,1024]{1,0:T(8,128)(2,1)}, u32[]{:S(2)}, u32[]{:S(2)}) collective-permute-start(bf16[128,1024]{1,0:T(8,128)(2,1)S(1)} %add.11), channel_id=1, source_target_pairs={{0,2},{1,3},{2,0},{3,1},{4,6},{5,7},{6,4},{7,5},{8,10},{9,11},{10,... | collective-permute-start | bytes 786440 | tf_op jit(solution)/shard_map/ppermute | solution.py:442
  31.3 0.9 %copy-done.7 = bf16[64,2048]{1,0:T(8,128)(2,1)S(1)} copy-done((bf16[64,2048]{1,0:T(8,128)(2,1)S(1)}, bf16[64,2048]{1,0:T(8,128)(2,1)}, u32[]{:S(2)}) %copy-start.7) | copy-done | bytes 262168
  32.2 0.9 %copy-done.9 = bf16[64,2048]{1,0:T(8,128)(2,1)S(1)} copy-done((bf16[64,2048]{1,0:T(8,128)(2,1)S(1)}, bf16[64,2048]{1,0:T(8,128)(2,1)}, u32[]{:S(2)}) %copy-start.9) | copy-done | bytes 262168
  33.2 2.5 %low_rank.1 = (bf16[64,256]{1,0:T(8,128)(2,1)S(1)}, s32[8,256]{1,0:T(8,128)S(1)}) custom-call(s32[1]{0:T(128)} %bitcast.7.here_ref, bf16[144,2048]{1,0:T(8,128)(2,1)S(1)} %copy-done.1, bf16[144,2048]{1,0:T(8,128)(2,1)S(1)} %collective-permute-done.5.refs_1_, bf16[128,2048]{1,0:T(8,128)(2,1)S(1)} %bitcast.11, ...), custom_call_target="tpu_custom_call" | custom-call | flops 1 | bytes 1 | tf_op jit(solution)/shard_map/low_rank/pallas_call | solution.py:329
  35.7 0.5 collective-permute-start.7
  36.3 1.5 %collective-permute-start.10 = (bf16[128,1024]{1,0:T(8,128)(2,1)S(1)}, bf16[128,1024]{1,0:T(8,128)(2,1)S(1)}, u32[]{:S(2)}, u32[]{:S(2)}) collective-permute-start(bf16[128,1024]{1,0:T(8,128)(2,1)S(1)} %bitcast.12), channel_id=1, source_target_pairs={{0,8},{4,12},{8,0},{12,4},{16,24},{20,28},{24,16},{28,20},{1,9},{5... | collective-permute-start | bytes 786440 | tf_op jit(solution)/shard_map/ppermute | solution.py:442
  37.7 0.5 collective-permute-start.11
  38.2 1.5 %collective-permute-start.12 = (bf16[128,1024]{1,0:T(8,128)(2,1)S(1)}, bf16[128,1024]{1,0:T(8,128)(2,1)S(1)}, u32[]{:S(2)}, u32[]{:S(2)}) collective-permute-start(bf16[128,1024]{1,0:T(8,128)(2,1)S(1)} %bitcast.14), channel_id=1, source_target_pairs={{0,24},{4,28},{8,16},{12,20},{16,8},{20,12},{24,0},{28,4},{1,25},{... | collective-permute-start | bytes 786440 | tf_op jit(solution)/shard_map/ppermute | solution.py:442
  39.7 3.1 %collective-permute-done.7 = bf16[64,256]{1,0:T(8,128)(2,1)S(1)} collective-permute-done((bf16[64,256]{1,0:T(8,128)(2,1)S(1)}, bf16[64,256]{1,0:T(8,128)(2,1)S(1)}, u32[]{:S(2)}, u32[]{:S(2)}) %collective-permute-start.7) | collective-permute-done | bytes 32800 | tf_op jit(solution)/shard_map/ppermute | solution.py:442
  42.9 0.1 collective-permute-start.9
  42.9 4.8 %collective-permute-done.9 = bf16[64,256]{1,0:T(8,128)(2,1)S(1)} collective-permute-done((bf16[64,256]{1,0:T(8,128)(2,1)S(1)}, bf16[64,256]{1,0:T(8,128)(2,1)S(1)}, u32[]{:S(2)}, u32[]{:S(2)}) %collective-permute-start.9) | collective-permute-done | bytes 32800 | tf_op jit(solution)/shard_map/ppermute | solution.py:442
  47.8 2.3 %collective-permute-done.11.refs_2_ = bf16[128,1024]{1,0:T(8,128)(2,1)S(1)} collective-permute-done((bf16[128,1024]{1,0:T(8,128)(2,1)S(1)}, bf16[128,1024]{1,0:T(8,128)(2,1)S(1)}, u32[]{:S(2)}, u32[]{:S(2)}) %collective-permute-start.11) | collective-permute-done | bytes 262176 | tf_op jit(solution)/shard_map/ppermute | solution.py:442
  50.1 0.7 %correct.1 = (bf16[128,1024]{1,0:T(8,128)(2,1)S(1)}, bf16[128,1024]{1,0:T(8,128)(2,1)S(1)}) custom-call(s32[1]{0:T(128)} %bitcast.7.here_ref, s32[8,256]{1,0:T(8,128)S(1)} %get-tuple-element.52.adapters_ref, bf16[64,256]{1,0:T(8,128)(2,1)S(1)} %add_convert_fusion.low_ref, bf16[128,1024]{1,0:T(8,128)(2,1)S(1)} %bitcast.15, ...), custom_call_target="tpu_custom_call" | custom-call | flops 1 | bytes 1 | tf_op jit(solution)/shard_map/correct/pallas_call | solution.py:380
  50.8 0.1 collective-permute-start.13
  50.9 1.5 %collective-permute-done.13.refs_3_ = bf16[128,1024]{1,0:T(8,128)(2,1)S(1)} collective-permute-done((bf16[128,1024]{1,0:T(8,128)(2,1)S(1)}, bf16[128,1024]{1,0:T(8,128)(2,1)S(1)}, u32[]{:S(2)}, u32[]{:S(2)}) %collective-permute-start.13) | collective-permute-done | bytes 262176 | tf_op jit(solution)/shard_map/ppermute | solution.py:442
  52.4 0.9 %copy-done.5 = bf16[128,1024]{1,0:T(8,128)(2,1)S(1)} copy-done((bf16[128,1024]{1,0:T(8,128)(2,1)S(1)}, bf16[128,1024]{1,0:T(8,128)(2,1)}, u32[]{:S(2)}) %copy-start.5) | copy-done | bytes 262168
  53.4 1.9 %finish.1 = bf16[128,1024]{1,0:T(8,128)(2,1)} custom-call(s32[1,128]{1,0:T(1,128)S(1)} %bitcast.16, bf16[128,1024]{1,0:T(8,128)(2,1)S(1)} %copy-done.5, bf16[128,1024]{1,0:T(8,128)(2,1)S(1)} %collective-permute-done.6.refs_0_, bf16[128,1024]{1,0:T(8,128)(2,1)} %collective-permute-done.8.refs_1_, bf16[128,1024]{1,0:T(8,128)(2,1)S(1)} %get-tuple-element.55.refs_2_, ...), custom_call_target="tpu_custom_call" | custom-call | flops 1 | bytes 1 | tf_op jit(solution)/shard_map/finish/pallas_call | solution.py:411
  (28 shorter events, 0.1 us)
Async XLA Ops:
  0.0 15.9 %collective-permute-start = (bf16[128,2048]{1,0:T(8,128)(2,1)}, bf16[128,2048]{1,0:T(8,128)(2,1)S(1)}, u32[]{:S(2)}, u32[]{:S(2)}) collective-permute-start(bf16[128,2048]{1,0:T(8,128)(2,1)} %bitcast.9), channel_id=1, source_target_pairs={{0,8},{4,12},{8,0},{12,4},{16,24},{20,28},{24,16},{28,20},{1,9},{5... | collective-permute-start | bytes 1572872 | tf_op jit(solution)/shard_map/ppermute | solution.py:442
  2.9 13.6 %collective-permute-start.1 = (bf16[128,2048]{1,0:T(8,128)(2,1)}, bf16[128,2048]{1,0:T(8,128)(2,1)S(1)}, u32[]{:S(2)}, u32[]{:S(2)}) collective-permute-start(bf16[128,2048]{1,0:T(8,128)(2,1)} %bitcast.10), channel_id=1, source_target_pairs={{0,16},{4,20},{8,24},{12,28},{16,0},{20,4},{24,8},{28,12},{1,17},{... | collective-permute-start | bytes 1572872 | tf_op jit(solution)/shard_map/ppermute | solution.py:442
  16.5 14.7 %collective-permute-start.5 = (bf16[144,2048]{1,0:T(8,128)(2,1)}, bf16[144,2048]{1,0:T(8,128)(2,1)S(1)}, u32[]{:S(2)}, u32[]{:S(2)}) collective-permute-start(bf16[144,2048]{1,0:T(8,128)(2,1)} %get-tuple-element.39.a_hbm.refs_0_), channel_id=1, source_target_pairs={{0,4},{4,0},{8,12},{12,8},{16,20},{20,16},{24,28},{28,24},{1,5},{5... | collective-permute-start | bytes 1769480 | tf_op jit(solution)/shard_map/ppermute | solution.py:442
  16.5 9.5 %collective-permute-start.2 = (bf16[128,1024]{1,0:T(8,128)(2,1)}, bf16[128,1024]{1,0:T(8,128)(2,1)S(1)}, u32[]{:S(2)}, u32[]{:S(2)}) collective-permute-start(bf16[128,1024]{1,0:T(8,128)(2,1)} %get-tuple-element.35), channel_id=1, source_target_pairs={{0,1},{1,0},{2,3},{3,2},{4,5},{5,4},{6,7},{7,6},{8,9},{9,8},{10,11... | collective-permute-start | bytes 786440 | tf_op jit(solution)/shard_map/ppermute | solution.py:442
  18.1 8.5 %collective-permute-start.3 = (bf16[64,2048]{1,0:T(8,128)(2,1)S(1)}, bf16[64,2048]{1,0:T(8,128)(2,1)S(1)}, u32[]{:S(2)}, u32[]{:S(2)}) collective-permute-start(bf16[64,2048]{1,0:T(8,128)(2,1)S(1)} %slice.6), channel_id=1, source_target_pairs={{0,16},{4,20},{8,24},{12,28},{16,0},{20,4},{24,8},{28,12},{1,17},{... | collective-permute-start | bytes 786440 | tf_op jit(solution)/shard_map/ppermute | solution.py:442
  19.7 8.2 %collective-permute-start.4 = (bf16[64,2048]{1,0:T(8,128)(2,1)S(1)}, bf16[64,2048]{1,0:T(8,128)(2,1)S(1)}, u32[]{:S(2)}, u32[]{:S(2)}) collective-permute-start(bf16[64,2048]{1,0:T(8,128)(2,1)S(1)} %slice.7), channel_id=1, source_target_pairs={{0,8},{4,12},{8,0},{12,4},{16,24},{20,28},{24,16},{28,20},{1,9},{5... | collective-permute-start | bytes 786440 | tf_op jit(solution)/shard_map/ppermute | solution.py:442
  20.3 15.4 %collective-permute-start.6 = (bf16[128,1024]{1,0:T(8,128)(2,1)}, bf16[128,1024]{1,0:T(8,128)(2,1)S(1)}, u32[]{:S(2)}, u32[]{:S(2)}) collective-permute-start(bf16[128,1024]{1,0:T(8,128)(2,1)} %get-tuple-element.46), channel_id=1, source_target_pairs={{0,1},{1,0},{2,3},{3,2},{4,5},{5,4},{6,7},{7,6},{8,9},{9,8},{10,11... | collective-permute-start | bytes 786440 | tf_op jit(solution)/shard_map/ppermute | solution.py:442
  20.8 1.1 %copy-start = (bf16[144,2048]{1,0:T(8,128)(2,1)S(1)}, bf16[144,2048]{1,0:T(8,128)(2,1)}, u32[]{:S(2)}) copy-start(bf16[144,2048]{1,0:T(8,128)(2,1)} %get-tuple-element.39.a_hbm.refs_0_) | copy-start | bytes 1769476
  21.9 9.4 %copy-start.1 = (bf16[144,2048]{1,0:T(8,128)(2,1)S(1)}, bf16[144,2048]{1,0:T(8,128)(2,1)}, u32[]{:S(2)}) copy-start(bf16[144,2048]{1,0:T(8,128)(2,1)} %get-tuple-element.39.a_hbm.refs_0_) | copy-start | bytes 1769476
  21.9 9.4 %copy-start.2 = (bf16[2,2048,64]{1,2,0:T(8,128)(2,1)S(1)}, bf16[2,2048,64]{1,2,0:T(8,128)(2,1)}, u32[]{:S(2)}) copy-start(bf16[2,2048,64]{1,2,0:T(8,128)(2,1)} %param.22) | copy-start | bytes 1572868
  21.9 14.4 %copy-start.3 = (bf16[2,64,1024]{2,1,0:T(8,128)(2,1)S(1)}, bf16[2,64,1024]{2,1,0:T(8,128)(2,1)}, u32[]{:S(2)}) copy-start(bf16[2,64,1024]{2,1,0:T(8,128)(2,1)} %param.23) | copy-start | bytes 786436
  21.9 30.6 %copy-start.10 = (s32[128]{0:T(128)S(1)}, s32[128]{0:T(128)}, u32[]{:S(2)}) copy-start(s32[128]{0:T(128)} %param.18) | copy-start | bytes 1540
  26.0 2.0 %copy-start.4 = (bf16[128,1024]{1,0:T(8,128)(2,1)}, bf16[128,1024]{1,0:T(8,128)(2,1)S(1)}, u32[]{:S(2)}) copy-start(bf16[128,1024]{1,0:T(8,128)(2,1)S(1)} %get-tuple-element.33.own_ref) | copy-start | bytes 786436
  26.6 0.7 %copy-start.6 = (bf16[64,2048]{1,0:T(8,128)(2,1)}, bf16[64,2048]{1,0:T(8,128)(2,1)S(1)}, u32[]{:S(2)}) copy-start(bf16[64,2048]{1,0:T(8,128)(2,1)S(1)} %collective-permute-done.3.refs_5_) | copy-start | bytes 786436
  28.0 0.7 %copy-start.8 = (bf16[64,2048]{1,0:T(8,128)(2,1)}, bf16[64,2048]{1,0:T(8,128)(2,1)S(1)}, u32[]{:S(2)}) copy-start(bf16[64,2048]{1,0:T(8,128)(2,1)S(1)} %collective-permute-done.4.refs_6_) | copy-start | bytes 786436
  28.7 14.2 %collective-permute-start.8 = (bf16[128,1024]{1,0:T(8,128)(2,1)S(1)}, bf16[128,1024]{1,0:T(8,128)(2,1)}, u32[]{:S(2)}, u32[]{:S(2)}) collective-permute-start(bf16[128,1024]{1,0:T(8,128)(2,1)S(1)} %add.11), channel_id=1, source_target_pairs={{0,2},{1,3},{2,0},{3,1},{4,6},{5,7},{6,4},{7,5},{8,10},{9,11},{10,... | collective-permute-start | bytes 786440 | tf_op jit(solution)/shard_map/ppermute | solution.py:442
  31.3 1.0 %copy-start.7 = (bf16[64,2048]{1,0:T(8,128)(2,1)S(1)}, bf16[64,2048]{1,0:T(8,128)(2,1)}, u32[]{:S(2)}) copy-start(bf16[64,2048]{1,0:T(8,128)(2,1)} %copy-done.6) | copy-start | bytes 786436
  32.2 0.9 %copy-start.9 = (bf16[64,2048]{1,0:T(8,128)(2,1)S(1)}, bf16[64,2048]{1,0:T(8,128)(2,1)}, u32[]{:S(2)}) copy-start(bf16[64,2048]{1,0:T(8,128)(2,1)} %copy-done.8) | copy-start | bytes 786436
  35.7 7.1 %collective-permute-start.7 = (bf16[64,256]{1,0:T(8,128)(2,1)S(1)}, bf16[64,256]{1,0:T(8,128)(2,1)S(1)}, u32[]{:S(2)}, u32[]{:S(2)}) collective-permute-start(bf16[64,256]{1,0:T(8,128)(2,1)S(1)} %get-tuple-element.48), channel_id=1, source_target_pairs={{0,1},{1,0},{2,3},{3,2},{4,5},{5,4},{6,7},{7,6},{8,9},{9,8},{10,11... | collective-permute-start | bytes 98312 | tf_op jit(solution)/shard_map/ppermute | solution.py:442
  36.3 11.5 %collective-permute-start.10 = (bf16[128,1024]{1,0:T(8,128)(2,1)S(1)}, bf16[128,1024]{1,0:T(8,128)(2,1)S(1)}, u32[]{:S(2)}, u32[]{:S(2)}) collective-permute-start(bf16[128,1024]{1,0:T(8,128)(2,1)S(1)} %bitcast.12), channel_id=1, source_target_pairs={{0,8},{4,12},{8,0},{12,4},{16,24},{20,28},{24,16},{28,20},{1,9},{5... | collective-permute-start | bytes 786440 | tf_op jit(solution)/shard_map/ppermute | solution.py:442
  37.7 12.4 %collective-permute-start.11 = (bf16[128,1024]{1,0:T(8,128)(2,1)S(1)}, bf16[128,1024]{1,0:T(8,128)(2,1)S(1)}, u32[]{:S(2)}, u32[]{:S(2)}) collective-permute-start(bf16[128,1024]{1,0:T(8,128)(2,1)S(1)} %bitcast.13), channel_id=1, source_target_pairs={{0,16},{4,20},{8,24},{12,28},{16,0},{20,4},{24,8},{28,12},{1,17},{... | collective-permute-start | bytes 786440 | tf_op jit(solution)/shard_map/ppermute | solution.py:442
  38.2 11.9 %collective-permute-start.12 = (bf16[128,1024]{1,0:T(8,128)(2,1)S(1)}, bf16[128,1024]{1,0:T(8,128)(2,1)S(1)}, u32[]{:S(2)}, u32[]{:S(2)}) collective-permute-start(bf16[128,1024]{1,0:T(8,128)(2,1)S(1)} %bitcast.14), channel_id=1, source_target_pairs={{0,24},{4,28},{8,16},{12,20},{16,8},{20,12},{24,0},{28,4},{1,25},{... | collective-permute-start | bytes 786440 | tf_op jit(solution)/shard_map/ppermute | solution.py:442
  42.9 4.9 %collective-permute-start.9 = (bf16[64,256]{1,0:T(8,128)(2,1)S(1)}, bf16[64,256]{1,0:T(8,128)(2,1)S(1)}, u32[]{:S(2)}, u32[]{:S(2)}) collective-permute-start(bf16[64,256]{1,0:T(8,128)(2,1)S(1)} %add_convert_fusion.1), channel_id=1, source_target_pairs={{0,2},{1,3},{2,0},{3,1},{4,6},{5,7},{6,4},{7,5},{8,10},{9,11},{10,... | collective-permute-start | bytes 98312 | tf_op jit(solution)/shard_map/ppermute | solution.py:442
  50.8 1.6 %collective-permute-start.13 = (bf16[128,1024]{1,0:T(8,128)(2,1)S(1)}, bf16[128,1024]{1,0:T(8,128)(2,1)S(1)}, u32[]{:S(2)}, u32[]{:S(2)}) collective-permute-start(bf16[128,1024]{1,0:T(8,128)(2,1)S(1)} %get-tuple-element.56), channel_id=1, source_target_pairs={{0,4},{4,0},{8,12},{12,8},{16,20},{20,16},{24,28},{28,24},{1,5},{5... | collective-permute-start | bytes 786440 | tf_op jit(solution)/shard_map/ppermute | solution.py:442
  52.4 1.0 %copy-start.5 = (bf16[128,1024]{1,0:T(8,128)(2,1)S(1)}, bf16[128,1024]{1,0:T(8,128)(2,1)}, u32[]{:S(2)}) copy-start(bf16[128,1024]{1,0:T(8,128)(2,1)} %copy-done.4) | copy-start | bytes 786436

commit v12 on v7

--- a/solution.py
+++ b/solution.py
@@ -399,7 +399,7 @@
     live = jnp.broadcast_to(occupied_ref[...].astype(jnp.float32), (128, rows)).T
     for j in range(0, out_ref.shape[1], 128):
         columns = slice(j, j + 128)
-        total = own_ref[:, columns]
+        total = own_ref[:, columns].astype(jnp.float32)
         for ref in part_refs:
             total += ref[:, columns].astype(jnp.float32)
         out_ref[:, columns] = (live * total).astype(out_ref.dtype)
@@ -513,7 +513,7 @@
         me,
         late,
         out_local,
-        [jnp.float32 if halved else jnp.bfloat16] * (len(late) - 1) + [jnp.float32],
+        [jnp.bfloat16] * len(late),
     )
     pieces, received[0], attended, shrink, expand = together(
         pieces, received[0], attended, shrink, expand
@@ -521,7 +521,7 @@
     expand = direct_blocks(expand)
     if halved:
         passed = received.pop(0).astype(jnp.float32)
-        pieces = [(pieces[0] + passed).astype(jnp.bfloat16)]
+        pieces = [(pieces[0].astype(jnp.float32) + passed).astype(jnp.bfloat16)]
     last = [exchange(part, "mp", step) for part, step in zip(pieces, late)]
 
     keys = tuple(shrink)
@@ -534,9 +534,9 @@
         arrived = exchange(low, "mp", step)
         low = (low.astype(jnp.float32) + arrived.astype(jnp.float32)).astype(jnp.bfloat16)
         step //= 2
-    low, last = together(low, last)
     blocks = [expand[key] for key in keys]
     correction, other = correct(low, adapters, blocks, 0, out_local, here, keys, rank)
+    other, last = together(other, last)
     parts = [*received, *last, correction, exchange(other, "dp", 1)]
     return finish(own, parts, occupied)
 

time: 53.9 us -> 54 us (level)
  transfers between devices with their start and end apart: 14 -> 14, of which waited for: 6 -> 6; matrix products, arithmetic and copies ran while one was open for 0% -> 0% of each run, Pallas kernels for 34% -> 35%
where the time goes in v12:
time: 54 us; the launch traced here: 53.8 us
  Pallas kernels  19.7 us (36%)
  waiting for transfers between devices  17.4 us (32%)
  starting transfers between devices  15.4 us (29%)
  local copies, waits for them, and re-layouts  1.11 us (2%)
    ppermute x14, waiting for transfers between devices, exchange(): return lax.ppermute(value, axis, [(i, i ^ step) for i in range(count)])  17.4 us
    ppermute x14, starting transfers between devices, exchange(): return lax.ppermute(value, axis, [(i, i ^ step) for i in range(count)])  15.4 us
    pallas_call x1, Pallas kernels, attend(): pl.pallas_call(functools.partial(attend_kernel, block, steps), in_specs=[...  11.4 us
    pallas_call x1, Pallas kernels, project(): pl.pallas_call(functools.partial(project_kernel, steps), in_specs=[pl.Blo...  4.08 us
    pallas_call x1, Pallas kernels, low_rank(): pl.pallas_call(functools.partial(low_kernel, rank, places, keys), in_spec...  2.54 us
  transfers between devices with their start and end apart: 14, of which 6 were waited for; matrix products, arithmetic and copies ran while one was open for 0% of the time, Pallas kernels for 35%

profile of v12, /device:TPU:0, one launch (start us, length us, event | category | flops | bytes accessed | tf_op | source)
XLA Modules:
  0.0 53.8 jit_solution(10731007452608345137)
XLA Ops:
  0.0 2.9 %collective-permute-start = (bf16[128,2048]{1,0:T(8,128)(2,1)}, bf16[128,2048]{1,0:T(8,128)(2,1)S(1)}, u32[]{:S(2)}, u32[]{:S(2)}) collective-permute-start(bf16[128,2048]{1,0:T(8,128)(2,1)} %bitcast.9), channel_id=1, source_target_pairs={{0,8},{4,12},{8,0},{12,4},{16,24},{20,28},{24,16},{28,20},{1,9},{5... | collective-permute-start | bytes 1572872 | tf_op jit(solution)/shard_map/ppermute | solution.py:424
  2.9 1.5 %collective-permute-start.1 = (bf16[128,2048]{1,0:T(8,128)(2,1)}, bf16[128,2048]{1,0:T(8,128)(2,1)S(1)}, u32[]{:S(2)}, u32[]{:S(2)}) collective-permute-start(bf16[128,2048]{1,0:T(8,128)(2,1)} %bitcast.10), channel_id=1, source_target_pairs={{0,16},{4,20},{8,24},{12,28},{16,0},{20,4},{24,8},{28,12},{1,17},{... | collective-permute-start | bytes 1572872 | tf_op jit(solution)/shard_map/ppermute | solution.py:424
  4.5 11.4 %attend.1 = (bf16[144,2048]{1,0:T(8,128)(2,1)}, bf16[128,1024]{1,0:T(8,128)(2,1)}, bf16[128,1024]{1,0:T(8,128)(2,1)}) custom-call(s32[128]{0:T(128)} %lengths_ref.1, s32[1]{0:T(128)} %bitcast.1.me_ref, bf16[128,16,128]{2,1,0:T(8,128)(2,1)} %q_hbm.1, bf16[128,2,128,128]{3,2,1,0:T(8,128)(2,1)} %k_hbm.1, bf16[128,2,128,128]{3,2,1,0:T(8,128)(2,1)} %v_hbm.1, ...), custom_call_target="tpu_custom_call" | custom-call | flops 1 | bytes 1 | tf_op jit(solution)/shard_map/attend/pallas_call | solution.py:204
  15.9 0.0 collective-permute-done.refs_3_
  15.9 0.6 %collective-permute-done.1.refs_4_ = bf16[128,2048]{1,0:T(8,128)(2,1)S(1)} collective-permute-done((bf16[128,2048]{1,0:T(8,128)(2,1)}, bf16[128,2048]{1,0:T(8,128)(2,1)S(1)}, u32[]{:S(2)}, u32[]{:S(2)}) %collective-permute-start.1) | collective-permute-done | bytes 524320 | tf_op jit(solution)/shard_map/ppermute | solution.py:424
  16.5 1.6 %collective-permute-start.2 = (bf16[128,1024]{1,0:T(8,128)(2,1)}, bf16[128,1024]{1,0:T(8,128)(2,1)S(1)}, u32[]{:S(2)}, u32[]{:S(2)}) collective-permute-start(bf16[128,1024]{1,0:T(8,128)(2,1)} %get-tuple-element.35), channel_id=1, source_target_pairs={{0,1},{1,0},{2,3},{3,2},{4,5},{5,4},{6,7},{7,6},{8,9},{9,8},{10,11... | collective-permute-start | bytes 786440 | tf_op jit(solution)/shard_map/ppermute | solution.py:424
  18.1 1.6 %collective-permute-start.3 = (bf16[64,2048]{1,0:T(8,128)(2,1)S(1)}, bf16[64,2048]{1,0:T(8,128)(2,1)S(1)}, u32[]{:S(2)}, u32[]{:S(2)}) collective-permute-start(bf16[64,2048]{1,0:T(8,128)(2,1)S(1)} %slice.6), channel_id=1, source_target_pairs={{0,16},{4,20},{8,24},{12,28},{16,0},{20,4},{24,8},{28,12},{1,17},{... | collective-permute-start | bytes 786440 | tf_op jit(solution)/shard_map/ppermute | solution.py:424
  19.7 0.6 %collective-permute-start.4 = (bf16[64,2048]{1,0:T(8,128)(2,1)S(1)}, bf16[64,2048]{1,0:T(8,128)(2,1)S(1)}, u32[]{:S(2)}, u32[]{:S(2)}) collective-permute-start(bf16[64,2048]{1,0:T(8,128)(2,1)S(1)} %slice.7), channel_id=1, source_target_pairs={{0,8},{4,12},{8,0},{12,4},{16,24},{20,28},{24,16},{28,20},{1,9},{5... | collective-permute-start | bytes 786440 | tf_op jit(solution)/shard_map/ppermute | solution.py:424
  20.3 0.4 collective-permute-start.6
  20.8 1.1 %copy-done = bf16[144,2048]{1,0:T(8,128)(2,1)S(1)} copy-done((bf16[144,2048]{1,0:T(8,128)(2,1)S(1)}, bf16[144,2048]{1,0:T(8,128)(2,1)}, u32[]{:S(2)}) %copy-start) | copy-done | bytes 589848
  21.9 4.1 %project.1 = (bf16[128,1024]{1,0:T(8,128)(2,1)S(1)}, bf16[128,1024]{1,0:T(8,128)(2,1)S(1)}) custom-call(s32[1]{0:T(128)} %bitcast.1.me_ref, bf16[144,2048]{1,0:T(8,128)(2,1)S(1)} %copy-done, bf16[2048,4096]{1,0:T(8,128)(2,1)} %w_ref.3), custom_call_target="tpu_custom_call" | custom-call | flops 1 | bytes 1 | tf_op jit(solution)/shard_map/project/pallas_call | solution.py:247
  26.0 0.0 collective-permute-done.2
  26.0 0.7 %collective-permute-done.3.refs_5_ = bf16[64,2048]{1,0:T(8,128)(2,1)S(1)} collective-permute-done((bf16[64,2048]{1,0:T(8,128)(2,1)S(1)}, bf16[64,2048]{1,0:T(8,128)(2,1)S(1)}, u32[]{:S(2)}, u32[]{:S(2)}) %collective-permute-start.3) | collective-permute-done | bytes 262176 | tf_op jit(solution)/shard_map/ppermute | solution.py:424
  26.6 1.3 %collective-permute-done.4.refs_6_ = bf16[64,2048]{1,0:T(8,128)(2,1)S(1)} collective-permute-done((bf16[64,2048]{1,0:T(8,128)(2,1)S(1)}, bf16[64,2048]{1,0:T(8,128)(2,1)S(1)}, u32[]{:S(2)}, u32[]{:S(2)}) %collective-permute-start.4) | collective-permute-done | bytes 262176 | tf_op jit(solution)/shard_map/ppermute | solution.py:424
  28.0 0.5 collective-permute-start.10
  28.5 1.5 %collective-permute-start.11 = (bf16[128,1024]{1,0:T(8,128)(2,1)S(1)}, bf16[128,1024]{1,0:T(8,128)(2,1)S(1)}, u32[]{:S(2)}, u32[]{:S(2)}) collective-permute-start(bf16[128,1024]{1,0:T(8,128)(2,1)S(1)} %bitcast.13), channel_id=1, source_target_pairs={{0,24},{4,28},{8,16},{12,20},{16,8},{20,12},{24,0},{28,4},{1,25},{... | collective-permute-start | bytes 786440 | tf_op jit(solution)/shard_map/ppermute | solution.py:424
  30.0 1.5 %collective-permute-start.9 = (bf16[128,1024]{1,0:T(8,128)(2,1)S(1)}, bf16[128,1024]{1,0:T(8,128)(2,1)S(1)}, u32[]{:S(2)}, u32[]{:S(2)}) collective-permute-start(bf16[128,1024]{1,0:T(8,128)(2,1)S(1)} %bitcast.14), channel_id=1, source_target_pairs={{0,8},{4,12},{8,0},{12,4},{16,24},{20,28},{24,16},{28,20},{1,9},{5... | collective-permute-start | bytes 786440 | tf_op jit(solution)/shard_map/ppermute | solution.py:424
  31.5 2.5 %low_rank.1 = (bf16[64,256]{1,0:T(8,128)(2,1)S(1)}, s32[8,256]{1,0:T(8,128)S(1)}) custom-call(s32[1]{0:T(128)} %bitcast.7.here_ref, bf16[144,2048]{1,0:T(8,128)(2,1)S(1)} %copy-done, bf16[144,2048]{1,0:T(8,128)(2,1)S(1)} %collective-permute-done.5.refs_1_, bf16[128,2048]{1,0:T(8,128)(2,1)S(1)} %bitcast.11, ...), custom_call_target="tpu_custom_call" | custom-call | flops 1 | bytes 1 | tf_op jit(solution)/shard_map/low_rank/pallas_call | solution.py:329
  34.0 0.0 collective-permute-done.6.refs_0_
  34.0 2.7 %collective-permute-start.7 = (bf16[64,256]{1,0:T(8,128)(2,1)S(1)}, bf16[64,256]{1,0:T(8,128)(2,1)S(1)}, u32[]{:S(2)}, u32[]{:S(2)}) collective-permute-start(bf16[64,256]{1,0:T(8,128)(2,1)S(1)} %get-tuple-element.49), channel_id=1, source_target_pairs={{0,2},{1,3},{2,0},{3,1},{4,6},{5,7},{6,4},{7,5},{8,10},{9,11},{10,... | collective-permute-start | bytes 98312 | tf_op jit(solution)/shard_map/ppermute | solution.py:424
  36.7 0.1 add_convert_fusion
  36.7 0.4 collective-permute-start.12
  37.1 7.7 %collective-permute-done.7 = bf16[64,256]{1,0:T(8,128)(2,1)S(1)} collective-permute-done((bf16[64,256]{1,0:T(8,128)(2,1)S(1)}, bf16[64,256]{1,0:T(8,128)(2,1)S(1)}, u32[]{:S(2)}, u32[]{:S(2)}) %collective-permute-start.7) | collective-permute-done | bytes 32800 | tf_op jit(solution)/shard_map/ppermute | solution.py:424
  44.9 0.1 collective-permute-start.8
  44.9 5.5 %collective-permute-done.8 = bf16[64,256]{1,0:T(8,128)(2,1)S(1)} collective-permute-done((bf16[64,256]{1,0:T(8,128)(2,1)S(1)}, bf16[64,256]{1,0:T(8,128)(2,1)S(1)}, u32[]{:S(2)}, u32[]{:S(2)}) %collective-permute-start.8) | collective-permute-done | bytes 32800 | tf_op jit(solution)/shard_map/ppermute | solution.py:424
  50.5 0.0 collective-permute-done.10.refs_2_
  50.5 0.0 collective-permute-done.11.refs_3_
  50.5 0.7 %correct.1 = (bf16[128,1024]{1,0:T(8,128)(2,1)S(1)}, bf16[128,1024]{1,0:T(8,128)(2,1)S(1)}) custom-call(s32[1]{0:T(128)} %bitcast.7.here_ref, s32[8,256]{1,0:T(8,128)S(1)} %get-tuple-element.48.adapters_ref, bf16[64,256]{1,0:T(8,128)(2,1)S(1)} %add_convert_fusion.1.low_ref, bf16[128,1024]{1,0:T(8,128)(2,1)S(1)} %bitcast.15, ...), custom_call_target="tpu_custom_call" | custom-call | flops 1 | bytes 1 | tf_op jit(solution)/shard_map/correct/pallas_call | solution.py:380
  51.2 0.0 collective-permute-done.12.refs_1_
  51.2 0.1 collective-permute-start.13
  51.3 1.5 %collective-permute-done.13.refs_3_ = bf16[128,1024]{1,0:T(8,128)(2,1)S(1)} collective-permute-done((bf16[128,1024]{1,0:T(8,128)(2,1)S(1)}, bf16[128,1024]{1,0:T(8,128)(2,1)S(1)}, u32[]{:S(2)}, u32[]{:S(2)}) %collective-permute-start.13) | collective-permute-done | bytes 262176 | tf_op jit(solution)/shard_map/ppermute | solution.py:424
  52.8 1.0 %finish.1 = bf16[128,1024]{1,0:T(8,128)(2,1)} custom-call(s32[1,128]{1,0:T(1,128)S(1)} %bitcast.16, bf16[128,1024]{1,0:T(8,128)(2,1)S(1)} %get-tuple-element.33.own_ref, bf16[128,1024]{1,0:T(8,128)(2,1)S(1)} %collective-permute-done.6.refs_0_, bf16[128,1024]{1,0:T(8,128)(2,1)S(1)} %collective-permute-done.12.refs_1_, ...), custom_call_target="tpu_custom_call" | custom-call | flops 1 | bytes 1 | tf_op jit(solution)/shard_map/finish/pallas_call | solution.py:411
  (14 shorter events, 0.1 us)
Async XLA Ops:
  0.0 15.9 %collective-permute-start = (bf16[128,2048]{1,0:T(8,128)(2,1)}, bf16[128,2048]{1,0:T(8,128)(2,1)S(1)}, u32[]{:S(2)}, u32[]{:S(2)}) collective-permute-start(bf16[128,2048]{1,0:T(8,128)(2,1)} %bitcast.9), channel_id=1, source_target_pairs={{0,8},{4,12},{8,0},{12,4},{16,24},{20,28},{24,16},{28,20},{1,9},{5... | collective-permute-start | bytes 1572872 | tf_op jit(solution)/shard_map/ppermute | solution.py:424
  2.9 13.6 %collective-permute-start.1 = (bf16[128,2048]{1,0:T(8,128)(2,1)}, bf16[128,2048]{1,0:T(8,128)(2,1)S(1)}, u32[]{:S(2)}, u32[]{:S(2)}) collective-permute-start(bf16[128,2048]{1,0:T(8,128)(2,1)} %bitcast.10), channel_id=1, source_target_pairs={{0,16},{4,20},{8,24},{12,28},{16,0},{20,4},{24,8},{28,12},{1,17},{... | collective-permute-start | bytes 1572872 | tf_op jit(solution)/shard_map/ppermute | solution.py:424
  16.5 14.9 %collective-permute-start.5 = (bf16[144,2048]{1,0:T(8,128)(2,1)}, bf16[144,2048]{1,0:T(8,128)(2,1)S(1)}, u32[]{:S(2)}, u32[]{:S(2)}) collective-permute-start(bf16[144,2048]{1,0:T(8,128)(2,1)} %get-tuple-element.39.a_hbm.refs_0_), channel_id=1, source_target_pairs={{0,4},{4,0},{8,12},{12,8},{16,20},{20,16},{24,28},{28,24},{1,5},{5... | collective-permute-start | bytes 1769480 | tf_op jit(solution)/shard_map/ppermute | solution.py:424
  16.5 9.4 %collective-permute-start.2 = (bf16[128,1024]{1,0:T(8,128)(2,1)}, bf16[128,1024]{1,0:T(8,128)(2,1)S(1)}, u32[]{:S(2)}, u32[]{:S(2)}) collective-permute-start(bf16[128,1024]{1,0:T(8,128)(2,1)} %get-tuple-element.35), channel_id=1, source_target_pairs={{0,1},{1,0},{2,3},{3,2},{4,5},{5,4},{6,7},{7,6},{8,9},{9,8},{10,11... | collective-permute-start | bytes 786440 | tf_op jit(solution)/shard_map/ppermute | solution.py:424
  18.1 8.5 %collective-permute-start.3 = (bf16[64,2048]{1,0:T(8,128)(2,1)S(1)}, bf16[64,2048]{1,0:T(8,128)(2,1)S(1)}, u32[]{:S(2)}, u32[]{:S(2)}) collective-permute-start(bf16[64,2048]{1,0:T(8,128)(2,1)S(1)} %slice.6), channel_id=1, source_target_pairs={{0,16},{4,20},{8,24},{12,28},{16,0},{20,4},{24,8},{28,12},{1,17},{... | collective-permute-start | bytes 786440 | tf_op jit(solution)/shard_map/ppermute | solution.py:424
  19.7 8.2 %collective-permute-start.4 = (bf16[64,2048]{1,0:T(8,128)(2,1)S(1)}, bf16[64,2048]{1,0:T(8,128)(2,1)S(1)}, u32[]{:S(2)}, u32[]{:S(2)}) collective-permute-start(bf16[64,2048]{1,0:T(8,128)(2,1)S(1)} %slice.7), channel_id=1, source_target_pairs={{0,8},{4,12},{8,0},{12,4},{16,24},{20,28},{24,16},{28,20},{1,9},{5... | collective-permute-start | bytes 786440 | tf_op jit(solution)/shard_map/ppermute | solution.py:424
  20.3 13.7 %collective-permute-start.6 = (bf16[128,1024]{1,0:T(8,128)(2,1)}, bf16[128,1024]{1,0:T(8,128)(2,1)S(1)}, u32[]{:S(2)}, u32[]{:S(2)}) collective-permute-start(bf16[128,1024]{1,0:T(8,128)(2,1)} %get-tuple-element.46), channel_id=1, source_target_pairs={{0,1},{1,0},{2,3},{3,2},{4,5},{5,4},{6,7},{7,6},{8,9},{9,8},{10,11... | collective-permute-start | bytes 786440 | tf_op jit(solution)/shard_map/ppermute | solution.py:424
  20.8 1.1 %copy-start = (bf16[144,2048]{1,0:T(8,128)(2,1)S(1)}, bf16[144,2048]{1,0:T(8,128)(2,1)}, u32[]{:S(2)}) copy-start(bf16[144,2048]{1,0:T(8,128)(2,1)} %get-tuple-element.39.a_hbm.refs_0_) | copy-start | bytes 1769476
  21.9 6.1 %copy-start.2 = (bf16[2,64,1024]{2,1,0:T(8,128)(2,1)S(1)}, bf16[2,64,1024]{2,1,0:T(8,128)(2,1)}, u32[]{:S(2)}) copy-start(bf16[2,64,1024]{2,1,0:T(8,128)(2,1)} %param.23) | copy-start | bytes 786436
  21.9 9.6 %copy-start.1 = (bf16[2,2048,64]{1,2,0:T(8,128)(2,1)S(1)}, bf16[2,2048,64]{1,2,0:T(8,128)(2,1)}, u32[]{:S(2)}) copy-start(bf16[2,2048,64]{1,2,0:T(8,128)(2,1)} %param.22) | copy-start | bytes 1572868
  21.9 31.0 %copy-start.3 = (s32[128]{0:T(128)S(1)}, s32[128]{0:T(128)}, u32[]{:S(2)}) copy-start(s32[128]{0:T(128)} %param.18) | copy-start | bytes 1540
  28.0 22.5 %collective-permute-start.10 = (bf16[128,1024]{1,0:T(8,128)(2,1)S(1)}, bf16[128,1024]{1,0:T(8,128)(2,1)S(1)}, u32[]{:S(2)}, u32[]{:S(2)}) collective-permute-start(bf16[128,1024]{1,0:T(8,128)(2,1)S(1)} %bitcast.12), channel_id=1, source_target_pairs={{0,16},{4,20},{8,24},{12,28},{16,0},{20,4},{24,8},{28,12},{1,17},{... | collective-permute-start | bytes 786440 | tf_op jit(solution)/shard_map/ppermute | solution.py:424
  28.5 22.0 %collective-permute-start.11 = (bf16[128,1024]{1,0:T(8,128)(2,1)S(1)}, bf16[128,1024]{1,0:T(8,128)(2,1)S(1)}, u32[]{:S(2)}, u32[]{:S(2)}) collective-permute-start(bf16[128,1024]{1,0:T(8,128)(2,1)S(1)} %bitcast.13), channel_id=1, source_target_pairs={{0,24},{4,28},{8,16},{12,20},{16,8},{20,12},{24,0},{28,4},{1,25},{... | collective-permute-start | bytes 786440 | tf_op jit(solution)/shard_map/ppermute | solution.py:424
  30.0 20.5 %collective-permute-start.9 = (bf16[128,1024]{1,0:T(8,128)(2,1)S(1)}, bf16[128,1024]{1,0:T(8,128)(2,1)S(1)}, u32[]{:S(2)}, u32[]{:S(2)}) collective-permute-start(bf16[128,1024]{1,0:T(8,128)(2,1)S(1)} %bitcast.14), channel_id=1, source_target_pairs={{0,8},{4,12},{8,0},{12,4},{16,24},{20,28},{24,16},{28,20},{1,9},{5... | collective-permute-start | bytes 786440 | tf_op jit(solution)/shard_map/ppermute | solution.py:424
  34.0 10.8 %collective-permute-start.7 = (bf16[64,256]{1,0:T(8,128)(2,1)S(1)}, bf16[64,256]{1,0:T(8,128)(2,1)S(1)}, u32[]{:S(2)}, u32[]{:S(2)}) collective-permute-start(bf16[64,256]{1,0:T(8,128)(2,1)S(1)} %get-tuple-element.49), channel_id=1, source_target_pairs={{0,2},{1,3},{2,0},{3,1},{4,6},{5,7},{6,4},{7,5},{8,10},{9,11},{10,... | collective-permute-start | bytes 98312 | tf_op jit(solution)/shard_map/ppermute | solution.py:424
  36.7 14.5 %collective-permute-start.12 = (bf16[128,1024]{1,0:T(8,128)(2,1)S(1)}, bf16[128,1024]{1,0:T(8,128)(2,1)S(1)}, u32[]{:S(2)}, u32[]{:S(2)}) collective-permute-start(bf16[128,1024]{1,0:T(8,128)(2,1)S(1)} %add_convert_fusion), channel_id=1, source_target_pairs={{0,2},{1,3},{2,0},{3,1},{4,6},{5,7},{6,4},{7,5},{8,10},{9,11},{10,... | collective-permute-start | bytes 786440 | tf_op jit(solution)/shard_map/ppermute | solution.py:424
  44.9 5.6 %collective-permute-start.8 = (bf16[64,256]{1,0:T(8,128)(2,1)S(1)}, bf16[64,256]{1,0:T(8,128)(2,1)S(1)}, u32[]{:S(2)}, u32[]{:S(2)}) collective-permute-start(bf16[64,256]{1,0:T(8,128)(2,1)S(1)} %add_convert_fusion.2), channel_id=1, source_target_pairs={{0,1},{1,0},{2,3},{3,2},{4,5},{5,4},{6,7},{7,6},{8,9},{9,8},{10,11... | collective-permute-start | bytes 98312 | tf_op jit(solution)/shard_map/ppermute | solution.py:424
  51.2 1.6 %collective-permute-start.13 = (bf16[128,1024]{1,0:T(8,128)(2,1)S(1)}, bf16[128,1024]{1,0:T(8,128)(2,1)S(1)}, u32[]{:S(2)}, u32[]{:S(2)}) collective-permute-start(bf16[128,1024]{1,0:T(8,128)(2,1)S(1)} %get-tuple-element.56), channel_id=1, source_target_pairs={{0,4},{4,0},{8,12},{12,8},{16,20},{20,16},{24,28},{28,24},{1,5},{5... | collective-permute-start | bytes 786440 | tf_op jit(solution)/shard_map/ppermute | solution.py:424
